TPU v7x, 32 devices: a whole 2x2x4 slice. The times are simulated.
32 devices in a mesh: tile: 8 (over z, y), mem: 4 (over x, core).
Axes of the slice: x: 2, y: 2, z: 4, core: 2. Of those that a mesh axis runs over, the one named last changes fastest.
Arguments:
- field: bfloat16 [61, 128, 1024], P(None, 'tile'), may hold values from -6 to 6
- vert_filter: bfloat16 [1, 60, 60], replicated, may hold values from -1 to 1.5
- loc_filter: bfloat16 [1, 60, 60], replicated, may hold values from -1 to 1.5
- alpha_table: float32 [16], replicated, may hold values from 0 to 1
- xscale_idx: int32 [2, 1024], replicated, may hold values from 0 to 15
- yscale_idx: int32 [2, 128], replicated, may hold values from 0 to 15
- members: bfloat16 [4, 61, 128, 1024], P('mem', None, 'tile'), may hold values from -6 to 6
Outputs:
- product: bfloat16 [61, 128, 1024], P(None, ('tile', 'mem'))
All inputs are finite; a program needn't handle non-finite values.
Results may differ from a plain program's by a relative error of at most 0.0075.
Values may be sent and summed in bfloat16 or wider, within the bound.
No kernel may reach another device: no remote copies, remote signals or barrier semaphores. Data moves between devices by JAX's collectives and lax.ppermute only.
A program may use at most 128 MiB of HBM per device.

v0:
```python
import math

import jax
import jax.numpy as jnp
from jax import lax
from jax.sharding import PartitionSpec as P


def shortened(array):

    def short(part):
        return part.astype(jnp.bfloat16) if part.dtype == jnp.float32 else part

    return jax.tree.map(short, array)


def lookup(table, entries):
    hits = entries[..., None] == jnp.arange(table.shape[0])
    return jnp.sum(jnp.where(hits, table, 0.0), axis=-1)


def pick_var(var_hits, table):
    return jnp.sum(jnp.where(var_hits[:, :, None], table[None, :, :], 0), axis=1)


def combine(earlier, later):
    return (earlier[0] * later[0], later[0] * earlier[1] + later[1])


def first_order(values, coeff, gain):
    length, line_count = values.shape
    block_len = math.gcd(length, 16)
    block_count = length // block_len
    driven = (gain[None, :] * values).reshape(block_count, block_len, line_count)
    carry = jnp.zeros((block_count, line_count), jnp.float32)
    states = []
    for step in range(block_len):
        carry = coeff[None, :] * carry + driven[:, step]
        states.append(carry)
    within = jnp.stack(states, 1)
    block_ends = within[:, block_len - 1]
    decay_block = jnp.broadcast_to(coeff**block_len, block_ends.shape)
    inclusive = lax.associative_scan(combine, (decay_block, block_ends), axis=0)[1]
    entering = jnp.concatenate([jnp.zeros((1, line_count), jnp.float32), inclusive[:-1]], 0)
    exponents = jnp.arange(1, block_len + 1, dtype=jnp.float32)
    powers = jnp.power(coeff[None, :], exponents[:, None])
    return (within + powers[None] * entering[:, None]).reshape(length, line_count)


def recursive_lines(values, alpha, axis):
    moved = jnp.moveaxis(values, axis, 0)
    length = moved.shape[0]
    flat_lines = moved.reshape(length, -1)
    coeff = jnp.moveaxis(alpha, axis, 0)[0].reshape(-1)
    gain_fwd = jnp.sqrt(1.0 - coeff * coeff)
    gain_back = (1.0 - coeff * coeff) / jnp.sqrt(1.0 + coeff * coeff)
    forward = first_order(flat_lines, coeff, gain_fwd)
    backward = jnp.flip(first_order(jnp.flip(forward, 0), coeff, gain_back), 0)
    return jnp.moveaxis(backward.reshape(moved.shape), 0, axis)


def body(field, vert_filter, loc_filter, alpha_table, xscale_idx, yscale_idx, members):
    tile_count = lax.axis_size("tile")
    mem_count = lax.axis_size("mem")
    tile_index = lax.axis_index("tile")
    mem_index = lax.axis_index("mem")
    slab_count, col_dev, row_count = field.shape
    var3_count, level_count = (vert_filter.shape[0], vert_filter.shape[1])
    level_rows = var3_count * level_count
    var_total = xscale_idx.shape[0]
    member_count = members.shape[0] * mem_count
    group = (slab_count + mem_count - 1) // mem_count
    band = row_count // tile_count
    blocks = jnp.zeros((group * mem_count, slab_count), jnp.bfloat16)
    blocks = blocks.at[0:level_count, 0:level_count].set(vert_filter[0])
    flat_pos = jnp.arange(level_rows, slab_count)
    blocks = blocks.at[flat_pos, flat_pos].set(jnp.ones(flat_pos.shape, jnp.bfloat16))
    selector = lax.dynamic_slice_in_dim(blocks, mem_index * group, group, 0)
    flat_field = field.reshape(slab_count, col_dev * row_count)
    outgoing = jnp.dot(selector, flat_field, preferred_element_type=jnp.float32).astype(
        jnp.bfloat16
    )
    outgoing = outgoing.reshape(group, col_dev, row_count)
    incoming = lax.all_to_all(outgoing, "tile", split_axis=2, concat_axis=1, tiled=True)
    lines = jnp.swapaxes(incoming, 1, 2).astype(jnp.float32)
    slab_ids = mem_index * group + jnp.arange(group, dtype=jnp.int32)
    var_ids = jnp.where(
        slab_ids < level_rows, slab_ids // level_count, var3_count + slab_ids - level_rows
    )
    var_ids = jnp.minimum(var_ids, var_total - 1)
    var_hits = var_ids[:, None] == jnp.arange(var_total)[None, :]
    row_entries = lax.dynamic_slice_in_dim(xscale_idx, tile_index * band, band, 1)
    alpha_x = lookup(alpha_table, pick_var(var_hits, row_entries))
    smooth_x = recursive_lines(lines, alpha_x[:, :, None], 2)
    returned = lax.all_to_all(
        jnp.swapaxes(smooth_x, 1, 2).astype(jnp.bfloat16),
        "tile",
        split_axis=1,
        concat_axis=2,
        tiled=True,
    ).astype(jnp.float32)
    col_entries = lax.dynamic_slice_in_dim(yscale_idx, tile_index * col_dev, col_dev, 1)
    alpha_y = lookup(alpha_table, pick_var(var_hits, col_entries))
    static_slab = recursive_lines(returned, alpha_y[:, :, None], 2)
    field_wide = field.astype(jnp.float32)
    member = members[0].astype(jnp.float32)
    scaled = (member * field_wide).astype(jnp.bfloat16)
    stacked = scaled[:level_rows].reshape(var3_count, level_count, col_dev * row_count)
    mixed = jnp.einsum("vij,vjp->vip", loc_filter, stacked, preferred_element_type=jnp.float32)
    mixed = mixed.reshape(level_rows, col_dev, row_count)
    localized = jnp.concatenate([mixed, scaled[level_rows:].astype(jnp.float32)], 0)
    running = member * localized
    ens_term = running / (member_count - 1)
    static_all = lax.all_to_all(
        shortened(static_slab), "mem", split_axis=1, concat_axis=0, tiled=True
    ).astype(static_slab.dtype)
    ens_part = lax.psum_scatter(ens_term, "mem", scatter_dimension=1, tiled=True)
    return (static_all[:slab_count] + ens_part).astype(jnp.bfloat16)


def solution(mesh):
    return jax.shard_map(
        body,
        mesh=mesh,
        in_specs=(P(None, "tile", None), P(), P(), P(), P(), P(), P("mem", None, "tile", None)),
        out_specs=P(None, ("tile", "mem"), None),
        check_vma=False,
    )
```

profile of v0, /device:TPU:0, one launch (start us, length us, event | category | flops | bytes accessed | tf_op | source)
XLA Modules:
  0.0 119.7 jit_solution(2935384601061233049)
XLA Ops:
  6.5 1.7 %pad.205 = bf16[64,16,1024]{2,1,0:T(8,128)(2,1)S(1)} pad(bf16[61,16,1024]{2,1,0:T(8,128)(2,1)} %param.11, bf16[]{:T(256)} %constant.101.clone.1), padding=0_3x0_0x0_0 | pad | bytes 4096002
  8.3 1.2 %copy.485 = bf16[8,8,16,1024]{3,1,2,0:T(8,128)(2,1)S(1)} copy(bf16[8,8,16,1024]{3,2,1,0:T(8,128)(2,1)S(1)} %bitcast.488) | data formatting | bytes 4194304
  9.7 0.4 convolution_convert_fusion
  10.0 0.3 copy.486
  10.3 4.7 %copy.336 = bf16[16,16,1024]{1,0,2:T(8,128)(2,1)} copy(bf16[16,16,1024]{2,1,0:T(8,128)(2,1)S(1)} %bitcast.496) | data formatting | bytes 1048576 | tf_op jit(solution)/shard_map/reshape | solution.py:83
  15.1 6.6 %reshape.4013 = bf16[8,2,16384]{2,1,0:T(2,128)(2,1)} reshape(bf16[1024,16,16]{2,1,0:T(8,128)(2,1)} %bitcast.451) | data formatting | bytes 1048576
  21.6 7.3 %all-to-all-start = ((bf16[8,2,16384]{2,1,0:T(2,128)(2,1)}), bf16[8,2,16384]{2,1,0:T(2,128)(2,1)S(1)}, u32[]{:S(2)}, u32[]{:S(2)}) async-start(bf16[8,2,16384]{2,1,0:T(2,128)(2,1)} %reshape.4013), calls=%async_computation | async-start | bytes 1048576 | tf_op jit(solution)/shard_map/all_to_all | solution.py:84
  29.0 3.7 %fusion = bf16[61,16,1024]{2,0,1:T(8,128)(2,1)S(1)} fusion(bf16[61,16,1024]{2,1,0:T(8,128)(2,1)} %param.11, bf16[1,61,16,1024]{3,2,1,0:T(8,128)(2,1)S(1)} %copy-done.2), kind=kLoop, calls=%fused_computation.3 | loop fusion | flops 3997696 | bytes 5996544 | tf_op jit(solution)/shard_map/convert_element_type | solution.py:107
  32.8 1.1 copy.416
  33.9 0.3 slice_bitcast_fusion
  34.2 1.6 %convolution_bitcast_fusion = f32[60,16,1024]{2,0,1:T(8,128)S(1)} fusion(bf16[16,1024,60]{1,0,2:T(8,128)(2,1)S(1)} %slice_bitcast_fusion, bf16[1,60,60]{2,1,0:T(8,128)(2,1)S(1)} %copy-done), kind=kOutput, calls=%fused_computation.5 | convolution fusion | flops 117964800 | bytes 5905440 | tf_op jit(solution)/shard_map/vij,vjp->vip/dot_general | solution.py:109
  35.8 3.7 %fusion.1 = f32[61,16,1024]{2,0,1:T(8,128)} fusion(f32[1,16,1024]{2,0,1:T(1,128)S(1)} %slice_convert_fusion, f32[60,16,1024]{2,0,1:T(8,128)S(1)} %convolution_bitcast_fusion, bf16[1,61,16,1024]{3,2,1,0:T(8,128)(2,1)S(1)} %copy-done.2), kind=kLoop, calls=%fused_computation.4 | loop fusion | flops 3997696 | bytes 9994240 | tf_op jit(solution)/shard_map/div | solution.py:113
  39.6 0.7 constant_dynamic-slice_fusion
  40.5 0.2 broadcast_power_fusion
  40.7 2.7 %all-to-all-done = bf16[8,2,16384]{2,1,0:T(2,128)(2,1)S(1)} async-done(((bf16[8,2,16384]{2,1,0:T(2,128)(2,1)}), bf16[8,2,16384]{2,1,0:T(2,128)(2,1)S(1)}, u32[]{:S(2)}, u32[]{:S(2)}) %all-to-all-start) | async-done | bytes 524320 | tf_op jit(solution)/shard_map/all_to_all | solution.py:84
  43.4 4.1 %reshape.4014 = bf16[1024,16,16]{2,1,0:T(8,128)(2,1)} reshape(bf16[8,2,16384]{2,1,0:T(2,128)(2,1)S(1)} %all-to-all-done) | data formatting | bytes 1048576
  47.5 4.6 %copy.337 = bf16[16,16,1024]{2,1,0:T(8,128)(2,1)S(1)} copy(bf16[16,16,1024]{1,0,2:T(8,128)(2,1)} %bitcast.452) | data formatting | bytes 1048576 | tf_op jit(solution)/shard_map/all_to_all | solution.py:84
  52.3 0.2 copy.338
  52.5 0.6 copy.339
  53.2 0.2 reshape.3990
  53.4 0.9 fusion.91
  54.3 0.3 bitcast_add_fusion.1
  56.0 0.1 multiply_add_fusion.3
  56.1 0.6 copy.356
  56.7 0.4 rev.14
  57.3 0.9 fusion.90
  58.2 0.3 bitcast_add_fusion.33
  60.0 0.3 copy.373
  60.3 0.6 rev.15
  60.9 0.9 copy.488
  61.8 3.8 %all-to-all-start.1 = ((bf16[16,128,128]{2,0,1:T(8,128)(2,1)}), bf16[16,128,128]{2,0,1:T(8,128)(2,1)S(1)}, u32[]{:S(2)}, u32[]{:S(2)}) async-start(bf16[16,128,128]{2,0,1:T(8,128)(2,1)} %bitcast.40), calls=%async_computation.1 | async-start | bytes 1048576 | tf_op jit(solution)/shard_map/all_to_all | solution.py:95
  65.8 0.2 select_reduce_fusion.1
  66.3 13.7 %all-to-all-done.1 = bf16[16,128,128]{2,0,1:T(8,128)(2,1)S(1)} async-done(((bf16[16,128,128]{2,0,1:T(8,128)(2,1)}), bf16[16,128,128]{2,0,1:T(8,128)(2,1)S(1)}, u32[]{:S(2)}, u32[]{:S(2)}) %all-to-all-start.1) | async-done | bytes 524320 | tf_op jit(solution)/shard_map/all_to_all | solution.py:95
  80.0 0.1 copy.374
  80.2 4.9 %reshape.4012 = f32[64,16,256]{1,0,2:T(8,128)} reshape(f32[1024,16,16]{0,2,1:T(8,128)S(1)} %bitcast_bitcast_fusion.1) | data formatting | bytes 2097152 | tf_op jit(solution)/shard_map/reshape | solution.py:53
  85.2 6.3 %copy.419 = f32[64,16,256]{2,1,0:T(8,128)S(1)} copy(f32[64,16,256]{1,0,2:T(8,128)} %reshape.4012) | data formatting | bytes 2097152 | tf_op jit(solution)/shard_map/reshape | solution.py:53
  91.6 0.9 fusion.89
  93.8 0.1 multiply_add_fusion.1
  93.9 0.6 copy.393
  94.5 0.5 rev.16
  95.1 0.9 fusion.88
  97.4 0.3 copy.410
  97.7 0.6 rev.17
  98.3 0.2 copy.411
  98.5 0.3 copy.412
  98.8 11.4 %all_to_all.12 = bf16[16,16,1024]{2,0,1:T(8,128)(2,1)S(1)} all-to-all(bf16[16,16,1024]{2,0,1:T(8,128)(2,1)S(1)} %copy.412), channel_id=1, replica_groups=mesh['tile'=8,'mem'=4] {'mem'}, dimensions={1} | all-to-all | bytes 1048576 | tf_op jit(solution)/shard_map/all_to_all | solution.py:114
  110.3 1.4 %add_convert_fusion = bf16[61,4,1024]{2,0,1:T(8,128)(2,1)S(1)} fusion(f32[61,4,1024]{2,0,1:T(8,128)} %reduce-scatter.2.cloned.1.call-done, bf16[64,4,1024]{2,0,1:T(8,128)(2,1)S(1)} %bitcast.503), kind=kLoop, calls=%fused_computation.11 | loop fusion | flops 749568 | bytes 1998848 | tf_op jit(solution)/shard_map/convert_element_type | solution.py:118
  111.7 1.2 copy.418
  (252 shorter events, 5.9 us)
Async XLA Ops:
  6.5 27.6 %copy-start = (bf16[1,60,60]{2,1,0:T(8,128)(2,1)S(1)}, bf16[1,60,60]{2,1,0:T(8,128)(2,1)}, u32[]{:S(2)}) copy-start(bf16[1,60,60]{2,1,0:T(8,128)(2,1)} %param.13) | copy-start | bytes 21604
  8.3 1.2 %copy-start.3 = (bf16[1,60,60]{2,1,0:T(8,128)(2,1)S(1)}, bf16[1,60,60]{2,1,0:T(8,128)(2,1)}, u32[]{:S(2)}) copy-start(bf16[1,60,60]{2,1,0:T(8,128)(2,1)} %param.12) | copy-start | bytes 21604
  15.1 13.9 %copy-start.2 = (bf16[1,61,16,1024]{3,2,1,0:T(8,128)(2,1)S(1)}, bf16[1,61,16,1024]{3,2,1,0:T(8,128)(2,1)}, u32[]{:S(2)}) copy-start(bf16[1,61,16,1024]{3,2,1,0:T(8,128)(2,1)} %param.17) | copy-start | bytes 5996548
  21.6 21.8 %all-to-all-start = ((bf16[8,2,16384]{2,1,0:T(2,128)(2,1)}), bf16[8,2,16384]{2,1,0:T(2,128)(2,1)S(1)}, u32[]{:S(2)}, u32[]{:S(2)}) async-start(bf16[8,2,16384]{2,1,0:T(2,128)(2,1)} %reshape.4013), calls=%async_computation | async-start | bytes 1048576 | tf_op jit(solution)/shard_map/all_to_all | solution.py:84
  28.9 81.4 %reduce-scatter.2.cloned.1.call-start = ((), (), s32[]{:S(2)}) async-start(), calls=%async_computation.4 | async-start | bytes 5242880 | tf_op jit(solution)/shard_map/reduce_scatter | solution.py:117
  39.5 0.8 copy-start.4
  59.9 5.7 %copy-start.5 = (s32[2,128]{1,0:T(2,128)S(1)}, s32[2,128]{1,0:T(2,128)}, u32[]{:S(2)}) copy-start(s32[2,128]{1,0:T(2,128)} %param.16) | copy-start | bytes 3076
  61.8 18.2 %all-to-all-start.1 = ((bf16[16,128,128]{2,0,1:T(8,128)(2,1)}), bf16[16,128,128]{2,0,1:T(8,128)(2,1)S(1)}, u32[]{:S(2)}, u32[]{:S(2)}) async-start(bf16[16,128,128]{2,0,1:T(8,128)(2,1)} %bitcast.40), calls=%async_computation.1 | async-start | bytes 1048576 | tf_op jit(solution)/shard_map/all_to_all | solution.py:95
  98.8 14.0 %copy-start.1 = (bf16[1,60,60]{2,1,0:T(8,128)(2,1)S(1)}, bf16[1,60,60]{2,1,0:T(8,128)(2,1)}, u32[]{:S(2)}) copy-start(bf16[1,60,60]{2,1,0:T(8,128)(2,1)} %param.13) | copy-start | bytes 21604
Sparse Core Ops, SparseCore 0:
  39.7 45.8 reduce-scatter.1
where the time goes:
time: 120 us
  local copies, waits for them, and re-layouts  50.1 us (42%)
  waiting for transfers between devices  16.4 us (14%)
  between operations  15 us (12%)
  other arithmetic  13.6 us (11%)
  blocking collectives  11.4 us (10%)
  starting transfers between devices  11.1 us (9%)
  matrix products  2 us (2%)
    unnamed x23, local copies, waits for them, and re-layouts  15.1 us
    all_to_all x1, waiting for transfers between devices, body(): lax.all_to_all(jnp.swapaxes(smooth_x, 1, 2).astype(jnp.bfloat16), 'tile',...  13.7 us
    reshape x6, local copies, waits for them, and re-layouts, recursive_lines(): flat_lines = moved.reshape(length, -1)  12.3 us
    all_to_all x1, blocking collectives, body(): lax.all_to_all(shortened(static_slab), 'mem', split_axis=1, concat_axis=0...  11.4 us
    all_to_all x1, starting transfers between devices, body(): lax.all_to_all(outgoing, 'tile', split_axis=2, concat_axis=1, tiled=True)  7.28 us
    reshape x1, local copies, waits for them, and re-layouts, body(): outgoing = outgoing.reshape(group, col_dev, row_count)  4.7 us
    all_to_all x1, local copies, waits for them, and re-layouts, body(): lax.all_to_all(outgoing, 'tile', split_axis=2, concat_axis=1, tiled=True)  4.6 us
    all_to_all x1, starting transfers between devices, body(): lax.all_to_all(jnp.swapaxes(smooth_x, 1, 2).astype(jnp.bfloat16), 'tile',...  3.83 us
  transfers between devices with their start and end apart: 3, of which 2 were waited for; matrix products, arithmetic and copies ran while one was open for 40% of the time, Pallas kernels for 0%

commit v1 on v0

v1 whole, which is shorter than its diff:
```python
import functools

import jax
import jax.numpy as jnp
from jax import lax
from jax.experimental import pallas as pl
from jax.experimental.pallas import tpu as pltpu
from jax.sharding import PartitionSpec as P

F32, BF16 = jnp.float32, jnp.bfloat16
SUB = 16
LANES = 256
BLOCK = 256
MIB = 1 << 20


def iota(shape, dim):
    return lax.broadcasted_iota(jnp.int32, shape, dim)


def dot(left, right):
    return jnp.dot(left, right, preferred_element_type=F32)


def gain_of(alpha):
    rest = (1.0 - alpha) * (1.0 + alpha)
    return jnp.sqrt(rest) * rest / jnp.sqrt(1.0 + alpha * alpha)


def lookup(table_ref, entries):
    found = jnp.zeros(entries.shape, F32)
    for entry in range(table_ref.shape[0]):
        found = jnp.where(entries == entry, table_ref[entry], found)
    return found


def padded(slab_count):
    return -(-slab_count // (4 * SUB)) * 4 * SUB


def to_columns(perm, flat_ref, out_ref, cols):
    total = flat_ref.shape[0]
    wanted = out_ref.shape[0]
    step = SUB * cols
    for chunk in range(out_ref.shape[1] // SUB):
        depth = min(step, total - chunk * step)
        part = flat_ref[chunk * step : chunk * step + depth, :]
        moved = dot(perm[:, :depth], part)
        out_ref[:, chunk * SUB : (chunk + 1) * SUB, :] = moved.reshape(wanted, SUB, -1)


def columns_kernel(levels, table_ref, entries_ref, field_ref, ends_ref, own_ref, coef_ref, work, tail):
    cols, slabs, lanes = work.shape
    own_cols = own_ref.shape[0]
    mem = lax.axis_index("mem")
    shape = (SUB * cols, SUB * cols)
    out_row, in_row = iota(shape, 0), iota(shape, 1)
    hit = (out_row % SUB == in_row // cols) & (out_row // SUB == in_row % cols)
    to_columns(hit.astype(BF16), field_ref, work, cols)
    pair = lookup(table_ref, entries_ref[...])
    alpha = jnp.where(iota((slabs, lanes), 0) < levels, pair[0:1], pair[1:2])
    state = work[0]
    for col in range(1, cols):
        state = alpha * state + work[col]
        work[col] = state
    for col in range(cols - 2, -1, -1):
        state = alpha * state + work[col]
        work[col] = state
    gain = gain_of(alpha)
    tail[0] = gain * work[cols - 1]
    tail[1] = gain * state
    share = pl.ds(pl.multiple_of(mem * SUB, SUB), SUB)
    ends_ref[...] = tail[:, share, :].astype(BF16)
    own_ref[...] = work[pl.ds(mem * own_cols, own_cols)] * gain[None]
    square = pair * pair
    power, sums = jnp.ones_like(pair), jnp.zeros_like(pair)
    rights, geometric = [], []
    for _ in range(cols):
        power, sums = power * pair, sums * square + 1.0
        rights.append(power)
        geometric.append(sums)
    for col in range(cols):
        coef_ref[0, col] = rights[col] * geometric[cols - 1 - col]
        coef_ref[1, col] = rights[cols - 1 - col]


def columns_call(table, entries, flat_field, levels, cols, own_cols):
    total, rows = flat_field.shape
    slabs = padded(total // cols)
    return pl.pallas_call(
        functools.partial(columns_kernel, levels),
        name="columns",
        grid=(rows // LANES,),
        in_specs=[
            pl.BlockSpec(memory_space=pltpu.SMEM),
            pl.BlockSpec((2, LANES), lambda i: (0, i)),
            pl.BlockSpec((total, LANES), lambda i: (0, i)),
        ],
        out_specs=[
            pl.BlockSpec((2, SUB, LANES), lambda i: (0, 0, i)),
            pl.BlockSpec((own_cols, slabs, LANES), lambda i: (0, 0, i)),
            pl.BlockSpec((2, cols, 2, LANES), lambda i: (0, 0, 0, i)),
        ],
        out_shape=[
            jax.ShapeDtypeStruct((2, SUB, rows), BF16),
            jax.ShapeDtypeStruct((own_cols, slabs, rows), F32),
            jax.ShapeDtypeStruct((2, cols, 2, rows), F32),
        ],
        scratch_shapes=[
            pltpu.VMEM((cols, slabs, LANES), F32),
            pltpu.VMEM((2, slabs, LANES), F32),
        ],
        compiler_params=pltpu.CompilerParams(vmem_limit_bytes=32 * MIB),
        cost_estimate=pl.CostEstimate(flops=5 * 10**8, bytes_accessed=4 * MIB, transcendentals=0),
    )(table, entries, flat_field)


def spread(matrix, levels, slabs, row_slab, row_col, col_slab, col_col):
    rows, cols = row_slab.shape
    size = matrix.shape[0]
    left = (iota((rows, size), 1) == row_slab[:, :size]).astype(BF16)
    right = (iota((size, cols), 0) == col_slab[:size, :]).astype(BF16)
    inner = dot(left, matrix).astype(BF16)
    full = dot(inner, right)
    full = jnp.where((row_slab >= levels) & (row_slab == col_slab), 1.0, full)
    return jnp.where(row_col == col_col, full, 0.0).astype(BF16)


def ensemble_kernel(levels, cols, loc_ref, field_ref, mine_ref, other_ref, send_ref, keep_ref, field_w, mine_w, other_w):
    own_cols, slabs, lanes = keep_ref.shape
    mem = lax.axis_index("mem")
    core, chip = mem % 2, mem // 2
    shape = (2 * own_cols * SUB, cols * SUB)
    out_row, in_row = iota(shape, 0), iota(shape, 1)
    slot = out_row // SUB
    first = jnp.where(slot < own_cols, (2 * (1 - chip) + core) * own_cols, (2 * chip + core) * own_cols)
    hit = (out_row % SUB == in_row // cols) & (first + slot % own_cols == in_row % cols)
    perm = hit.astype(BF16)
    to_columns(perm, field_ref, field_w, cols)
    to_columns(perm, mine_ref, mine_w, cols)
    to_columns(perm, other_ref, other_w, cols)
    side = own_cols * slabs
    row, col = iota((side, side), 0), iota((side, side), 1)
    local = spread(loc_ref[...], levels, slabs, row % slabs, row // slabs, col % slabs, col // slabs)
    for half in range(2):
        part = slice(half * own_cols, (half + 1) * own_cols)
        field = field_w[part]
        total = None
        for member_w in (mine_w, other_w):
            member = member_w[part]
            scaled = (member * field).astype(BF16).reshape(side, lanes)
            term = member * dot(local, scaled).reshape(own_cols, slabs, lanes)
            total = term if total is None else total + term
        if half == 0:
            send_ref[...] = total.astype(BF16)
        else:
            keep_ref[...] = total


def ensemble_call(loc, flat_field, mine, other, levels, cols, own_cols):
    total, rows = flat_field.shape
    slabs = padded(total // cols)
    wide = pl.BlockSpec((total, LANES), lambda i: (0, i))
    out = pl.BlockSpec((own_cols, slabs, LANES), lambda i: (0, 0, i))
    return pl.pallas_call(
        functools.partial(ensemble_kernel, levels, cols),
        name="ensemble",
        grid=(rows // LANES,),
        in_specs=[pl.BlockSpec(loc.shape, lambda i: (0, 0)), wide, wide, wide],
        out_specs=[out, out],
        out_shape=[
            jax.ShapeDtypeStruct((own_cols, slabs, rows), BF16),
            jax.ShapeDtypeStruct((own_cols, slabs, rows), F32),
        ],
        scratch_shapes=[pltpu.VMEM((2 * own_cols, slabs, LANES), F32)] * 3,
        compiler_params=pltpu.CompilerParams(vmem_limit_bytes=32 * MIB),
        cost_estimate=pl.CostEstimate(flops=5 * 10**8, bytes_accessed=8 * MIB, transcendentals=0),
    )(loc, flat_field, mine, other)


def tables_kernel(levels, own_cols, col_dev, slabs, table_ref, entries_ref, vert_ref, mat_ref, coef_ref, vert_out):
    first = lax.axis_index("tile") * col_dev + lax.axis_index("mem") * own_cols
    count = 2 * own_cols
    alphas = [table_ref[entries_ref[var, first + col]] for var in range(2) for col in range(own_cols)]
    by_lane = jnp.zeros((1, 128), F32)
    by_row = jnp.zeros((count, 1), F32)
    for k, alpha in enumerate(alphas):
        by_lane = jnp.where(iota((1, 128), 1) == k, alpha, by_lane)
        by_row = jnp.where(iota((count, 1), 0) == k, alpha, by_row)

    def series(alpha, number):
        alpha = jnp.broadcast_to(alpha, number.shape)
        total, unit = jnp.zeros(number.shape, F32), jnp.ones(number.shape, F32)
        single, power, both = alpha, alpha * alpha, jnp.ones(number.shape, F32)
        for bit in range(BLOCK.bit_length()):
            here = (number >> bit) % 2 == 1
            total = jnp.where(here, unit + power * total, total)
            both = jnp.where(here, both * single, both)
            unit, single, power = unit * (1.0 + power), single * single, power * power
        return total, both

    down, _ = series(by_lane, BLOCK - iota((BLOCK, 128), 0))
    place = iota((count, BLOCK), 1)
    across, right = series(by_row, BLOCK - place)
    _, left = series(by_row, place + 1)
    coef_ref[0] = left * across
    coef_ref[1] = right
    coef_ref[2] = jnp.broadcast_to(right[:, 0:1], right.shape)
    coef_ref[3] = jnp.broadcast_to(left[:, 0:1] * across[:, 0:1], right.shape)
    far = jnp.abs(iota((BLOCK, BLOCK), 0) - iota((BLOCK, BLOCK), 1)).astype(F32)
    for k in range(count):
        alpha = by_row[k : k + 1]
        decay = jnp.exp(far * jnp.log(jnp.maximum(alpha, 1e-30)))
        reach = jnp.minimum(down[:, k : k + 1], across[k : k + 1])
        mat_ref[k] = (gain_of(alpha) * decay * reach).astype(BF16)
    shape = vert_out.shape
    row, col = iota(shape, 0), iota(shape, 1)
    vert_out[...] = spread(vert_ref[...], levels, slabs, row // 8, row % 8, col % slabs, col // slabs)


def tables_call(table, entries, vert, levels, own_cols, col_dev, slabs):
    count = 2 * own_cols
    smem = pl.BlockSpec(memory_space=pltpu.SMEM)
    return pl.pallas_call(
        functools.partial(tables_kernel, levels, own_cols, col_dev, slabs),
        name="tables",
        in_specs=[smem, smem, pl.BlockSpec(memory_space=pltpu.VMEM)],
        out_specs=[pl.BlockSpec(memory_space=pltpu.VMEM)] * 3,
        out_shape=[
            jax.ShapeDtypeStruct((count, BLOCK, BLOCK), BF16),
            jax.ShapeDtypeStruct((4, count, BLOCK), F32),
            jax.ShapeDtypeStruct((8 * slabs, own_cols * slabs), BF16),
        ],
        compiler_params=pltpu.CompilerParams(vmem_limit_bytes=32 * MIB),
        cost_estimate=pl.CostEstimate(flops=10**8, bytes_accessed=2 * MIB, transcendentals=0),
    )(table, entries, vert)


def along_rows(lines, matrix, coef):
    count, rows = lines.shape
    blocks = rows // BLOCK
    parts = jnp.concatenate([lines[:, b * BLOCK : (b + 1) * BLOCK] for b in range(blocks)], 0)
    local = dot(parts.astype(BF16), matrix)
    local = [local[b * count : (b + 1) * count] for b in range(blocks)]
    into, right, decay, turn = coef[0:1], coef[1:2], coef[2:3, 0:1], coef[3:4, 0:1]
    forward, state = [None], None
    for b in range(blocks - 1):
        end = local[b][:, BLOCK - 1 : BLOCK]
        state = end if state is None else decay * state + end
        forward.append(state)
    out, state = [None] * blocks, None
    for b in range(blocks - 1, -1, -1):
        piece = local[b]
        if forward[b] is not None:
            piece = piece + into * forward[b]
        if state is not None:
            piece = piece + right * state
        out[b] = piece
        if b:
            start = local[b][:, 0:1] + turn * forward[b]
            state = start if state is None else decay * state + start
    return out


def final_kernel(
    levels, scale, own_ref, coef_ref, mine_ref, core_ref, chip_ref, far_ref, mat_ref, row_coef_ref, vert_ref,
    keep_ref, came_ref, out_ref, carry, smooth, filt
):
    own_cols, slabs, rows = own_ref.shape
    mem = lax.axis_index("mem")
    for flip, ref in ((0, mine_ref), (1, core_ref), (2, chip_ref), (3, far_ref)):
        share = pl.ds(pl.multiple_of((mem ^ flip) * SUB, SUB), SUB)
        carry[:, share, :] = ref[...].astype(F32)
    top = levels // 8 * 8
    for col in range(own_cols):
        pair = coef_ref[:, mem * own_cols + col]
        is_level = iota((slabs, rows), 0) < levels
        from_left = jnp.where(is_level, pair[0, 0:1], pair[0, 1:2])
        from_right = jnp.where(is_level, pair[1, 0:1], pair[1, 1:2])
        smooth[col] = own_ref[col] + from_left * carry[0] + from_right * carry[1]
    for col in range(own_cols):
        lines = smooth[col]
        main = along_rows(lines, mat_ref[col], row_coef_ref[:, col])
        last = along_rows(lines[top : top + 8], mat_ref[own_cols + col], row_coef_ref[:, own_cols + col])
        for b, (piece, extra) in enumerate(zip(main, last)):
            place = slice(b * BLOCK, (b + 1) * BLOCK)
            filt[col * slabs : col * slabs + slabs, place] = piece
            filt[col * slabs + top : col * slabs + top + 8, place] = jnp.where(
                iota((8, BLOCK), 0) < levels - top, piece[top : top + 8], extra
            )
    shape = vert_ref.shape
    row, place = iota(shape, 0), iota(shape, 1)
    order = ((row // 8 == place % slabs) & (row % 8 == place // slabs)).astype(BF16)
    count = out_ref.shape[0]
    side = own_cols * slabs
    for start in range(0, rows, BLOCK):
        part = slice(start, start + BLOCK)
        static = filt[:, part]
        ens = (keep_ref[:, :, part] + came_ref[:, :, part].astype(F32)).reshape(side, BLOCK) * scale
        static_hi, ens_hi = static.astype(BF16), ens.astype(BF16)
        static_lo = (static - static_hi.astype(F32)).astype(BF16)
        ens_lo = (ens - ens_hi.astype(F32)).astype(BF16)
        total = dot(vert_ref[...], static_hi) + dot(vert_ref[...], static_lo) + dot(order, ens_hi) + dot(order, ens_lo)
        total = total.reshape(slabs, 8, BLOCK)
        out_ref[:, :, part] = total[:count, :own_cols].astype(BF16)


def final_call(slab_count, levels, scale, args):
    own_cols, slabs, rows = args[0].shape
    vmem = pl.BlockSpec(memory_space=pltpu.VMEM)
    return pl.pallas_call(
        functools.partial(final_kernel, levels, scale),
        name="final",
        in_specs=[vmem] * len(args),
        out_specs=vmem,
        out_shape=jax.ShapeDtypeStruct((slab_count, own_cols, rows), BF16),
        scratch_shapes=[
            pltpu.VMEM((2, slabs, rows), F32),
            pltpu.VMEM((own_cols, slabs, rows), F32),
            pltpu.VMEM((own_cols * slabs, rows), F32),
        ],
        compiler_params=pltpu.CompilerParams(vmem_limit_bytes=32 * MIB),
        cost_estimate=pl.CostEstimate(flops=10**9, bytes_accessed=6 * MIB, transcendentals=0),
    )(*args)


def tile_carries(ends, coef, levels, tile_count):
    tile, mem = lax.axis_index("tile"), lax.axis_index("mem")
    slab = mem * SUB + jnp.arange(SUB)[:, None]
    decay = jnp.where(slab < levels, coef[1, 0, 0], coef[1, 0, 1])
    turn = jnp.where(slab < levels, coef[0, 0, 0], coef[0, 0, 1])
    one, none = jnp.ones_like(decay), jnp.zeros_like(decay)
    from_left, from_right, turned = one, one, none
    left, right = none, none
    block = ends.astype(F32)
    span = 1
    while span < tile_count:
        sent = block.astype(BF16)
        came = lax.ppermute(sent, "tile", [(i, i ^ span) for i in range(tile_count)]).astype(F32)
        second = (tile // span) % 2 == 1
        lower = jnp.where(second, came, block)
        upper = jnp.where(second, block, came)
        bent = turn * lower[0] + upper[1]
        left = left + jnp.where(second, from_left * lower[0], 0.0)
        right = right + jnp.where(second, turned * lower[0], from_right * bent)
        block = jnp.stack([decay * lower[0] + upper[0], lower[1] + decay * bent])
        turned = jnp.where(second, turned * decay, turned + from_right * turn * decay)
        from_left = jnp.where(second, from_left * decay, from_left)
        from_right = jnp.where(second, from_right, from_right * decay)
        turn = turn * (1.0 + decay * decay)
        decay = decay * decay
        span *= 2
    return jnp.stack([left, right]).astype(BF16)


def body(field, vert_filter, loc_filter, alpha_table, xscale_idx, yscale_idx, members):
    tile_count, mem_count = lax.axis_size("tile"), lax.axis_size("mem")
    slab_count, cols, rows = field.shape
    levels = vert_filter.shape[1]
    own_cols = cols // mem_count
    slabs = padded(slab_count)

    def swap(array, flip):
        return lax.ppermute(array, "mem", [(i, i ^ flip) for i in range(mem_count)])

    flat_field = field.reshape(slab_count * cols, rows)
    mine = members.reshape(slab_count * cols, rows)
    other = swap(mine, 1)
    ends, own, coef = columns_call(alpha_table, xscale_idx, flat_field, levels, cols, own_cols)
    mats, row_coef, vert = tables_call(alpha_table, yscale_idx, vert_filter[0], levels, own_cols, cols, slabs)
    send, keep = ensemble_call(loc_filter[0], flat_field, mine, other, levels, cols, own_cols)
    came = swap(send, 2)
    carried = tile_carries(ends, coef, levels, tile_count)
    shares = [carried] + [swap(carried, flip) for flip in range(1, mem_count)]
    scale = 1.0 / (mem_count * members.shape[0] - 1)
    return final_call(slab_count, levels, scale, [own, coef, *shares, mats, row_coef, vert, keep, came])


def solution(mesh):
    return jax.shard_map(
        body,
        mesh=mesh,
        in_specs=(P(None, "tile", None), P(), P(), P(), P(), P(), P("mem", None, "tile", None)),
        out_specs=P(None, ("tile", "mem"), None),
        check_vma=False,
    )
```

time: 120 us -> 51.8 us (0.43)
  local copies, waits for them, and re-layouts: 50.1 us -> 7.02 us
  between operations: 15 us -> 0.23 us
  Pallas kernels: 0 us -> 12.4 us
  blocking collectives: 11.4 us -> 0 us
  other arithmetic: 13.6 us -> 4.34 us
  matrix products: 2 us -> 0 us
    reshape x7 -> x0, local copies, waits for them, and re-layouts: 17 us -> none  [the longest x6 12.3 us: recursive_lines(): flat_lines = moved.reshape(length, -1)]
    all_to_all x2 -> x0, waiting for transfers between devices: 16.4 us -> none  [the longest x1 13.7 us: body(): lax.all_to_all(jnp.swapaxes(smooth_x, 1, 2).astype(jnp.bfloat16), 'tile',...]
    ppermute x0 -> x8, waiting for transfers between devices: none -> 16.1 us  [the longest x3 8.31 us: tile_carries(): lax.ppermute(sent, 'tile', [(i, i ^ span) for i in range(tile_count)])]
    pallas_call x0 -> x4, Pallas kernels: none -> 12.4 us  [the longest x1 5.07 us: ensemble_call(): pl.pallas_call(functools.partial(ensemble_kernel, levels, cols), name='en...]
    all_to_all x1 -> x0, blocking collectives: 11.4 us -> none  [body(): lax.all_to_all(shortened(static_slab), 'mem', split_axis=1, concat_axis=0...]
    ppermute x0 -> x8, starting transfers between devices: none -> 11.3 us  [the longest x3 7.17 us: tile_carries(): lax.ppermute(sent, 'tile', [(i, i ^ span) for i in range(tile_count)])]
    all_to_all x2 -> x0, starting transfers between devices: 11.1 us -> none  [the longest x1 7.28 us: body(): lax.all_to_all(outgoing, 'tile', split_axis=2, concat_axis=1, tiled=True)]
    unnamed x23 -> x40, local copies, waits for them, and re-layouts: 15.1 us -> 7 us
  transfers between devices with their start and end apart: 3 -> 8, of which waited for: 2 -> 4; matrix products, arithmetic and copies ran while one was open for 40% -> 8% of each run, Pallas kernels for 0% -> 9%
where the time goes in v1:
time: 51.8 us; the launch traced here: 51.4 us
  waiting for transfers between devices  16.1 us (31%)
  Pallas kernels  12.4 us (24%)
  starting transfers between devices  11.3 us (22%)
  local copies, waits for them, and re-layouts  7.02 us (14%)
  other arithmetic  4.34 us (8%)
    ppermute x3, waiting for transfers between devices, tile_carries(): lax.ppermute(sent, 'tile', [(i, i ^ span) for i in range(tile_count)])  8.31 us
    ppermute x5, waiting for transfers between devices, swap(): return lax.ppermute(array, 'mem', [(i, i ^ flip) for i in range(mem_count)])  7.75 us
    ppermute x3, starting transfers between devices, tile_carries(): lax.ppermute(sent, 'tile', [(i, i ^ span) for i in range(tile_count)])  7.17 us
    unnamed x40, local copies, waits for them, and re-layouts  7 us
    pallas_call x1, Pallas kernels, ensemble_call(): pl.pallas_call(functools.partial(ensemble_kernel, levels, cols), name='en...  5.07 us
    ppermute x5, starting transfers between devices, swap(): return lax.ppermute(array, 'mem', [(i, i ^ flip) for i in range(mem_count)])  4.18 us
    pallas_call x1, Pallas kernels, columns_call(): pl.pallas_call(functools.partial(columns_kernel, levels), name='columns',...  2.8 us
    pallas_call x1, Pallas kernels, final_call(): pl.pallas_call(functools.partial(final_kernel, levels, scale), name='fina...  2.67 us
  transfers between devices with their start and end apart: 8, of which 4 were waited for; matrix products, arithmetic and copies ran while one was open for 8% of the time, Pallas kernels for 9%

profile of v1, /device:TPU:0, one launch (start us, length us, event | category | flops | bytes accessed | tf_op | source)
XLA Modules:
  0.0 51.4 jit_solution(10875518568813343644)
XLA Ops:
  0.0 0.5 collective-permute-start.6
  0.5 1.6 %copy-done = bf16[61,16,1024]{2,1,0:T(8,128)(2,1)S(1)} copy-done((bf16[61,16,1024]{2,1,0:T(8,128)(2,1)S(1)}, bf16[61,16,1024]{2,1,0:T(8,128)(2,1)}, u32[]{:S(2)}) %copy-start) | copy-done | bytes 1998872
  2.0 0.7 %copy-done.4 = s32[2,1024]{1,0:T(2,128)S(1)} copy-done((s32[2,1024]{1,0:T(2,128)S(1)}, s32[2,1024]{1,0:T(2,128)}, u32[]{:S(2)}) %copy-start.4) | copy-done | bytes 8216
  2.7 0.7 %copy-done.5 = f32[16]{0:T(128)S(1)} copy-done((f32[16]{0:T(128)S(1)}, f32[16]{0:T(128)}, u32[]{:S(2)}) %copy-start.5) | copy-done | bytes 88
  3.4 2.8 %columns.1 = (bf16[2,16,1024]{2,1,0:T(8,128)(2,1)S(1)}, f32[4,64,1024]{2,1,0:T(8,128)S(1)}, f32[2,16,2,1024]{3,2,1,0:T(2,128)S(1)}) custom-call(f32[16]{0:T(128)S(1)} %copy-done.5, s32[2,1024]{1,0:T(2,128)S(1)} %copy-done.4, bf16[976,1024]{1,0:T(8,128)(2,1)S(1)} %bitcast.8), custom_call_target="tpu_custom_call" | custom-call | flops 500000000 | bytes 4194304 | tf_op jit(solution)/shard_map/columns/pallas_call | solution.py:90
  6.2 2.6 %collective-permute-start = (bf16[2,16,1024]{2,1,0:T(8,128)(2,1)S(1)}, bf16[2,16,1024]{2,1,0:T(8,128)(2,1)}, u32[]{:S(2)}, u32[]{:S(2)}) collective-permute-start(bf16[2,16,1024]{2,1,0:T(8,128)(2,1)S(1)} %get-tuple-element.15), channel_id=1, source_target_pairs={{0,4},{4,0},{8,12},{12,8},{16,20},{20,16},{24,28},{28,24},{1,5},{5... | collective-permute-start | bytes 196616 | tf_op jit(solution)/shard_map/ppermute | solution.py:339
  8.8 2.8 %collective-permute-done = bf16[2,16,1024]{2,1,0:T(8,128)(2,1)} collective-permute-done((bf16[2,16,1024]{2,1,0:T(8,128)(2,1)S(1)}, bf16[2,16,1024]{2,1,0:T(8,128)(2,1)}, u32[]{:S(2)}, u32[]{:S(2)}) %collective-permute-start) | collective-permute-done | bytes 65568 | tf_op jit(solution)/shard_map/ppermute | solution.py:339
  11.6 0.9 %convert_select_fusion.2 = (f32[2,16,1024]{2,1,0:T(8,128)S(1)}, f32[2,16,1024]{2,1,0:T(8,128)S(1)}) fusion(bf16[2,16,1024]{2,1,0:T(8,128)(2,1)S(1)} %get-tuple-element.15, bf16[2,16,1024]{2,1,0:T(8,128)(2,1)} %collective-permute-done, pred[]{:T(512)S(6)} %eq.13), kind=kLoop, calls=%fused_computation.22 | loop fusion | flops 131072 | bytes 393217 | tf_op jit(solution)/shard_map/jit(_where)/select_n | solution.py:342
  12.5 0.0 copy-start.15
  12.5 0.6 %copy-done.15 = f32[2,16,1024]{2,1,0:T(8,128)} copy-done((f32[2,16,1024]{2,1,0:T(8,128)}, f32[2,16,1024]{2,1,0:T(8,128)S(1)}, u32[]{:S(2)}) %copy-start.15) | copy-done | bytes 131096
  13.1 0.1 fusion.43
  13.2 0.0 copy-start.19
  13.2 0.6 %copy-done.19 = f32[1,16,1024]{2,1,0:T(8,128)} copy-done((f32[1,16,1024]{2,1,0:T(8,128)}, f32[1,16,1024]{2,1,0:T(8,128)S(1)}, u32[]{:S(2)}) %copy-start.19) | copy-done | bytes 65560
  13.8 0.6 %fusion.14 = bf16[2,16,1024]{2,1,0:T(8,128)(2,1)} fusion(f32[1,16,1024]{2,1,0:T(8,128)S(1)} %get-tuple-element.24, f32[1,16,1024]{2,1,0:T(8,128)S(1)} %get-tuple-element.23), kind=kLoop, calls=%fused_computation.33 | loop fusion | flops 32768 | bytes 196608 | tf_op jit(solution)/shard_map/convert_element_type | solution.py:338
  14.5 1.8 %collective-permute-start.1 = (bf16[2,16,1024]{2,1,0:T(8,128)(2,1)}, bf16[2,16,1024]{2,1,0:T(8,128)(2,1)}, u32[]{:S(2)}, u32[]{:S(2)}) collective-permute-start(bf16[2,16,1024]{2,1,0:T(8,128)(2,1)} %fusion.14), channel_id=1, source_target_pairs={{0,8},{4,12},{8,0},{12,4},{16,24},{20,28},{24,16},{28,20},{1,9},{5... | collective-permute-start | bytes 196616 | tf_op jit(solution)/shard_map/ppermute | solution.py:339
  16.3 2.8 %collective-permute-done.1 = bf16[2,16,1024]{2,1,0:T(8,128)(2,1)} collective-permute-done((bf16[2,16,1024]{2,1,0:T(8,128)(2,1)}, bf16[2,16,1024]{2,1,0:T(8,128)(2,1)}, u32[]{:S(2)}, u32[]{:S(2)}) %collective-permute-start.1) | collective-permute-done | bytes 65568 | tf_op jit(solution)/shard_map/ppermute | solution.py:339
  19.1 0.9 %convert_select_fusion.1 = (f32[2,16,1024]{2,1,0:T(8,128)S(1)}, f32[2,16,1024]{2,1,0:T(8,128)S(1)}) fusion(bf16[2,16,1024]{2,1,0:T(8,128)(2,1)} %collective-permute-done.1, f32[1,16,1024]{2,1,0:T(8,128)} %copy-done.19, f32[1,16,1024]{2,1,0:T(8,128)S(1)} %get-tuple-element.23, pred[]{:T(512)S(6)} %eq.14), kind=kLoop, calls=%fused_computation.21 | loop fusion | flops 131072 | bytes 458753 | tf_op jit(solution)/shard_map/jit(_where)/select_n | solution.py:341
  20.0 0.0 copy-start.9
  20.0 0.6 %copy-done.9 = f32[2,16,1024]{2,1,0:T(8,128)} copy-done((f32[2,16,1024]{2,1,0:T(8,128)}, f32[2,16,1024]{2,1,0:T(8,128)S(1)}, u32[]{:S(2)}) %copy-start.9) | copy-done | bytes 131096
  20.6 0.1 fusion.41
  20.7 0.0 copy-start.13
  20.7 0.0 copy-start.11
  20.7 0.6 %copy-done.13 = f32[1,16,1024]{2,1,0:T(8,128)} copy-done((f32[1,16,1024]{2,1,0:T(8,128)}, f32[1,16,1024]{2,1,0:T(8,128)S(1)}, u32[]{:S(2)}) %copy-start.13) | copy-done | bytes 65560
  21.3 0.6 %fusion.11 = bf16[2,16,1024]{2,1,0:T(8,128)(2,1)} fusion(f32[1,16,1024]{2,1,0:T(8,128)S(1)} %get-tuple-element.21, f32[1,16,1024]{2,1,0:T(8,128)S(1)} %get-tuple-element.22), kind=kLoop, calls=%fused_computation.27 | loop fusion | flops 32768 | bytes 196608 | tf_op jit(solution)/shard_map/convert_element_type | solution.py:338
  22.0 2.8 %collective-permute-start.2 = (bf16[2,16,1024]{2,1,0:T(8,128)(2,1)}, bf16[2,16,1024]{2,1,0:T(8,128)(2,1)}, u32[]{:S(2)}, u32[]{:S(2)}) collective-permute-start(bf16[2,16,1024]{2,1,0:T(8,128)(2,1)} %fusion.11), channel_id=1, source_target_pairs={{0,16},{4,20},{8,24},{12,28},{16,0},{20,4},{24,8},{28,12},{1,17},{... | collective-permute-start | bytes 196616 | tf_op jit(solution)/shard_map/ppermute | solution.py:339
  24.8 2.7 %collective-permute-done.2 = bf16[2,16,1024]{2,1,0:T(8,128)(2,1)} collective-permute-done((bf16[2,16,1024]{2,1,0:T(8,128)(2,1)}, bf16[2,16,1024]{2,1,0:T(8,128)(2,1)}, u32[]{:S(2)}, u32[]{:S(2)}) %collective-permute-start.2) | collective-permute-done | bytes 65568 | tf_op jit(solution)/shard_map/ppermute | solution.py:339
  27.5 0.8 %convert_element_type.25 = f32[2,16,1024]{2,1,0:T(8,128)S(1)} convert(bf16[2,16,1024]{2,1,0:T(8,128)(2,1)} %collective-permute-done.2) | non-fusion elementwise | flops 32768 | bytes 196608 | tf_op jit(solution)/shard_map/convert_element_type | solution.py:339
  28.3 0.0 collective-permute-done.6.other_ref
  28.4 0.0 copy-start.2
  28.4 1.5 %copy-done.2 = bf16[1,61,16,1024]{3,2,1,0:T(8,128)(2,1)S(1)} copy-done((bf16[1,61,16,1024]{3,2,1,0:T(8,128)(2,1)S(1)}, bf16[1,61,16,1024]{3,2,1,0:T(8,128)(2,1)}, u32[]{:S(2)}) %copy-start.2) | copy-done | bytes 1998872
  29.9 0.0 copy-start.6
  29.9 0.0 copy-start.7
  30.0 0.0 copy-start.8
  30.0 5.1 %ensemble.1 = (bf16[4,64,1024]{2,1,0:T(8,128)(2,1)S(1)}, f32[4,64,1024]{2,1,0:T(8,128)S(1)}) custom-call(bf16[60,60]{1,0:T(8,128)(2,1)S(1)} %bitcast.12, bf16[976,1024]{1,0:T(8,128)(2,1)S(1)} %bitcast.9, bf16[976,1024]{1,0:T(8,128)(2,1)S(1)} %bitcast.11, bf16[976,1024]{1,0:T(8,128)(2,1)} %collective-permute-done.6.other_ref), custom_call_target="tpu_custom_call" | custom-call | flops 500000000 | bytes 8388608 | tf_op jit(solution)/shard_map/ensemble/pallas_call | solution.py:165
  35.0 1.8 %collective-permute-start.7 = (bf16[4,64,1024]{2,1,0:T(8,128)(2,1)S(1)}, bf16[4,64,1024]{2,1,0:T(8,128)(2,1)S(1)}, u32[]{:S(2)}, u32[]{:S(2)}) collective-permute-start(bf16[4,64,1024]{2,1,0:T(8,128)(2,1)S(1)} %get-tuple-element.20), channel_id=1, source_target_pairs={{0,2},{1,3},{2,0},{3,1},{4,6},{5,7},{6,4},{7,5},{8,10},{9,11},{10,... | collective-permute-start | bytes 1572872 | tf_op jit(solution)/shard_map/ppermute | solution.py:364
  36.9 0.0 copy-done.14
  36.9 0.1 fusion.18
  37.0 0.2 fusion.25
  37.2 0.1 collective-permute-start.3
  37.2 0.4 collective-permute-start.4
  37.6 1.5 %collective-permute-start.5 = (bf16[2,16,1024]{2,1,0:T(8,128)(2,1)S(1)}, bf16[2,16,1024]{2,1,0:T(8,128)(2,1)S(1)}, u32[]{:S(2)}, u32[]{:S(2)}) collective-permute-start(bf16[2,16,1024]{2,1,0:T(8,128)(2,1)S(1)} %pad_maximum_fusion.2.mine_ref), channel_id=1, source_target_pairs={{0,3},{1,2},{2,1},{3,0},{4,7},{5,6},{6,5},{7,4},{8,11},{9,10},{10,... | collective-permute-start | bytes 196616 | tf_op jit(solution)/shard_map/ppermute | solution.py:364
  39.1 0.0 copy-done.6
  39.1 1.8 %tables.1 = (bf16[8,256,256]{2,1,0:T(8,128)(2,1)S(1)}, f32[4,8,256]{2,1,0:T(8,128)S(1)}, bf16[512,256]{1,0:T(8,128)(2,1)S(1)}) custom-call(f32[16]{0:T(128)S(1)} %copy-done.6, s32[2,128]{1,0:T(2,128)S(1)} %copy-done.8, bf16[60,60]{1,0:T(8,128)(2,1)S(1)} %bitcast.13), custom_call_target="tpu_custom_call" | custom-call | flops 100000000 | bytes 2097152 | tf_op jit(solution)/shard_map/tables/pallas_call | solution.py:224
  40.9 0.0 collective-permute-done.3.core_ref
  40.9 7.7 %collective-permute-done.4.chip_ref = bf16[2,16,1024]{2,1,0:T(8,128)(2,1)S(1)} collective-permute-done((bf16[2,16,1024]{2,1,0:T(8,128)(2,1)S(1)}, bf16[2,16,1024]{2,1,0:T(8,128)(2,1)S(1)}, u32[]{:S(2)}, u32[]{:S(2)}) %collective-permute-start.4) | collective-permute-done | bytes 65568 | tf_op jit(solution)/shard_map/ppermute | solution.py:364
  48.7 0.0 collective-permute-done.5.far_ref
  48.7 0.0 collective-permute-done.7.came_ref
  48.7 2.7 %final.1 = bf16[61,4,1024]{2,1,0:T(4,128)(2,1)} custom-call(f32[4,64,1024]{2,1,0:T(8,128)S(1)} %get-tuple-element.13.own_ref, f32[2,16,2,1024]{3,2,1,0:T(2,128)S(1)} %get-tuple-element.14.coef_ref, bf16[2,16,1024]{2,1,0:T(8,128)(2,1)S(1)} %pad_maximum_fusion.2.mine_ref, bf16[2,16,1024]{2,1,0:T(8,128)(2,1)S(1)} %collective-permute-done.3.core_ref, ...), custom_call_target="tpu_custom_call" | custom-call | flops 1000000000 | bytes 6291456 | tf_op jit(solution)/shard_map/final/pallas_call | solution.py:311
  (24 shorter events, 0.1 us)
Async XLA Ops:
  0.0 28.3 %collective-permute-start.6 = (bf16[976,1024]{1,0:T(8,128)(2,1)}, bf16[976,1024]{1,0:T(8,128)(2,1)}, u32[]{:S(2)}, u32[]{:S(2)}) collective-permute-start(bf16[976,1024]{1,0:T(8,128)(2,1)} %bitcast.10), channel_id=1, source_target_pairs={{0,1},{1,0},{2,3},{3,2},{4,5},{5,4},{6,7},{7,6},{8,9},{9,8},{10,11... | collective-permute-start | bytes 5996552 | tf_op jit(solution)/shard_map/ppermute | solution.py:364
  0.5 1.6 %copy-start = (bf16[61,16,1024]{2,1,0:T(8,128)(2,1)S(1)}, bf16[61,16,1024]{2,1,0:T(8,128)(2,1)}, u32[]{:S(2)}) copy-start(bf16[61,16,1024]{2,1,0:T(8,128)(2,1)} %param.7) | copy-start | bytes 5996548
  2.0 0.7 %copy-start.4 = (s32[2,1024]{1,0:T(2,128)S(1)}, s32[2,1024]{1,0:T(2,128)}, u32[]{:S(2)}) copy-start(s32[2,1024]{1,0:T(2,128)} %entries_ref.2) | copy-start | bytes 24580
  2.7 0.7 %copy-start.5 = (f32[16]{0:T(128)S(1)}, f32[16]{0:T(128)}, u32[]{:S(2)}) copy-start(f32[16]{0:T(128)} %table_ref.3) | copy-start | bytes 196
  3.4 25.0 %copy-start.1 = (bf16[61,16,1024]{2,1,0:T(8,128)(2,1)S(1)}, bf16[61,16,1024]{2,1,0:T(8,128)(2,1)}, u32[]{:S(2)}) copy-start(bf16[61,16,1024]{2,1,0:T(8,128)(2,1)} %param.7) | copy-start | bytes 5996548
  3.4 25.0 %copy-start.3 = (bf16[1,60,60]{2,1,0:T(8,128)(2,1)S(1)}, bf16[1,60,60]{2,1,0:T(8,128)(2,1)}, u32[]{:S(2)}) copy-start(bf16[1,60,60]{2,1,0:T(8,128)(2,1)} %param.9) | copy-start | bytes 21604
  6.2 5.4 %collective-permute-start = (bf16[2,16,1024]{2,1,0:T(8,128)(2,1)S(1)}, bf16[2,16,1024]{2,1,0:T(8,128)(2,1)}, u32[]{:S(2)}, u32[]{:S(2)}) collective-permute-start(bf16[2,16,1024]{2,1,0:T(8,128)(2,1)S(1)} %get-tuple-element.15), channel_id=1, source_target_pairs={{0,4},{4,0},{8,12},{12,8},{16,20},{20,16},{24,28},{28,24},{1,5},{5... | collective-permute-start | bytes 196616 | tf_op jit(solution)/shard_map/ppermute | solution.py:339
  12.5 0.6 %copy-start.15 = (f32[2,16,1024]{2,1,0:T(8,128)}, f32[2,16,1024]{2,1,0:T(8,128)S(1)}, u32[]{:S(2)}) copy-start(f32[2,16,1024]{2,1,0:T(8,128)S(1)} %get-tuple-element.31) | copy-start | bytes 393220
  13.2 0.6 %copy-start.19 = (f32[1,16,1024]{2,1,0:T(8,128)}, f32[1,16,1024]{2,1,0:T(8,128)S(1)}, u32[]{:S(2)}) copy-start(f32[1,16,1024]{2,1,0:T(8,128)S(1)} %get-tuple-element.24) | copy-start | bytes 196612
  14.5 4.6 %collective-permute-start.1 = (bf16[2,16,1024]{2,1,0:T(8,128)(2,1)}, bf16[2,16,1024]{2,1,0:T(8,128)(2,1)}, u32[]{:S(2)}, u32[]{:S(2)}) collective-permute-start(bf16[2,16,1024]{2,1,0:T(8,128)(2,1)} %fusion.14), channel_id=1, source_target_pairs={{0,8},{4,12},{8,0},{12,4},{16,24},{20,28},{24,16},{28,20},{1,9},{5... | collective-permute-start | bytes 196616 | tf_op jit(solution)/shard_map/ppermute | solution.py:339
  20.0 0.7 %copy-start.9 = (f32[2,16,1024]{2,1,0:T(8,128)}, f32[2,16,1024]{2,1,0:T(8,128)S(1)}, u32[]{:S(2)}) copy-start(f32[2,16,1024]{2,1,0:T(8,128)S(1)} %get-tuple-element.29) | copy-start | bytes 393220
  20.0 2.0 %copy-start.17 = (f32[2,16,1024]{2,1,0:T(8,128)}, f32[2,16,1024]{2,1,0:T(8,128)S(1)}, u32[]{:S(2)}) copy-start(f32[2,16,1024]{2,1,0:T(8,128)S(1)} %get-tuple-element.30) | copy-start | bytes 393220
  20.7 0.6 %copy-start.13 = (f32[1,16,1024]{2,1,0:T(8,128)}, f32[1,16,1024]{2,1,0:T(8,128)S(1)}, u32[]{:S(2)}) copy-start(f32[1,16,1024]{2,1,0:T(8,128)S(1)} %get-tuple-element.22) | copy-start | bytes 196612
  20.7 7.6 %copy-start.11 = (f32[1,16,1024]{2,1,0:T(8,128)}, f32[1,16,1024]{2,1,0:T(8,128)S(1)}, u32[]{:S(2)}) copy-start(f32[1,16,1024]{2,1,0:T(8,128)S(1)} %get-tuple-element.21) | copy-start | bytes 196612
  22.0 5.5 %collective-permute-start.2 = (bf16[2,16,1024]{2,1,0:T(8,128)(2,1)}, bf16[2,16,1024]{2,1,0:T(8,128)(2,1)}, u32[]{:S(2)}, u32[]{:S(2)}) collective-permute-start(bf16[2,16,1024]{2,1,0:T(8,128)(2,1)} %fusion.11), channel_id=1, source_target_pairs={{0,16},{4,20},{8,24},{12,28},{16,0},{20,4},{24,8},{28,12},{1,17},{... | collective-permute-start | bytes 196616 | tf_op jit(solution)/shard_map/ppermute | solution.py:339
  28.4 1.6 %copy-start.2 = (bf16[1,61,16,1024]{3,2,1,0:T(8,128)(2,1)S(1)}, bf16[1,61,16,1024]{3,2,1,0:T(8,128)(2,1)}, u32[]{:S(2)}) copy-start(bf16[1,61,16,1024]{3,2,1,0:T(8,128)(2,1)} %param.13) | copy-start | bytes 5996548
  29.9 6.9 %copy-start.10 = (f32[2,16,1024]{2,1,0:T(8,128)S(1)}, f32[2,16,1024]{2,1,0:T(8,128)}, u32[]{:S(2)}) copy-start(f32[2,16,1024]{2,1,0:T(8,128)} %copy-done.9) | copy-start | bytes 393220
  29.9 6.9 %copy-start.12 = (f32[1,16,1024]{2,1,0:T(8,128)S(1)}, f32[1,16,1024]{2,1,0:T(8,128)}, u32[]{:S(2)}) copy-start(f32[1,16,1024]{2,1,0:T(8,128)} %copy-done.11) | copy-start | bytes 196612
  29.9 6.9 %copy-start.14 = (f32[1,16,1024]{2,1,0:T(8,128)S(1)}, f32[1,16,1024]{2,1,0:T(8,128)}, u32[]{:S(2)}) copy-start(f32[1,16,1024]{2,1,0:T(8,128)} %copy-done.13) | copy-start | bytes 196612
  29.9 7.0 %copy-start.16 = (f32[2,16,1024]{2,1,0:T(8,128)S(1)}, f32[2,16,1024]{2,1,0:T(8,128)}, u32[]{:S(2)}) copy-start(f32[2,16,1024]{2,1,0:T(8,128)} %copy-done.15) | copy-start | bytes 393220
  29.9 7.0 %copy-start.18 = (f32[2,16,1024]{2,1,0:T(8,128)S(1)}, f32[2,16,1024]{2,1,0:T(8,128)}, u32[]{:S(2)}) copy-start(f32[2,16,1024]{2,1,0:T(8,128)} %copy-done.17) | copy-start | bytes 393220
  29.9 9.2 %copy-start.6 = (f32[16]{0:T(128)S(1)}, f32[16]{0:T(128)}, u32[]{:S(2)}) copy-start(f32[16]{0:T(128)} %table_ref.3) | copy-start | bytes 196
  29.9 9.2 %copy-start.7 = (bf16[1,60,60]{2,1,0:T(8,128)(2,1)S(1)}, bf16[1,60,60]{2,1,0:T(8,128)(2,1)}, u32[]{:S(2)}) copy-start(bf16[1,60,60]{2,1,0:T(8,128)(2,1)} %param.8) | copy-start | bytes 21604
  30.0 9.1 %copy-start.8 = (s32[2,128]{1,0:T(2,128)S(1)}, s32[2,128]{1,0:T(2,128)}, u32[]{:S(2)}) copy-start(s32[2,128]{1,0:T(2,128)} %entries_ref.3) | copy-start | bytes 3076
  35.0 13.6 %collective-permute-start.7 = (bf16[4,64,1024]{2,1,0:T(8,128)(2,1)S(1)}, bf16[4,64,1024]{2,1,0:T(8,128)(2,1)S(1)}, u32[]{:S(2)}, u32[]{:S(2)}) collective-permute-start(bf16[4,64,1024]{2,1,0:T(8,128)(2,1)S(1)} %get-tuple-element.20), channel_id=1, source_target_pairs={{0,2},{1,3},{2,0},{3,1},{4,6},{5,7},{6,4},{7,5},{8,10},{9,11},{10,... | collective-permute-start | bytes 1572872 | tf_op jit(solution)/shard_map/ppermute | solution.py:364
  37.2 3.8 %collective-permute-start.3 = (bf16[2,16,1024]{2,1,0:T(8,128)(2,1)S(1)}, bf16[2,16,1024]{2,1,0:T(8,128)(2,1)S(1)}, u32[]{:S(2)}, u32[]{:S(2)}) collective-permute-start(bf16[2,16,1024]{2,1,0:T(8,128)(2,1)S(1)} %pad_maximum_fusion.2.mine_ref), channel_id=1, source_target_pairs={{0,1},{1,0},{2,3},{3,2},{4,5},{5,4},{6,7},{7,6},{8,9},{9,8},{10,11... | collective-permute-start | bytes 196616 | tf_op jit(solution)/shard_map/ppermute | solution.py:364
  37.2 11.5 %collective-permute-start.4 = (bf16[2,16,1024]{2,1,0:T(8,128)(2,1)S(1)}, bf16[2,16,1024]{2,1,0:T(8,128)(2,1)S(1)}, u32[]{:S(2)}, u32[]{:S(2)}) collective-permute-start(bf16[2,16,1024]{2,1,0:T(8,128)(2,1)S(1)} %pad_maximum_fusion.2.mine_ref), channel_id=1, source_target_pairs={{0,2},{1,3},{2,0},{3,1},{4,6},{5,7},{6,4},{7,5},{8,10},{9,11},{10,... | collective-permute-start | bytes 196616 | tf_op jit(solution)/shard_map/ppermute | solution.py:364
  37.6 11.1 %collective-permute-start.5 = (bf16[2,16,1024]{2,1,0:T(8,128)(2,1)S(1)}, bf16[2,16,1024]{2,1,0:T(8,128)(2,1)S(1)}, u32[]{:S(2)}, u32[]{:S(2)}) collective-permute-start(bf16[2,16,1024]{2,1,0:T(8,128)(2,1)S(1)} %pad_maximum_fusion.2.mine_ref), channel_id=1, source_target_pairs={{0,3},{1,2},{2,1},{3,0},{4,7},{5,6},{6,5},{7,4},{8,11},{9,10},{10,... | collective-permute-start | bytes 196616 | tf_op jit(solution)/shard_map/ppermute | solution.py:364

commit v2 on v1

--- a/solution.py
+++ b/solution.py
@@ -8,10 +8,12 @@
 from jax.sharding import PartitionSpec as P
 
 F32, BF16 = jnp.float32, jnp.bfloat16
+COL_BITS = 4
 SUB = 16
 LANES = 256
 BLOCK = 256
 MIB = 1 << 20
+VMEM = 32 * MIB
 
 
 def iota(shape, dim):
@@ -49,16 +51,8 @@
         out_ref[:, chunk * SUB : (chunk + 1) * SUB, :] = moved.reshape(wanted, SUB, -1)
 
 
-def columns_kernel(levels, table_ref, entries_ref, field_ref, ends_ref, own_ref, coef_ref, work, tail):
-    cols, slabs, lanes = work.shape
-    own_cols = own_ref.shape[0]
-    mem = lax.axis_index("mem")
-    shape = (SUB * cols, SUB * cols)
-    out_row, in_row = iota(shape, 0), iota(shape, 1)
-    hit = (out_row % SUB == in_row // cols) & (out_row // SUB == in_row % cols)
-    to_columns(hit.astype(BF16), field_ref, work, cols)
-    pair = lookup(table_ref, entries_ref[...])
-    alpha = jnp.where(iota((slabs, lanes), 0) < levels, pair[0:1], pair[1:2])
+def sweep(work, alpha):
+    cols = work.shape[0]
     state = work[0]
     for col in range(1, cols):
         state = alpha * state + work[col]
@@ -66,12 +60,60 @@
     for col in range(cols - 2, -1, -1):
         state = alpha * state + work[col]
         work[col] = state
+
+
+def transposer(cols):
+    shape = (SUB * cols, SUB * cols)
+    out_row, in_row = iota(shape, 0), iota(shape, 1)
+    hit = (out_row % SUB == in_row // cols) & (out_row // SUB == in_row % cols)
+    return hit.astype(BF16)
+
+
+def ends_kernel(levels, slab_count, mem_ref, table_ref, entries_ref, field_ref, ends_ref, work):
+    cols, _, lanes = work.shape
+    first = mem_ref[0] * SUB
+    shape = field_ref.shape
+    held = jnp.where(iota(shape, 0) // cols + first < slab_count, field_ref[...], 0)
+    work[...] = dot(transposer(cols), held).reshape(work.shape)
+    pair = lookup(table_ref, entries_ref[...])
+    alpha = jnp.where(iota((SUB, lanes), 0) + first < levels, pair[0:1], pair[1:2])
+    sweep(work, alpha)
     gain = gain_of(alpha)
-    tail[0] = gain * work[cols - 1]
-    tail[1] = gain * state
-    share = pl.ds(pl.multiple_of(mem * SUB, SUB), SUB)
-    ends_ref[...] = tail[:, share, :].astype(BF16)
-    own_ref[...] = work[pl.ds(mem * own_cols, own_cols)] * gain[None]
+    ends_ref[0] = (gain * work[cols - 1]).astype(BF16)
+    ends_ref[1] = (gain * work[0]).astype(BF16)
+
+
+def ends_call(mem, table, entries, flat_field, levels, cols):
+    total, rows = flat_field.shape
+    return pl.pallas_call(
+        functools.partial(ends_kernel, levels, total // cols),
+        name="ends",
+        grid_spec=pltpu.PrefetchScalarGridSpec(
+            num_scalar_prefetch=1,
+            grid=(rows // LANES,),
+            in_specs=[
+                pl.BlockSpec(memory_space=pltpu.SMEM),
+                pl.BlockSpec((2, LANES), lambda i, mem: (0, i)),
+                pl.BlockSpec((SUB * cols, LANES), lambda i, mem: (mem[0], i)),
+            ],
+            out_specs=pl.BlockSpec((2, SUB, LANES), lambda i, mem: (0, 0, i)),
+            scratch_shapes=[pltpu.VMEM((cols, SUB, LANES), F32)],
+        ),
+        out_shape=jax.ShapeDtypeStruct((2, SUB, rows), BF16),
+        compiler_params=pltpu.CompilerParams(vmem_limit_bytes=VMEM),
+        cost_estimate=pl.CostEstimate(flops=10**8, bytes_accessed=MIB, transcendentals=0),
+    )(mem, table, entries, flat_field)
+
+
+def local_kernel(levels, table_ref, entries_ref, field_ref, after_ref, own_ref, coef_ref, work):
+    cols, slabs, lanes = work.shape
+    own_cols = own_ref.shape[0]
+    mem = lax.axis_index("mem")
+    to_columns(transposer(cols), field_ref, work, cols)
+    pair = lookup(table_ref, entries_ref[...])
+    alpha = jnp.where(iota((slabs, lanes), 0) < levels, pair[0:1], pair[1:2])
+    sweep(work, alpha)
+    own_ref[...] = work[pl.ds(mem * own_cols, own_cols)] * gain_of(alpha)[None]
     square = pair * pair
     power, sums = jnp.ones_like(pair), jnp.zeros_like(pair)
     rights, geometric = [], []
@@ -84,35 +126,31 @@
         coef_ref[1, col] = rights[cols - 1 - col]
 
 
-def columns_call(table, entries, flat_field, levels, cols, own_cols):
+def local_call(table, entries, flat_field, after, levels, cols, own_cols):
     total, rows = flat_field.shape
     slabs = padded(total // cols)
     return pl.pallas_call(
-        functools.partial(columns_kernel, levels),
-        name="columns",
+        functools.partial(local_kernel, levels),
+        name="local",
         grid=(rows // LANES,),
         in_specs=[
             pl.BlockSpec(memory_space=pltpu.SMEM),
             pl.BlockSpec((2, LANES), lambda i: (0, i)),
             pl.BlockSpec((total, LANES), lambda i: (0, i)),
+            pl.BlockSpec(memory_space=pl.ANY),
         ],
         out_specs=[
-            pl.BlockSpec((2, SUB, LANES), lambda i: (0, 0, i)),
             pl.BlockSpec((own_cols, slabs, LANES), lambda i: (0, 0, i)),
             pl.BlockSpec((2, cols, 2, LANES), lambda i: (0, 0, 0, i)),
         ],
         out_shape=[
-            jax.ShapeDtypeStruct((2, SUB, rows), BF16),
             jax.ShapeDtypeStruct((own_cols, slabs, rows), F32),
             jax.ShapeDtypeStruct((2, cols, 2, rows), F32),
         ],
-        scratch_shapes=[
-            pltpu.VMEM((cols, slabs, LANES), F32),
-            pltpu.VMEM((2, slabs, LANES), F32),
-        ],
-        compiler_params=pltpu.CompilerParams(vmem_limit_bytes=32 * MIB),
+        scratch_shapes=[pltpu.VMEM((cols, slabs, LANES), F32)],
+        compiler_params=pltpu.CompilerParams(vmem_limit_bytes=VMEM),
         cost_estimate=pl.CostEstimate(flops=5 * 10**8, bytes_accessed=4 * MIB, transcendentals=0),
-    )(table, entries, flat_field)
+    )(table, entries, flat_field, after)
 
 
 def spread(matrix, levels, slabs, row_slab, row_col, col_slab, col_col):
@@ -126,7 +164,7 @@
     return jnp.where(row_col == col_col, full, 0.0).astype(BF16)
 
 
-def ensemble_kernel(levels, cols, loc_ref, field_ref, mine_ref, other_ref, send_ref, keep_ref, field_w, mine_w, other_w):
+def ensemble_kernel(levels, cols, loc_ref, field_ref, mine_ref, other_ref, after_ref, send_ref, keep_ref, field_w, mine_w, other_w):
     own_cols, slabs, lanes = keep_ref.shape
     mem = lax.axis_index("mem")
     core, chip = mem % 2, mem // 2
@@ -157,7 +195,7 @@
             keep_ref[...] = total
 
 
-def ensemble_call(loc, flat_field, mine, other, levels, cols, own_cols):
+def ensemble_call(loc, flat_field, mine, other, after, levels, cols, own_cols):
     total, rows = flat_field.shape
     slabs = padded(total // cols)
     wide = pl.BlockSpec((total, LANES), lambda i: (0, i))
@@ -166,19 +204,19 @@
         functools.partial(ensemble_kernel, levels, cols),
         name="ensemble",
         grid=(rows // LANES,),
-        in_specs=[pl.BlockSpec(loc.shape, lambda i: (0, 0)), wide, wide, wide],
+        in_specs=[pl.BlockSpec(loc.shape, lambda i: (0, 0)), wide, wide, wide, pl.BlockSpec(memory_space=pl.ANY)],
         out_specs=[out, out],
         out_shape=[
             jax.ShapeDtypeStruct((own_cols, slabs, rows), BF16),
             jax.ShapeDtypeStruct((own_cols, slabs, rows), F32),
         ],
         scratch_shapes=[pltpu.VMEM((2 * own_cols, slabs, LANES), F32)] * 3,
-        compiler_params=pltpu.CompilerParams(vmem_limit_bytes=32 * MIB),
+        compiler_params=pltpu.CompilerParams(vmem_limit_bytes=VMEM),
         cost_estimate=pl.CostEstimate(flops=5 * 10**8, bytes_accessed=8 * MIB, transcendentals=0),
-    )(loc, flat_field, mine, other)
-
-
-def tables_kernel(levels, own_cols, col_dev, slabs, table_ref, entries_ref, vert_ref, mat_ref, coef_ref, vert_out):
+    )(loc, flat_field, mine, other, after)
+
+
+def tables_kernel(levels, own_cols, col_dev, slabs, table_ref, entries_ref, vert_ref, after_ref, mat_ref, coef_ref, vert_out):
     first = lax.axis_index("tile") * col_dev + lax.axis_index("mem") * own_cols
     count = 2 * own_cols
     alphas = [table_ref[entries_ref[var, first + col]] for var in range(2) for col in range(own_cols)]
@@ -218,22 +256,22 @@
     vert_out[...] = spread(vert_ref[...], levels, slabs, row // 8, row % 8, col % slabs, col // slabs)
 
 
-def tables_call(table, entries, vert, levels, own_cols, col_dev, slabs):
+def tables_call(table, entries, vert, after, levels, own_cols, col_dev, slabs):
     count = 2 * own_cols
     smem = pl.BlockSpec(memory_space=pltpu.SMEM)
     return pl.pallas_call(
         functools.partial(tables_kernel, levels, own_cols, col_dev, slabs),
         name="tables",
-        in_specs=[smem, smem, pl.BlockSpec(memory_space=pltpu.VMEM)],
+        in_specs=[smem, smem, pl.BlockSpec(memory_space=pltpu.VMEM), pl.BlockSpec(memory_space=pl.ANY)],
         out_specs=[pl.BlockSpec(memory_space=pltpu.VMEM)] * 3,
         out_shape=[
             jax.ShapeDtypeStruct((count, BLOCK, BLOCK), BF16),
             jax.ShapeDtypeStruct((4, count, BLOCK), F32),
             jax.ShapeDtypeStruct((8 * slabs, own_cols * slabs), BF16),
         ],
-        compiler_params=pltpu.CompilerParams(vmem_limit_bytes=32 * MIB),
+        compiler_params=pltpu.CompilerParams(vmem_limit_bytes=VMEM),
         cost_estimate=pl.CostEstimate(flops=10**8, bytes_accessed=2 * MIB, transcendentals=0),
-    )(table, entries, vert)
+    )(table, entries, vert, after)
 
 
 def along_rows(lines, matrix, coef):
@@ -319,38 +357,64 @@
             pltpu.VMEM((own_cols, slabs, rows), F32),
             pltpu.VMEM((own_cols * slabs, rows), F32),
         ],
-        compiler_params=pltpu.CompilerParams(vmem_limit_bytes=32 * MIB),
+        compiler_params=pltpu.CompilerParams(vmem_limit_bytes=VMEM),
         cost_estimate=pl.CostEstimate(flops=10**9, bytes_accessed=6 * MIB, transcendentals=0),
     )(*args)
 
 
-def tile_carries(ends, coef, levels, tile_count):
+def merge_kernel(levels, last, step, after_count, *refs):
+    table_ref, entries_ref = refs[:2]
+    pairs = refs[2 : 4 + 2 * step]
+    out_ref = refs[4 + 2 * step + after_count]
+    _, subs, rows = out_ref.shape
     tile, mem = lax.axis_index("tile"), lax.axis_index("mem")
-    slab = mem * SUB + jnp.arange(SUB)[:, None]
-    decay = jnp.where(slab < levels, coef[1, 0, 0], coef[1, 0, 1])
-    turn = jnp.where(slab < levels, coef[0, 0, 0], coef[0, 0, 1])
-    one, none = jnp.ones_like(decay), jnp.zeros_like(decay)
-    from_left, from_right, turned = one, one, none
-    left, right = none, none
-    block = ends.astype(F32)
-    span = 1
-    while span < tile_count:
-        sent = block.astype(BF16)
-        came = lax.ppermute(sent, "tile", [(i, i ^ span) for i in range(tile_count)]).astype(F32)
-        second = (tile // span) % 2 == 1
-        lower = jnp.where(second, came, block)
-        upper = jnp.where(second, block, came)
-        bent = turn * lower[0] + upper[1]
-        left = left + jnp.where(second, from_left * lower[0], 0.0)
-        right = right + jnp.where(second, turned * lower[0], from_right * bent)
-        block = jnp.stack([decay * lower[0] + upper[0], lower[1] + decay * bent])
-        turned = jnp.where(second, turned * decay, turned + from_right * turn * decay)
-        from_left = jnp.where(second, from_left * decay, from_left)
-        from_right = jnp.where(second, from_right, from_right * decay)
+    pair = lookup(table_ref, entries_ref[...])
+    decay, turn = pair, jnp.ones_like(pair)
+    for _ in range(COL_BITS):
         turn = turn * (1.0 + decay * decay)
         decay = decay * decay
-        span *= 2
-    return jnp.stack([left, right]).astype(BF16)
+    turn = pair * turn
+    is_level = iota((subs, rows), 0) + mem * SUB < levels
+    decay = jnp.where(is_level, decay[0:1], decay[1:2])
+    turn = jnp.where(is_level, turn[0:1], turn[1:2])
+    one, none = jnp.ones_like(decay), jnp.zeros_like(decay)
+    from_left, from_right, turned, left, right = one, one, none, none, none
+    for level in range(step + 1):
+        second = (tile >> level) % 2 == 1
+        if last or level == step:
+            mine, came = (pairs[2 * level + k][...].astype(F32) for k in range(2))
+            lower = jnp.where(second, came, mine)
+            upper = jnp.where(second, mine, came)
+            bent = turn * lower[0] + upper[1]
+        if last:
+            left = left + jnp.where(second, from_left * lower[0], 0.0)
+            right = right + jnp.where(second, turned * lower[0], from_right * bent)
+            turned = jnp.where(second, turned * decay, turned + from_right * turn * decay)
+            from_left = jnp.where(second, from_left * decay, from_left)
+            from_right = jnp.where(second, from_right, from_right * decay)
+        elif level == step:
+            left = decay * lower[0] + upper[0]
+            right = lower[1] + decay * bent
+        turn = turn * (1.0 + decay * decay)
+        decay = decay * decay
+    out_ref[0] = left.astype(BF16)
+    out_ref[1] = right.astype(BF16)
+
+
+def merge_call(table, entries, pairs, after, levels, last):
+    step = len(pairs) // 2 - 1
+    vmem, smem = pl.BlockSpec(memory_space=pltpu.VMEM), pl.BlockSpec(memory_space=pltpu.SMEM)
+    held = [pl.BlockSpec(memory_space=pl.ANY)] * len(after)
+    return pl.pallas_call(
+        functools.partial(merge_kernel, levels, last, step, len(after)),
+        name="merge",
+        in_specs=[smem] + [vmem] * (1 + len(pairs)) + held,
+        out_specs=[vmem] + held,
+        out_shape=[jax.ShapeDtypeStruct(array.shape, array.dtype) for array in [pairs[0], *after]],
+        input_output_aliases={2 + len(pairs) + k: 1 + k for k in range(len(after))},
+        compiler_params=pltpu.CompilerParams(vmem_limit_bytes=VMEM),
+        cost_estimate=pl.CostEstimate(flops=10**6, bytes_accessed=MIB // 4, transcendentals=0),
+    )(table, entries, *pairs, *after)
 
 
 def body(field, vert_filter, loc_filter, alpha_table, xscale_idx, yscale_idx, members):
@@ -360,18 +424,37 @@
     own_cols = cols // mem_count
     slabs = padded(slab_count)
 
-    def swap(array, flip):
-        return lax.ppermute(array, "mem", [(i, i ^ flip) for i in range(mem_count)])
-
-    flat_field = field.reshape(slab_count * cols, rows)
+    def swap(array, flip, axis="mem"):
+        return lax.ppermute(array, axis, [(i, i ^ flip) for i in range(lax.axis_size(axis))])
+
+    flat_field = pltpu.with_memory_space_constraint(field.reshape(slab_count * cols, rows), pltpu.HBM)
     mine = members.reshape(slab_count * cols, rows)
     other = swap(mine, 1)
-    ends, own, coef = columns_call(alpha_table, xscale_idx, flat_field, levels, cols, own_cols)
-    mats, row_coef, vert = tables_call(alpha_table, yscale_idx, vert_filter[0], levels, own_cols, cols, slabs)
-    send, keep = ensemble_call(loc_filter[0], flat_field, mine, other, levels, cols, own_cols)
-    came = swap(send, 2)
-    carried = tile_carries(ends, coef, levels, tile_count)
-    shares = [carried] + [swap(carried, flip) for flip in range(1, mem_count)]
+    mem = lax.axis_index("mem").astype(jnp.int32).reshape(1)
+    alpha_table = pltpu.with_memory_space_constraint(alpha_table, pltpu.HBM)
+    xscale_idx = pltpu.with_memory_space_constraint(xscale_idx, pltpu.HBM)
+    block = ends_call(mem, alpha_table, xscale_idx, flat_field, levels, cols)
+
+    pairs, span, step = [], 1, 0
+    while span < tile_count:
+        pairs += [block, swap(block, span, "tile")]
+        span, last = 2 * span, 2 * span >= tile_count
+        if step == 0:
+            own, coef = local_call(alpha_table, xscale_idx, flat_field, block, levels, cols, own_cols)
+            block, own = merge_call(alpha_table, xscale_idx, pairs, [own], levels, last)
+        elif step == 1:
+            send, keep = ensemble_call(loc_filter[0], field.reshape(slab_count * cols, rows), mine, other, block, levels, cols, own_cols)
+            block, send = merge_call(alpha_table, xscale_idx, pairs, [send], levels, last)
+            came = swap(send, 2)
+        elif step == 2:
+            mats, row_coef, vert = tables_call(
+                alpha_table, yscale_idx, vert_filter[0], block, levels, own_cols, cols, slabs
+            )
+            block, mats = merge_call(alpha_table, xscale_idx, pairs, [mats], levels, last)
+        else:
+            (block,) = merge_call(alpha_table, xscale_idx, pairs, [], levels, last)
+        step += 1
+    shares = [block] + [swap(block, flip) for flip in range(1, mem_count)]
     scale = 1.0 / (mem_count * members.shape[0] - 1)
     return final_call(slab_count, levels, scale, [own, coef, *shares, mats, row_coef, vert, keep, came])
 

time: 51.8 us -> 36.7 us (0.71)
  waiting for transfers between devices: 16.1 us -> 7.75 us
  local copies, waits for them, and re-layouts: 7.02 us -> 0.03 us
  Pallas kernels: 12.4 us -> 17.7 us
  other arithmetic: 4.34 us -> 0 us
  starting transfers between devices: 11.3 us -> 10.7 us
    ppermute x8, waiting for transfers between devices: 16.1 us -> 7.75 us  [swap(): lax.ppermute(array, axis, [(i, i ^ flip) for i in range(lax.axis_size(axi...]
    unnamed x40 -> x10, local copies, waits for them, and re-layouts: 7 us -> 0.03 us
    pallas_call x1 -> x5, Pallas kernels: 2.8 us -> 8.93 us  [the longest x1 3.64 us: local_call(): pl.pallas_call(functools.partial(local_kernel, levels), name='local', gri...]
    convert_element_type x3 -> x0, other arithmetic: 2.11 us -> none  [the longest x2 1.26 us: tile_carries(): sent = block.astype(BF16)]
    select_n x2 -> x0, other arithmetic: 1.75 us -> none  [the longest x1 0.89 us: tile_carries(): lower = jnp.where(second, came, block)]
    pallas_call x1, Pallas kernels: 5.07 us -> 4.15 us  [ensemble_call(): pl.pallas_call(functools.partial(ensemble_kernel, levels, cols), name='en...]
    ppermute x8, starting transfers between devices: 11.3 us -> 10.7 us  [swap(): lax.ppermute(array, axis, [(i, i ^ flip) for i in range(lax.axis_size(axi...]
  transfers between devices with their start and end apart: 8 -> 8, of which waited for: 4 -> 3; matrix products, arithmetic and copies ran while one was open for 8% -> 0% of each run, Pallas kernels for 9% -> 39%
where the time goes in v2:
time: 36.7 us; the launch traced here: 36.3 us
  Pallas kernels  17.7 us (48%)
  starting transfers between devices  10.7 us (29%)
  waiting for transfers between devices  7.75 us (21%)
    ppermute x8, starting transfers between devices, swap(): lax.ppermute(array, axis, [(i, i ^ flip) for i in range(lax.axis_size(axi...  10.7 us
    ppermute x8, waiting for transfers between devices, swap(): lax.ppermute(array, axis, [(i, i ^ flip) for i in range(lax.axis_size(axi...  7.75 us
    pallas_call x1, Pallas kernels, ensemble_call(): pl.pallas_call(functools.partial(ensemble_kernel, levels, cols), name='en...  4.15 us
    pallas_call x1, Pallas kernels, local_call(): pl.pallas_call(functools.partial(local_kernel, levels), name='local', gri...  3.64 us
    pallas_call x1, Pallas kernels, ends_call(): pl.pallas_call(functools.partial(ends_kernel, levels, total // cols), nam...  2.86 us
    pallas_call x1, Pallas kernels, final_call(): pl.pallas_call(functools.partial(final_kernel, levels, scale), name='fina...  2.67 us
    pallas_call x3, Pallas kernels, merge_call(): pl.pallas_call(functools.partial(merge_kernel, levels, last, step, len(af...  2.43 us
    pallas_call x1, Pallas kernels, tables_call(): pl.pallas_call(functools.partial(tables_kernel, levels, own_cols, col_dev...  1.94 us
  transfers between devices with their start and end apart: 8, of which 3 were waited for; matrix products, arithmetic and copies ran while one was open for 0% of the time, Pallas kernels for 39%

profile of v2, /device:TPU:0, one launch (start us, length us, event | category | flops | bytes accessed | tf_op | source)
XLA Modules:
  0.0 36.3 jit_solution(1615988040219799027)
XLA Ops:
  0.0 0.5 %collective-permute-start.2 = (bf16[976,1024]{1,0:T(8,128)(2,1)}, bf16[976,1024]{1,0:T(8,128)(2,1)S(1)}, u32[]{:S(2)}, u32[]{:S(2)}) collective-permute-start(bf16[976,1024]{1,0:T(8,128)(2,1)} %bitcast.8), channel_id=1, source_target_pairs={{0,1},{1,0},{2,3},{3,2},{4,5},{5,4},{6,7},{7,6},{8,9},{9,8},{10,11... | collective-permute-start | bytes 5996552 | tf_op jit(solution)/shard_map/ppermute | solution.py:428
  0.5 0.0 copy-start.1
  0.5 2.9 %ends.1.after_ref.refs_2_ = bf16[2,16,1024]{2,1,0:T(8,128)(2,1)S(1)} custom-call(s32[1]{0:T(128)} %bitcast.mem_ref, f32[16]{0:T(128)} %refs_0_.5, s32[2,1024]{1,0:T(2,128)} %refs_1_.5, bf16[976,1024]{1,0:T(8,128)(2,1)} %bitcast.5), custom_call_target="tpu_custom_call" | custom-call | flops 100000000 | bytes 1048576 | tf_op jit(solution)/shard_map/ends/pallas_call | solution.py:88
  3.3 0.0 copy-start
  3.3 0.0 copy-start.2
  3.3 2.6 %collective-permute-start = (bf16[2,16,1024]{2,1,0:T(8,128)(2,1)S(1)}, bf16[2,16,1024]{2,1,0:T(8,128)(2,1)S(1)}, u32[]{:S(2)}, u32[]{:S(2)}) collective-permute-start(bf16[2,16,1024]{2,1,0:T(8,128)(2,1)S(1)} %ends.1.after_ref.refs_2_), channel_id=1, source_target_pairs={{0,4},{4,0},{8,12},{12,8},{16,20},{20,16},{24,28},{28,24},{1,5},{5... | collective-permute-start | bytes 196616 | tf_op jit(solution)/shard_map/ppermute | solution.py:428
  5.9 3.6 %local.1 = (f32[4,64,1024]{2,1,0:T(8,128)S(1)}, f32[2,16,2,1024]{3,2,1,0:T(2,128)S(1)}) custom-call(f32[16]{0:T(128)} %refs_0_.5, s32[2,1024]{1,0:T(2,128)} %refs_1_.5, bf16[976,1024]{1,0:T(8,128)(2,1)} %bitcast.6, bf16[2,16,1024]{2,1,0:T(8,128)(2,1)S(1)} %ends.1.after_ref.refs_2_), custom_call_target="tpu_custom_call" | custom-call | flops 500000000 | bytes 4194304 | tf_op jit(solution)/shard_map/local/pallas_call | solution.py:132
  9.6 0.0 collective-permute-done.refs_3_
  9.6 0.8 %merge.3 = (bf16[2,16,1024]{2,1,0:T(8,128)(2,1)S(1)}, f32[4,64,1024]{2,1,0:T(8,128)S(1)}) custom-call(f32[16]{0:T(128)} %refs_0_.5, s32[2,1024]{1,0:T(2,128)} %refs_1_.5, bf16[2,16,1024]{2,1,0:T(8,128)(2,1)S(1)} %ends.1.after_ref.refs_2_, bf16[2,16,1024]{2,1,0:T(8,128)(2,1)S(1)} %collective-permute-done.refs_3_, ...), custom_call_target="tpu_custom_call", output_to_operand_aliasing={{1}: (4, {})} | custom-call | flops 1000000 | bytes 262144 | tf_op jit(solution)/shard_map/merge/pallas_call | solution.py:408
  10.4 1.6 %collective-permute-start.1 = (bf16[2,16,1024]{2,1,0:T(8,128)(2,1)S(1)}, bf16[2,16,1024]{2,1,0:T(8,128)(2,1)S(1)}, u32[]{:S(2)}, u32[]{:S(2)}) collective-permute-start(bf16[2,16,1024]{2,1,0:T(8,128)(2,1)S(1)} %get-tuple-element.21.after_ref.refs_4_), channel_id=1, source_target_pairs={{0,8},{4,12},{8,0},{12,4},{16,24},{20,28},{24,16},{28,20},{1,9},{5... | collective-permute-start | bytes 196616 | tf_op jit(solution)/shard_map/ppermute | solution.py:428
  12.0 0.0 collective-permute-done.2.other_ref
  12.0 0.0 copy-done.1
  12.0 0.0 copy-done
  12.0 0.0 copy-done.2
  12.0 0.0 copy-start.3
  12.1 0.0 copy-start.4
  12.1 4.1 %ensemble.1 = (bf16[4,64,1024]{2,1,0:T(8,128)(2,1)S(1)}, f32[4,64,1024]{2,1,0:T(8,128)S(1)}) custom-call(bf16[60,60]{1,0:T(8,128)(2,1)S(1)} %bitcast.10, bf16[976,1024]{1,0:T(8,128)(2,1)S(1)} %bitcast.7, bf16[976,1024]{1,0:T(8,128)(2,1)S(1)} %bitcast.9, bf16[976,1024]{1,0:T(8,128)(2,1)S(1)} %collective-permute-done.2.other_ref, ...), custom_call_target="tpu_custom_call" | custom-call | flops 500000000 | bytes 8388608 | tf_op jit(solution)/shard_map/ensemble/pallas_call | solution.py:203
  16.2 0.0 collective-permute-done.1.refs_5_
  16.2 0.8 %merge.4 = (bf16[2,16,1024]{2,1,0:T(8,128)(2,1)S(1)}, bf16[4,64,1024]{2,1,0:T(8,128)(2,1)S(1)}) custom-call(f32[16]{0:T(128)} %refs_0_.5, s32[2,1024]{1,0:T(2,128)} %refs_1_.5, bf16[2,16,1024]{2,1,0:T(8,128)(2,1)S(1)} %ends.1.after_ref.refs_2_, bf16[2,16,1024]{2,1,0:T(8,128)(2,1)S(1)} %collective-permute-done.refs_3_, ...), custom_call_target="tpu_custom_call", output_to_operand_aliasing={{1}: (6, {})} | custom-call | flops 1000000 | bytes 262144 | tf_op jit(solution)/shard_map/merge/pallas_call | solution.py:408
  17.0 1.6 %collective-permute-start.7 = (bf16[4,64,1024]{2,1,0:T(8,128)(2,1)S(1)}, bf16[4,64,1024]{2,1,0:T(8,128)(2,1)S(1)}, u32[]{:S(2)}, u32[]{:S(2)}) collective-permute-start(bf16[4,64,1024]{2,1,0:T(8,128)(2,1)S(1)} %get-tuple-element.30), channel_id=1, source_target_pairs={{0,2},{1,3},{2,0},{3,1},{4,6},{5,7},{6,4},{7,5},{8,10},{9,11},{10,... | collective-permute-start | bytes 1572872 | tf_op jit(solution)/shard_map/ppermute | solution.py:428
  18.6 2.6 %collective-permute-start.3 = (bf16[2,16,1024]{2,1,0:T(8,128)(2,1)S(1)}, bf16[2,16,1024]{2,1,0:T(8,128)(2,1)S(1)}, u32[]{:S(2)}, u32[]{:S(2)}) collective-permute-start(bf16[2,16,1024]{2,1,0:T(8,128)(2,1)S(1)} %get-tuple-element.23.after_ref.refs_6_), channel_id=1, source_target_pairs={{0,16},{4,20},{8,24},{12,28},{16,0},{20,4},{24,8},{28,12},{1,17},{... | collective-permute-start | bytes 196616 | tf_op jit(solution)/shard_map/ppermute | solution.py:428
  21.2 0.0 copy-done.3
  21.2 0.0 copy-done.4
  21.2 1.9 %tables.1 = (bf16[8,256,256]{2,1,0:T(8,128)(2,1)S(1)}, f32[4,8,256]{2,1,0:T(8,128)S(1)}, bf16[512,256]{1,0:T(8,128)(2,1)S(1)}) custom-call(f32[16]{0:T(128)} %refs_0_.5, s32[2,128]{1,0:T(2,128)S(1)} %copy-done.4, bf16[60,60]{1,0:T(8,128)(2,1)S(1)} %bitcast.11, bf16[2,16,1024]{2,1,0:T(8,128)(2,1)S(1)} %get-tuple-element.23.after_ref.refs_6_), custom_call_target="tpu_custom_call" | custom-call | flops 100000000 | bytes 2097152 | tf_op jit(solution)/shard_map/tables/pallas_call | solution.py:262
  23.1 1.3 %collective-permute-done.3.refs_7_ = bf16[2,16,1024]{2,1,0:T(8,128)(2,1)S(1)} collective-permute-done((bf16[2,16,1024]{2,1,0:T(8,128)(2,1)S(1)}, bf16[2,16,1024]{2,1,0:T(8,128)(2,1)S(1)}, u32[]{:S(2)}, u32[]{:S(2)}) %collective-permute-start.3) | collective-permute-done | bytes 65568 | tf_op jit(solution)/shard_map/ppermute | solution.py:428
  24.4 0.9 %merge.5 = (bf16[2,16,1024]{2,1,0:T(8,128)(2,1)S(1)}, bf16[8,256,256]{2,1,0:T(8,128)(2,1)S(1)}) custom-call(f32[16]{0:T(128)} %refs_0_.5, s32[2,1024]{1,0:T(2,128)} %refs_1_.5, bf16[2,16,1024]{2,1,0:T(8,128)(2,1)S(1)} %ends.1.after_ref.refs_2_, bf16[2,16,1024]{2,1,0:T(8,128)(2,1)S(1)} %collective-permute-done.refs_3_, ...), custom_call_target="tpu_custom_call", output_to_operand_aliasing={{1}: (8, {})} | custom-call | flops 1000000 | bytes 262144 | tf_op jit(solution)/shard_map/merge/pallas_call | solution.py:408
  25.3 0.1 collective-permute-start.6
  25.4 0.6 %collective-permute-start.5 = (bf16[2,16,1024]{2,1,0:T(8,128)(2,1)S(1)}, bf16[2,16,1024]{2,1,0:T(8,128)(2,1)S(1)}, u32[]{:S(2)}, u32[]{:S(2)}) collective-permute-start(bf16[2,16,1024]{2,1,0:T(8,128)(2,1)S(1)} %get-tuple-element.25.mine_ref), channel_id=1, source_target_pairs={{0,2},{1,3},{2,0},{3,1},{4,6},{5,7},{6,4},{7,5},{8,10},{9,11},{10,... | collective-permute-start | bytes 196616 | tf_op jit(solution)/shard_map/ppermute | solution.py:428
  26.0 1.2 %collective-permute-start.4 = (bf16[2,16,1024]{2,1,0:T(8,128)(2,1)S(1)}, bf16[2,16,1024]{2,1,0:T(8,128)(2,1)S(1)}, u32[]{:S(2)}, u32[]{:S(2)}) collective-permute-start(bf16[2,16,1024]{2,1,0:T(8,128)(2,1)S(1)} %get-tuple-element.25.mine_ref), channel_id=1, source_target_pairs={{0,1},{1,0},{2,3},{3,2},{4,5},{5,4},{6,7},{7,6},{8,9},{9,8},{10,11... | collective-permute-start | bytes 196616 | tf_op jit(solution)/shard_map/ppermute | solution.py:428
  27.2 4.7 %collective-permute-done.6.far_ref = bf16[2,16,1024]{2,1,0:T(8,128)(2,1)S(1)} collective-permute-done((bf16[2,16,1024]{2,1,0:T(8,128)(2,1)S(1)}, bf16[2,16,1024]{2,1,0:T(8,128)(2,1)S(1)}, u32[]{:S(2)}, u32[]{:S(2)}) %collective-permute-start.6) | collective-permute-done | bytes 65568 | tf_op jit(solution)/shard_map/ppermute | solution.py:428
  31.9 1.7 %collective-permute-done.5.chip_ref = bf16[2,16,1024]{2,1,0:T(8,128)(2,1)S(1)} collective-permute-done((bf16[2,16,1024]{2,1,0:T(8,128)(2,1)S(1)}, bf16[2,16,1024]{2,1,0:T(8,128)(2,1)S(1)}, u32[]{:S(2)}, u32[]{:S(2)}) %collective-permute-start.5) | collective-permute-done | bytes 65568 | tf_op jit(solution)/shard_map/ppermute | solution.py:428
  33.7 0.0 collective-permute-done.4.core_ref
  33.7 0.0 collective-permute-done.7.came_ref
  33.7 2.7 %final.1 = bf16[61,4,1024]{2,1,0:T(4,128)(2,1)} custom-call(f32[4,64,1024]{2,1,0:T(8,128)S(1)} %get-tuple-element.19.own_ref, f32[2,16,2,1024]{3,2,1,0:T(2,128)S(1)} %get-tuple-element.20.coef_ref, bf16[2,16,1024]{2,1,0:T(8,128)(2,1)S(1)} %get-tuple-element.25.mine_ref, bf16[2,16,1024]{2,1,0:T(8,128)(2,1)S(1)} %collective-permute-done.4.core_ref, ...), custom_call_target="tpu_custom_call" | custom-call | flops 1000000000 | bytes 6291456 | tf_op jit(solution)/shard_map/final/pallas_call | solution.py:349
Async XLA Ops:
  0.0 12.0 %collective-permute-start.2 = (bf16[976,1024]{1,0:T(8,128)(2,1)}, bf16[976,1024]{1,0:T(8,128)(2,1)S(1)}, u32[]{:S(2)}, u32[]{:S(2)}) collective-permute-start(bf16[976,1024]{1,0:T(8,128)(2,1)} %bitcast.8), channel_id=1, source_target_pairs={{0,1},{1,0},{2,3},{3,2},{4,5},{5,4},{6,7},{7,6},{8,9},{9,8},{10,11... | collective-permute-start | bytes 5996552 | tf_op jit(solution)/shard_map/ppermute | solution.py:428
  0.5 11.6 %copy-start.1 = (bf16[1,61,16,1024]{3,2,1,0:T(8,128)(2,1)S(1)}, bf16[1,61,16,1024]{3,2,1,0:T(8,128)(2,1)}, u32[]{:S(2)}) copy-start(bf16[1,61,16,1024]{3,2,1,0:T(8,128)(2,1)} %param.13) | copy-start | bytes 5996548
  3.3 8.7 %copy-start = (bf16[61,16,1024]{2,1,0:T(8,128)(2,1)S(1)}, bf16[61,16,1024]{2,1,0:T(8,128)(2,1)}, u32[]{:S(2)}) copy-start(bf16[61,16,1024]{2,1,0:T(8,128)(2,1)} %param.7) | copy-start | bytes 5996548
  3.3 8.7 %copy-start.2 = (bf16[1,60,60]{2,1,0:T(8,128)(2,1)S(1)}, bf16[1,60,60]{2,1,0:T(8,128)(2,1)}, u32[]{:S(2)}) copy-start(bf16[1,60,60]{2,1,0:T(8,128)(2,1)} %param.9) | copy-start | bytes 21604
  3.3 6.2 %collective-permute-start = (bf16[2,16,1024]{2,1,0:T(8,128)(2,1)S(1)}, bf16[2,16,1024]{2,1,0:T(8,128)(2,1)S(1)}, u32[]{:S(2)}, u32[]{:S(2)}) collective-permute-start(bf16[2,16,1024]{2,1,0:T(8,128)(2,1)S(1)} %ends.1.after_ref.refs_2_), channel_id=1, source_target_pairs={{0,4},{4,0},{8,12},{12,8},{16,20},{20,16},{24,28},{28,24},{1,5},{5... | collective-permute-start | bytes 196616 | tf_op jit(solution)/shard_map/ppermute | solution.py:428
  10.4 5.8 %collective-permute-start.1 = (bf16[2,16,1024]{2,1,0:T(8,128)(2,1)S(1)}, bf16[2,16,1024]{2,1,0:T(8,128)(2,1)S(1)}, u32[]{:S(2)}, u32[]{:S(2)}) collective-permute-start(bf16[2,16,1024]{2,1,0:T(8,128)(2,1)S(1)} %get-tuple-element.21.after_ref.refs_4_), channel_id=1, source_target_pairs={{0,8},{4,12},{8,0},{12,4},{16,24},{20,28},{24,16},{28,20},{1,9},{5... | collective-permute-start | bytes 196616 | tf_op jit(solution)/shard_map/ppermute | solution.py:428
  12.0 9.1 %copy-start.3 = (bf16[1,60,60]{2,1,0:T(8,128)(2,1)S(1)}, bf16[1,60,60]{2,1,0:T(8,128)(2,1)}, u32[]{:S(2)}) copy-start(bf16[1,60,60]{2,1,0:T(8,128)(2,1)} %param.8) | copy-start | bytes 21604
  12.1 9.1 %copy-start.4 = (s32[2,128]{1,0:T(2,128)S(1)}, s32[2,128]{1,0:T(2,128)}, u32[]{:S(2)}) copy-start(s32[2,128]{1,0:T(2,128)} %entries_ref.5) | copy-start | bytes 3076
  17.0 16.6 %collective-permute-start.7 = (bf16[4,64,1024]{2,1,0:T(8,128)(2,1)S(1)}, bf16[4,64,1024]{2,1,0:T(8,128)(2,1)S(1)}, u32[]{:S(2)}, u32[]{:S(2)}) collective-permute-start(bf16[4,64,1024]{2,1,0:T(8,128)(2,1)S(1)} %get-tuple-element.30), channel_id=1, source_target_pairs={{0,2},{1,3},{2,0},{3,1},{4,6},{5,7},{6,4},{7,5},{8,10},{9,11},{10,... | collective-permute-start | bytes 1572872 | tf_op jit(solution)/shard_map/ppermute | solution.py:428
  18.6 5.8 %collective-permute-start.3 = (bf16[2,16,1024]{2,1,0:T(8,128)(2,1)S(1)}, bf16[2,16,1024]{2,1,0:T(8,128)(2,1)S(1)}, u32[]{:S(2)}, u32[]{:S(2)}) collective-permute-start(bf16[2,16,1024]{2,1,0:T(8,128)(2,1)S(1)} %get-tuple-element.23.after_ref.refs_6_), channel_id=1, source_target_pairs={{0,16},{4,20},{8,24},{12,28},{16,0},{20,4},{24,8},{28,12},{1,17},{... | collective-permute-start | bytes 196616 | tf_op jit(solution)/shard_map/ppermute | solution.py:428
  25.3 6.7 %collective-permute-start.6 = (bf16[2,16,1024]{2,1,0:T(8,128)(2,1)S(1)}, bf16[2,16,1024]{2,1,0:T(8,128)(2,1)S(1)}, u32[]{:S(2)}, u32[]{:S(2)}) collective-permute-start(bf16[2,16,1024]{2,1,0:T(8,128)(2,1)S(1)} %get-tuple-element.25.mine_ref), channel_id=1, source_target_pairs={{0,3},{1,2},{2,1},{3,0},{4,7},{5,6},{6,5},{7,4},{8,11},{9,10},{10,... | collective-permute-start | bytes 196616 | tf_op jit(solution)/shard_map/ppermute | solution.py:428
  25.4 8.3 %collective-permute-start.5 = (bf16[2,16,1024]{2,1,0:T(8,128)(2,1)S(1)}, bf16[2,16,1024]{2,1,0:T(8,128)(2,1)S(1)}, u32[]{:S(2)}, u32[]{:S(2)}) collective-permute-start(bf16[2,16,1024]{2,1,0:T(8,128)(2,1)S(1)} %get-tuple-element.25.mine_ref), channel_id=1, source_target_pairs={{0,2},{1,3},{2,0},{3,1},{4,6},{5,7},{6,4},{7,5},{8,10},{9,11},{10,... | collective-permute-start | bytes 196616 | tf_op jit(solution)/shard_map/ppermute | solution.py:428
  26.0 7.7 %collective-permute-start.4 = (bf16[2,16,1024]{2,1,0:T(8,128)(2,1)S(1)}, bf16[2,16,1024]{2,1,0:T(8,128)(2,1)S(1)}, u32[]{:S(2)}, u32[]{:S(2)}) collective-permute-start(bf16[2,16,1024]{2,1,0:T(8,128)(2,1)S(1)} %get-tuple-element.25.mine_ref), channel_id=1, source_target_pairs={{0,1},{1,0},{2,3},{3,2},{4,5},{5,4},{6,7},{7,6},{8,9},{9,8},{10,11... | collective-permute-start | bytes 196616 | tf_op jit(solution)/shard_map/ppermute | solution.py:428

commit v3 on v2

--- a/solution.py
+++ b/solution.py
@@ -10,7 +10,7 @@
 F32, BF16 = jnp.float32, jnp.bfloat16
 COL_BITS = 4
 SUB = 16
-LANES = 256
+SWEEP_LANES = 512
 BLOCK = 256
 MIB = 1 << 20
 VMEM = 32 * MIB
@@ -90,14 +90,14 @@
         name="ends",
         grid_spec=pltpu.PrefetchScalarGridSpec(
             num_scalar_prefetch=1,
-            grid=(rows // LANES,),
+            grid=(1,),
             in_specs=[
                 pl.BlockSpec(memory_space=pltpu.SMEM),
-                pl.BlockSpec((2, LANES), lambda i, mem: (0, i)),
-                pl.BlockSpec((SUB * cols, LANES), lambda i, mem: (mem[0], i)),
+                pl.BlockSpec((2, rows), lambda i, mem: (0, i)),
+                pl.BlockSpec((SUB * cols, rows), lambda i, mem: (mem[0], i)),
             ],
-            out_specs=pl.BlockSpec((2, SUB, LANES), lambda i, mem: (0, 0, i)),
-            scratch_shapes=[pltpu.VMEM((cols, SUB, LANES), F32)],
+            out_specs=pl.BlockSpec((2, SUB, rows), lambda i, mem: (0, 0, i)),
+            scratch_shapes=[pltpu.VMEM((cols, SUB, rows), F32)],
         ),
         out_shape=jax.ShapeDtypeStruct((2, SUB, rows), BF16),
         compiler_params=pltpu.CompilerParams(vmem_limit_bytes=VMEM),
@@ -132,22 +132,22 @@
     return pl.pallas_call(
         functools.partial(local_kernel, levels),
         name="local",
-        grid=(rows // LANES,),
+        grid=(rows // SWEEP_LANES,),
         in_specs=[
             pl.BlockSpec(memory_space=pltpu.SMEM),
-            pl.BlockSpec((2, LANES), lambda i: (0, i)),
-            pl.BlockSpec((total, LANES), lambda i: (0, i)),
+            pl.BlockSpec((2, SWEEP_LANES), lambda i: (0, i)),
+            pl.BlockSpec((total, SWEEP_LANES), lambda i: (0, i)),
             pl.BlockSpec(memory_space=pl.ANY),
         ],
         out_specs=[
-            pl.BlockSpec((own_cols, slabs, LANES), lambda i: (0, 0, i)),
-            pl.BlockSpec((2, cols, 2, LANES), lambda i: (0, 0, 0, i)),
+            pl.BlockSpec((own_cols, slabs, SWEEP_LANES), lambda i: (0, 0, i)),
+            pl.BlockSpec((2, cols, 2, SWEEP_LANES), lambda i: (0, 0, 0, i)),
         ],
         out_shape=[
             jax.ShapeDtypeStruct((own_cols, slabs, rows), F32),
             jax.ShapeDtypeStruct((2, cols, 2, rows), F32),
         ],
-        scratch_shapes=[pltpu.VMEM((cols, slabs, LANES), F32)],
+        scratch_shapes=[pltpu.VMEM((cols, slabs, SWEEP_LANES), F32)],
         compiler_params=pltpu.CompilerParams(vmem_limit_bytes=VMEM),
         cost_estimate=pl.CostEstimate(flops=5 * 10**8, bytes_accessed=4 * MIB, transcendentals=0),
     )(table, entries, flat_field, after)
@@ -164,8 +164,9 @@
     return jnp.where(row_col == col_col, full, 0.0).astype(BF16)
 
 
-def ensemble_kernel(levels, cols, loc_ref, field_ref, mine_ref, other_ref, after_ref, send_ref, keep_ref, field_w, mine_w, other_w):
-    own_cols, slabs, lanes = keep_ref.shape
+def ensemble_kernel(levels, cols, loc_ref, field_ref, mine_ref, other_ref, after_ref, send_ref, keep_ref, *work):
+    own_cols, count = work[0].shape[0] // 2, keep_ref.shape[0]
+    _, slabs, lanes = work[0].shape
     mem = lax.axis_index("mem")
     core, chip = mem % 2, mem // 2
     shape = (2 * own_cols * SUB, cols * SUB)
@@ -174,45 +175,45 @@
     first = jnp.where(slot < own_cols, (2 * (1 - chip) + core) * own_cols, (2 * chip + core) * own_cols)
     hit = (out_row % SUB == in_row // cols) & (first + slot % own_cols == in_row % cols)
     perm = hit.astype(BF16)
-    to_columns(perm, field_ref, field_w, cols)
-    to_columns(perm, mine_ref, mine_w, cols)
-    to_columns(perm, other_ref, other_w, cols)
+    for ref, out in zip((field_ref, mine_ref, other_ref), work):
+        to_columns(perm, ref, out, cols)
     side = own_cols * slabs
     row, col = iota((side, side), 0), iota((side, side), 1)
     local = spread(loc_ref[...], levels, slabs, row % slabs, row // slabs, col % slabs, col // slabs)
-    for half in range(2):
+    order = ((row // own_cols == col % slabs) & (row % own_cols == col // slabs)).astype(BF16)
+    for half, out_ref in enumerate((send_ref, keep_ref)):
         part = slice(half * own_cols, (half + 1) * own_cols)
-        field = field_w[part]
+        field = work[0][part]
         total = None
-        for member_w in (mine_w, other_w):
+        for member_w in work[1:]:
             member = member_w[part]
             scaled = (member * field).astype(BF16).reshape(side, lanes)
             term = member * dot(local, scaled).reshape(own_cols, slabs, lanes)
             total = term if total is None else total + term
-        if half == 0:
-            send_ref[...] = total.astype(BF16)
-        else:
-            keep_ref[...] = total
-
-
-def ensemble_call(loc, flat_field, mine, other, after, levels, cols, own_cols):
+        total = total.reshape(side, lanes)
+        high = total.astype(BF16)
+        ordered = dot(order, high)
+        if out_ref is keep_ref:
+            ordered = ordered + dot(order, (total - high.astype(F32)).astype(BF16))
+        out_ref[...] = ordered[:count].astype(out_ref.dtype)
+
+
+def ensemble_call(half, loc, flat_field, mine, other, after, levels, cols, own_cols):
     total, rows = flat_field.shape
-    slabs = padded(total // cols)
-    wide = pl.BlockSpec((total, LANES), lambda i: (0, i))
-    out = pl.BlockSpec((own_cols, slabs, LANES), lambda i: (0, 0, i))
+    slab_count, lanes = total // cols, rows // 2
+    wide = pl.BlockSpec((total, lanes), lambda i: (0, half))
+    out_shape = (slab_count * own_cols, lanes)
+    out = pl.BlockSpec(out_shape, lambda i: (0, 0))
     return pl.pallas_call(
         functools.partial(ensemble_kernel, levels, cols),
         name="ensemble",
-        grid=(rows // LANES,),
+        grid=(1,),
         in_specs=[pl.BlockSpec(loc.shape, lambda i: (0, 0)), wide, wide, wide, pl.BlockSpec(memory_space=pl.ANY)],
         out_specs=[out, out],
-        out_shape=[
-            jax.ShapeDtypeStruct((own_cols, slabs, rows), BF16),
-            jax.ShapeDtypeStruct((own_cols, slabs, rows), F32),
-        ],
-        scratch_shapes=[pltpu.VMEM((2 * own_cols, slabs, LANES), F32)] * 3,
-        compiler_params=pltpu.CompilerParams(vmem_limit_bytes=VMEM),
-        cost_estimate=pl.CostEstimate(flops=5 * 10**8, bytes_accessed=8 * MIB, transcendentals=0),
+        out_shape=[jax.ShapeDtypeStruct(out_shape, BF16), jax.ShapeDtypeStruct(out_shape, F32)],
+        scratch_shapes=[pltpu.VMEM((2 * own_cols, padded(slab_count), lanes), F32)] * 3,
+        compiler_params=pltpu.CompilerParams(vmem_limit_bytes=VMEM),
+        cost_estimate=pl.CostEstimate(flops=5 * 10**8, bytes_accessed=4 * MIB, transcendentals=0),
     )(loc, flat_field, mine, other, after)
 
 
@@ -253,7 +254,7 @@
         mat_ref[k] = (gain_of(alpha) * decay * reach).astype(BF16)
     shape = vert_out.shape
     row, col = iota(shape, 0), iota(shape, 1)
-    vert_out[...] = spread(vert_ref[...], levels, slabs, row // 8, row % 8, col % slabs, col // slabs)
+    vert_out[...] = spread(vert_ref[...], levels, slabs, row // own_cols, row % own_cols, col % slabs, col // slabs)
 
 
 def tables_call(table, entries, vert, after, levels, own_cols, col_dev, slabs):
@@ -267,7 +268,7 @@
         out_shape=[
             jax.ShapeDtypeStruct((count, BLOCK, BLOCK), BF16),
             jax.ShapeDtypeStruct((4, count, BLOCK), F32),
-            jax.ShapeDtypeStruct((8 * slabs, own_cols * slabs), BF16),
+            jax.ShapeDtypeStruct((own_cols * slabs, own_cols * slabs), BF16),
         ],
         compiler_params=pltpu.CompilerParams(vmem_limit_bytes=VMEM),
         cost_estimate=pl.CostEstimate(flops=10**8, bytes_accessed=2 * MIB, transcendentals=0),
@@ -302,7 +303,7 @@
 
 def final_kernel(
     levels, scale, own_ref, coef_ref, mine_ref, core_ref, chip_ref, far_ref, mat_ref, row_coef_ref, vert_ref,
-    keep_ref, came_ref, out_ref, carry, smooth, filt
+    keep_0_ref, keep_1_ref, came_0_ref, came_1_ref, out_ref, carry, smooth, filt
 ):
     own_cols, slabs, rows = own_ref.shape
     mem = lax.axis_index("mem")
@@ -326,21 +327,19 @@
             filt[col * slabs + top : col * slabs + top + 8, place] = jnp.where(
                 iota((8, BLOCK), 0) < levels - top, piece[top : top + 8], extra
             )
-    shape = vert_ref.shape
-    row, place = iota(shape, 0), iota(shape, 1)
-    order = ((row // 8 == place % slabs) & (row % 8 == place // slabs)).astype(BF16)
     count = out_ref.shape[0]
-    side = own_cols * slabs
+    half = rows // 2
     for start in range(0, rows, BLOCK):
         part = slice(start, start + BLOCK)
         static = filt[:, part]
-        ens = (keep_ref[:, :, part] + came_ref[:, :, part].astype(F32)).reshape(side, BLOCK) * scale
-        static_hi, ens_hi = static.astype(BF16), ens.astype(BF16)
-        static_lo = (static - static_hi.astype(F32)).astype(BF16)
-        ens_lo = (ens - ens_hi.astype(F32)).astype(BF16)
-        total = dot(vert_ref[...], static_hi) + dot(vert_ref[...], static_lo) + dot(order, ens_hi) + dot(order, ens_lo)
-        total = total.reshape(slabs, 8, BLOCK)
-        out_ref[:, :, part] = total[:count, :own_cols].astype(BF16)
+        high = static.astype(BF16)
+        low = (static - high.astype(F32)).astype(BF16)
+        total = dot(vert_ref[...], high) + dot(vert_ref[...], low)
+        keep_ref, came_ref = ((keep_0_ref, came_0_ref), (keep_1_ref, came_1_ref))[start // half]
+        inside = slice(start % half, start % half + BLOCK)
+        ens = keep_ref[:, inside] + came_ref[:, inside].astype(F32)
+        total = total[: count * own_cols] + ens * scale
+        out_ref[:, :, part] = total.reshape(count, own_cols, BLOCK).astype(BF16)
 
 
 def final_call(slab_count, levels, scale, args):
@@ -366,7 +365,7 @@
     table_ref, entries_ref = refs[:2]
     pairs = refs[2 : 4 + 2 * step]
     out_ref = refs[4 + 2 * step + after_count]
-    _, subs, rows = out_ref.shape
+    subs, rows = out_ref.shape[-2:]
     tile, mem = lax.axis_index("tile"), lax.axis_index("mem")
     pair = lookup(table_ref, entries_ref[...])
     decay, turn = pair, jnp.ones_like(pair)
@@ -383,8 +382,11 @@
         second = (tile >> level) % 2 == 1
         if last or level == step:
             mine, came = (pairs[2 * level + k][...].astype(F32) for k in range(2))
-            lower = jnp.where(second, came, mine)
-            upper = jnp.where(second, mine, came)
+            if last and level == step:
+                lower, upper = [jnp.where(second, came, mine)], [None, came]
+            else:
+                lower = jnp.where(second, came, mine)
+                upper = jnp.where(second, mine, came)
             bent = turn * lower[0] + upper[1]
         if last:
             left = left + jnp.where(second, from_left * lower[0], 0.0)
@@ -397,20 +399,26 @@
             right = lower[1] + decay * bent
         turn = turn * (1.0 + decay * decay)
         decay = decay * decay
-    out_ref[0] = left.astype(BF16)
-    out_ref[1] = right.astype(BF16)
-
-
-def merge_call(table, entries, pairs, after, levels, last):
+    if len(out_ref.shape) == 2:
+        second = (tile >> (step + 1)) % 2 == 1
+        out_ref[...] = jnp.where(second, right, left).astype(BF16)
+    else:
+        out_ref[0] = left.astype(BF16)
+        out_ref[1] = right.astype(BF16)
+
+
+def merge_call(table, entries, pairs, after, levels, remaining):
     step = len(pairs) // 2 - 1
+    out_shape = pairs[0].shape[1:] if remaining == 1 else pairs[0].shape
     vmem, smem = pl.BlockSpec(memory_space=pltpu.VMEM), pl.BlockSpec(memory_space=pltpu.SMEM)
     held = [pl.BlockSpec(memory_space=pl.ANY)] * len(after)
     return pl.pallas_call(
-        functools.partial(merge_kernel, levels, last, step, len(after)),
+        functools.partial(merge_kernel, levels, remaining == 0, step, len(after)),
         name="merge",
         in_specs=[smem] + [vmem] * (1 + len(pairs)) + held,
         out_specs=[vmem] + held,
-        out_shape=[jax.ShapeDtypeStruct(array.shape, array.dtype) for array in [pairs[0], *after]],
+        out_shape=[jax.ShapeDtypeStruct(out_shape, BF16)]
+        + [jax.ShapeDtypeStruct(array.shape, array.dtype) for array in after],
         input_output_aliases={2 + len(pairs) + k: 1 + k for k in range(len(after))},
         compiler_params=pltpu.CompilerParams(vmem_limit_bytes=VMEM),
         cost_estimate=pl.CostEstimate(flops=10**6, bytes_accessed=MIB // 4, transcendentals=0),
@@ -427,36 +435,46 @@
     def swap(array, flip, axis="mem"):
         return lax.ppermute(array, axis, [(i, i ^ flip) for i in range(lax.axis_size(axis))])
 
-    flat_field = pltpu.with_memory_space_constraint(field.reshape(slab_count * cols, rows), pltpu.HBM)
+    full_field = field.reshape(slab_count * cols, rows)
+    flat_field = pltpu.with_memory_space_constraint(full_field, pltpu.HBM)
     mine = members.reshape(slab_count * cols, rows)
+    held = pltpu.with_memory_space_constraint(mine, pltpu.HBM)
     other = swap(mine, 1)
     mem = lax.axis_index("mem").astype(jnp.int32).reshape(1)
     alpha_table = pltpu.with_memory_space_constraint(alpha_table, pltpu.HBM)
     xscale_idx = pltpu.with_memory_space_constraint(xscale_idx, pltpu.HBM)
     block = ends_call(mem, alpha_table, xscale_idx, flat_field, levels, cols)
 
-    pairs, span, step = [], 1, 0
-    while span < tile_count:
-        pairs += [block, swap(block, span, "tile")]
-        span, last = 2 * span, 2 * span >= tile_count
+    def ensemble(half, after):
+        return ensemble_call(half, loc_filter[0], full_field, held, other, after, levels, cols, own_cols)
+
+    def merge(pairs, after):
+        return merge_call(alpha_table, xscale_idx, pairs, after, levels, steps - len(pairs) // 2)
+
+    steps = tile_count.bit_length() - 1
+    pairs = []
+    for step in range(steps):
+        pairs += [block, swap(block, 1 << step, "tile")]
         if step == 0:
-            own, coef = local_call(alpha_table, xscale_idx, flat_field, block, levels, cols, own_cols)
-            block, own = merge_call(alpha_table, xscale_idx, pairs, [own], levels, last)
+            own, coef = local_call(alpha_table, xscale_idx, full_field, block, levels, cols, own_cols)
+            send_0, keep_0 = ensemble(0, own)
+            block, send_0 = merge(pairs, [send_0])
+            came_0 = swap(send_0, 2)
         elif step == 1:
-            send, keep = ensemble_call(loc_filter[0], field.reshape(slab_count * cols, rows), mine, other, block, levels, cols, own_cols)
-            block, send = merge_call(alpha_table, xscale_idx, pairs, [send], levels, last)
-            came = swap(send, 2)
+            send_1, keep_1 = ensemble(1, block)
+            block, send_1 = merge(pairs, [send_1])
+            came_1 = swap(send_1, 2)
         elif step == 2:
             mats, row_coef, vert = tables_call(
                 alpha_table, yscale_idx, vert_filter[0], block, levels, own_cols, cols, slabs
             )
-            block, mats = merge_call(alpha_table, xscale_idx, pairs, [mats], levels, last)
+            block, mats = merge(pairs, [mats])
         else:
-            (block,) = merge_call(alpha_table, xscale_idx, pairs, [], levels, last)
-        step += 1
+            (block,) = merge(pairs, [])
     shares = [block] + [swap(block, flip) for flip in range(1, mem_count)]
     scale = 1.0 / (mem_count * members.shape[0] - 1)
-    return final_call(slab_count, levels, scale, [own, coef, *shares, mats, row_coef, vert, keep, came])
+    ens = [keep_0, keep_1, came_0, came_1]
+    return final_call(slab_count, levels, scale, [own, coef, *shares, mats, row_coef, vert, *ens])
 
 
 def solution(mesh):

time: 36.7 us -> 32.9 us (0.90)
  waiting for transfers between devices: 7.75 us -> 4.54 us
  Pallas kernels: 17.7 us -> 16.6 us
  starting transfers between devices: 10.7 us -> 11.3 us
    ppermute x8 -> x9, waiting for transfers between devices: 7.75 us -> 4.54 us  [swap(): lax.ppermute(array, axis, [(i, i ^ flip) for i in range(lax.axis_size(axi...]
    pallas_call x1 -> x2, Pallas kernels: 4.15 us -> 6.44 us  [ensemble_call(): pl.pallas_call(functools.partial(ensemble_kernel, levels, cols), name='en...]
    pallas_call x1, Pallas kernels: 3.64 us -> 2.23 us  [local_call(): pl.pallas_call(functools.partial(local_kernel, levels), name='local', gri...]
    pallas_call x1, Pallas kernels: 2.86 us -> 1.63 us  [ends_call(): pl.pallas_call(functools.partial(ends_kernel, levels, total // cols), nam...]
    pallas_call x1, Pallas kernels: 2.67 us -> 1.96 us  [final_call(): pl.pallas_call(functools.partial(final_kernel, levels, scale), name='fina...]
    ppermute x8 -> x9, starting transfers between devices: 10.7 us -> 11.3 us  [swap(): lax.ppermute(array, axis, [(i, i ^ flip) for i in range(lax.axis_size(axi...]
  transfers between devices with their start and end apart: 8 -> 9, of which waited for: 3 -> 3; matrix products, arithmetic and copies ran while one was open for 0% -> 0% of each run, Pallas kernels for 39% -> 43%
where the time goes in v3:
time: 32.9 us; the launch traced here: 32.5 us
  Pallas kernels  16.6 us (50%)
  starting transfers between devices  11.3 us (34%)
  waiting for transfers between devices  4.54 us (14%)
    ppermute x9, starting transfers between devices, swap(): lax.ppermute(array, axis, [(i, i ^ flip) for i in range(lax.axis_size(axi...  11.3 us
    pallas_call x2, Pallas kernels, ensemble_call(): pl.pallas_call(functools.partial(ensemble_kernel, levels, cols), name='en...  6.44 us
    ppermute x9, waiting for transfers between devices, swap(): lax.ppermute(array, axis, [(i, i ^ flip) for i in range(lax.axis_size(axi...  4.54 us
    pallas_call x3, Pallas kernels, merge_call(): pl.pallas_call(functools.partial(merge_kernel, levels, remaining == 0, st...  2.43 us
    pallas_call x1, Pallas kernels, local_call(): pl.pallas_call(functools.partial(local_kernel, levels), name='local', gri...  2.23 us
    pallas_call x1, Pallas kernels, final_call(): pl.pallas_call(functools.partial(final_kernel, levels, scale), name='fina...  1.96 us
    pallas_call x1, Pallas kernels, tables_call(): pl.pallas_call(functools.partial(tables_kernel, levels, own_cols, col_dev...  1.89 us
    pallas_call x1, Pallas kernels, ends_call(): pl.pallas_call(functools.partial(ends_kernel, levels, total // cols), nam...  1.63 us
  transfers between devices with their start and end apart: 9, of which 3 were waited for; matrix products, arithmetic and copies ran while one was open for 0% of the time, Pallas kernels for 43%

profile of v3, /device:TPU:0, one launch (start us, length us, event | category | flops | bytes accessed | tf_op | source)
XLA Modules:
  0.0 32.5 jit_solution(4456642617481685889)
XLA Ops:
  0.0 0.0 copy-start
  0.0 0.5 %collective-permute-start.1 = (bf16[976,1024]{1,0:T(8,128)(2,1)}, bf16[976,1024]{1,0:T(8,128)(2,1)}, u32[]{:S(2)}, u32[]{:S(2)}) collective-permute-start(bf16[976,1024]{1,0:T(8,128)(2,1)} %bitcast.12), channel_id=1, source_target_pairs={{0,1},{1,0},{2,3},{3,2},{4,5},{5,4},{6,7},{7,6},{8,9},{9,8},{10,11... | collective-permute-start | bytes 5996552 | tf_op jit(solution)/shard_map/ppermute | solution.py:436
  0.5 0.0 copy-start.1
  0.5 1.6 %ends.1.after_ref.refs_2_ = bf16[2,16,1024]{2,1,0:T(8,128)(2,1)S(1)} custom-call(s32[1]{0:T(128)} %bitcast.1.mem_ref, f32[16]{0:T(128)} %refs_0_.5, s32[2,1024]{1,0:T(2,128)} %refs_1_.5, bf16[976,1024]{1,0:T(8,128)(2,1)} %bitcast.5), custom_call_target="tpu_custom_call" | custom-call | flops 100000000 | bytes 1048576 | tf_op jit(solution)/shard_map/ends/pallas_call | solution.py:88
  2.1 2.6 %collective-permute-start = (bf16[2,16,1024]{2,1,0:T(8,128)(2,1)S(1)}, bf16[2,16,1024]{2,1,0:T(8,128)(2,1)S(1)}, u32[]{:S(2)}, u32[]{:S(2)}) collective-permute-start(bf16[2,16,1024]{2,1,0:T(8,128)(2,1)S(1)} %ends.1.after_ref.refs_2_), channel_id=1, source_target_pairs={{0,4},{4,0},{8,12},{12,8},{16,20},{20,16},{24,28},{28,24},{1,5},{5... | collective-permute-start | bytes 196616 | tf_op jit(solution)/shard_map/ppermute | solution.py:436
  4.7 0.0 copy-done
  4.7 2.2 %local.1 = (f32[4,64,1024]{2,1,0:T(8,128)S(1)}, f32[2,16,2,1024]{3,2,1,0:T(2,128)S(1)}) custom-call(f32[16]{0:T(128)} %refs_0_.5, s32[2,1024]{1,0:T(2,128)} %refs_1_.5, bf16[976,1024]{1,0:T(8,128)(2,1)S(1)} %bitcast.6, bf16[2,16,1024]{2,1,0:T(8,128)(2,1)S(1)} %ends.1.after_ref.refs_2_), custom_call_target="tpu_custom_call" | custom-call | flops 500000000 | bytes 4194304 | tf_op jit(solution)/shard_map/local/pallas_call | solution.py:132
  6.9 0.0 collective-permute-done.1.other_ref
  6.9 0.0 copy-done.1
  6.9 3.2 %ensemble.2 = (bf16[244,512]{1,0:T(8,128)(2,1)S(1)}, f32[244,512]{1,0:T(8,128)S(1)}) custom-call(bf16[60,60]{1,0:T(8,128)(2,1)S(1)} %bitcast.9, bf16[976,1024]{1,0:T(8,128)(2,1)S(1)} %bitcast.7, bf16[976,1024]{1,0:T(8,128)(2,1)} %bitcast.13, bf16[976,1024]{1,0:T(8,128)(2,1)} %collective-permute-done.1.other_ref, ...), custom_call_target="tpu_custom_call" | custom-call | flops 500000000 | bytes 4194304 | tf_op jit(solution)/shard_map/ensemble/pallas_call | solution.py:207
  10.2 0.0 collective-permute-done.refs_3_
  10.2 0.8 %merge.3 = (bf16[2,16,1024]{2,1,0:T(8,128)(2,1)S(1)}, bf16[244,512]{1,0:T(8,128)(2,1)S(1)}) custom-call(f32[16]{0:T(128)} %refs_0_.5, s32[2,1024]{1,0:T(2,128)} %refs_1_.5, bf16[2,16,1024]{2,1,0:T(8,128)(2,1)S(1)} %ends.1.after_ref.refs_2_, bf16[2,16,1024]{2,1,0:T(8,128)(2,1)S(1)} %collective-permute-done.refs_3_, ...), custom_call_target="tpu_custom_call", output_to_operand_aliasing={{1}: (4, {})} | custom-call | flops 1000000 | bytes 262144 | tf_op jit(solution)/shard_map/merge/pallas_call | solution.py:415
  11.0 1.6 %collective-permute-start.2 = (bf16[2,16,1024]{2,1,0:T(8,128)(2,1)S(1)}, bf16[2,16,1024]{2,1,0:T(8,128)(2,1)S(1)}, u32[]{:S(2)}, u32[]{:S(2)}) collective-permute-start(bf16[2,16,1024]{2,1,0:T(8,128)(2,1)S(1)} %get-tuple-element.23.after_ref.refs_4_), channel_id=1, source_target_pairs={{0,8},{4,12},{8,0},{12,4},{16,24},{20,28},{24,16},{28,20},{1,9},{5... | collective-permute-start | bytes 196616 | tf_op jit(solution)/shard_map/ppermute | solution.py:436
  12.6 0.0 copy-start.2
  12.6 0.0 copy-start.3
  12.6 1.5 %collective-permute-start.7 = (bf16[244,512]{1,0:T(8,128)(2,1)S(1)}, bf16[244,512]{1,0:T(8,128)(2,1)S(1)}, u32[]{:S(2)}, u32[]{:S(2)}) collective-permute-start(bf16[244,512]{1,0:T(8,128)(2,1)S(1)} %get-tuple-element.33), channel_id=1, source_target_pairs={{0,2},{1,3},{2,0},{3,1},{4,6},{5,7},{6,4},{7,5},{8,10},{9,11},{10,... | collective-permute-start | bytes 749576 | tf_op jit(solution)/shard_map/ppermute | solution.py:436
  14.1 3.2 %ensemble.3 = (bf16[244,512]{1,0:T(8,128)(2,1)S(1)}, f32[244,512]{1,0:T(8,128)S(1)}) custom-call(bf16[60,60]{1,0:T(8,128)(2,1)S(1)} %bitcast.10, bf16[976,1024]{1,0:T(8,128)(2,1)S(1)} %bitcast.8, bf16[976,1024]{1,0:T(8,128)(2,1)} %bitcast.14, bf16[976,1024]{1,0:T(8,128)(2,1)} %collective-permute-done.1.other_ref, ...), custom_call_target="tpu_custom_call" | custom-call | flops 500000000 | bytes 4194304 | tf_op jit(solution)/shard_map/ensemble/pallas_call | solution.py:207
  17.3 0.0 collective-permute-done.2.refs_5_
  17.3 0.8 %merge.4 = (bf16[16,1024]{1,0:T(8,128)(2,1)S(1)}, bf16[244,512]{1,0:T(8,128)(2,1)S(1)}) custom-call(f32[16]{0:T(128)} %refs_0_.5, s32[2,1024]{1,0:T(2,128)} %refs_1_.5, bf16[2,16,1024]{2,1,0:T(8,128)(2,1)S(1)} %ends.1.after_ref.refs_2_, bf16[2,16,1024]{2,1,0:T(8,128)(2,1)S(1)} %collective-permute-done.refs_3_, ...), custom_call_target="tpu_custom_call", output_to_operand_aliasing={{1}: (6, {})} | custom-call | flops 1000000 | bytes 262144 | tf_op jit(solution)/shard_map/merge/pallas_call | solution.py:415
  18.1 0.6 %collective-permute-start.8 = (bf16[244,512]{1,0:T(8,128)(2,1)S(1)}, bf16[244,512]{1,0:T(8,128)(2,1)S(1)}, u32[]{:S(2)}, u32[]{:S(2)}) collective-permute-start(bf16[244,512]{1,0:T(8,128)(2,1)S(1)} %get-tuple-element.34), channel_id=1, source_target_pairs={{0,2},{1,3},{2,0},{3,1},{4,6},{5,7},{6,4},{7,5},{8,10},{9,11},{10,... | collective-permute-start | bytes 749576 | tf_op jit(solution)/shard_map/ppermute | solution.py:436
  18.7 2.6 %collective-permute-start.3 = (bf16[16,1024]{1,0:T(8,128)(2,1)S(1)}, bf16[16,1024]{1,0:T(8,128)(2,1)S(1)}, u32[]{:S(2)}, u32[]{:S(2)}) collective-permute-start(bf16[16,1024]{1,0:T(8,128)(2,1)S(1)} %get-tuple-element.25.after_ref.refs_6_), channel_id=1, source_target_pairs={{0,16},{4,20},{8,24},{12,28},{16,0},{20,4},{24,8},{28,12},{1,17},{... | collective-permute-start | bytes 98312 | tf_op jit(solution)/shard_map/ppermute | solution.py:436
  21.3 0.0 copy-done.2
  21.3 0.0 copy-done.3
  21.3 1.9 %tables.1 = (bf16[8,256,256]{2,1,0:T(8,128)(2,1)S(1)}, f32[4,8,256]{2,1,0:T(8,128)S(1)}, bf16[256,256]{1,0:T(8,128)(2,1)S(1)}) custom-call(f32[16]{0:T(128)} %refs_0_.5, s32[2,128]{1,0:T(2,128)S(1)} %copy-done.3, bf16[60,60]{1,0:T(8,128)(2,1)S(1)} %bitcast.11, bf16[16,1024]{1,0:T(8,128)(2,1)S(1)} %get-tuple-element.25.after_ref.refs_6_), custom_call_target="tpu_custom_call" | custom-call | flops 100000000 | bytes 2097152 | tf_op jit(solution)/shard_map/tables/pallas_call | solution.py:263
  23.2 0.6 %collective-permute-done.3.refs_7_ = bf16[16,1024]{1,0:T(8,128)(2,1)S(1)} collective-permute-done((bf16[16,1024]{1,0:T(8,128)(2,1)S(1)}, bf16[16,1024]{1,0:T(8,128)(2,1)S(1)}, u32[]{:S(2)}, u32[]{:S(2)}) %collective-permute-start.3) | collective-permute-done | bytes 32800 | tf_op jit(solution)/shard_map/ppermute | solution.py:436
  23.8 0.9 %merge.5 = (bf16[2,16,1024]{2,1,0:T(8,128)(2,1)S(1)}, bf16[8,256,256]{2,1,0:T(8,128)(2,1)S(1)}) custom-call(f32[16]{0:T(128)} %refs_0_.5, s32[2,1024]{1,0:T(2,128)} %refs_1_.5, bf16[2,16,1024]{2,1,0:T(8,128)(2,1)S(1)} %ends.1.after_ref.refs_2_, bf16[2,16,1024]{2,1,0:T(8,128)(2,1)S(1)} %collective-permute-done.refs_3_, ...), custom_call_target="tpu_custom_call", output_to_operand_aliasing={{1}: (8, {})} | custom-call | flops 1000000 | bytes 262144 | tf_op jit(solution)/shard_map/merge/pallas_call | solution.py:415
  24.7 0.1 collective-permute-start.6
  24.7 1.5 %collective-permute-start.5 = (bf16[2,16,1024]{2,1,0:T(8,128)(2,1)S(1)}, bf16[2,16,1024]{2,1,0:T(8,128)(2,1)S(1)}, u32[]{:S(2)}, u32[]{:S(2)}) collective-permute-start(bf16[2,16,1024]{2,1,0:T(8,128)(2,1)S(1)} %get-tuple-element.27.mine_ref), channel_id=1, source_target_pairs={{0,2},{1,3},{2,0},{3,1},{4,6},{5,7},{6,4},{7,5},{8,10},{9,11},{10,... | collective-permute-start | bytes 196616 | tf_op jit(solution)/shard_map/ppermute | solution.py:436
  26.3 0.3 %collective-permute-start.4 = (bf16[2,16,1024]{2,1,0:T(8,128)(2,1)S(1)}, bf16[2,16,1024]{2,1,0:T(8,128)(2,1)S(1)}, u32[]{:S(2)}, u32[]{:S(2)}) collective-permute-start(bf16[2,16,1024]{2,1,0:T(8,128)(2,1)S(1)} %get-tuple-element.27.mine_ref), channel_id=1, source_target_pairs={{0,1},{1,0},{2,3},{3,2},{4,5},{5,4},{6,7},{7,6},{8,9},{9,8},{10,11... | collective-permute-start | bytes 196616 | tf_op jit(solution)/shard_map/ppermute | solution.py:436
  26.6 2.5 %collective-permute-done.6.far_ref = bf16[2,16,1024]{2,1,0:T(8,128)(2,1)S(1)} collective-permute-done((bf16[2,16,1024]{2,1,0:T(8,128)(2,1)S(1)}, bf16[2,16,1024]{2,1,0:T(8,128)(2,1)S(1)}, u32[]{:S(2)}, u32[]{:S(2)}) %collective-permute-start.6) | collective-permute-done | bytes 65568 | tf_op jit(solution)/shard_map/ppermute | solution.py:436
  29.1 1.4 %collective-permute-done.5.chip_ref = bf16[2,16,1024]{2,1,0:T(8,128)(2,1)S(1)} collective-permute-done((bf16[2,16,1024]{2,1,0:T(8,128)(2,1)S(1)}, bf16[2,16,1024]{2,1,0:T(8,128)(2,1)S(1)}, u32[]{:S(2)}, u32[]{:S(2)}) %collective-permute-start.5) | collective-permute-done | bytes 65568 | tf_op jit(solution)/shard_map/ppermute | solution.py:436
  30.5 0.0 collective-permute-done.4.core_ref
  30.5 0.0 collective-permute-done.7.came_0_ref
  30.5 0.0 collective-permute-done.8.came_1_ref
  30.5 2.0 %final.1 = bf16[61,4,1024]{2,1,0:T(4,128)(2,1)} custom-call(f32[4,64,1024]{2,1,0:T(8,128)S(1)} %get-tuple-element.20.after_ref.own_ref, f32[2,16,2,1024]{3,2,1,0:T(2,128)S(1)} %get-tuple-element.21.coef_ref, bf16[2,16,1024]{2,1,0:T(8,128)(2,1)S(1)} %get-tuple-element.27.mine_ref, bf16[2,16,1024]{2,1,0:T(8,128)(2,1)S(1)} %collective-permute-done.4.core_ref, ...), custom_call_target="tpu_custom_call" | custom-call | flops 1000000000 | bytes 6291456 | tf_op jit(solution)/shard_map/final/pallas_call | solution.py:348
Async XLA Ops:
  0.0 4.7 %copy-start = (bf16[61,16,1024]{2,1,0:T(8,128)(2,1)S(1)}, bf16[61,16,1024]{2,1,0:T(8,128)(2,1)}, u32[]{:S(2)}) copy-start(bf16[61,16,1024]{2,1,0:T(8,128)(2,1)} %param.7) | copy-start | bytes 5996548
  0.0 6.9 %collective-permute-start.1 = (bf16[976,1024]{1,0:T(8,128)(2,1)}, bf16[976,1024]{1,0:T(8,128)(2,1)}, u32[]{:S(2)}, u32[]{:S(2)}) collective-permute-start(bf16[976,1024]{1,0:T(8,128)(2,1)} %bitcast.12), channel_id=1, source_target_pairs={{0,1},{1,0},{2,3},{3,2},{4,5},{5,4},{6,7},{7,6},{8,9},{9,8},{10,11... | collective-permute-start | bytes 5996552 | tf_op jit(solution)/shard_map/ppermute | solution.py:436
  0.5 6.5 %copy-start.1 = (bf16[1,60,60]{2,1,0:T(8,128)(2,1)S(1)}, bf16[1,60,60]{2,1,0:T(8,128)(2,1)}, u32[]{:S(2)}) copy-start(bf16[1,60,60]{2,1,0:T(8,128)(2,1)} %param.9) | copy-start | bytes 21604
  2.1 8.1 %collective-permute-start = (bf16[2,16,1024]{2,1,0:T(8,128)(2,1)S(1)}, bf16[2,16,1024]{2,1,0:T(8,128)(2,1)S(1)}, u32[]{:S(2)}, u32[]{:S(2)}) collective-permute-start(bf16[2,16,1024]{2,1,0:T(8,128)(2,1)S(1)} %ends.1.after_ref.refs_2_), channel_id=1, source_target_pairs={{0,4},{4,0},{8,12},{12,8},{16,20},{20,16},{24,28},{28,24},{1,5},{5... | collective-permute-start | bytes 196616 | tf_op jit(solution)/shard_map/ppermute | solution.py:436
  11.0 6.4 %collective-permute-start.2 = (bf16[2,16,1024]{2,1,0:T(8,128)(2,1)S(1)}, bf16[2,16,1024]{2,1,0:T(8,128)(2,1)S(1)}, u32[]{:S(2)}, u32[]{:S(2)}) collective-permute-start(bf16[2,16,1024]{2,1,0:T(8,128)(2,1)S(1)} %get-tuple-element.23.after_ref.refs_4_), channel_id=1, source_target_pairs={{0,8},{4,12},{8,0},{12,4},{16,24},{20,28},{24,16},{28,20},{1,9},{5... | collective-permute-start | bytes 196616 | tf_op jit(solution)/shard_map/ppermute | solution.py:436
  12.6 8.7 %copy-start.2 = (bf16[1,60,60]{2,1,0:T(8,128)(2,1)S(1)}, bf16[1,60,60]{2,1,0:T(8,128)(2,1)}, u32[]{:S(2)}) copy-start(bf16[1,60,60]{2,1,0:T(8,128)(2,1)} %param.8) | copy-start | bytes 21604
  12.6 8.7 %copy-start.3 = (s32[2,128]{1,0:T(2,128)S(1)}, s32[2,128]{1,0:T(2,128)}, u32[]{:S(2)}) copy-start(s32[2,128]{1,0:T(2,128)} %entries_ref.5) | copy-start | bytes 3076
  12.6 17.9 %collective-permute-start.7 = (bf16[244,512]{1,0:T(8,128)(2,1)S(1)}, bf16[244,512]{1,0:T(8,128)(2,1)S(1)}, u32[]{:S(2)}, u32[]{:S(2)}) collective-permute-start(bf16[244,512]{1,0:T(8,128)(2,1)S(1)} %get-tuple-element.33), channel_id=1, source_target_pairs={{0,2},{1,3},{2,0},{3,1},{4,6},{5,7},{6,4},{7,5},{8,10},{9,11},{10,... | collective-permute-start | bytes 749576 | tf_op jit(solution)/shard_map/ppermute | solution.py:436
  18.1 12.4 %collective-permute-start.8 = (bf16[244,512]{1,0:T(8,128)(2,1)S(1)}, bf16[244,512]{1,0:T(8,128)(2,1)S(1)}, u32[]{:S(2)}, u32[]{:S(2)}) collective-permute-start(bf16[244,512]{1,0:T(8,128)(2,1)S(1)} %get-tuple-element.34), channel_id=1, source_target_pairs={{0,2},{1,3},{2,0},{3,1},{4,6},{5,7},{6,4},{7,5},{8,10},{9,11},{10,... | collective-permute-start | bytes 749576 | tf_op jit(solution)/shard_map/ppermute | solution.py:436
  18.7 5.1 %collective-permute-start.3 = (bf16[16,1024]{1,0:T(8,128)(2,1)S(1)}, bf16[16,1024]{1,0:T(8,128)(2,1)S(1)}, u32[]{:S(2)}, u32[]{:S(2)}) collective-permute-start(bf16[16,1024]{1,0:T(8,128)(2,1)S(1)} %get-tuple-element.25.after_ref.refs_6_), channel_id=1, source_target_pairs={{0,16},{4,20},{8,24},{12,28},{16,0},{20,4},{24,8},{28,12},{1,17},{... | collective-permute-start | bytes 98312 | tf_op jit(solution)/shard_map/ppermute | solution.py:436
  24.7 4.4 %collective-permute-start.6 = (bf16[2,16,1024]{2,1,0:T(8,128)(2,1)S(1)}, bf16[2,16,1024]{2,1,0:T(8,128)(2,1)S(1)}, u32[]{:S(2)}, u32[]{:S(2)}) collective-permute-start(bf16[2,16,1024]{2,1,0:T(8,128)(2,1)S(1)} %get-tuple-element.27.mine_ref), channel_id=1, source_target_pairs={{0,3},{1,2},{2,1},{3,0},{4,7},{5,6},{6,5},{7,4},{8,11},{9,10},{10,... | collective-permute-start | bytes 196616 | tf_op jit(solution)/shard_map/ppermute | solution.py:436
  24.7 5.8 %collective-permute-start.5 = (bf16[2,16,1024]{2,1,0:T(8,128)(2,1)S(1)}, bf16[2,16,1024]{2,1,0:T(8,128)(2,1)S(1)}, u32[]{:S(2)}, u32[]{:S(2)}) collective-permute-start(bf16[2,16,1024]{2,1,0:T(8,128)(2,1)S(1)} %get-tuple-element.27.mine_ref), channel_id=1, source_target_pairs={{0,2},{1,3},{2,0},{3,1},{4,6},{5,7},{6,4},{7,5},{8,10},{9,11},{10,... | collective-permute-start | bytes 196616 | tf_op jit(solution)/shard_map/ppermute | solution.py:436
  26.3 4.3 %collective-permute-start.4 = (bf16[2,16,1024]{2,1,0:T(8,128)(2,1)S(1)}, bf16[2,16,1024]{2,1,0:T(8,128)(2,1)S(1)}, u32[]{:S(2)}, u32[]{:S(2)}) collective-permute-start(bf16[2,16,1024]{2,1,0:T(8,128)(2,1)S(1)} %get-tuple-element.27.mine_ref), channel_id=1, source_target_pairs={{0,1},{1,0},{2,3},{3,2},{4,5},{5,4},{6,7},{7,6},{8,9},{9,8},{10,11... | collective-permute-start | bytes 196616 | tf_op jit(solution)/shard_map/ppermute | solution.py:436

commit v4 on v3

v4 whole, which is shorter than its diff:
```python
import functools

import jax
import jax.numpy as jnp
from jax import lax
from jax.experimental import pallas as pl
from jax.experimental.pallas import tpu as pltpu
from jax.sharding import PartitionSpec as P

F32, BF16 = jnp.float32, jnp.bfloat16
SUB = 16
CORES = 2
LANES = 256
BLOCK = 256
MIB = 1 << 20
VMEM = 32 * MIB


def iota(shape, dim):
    return lax.broadcasted_iota(jnp.int32, shape, dim)


def split(number, size):
    assert size & (size - 1) == 0
    return number >> (size.bit_length() - 1), number & (size - 1)


def dot(left, right):
    return jnp.dot(left, right, preferred_element_type=F32)


def gain_of(alpha):
    rest = (1.0 - alpha) * (1.0 + alpha)
    return jnp.sqrt(rest) * rest / jnp.sqrt(1.0 + alpha * alpha)


def lookup(table_ref, entries):
    found = jnp.zeros(entries.shape, F32)
    for entry in range(table_ref.shape[0]):
        found = jnp.where(entries == entry, table_ref[entry], found)
    return found


def padded(slab_count):
    return -(-slab_count // (4 * SUB)) * 4 * SUB


def to_columns(perm, flat, out_ref, cols):
    total = flat.shape[0]
    wanted = out_ref.shape[0]
    step = SUB * cols
    for chunk in range(out_ref.shape[1] // SUB):
        depth = min(step, total - chunk * step)
        moved = dot(perm[:, :depth], flat[chunk * step : chunk * step + depth])
        out_ref[:, chunk * SUB : (chunk + 1) * SUB, :] = moved.reshape(wanted, SUB, -1)


def sweep(work, alpha):
    cols = work.shape[0]
    state = work[0]
    for col in range(1, cols):
        state = alpha * state + work[col]
        work[col] = state
    for col in range(cols - 2, -1, -1):
        state = alpha * state + work[col]
        work[col] = state


def transposer(cols):
    shape = (SUB * cols, SUB * cols)
    (out_col, out_slab), (in_slab, in_col) = split(iota(shape, 0), SUB), split(iota(shape, 1), cols)
    return ((out_slab == in_slab) & (out_col == in_col)).astype(BF16)


def ends_kernel(levels, slab_count, core_ref, table_ref, entries_ref, field_ref, ends_ref, work):
    _, cols, subs, lanes = work.shape
    first = core_ref[0] * subs
    perm = transposer(cols)
    for chunk in range(work.shape[0]):
        part = slice(chunk * lanes, (chunk + 1) * lanes)
        held = jnp.where(iota((cols * subs, lanes), 0) < (slab_count - first) * cols, field_ref[:, part], 0)
        to_columns(perm, held, work.at[chunk], cols)
        pair = lookup(table_ref, entries_ref[:, part])
        alpha = jnp.where(iota((subs, lanes), 0) + first < levels, pair[0:1], pair[1:2])
        sweep(work.at[chunk], alpha)
        gain = gain_of(alpha)
        ends_ref[0, :, part] = (gain * work[chunk, cols - 1]).astype(BF16)
        ends_ref[1, :, part] = (gain * work[chunk, 0]).astype(BF16)


def ends_call(core, table, entries, flat_field, levels, cols):
    total, rows = flat_field.shape
    subs = padded(total // cols) // CORES
    return pl.pallas_call(
        functools.partial(ends_kernel, levels, total // cols),
        name="ends",
        grid_spec=pltpu.PrefetchScalarGridSpec(
            num_scalar_prefetch=1,
            grid=(1,),
            in_specs=[
                pl.BlockSpec(memory_space=pltpu.SMEM),
                pl.BlockSpec(entries.shape, lambda i, core: (0, 0)),
                pl.BlockSpec((subs * cols, rows), lambda i, core: (core[0], 0)),
            ],
            out_specs=pl.BlockSpec((2, subs, rows), lambda i, core: (0, 0, 0)),
            scratch_shapes=[pltpu.VMEM((rows // LANES, cols, subs, LANES), F32)],
        ),
        out_shape=jax.ShapeDtypeStruct((2, subs, rows), BF16),
        compiler_params=pltpu.CompilerParams(vmem_limit_bytes=VMEM),
        cost_estimate=pl.CostEstimate(flops=10**8, bytes_accessed=2 * MIB, transcendentals=0),
    )(core, table, entries, flat_field)


def line_coefs(pair, cols):
    decay, turn = pair, pair
    while cols > 1:
        turn = turn * (1.0 + decay * decay)
        decay = decay * decay
        cols //= 2
    return decay, turn


def local_kernel(levels, steps, table_ref, entries_ref, field_ref, after_ref, own_ref, coef_ref, work):
    _, cols, slabs, lanes = work.shape
    own_cols = own_ref.shape[0]
    tile, mem = lax.axis_index("tile"), lax.axis_index("mem")
    perm = transposer(cols)
    for chunk in range(work.shape[0]):
        part = slice(chunk * lanes, (chunk + 1) * lanes)
        to_columns(perm, field_ref.at[:, part], work.at[chunk], cols)
        pair = lookup(table_ref, entries_ref[:, part])
        alpha = jnp.where(iota((slabs, lanes), 0) < levels, pair[0:1], pair[1:2])
        sweep(work.at[chunk], alpha)
        own_ref[:, :, part] = work[chunk, pl.ds(mem * own_cols, own_cols)] * gain_of(alpha)[None]
    pair = lookup(table_ref, entries_ref[...])
    square = pair * pair
    power, sums = jnp.ones_like(pair), jnp.zeros_like(pair)
    rights, geometric = [], []
    for _ in range(cols):
        power, sums = power * pair, sums * square + 1.0
        rights.append(power)
        geometric.append(sums)
    for col in range(cols):
        coef_ref[0, col] = rights[col] * geometric[cols - 1 - col]
        coef_ref[1, col] = rights[cols - 1 - col]
    decay, turn = line_coefs(pair, cols)
    from_left, from_right, turned = jnp.ones_like(pair), jnp.ones_like(pair), jnp.zeros_like(pair)
    for level in range(steps - 1):
        second = ((tile >> level) & 1) == 1
        turned = jnp.where(second, turned * decay, turned + from_right * turn * decay)
        from_left = jnp.where(second, from_left * decay, from_left)
        from_right = jnp.where(second, from_right, from_right * decay)
        turn = turn * (1.0 + decay * decay)
        decay = decay * decay
    second = ((tile >> (steps - 1)) & 1) == 1
    coef_ref[0, cols] = jnp.where(second, from_left, 0.0)
    coef_ref[1, cols] = jnp.where(second, turned, from_right)


def local_call(table, entries, flat_field, after, levels, steps, cols, own_cols):
    total, rows = flat_field.shape
    slabs = padded(total // cols)
    vmem, smem = pl.BlockSpec(memory_space=pltpu.VMEM), pl.BlockSpec(memory_space=pltpu.SMEM)
    return pl.pallas_call(
        functools.partial(local_kernel, levels, steps),
        name="local",
        in_specs=[smem, vmem, vmem, pl.BlockSpec(memory_space=pl.ANY)],
        out_specs=[vmem, vmem],
        out_shape=[
            jax.ShapeDtypeStruct((own_cols, slabs, rows), F32),
            jax.ShapeDtypeStruct((2, cols + 1, 2, rows), F32),
        ],
        scratch_shapes=[pltpu.VMEM((rows // LANES, cols, slabs, LANES), F32)],
        compiler_params=pltpu.CompilerParams(vmem_limit_bytes=VMEM),
        cost_estimate=pl.CostEstimate(flops=5 * 10**8, bytes_accessed=4 * MIB, transcendentals=0),
    )(table, entries, flat_field, after)


def spread(matrix, levels, row_slab, row_col, col_slab, col_col):
    rows, cols = row_slab.shape
    size = matrix.shape[0]
    left = (iota((rows, size), 1) == row_slab[:, :size]).astype(BF16)
    right = (iota((size, cols), 0) == col_slab[:size, :]).astype(BF16)
    inner = dot(left, matrix).astype(BF16)
    full = dot(inner, right)
    full = jnp.where((row_slab >= levels) & (row_slab == col_slab), 1.0, full)
    return jnp.where(row_col == col_col, full, 0.0).astype(BF16)


def ensemble_kernel(levels, cols, loc_ref, field_ref, mine_ref, other_ref, after_ref, send_ref, keep_ref, *work):
    own_cols, count = work[0].shape[0] // 2, keep_ref.shape[0]
    _, slabs, lanes = work[0].shape
    mem = lax.axis_index("mem")
    chip, core = split(mem, 2)
    shape = (2 * own_cols * SUB, cols * SUB)
    (slot, out_slab), (in_slab, in_col) = split(iota(shape, 0), SUB), split(iota(shape, 1), cols)
    first = jnp.where(slot < own_cols, (2 * (1 - chip) + core) * own_cols, (2 * chip + core) * own_cols)
    hit = (out_slab == in_slab) & (first + (slot & (own_cols - 1)) == in_col)
    perm = hit.astype(BF16)
    for ref, out in zip((field_ref, mine_ref, other_ref), work):
        to_columns(perm, ref, out, cols)
    side = own_cols * slabs
    row, col = iota((side, side), 0), iota((side, side), 1)
    (row_col, row_slab), (col_col, col_slab) = split(row, slabs), split(col, slabs)
    local = spread(loc_ref[...], levels, row_slab, row_col, col_slab, col_col)
    row_slab, row_col = split(row, own_cols)
    order = ((row_slab == col_slab) & (row_col == col_col)).astype(BF16)
    for half, out_ref in enumerate((send_ref, keep_ref)):
        part = slice(half * own_cols, (half + 1) * own_cols)
        field = work[0][part]
        total = None
        for member_w in work[1:]:
            member = member_w[part]
            scaled = (member * field).astype(BF16).reshape(side, lanes)
            term = member * dot(local, scaled).reshape(own_cols, slabs, lanes)
            total = term if total is None else total + term
        total = total.reshape(side, lanes)
        high = total.astype(BF16)
        ordered = dot(order, high)
        if out_ref is keep_ref:
            ordered = ordered + dot(order, (total - high.astype(F32)).astype(BF16))
        out_ref[...] = ordered[:count].astype(out_ref.dtype)


def ensemble_call(loc, flat_field, mine, other, after, levels, cols, own_cols):
    total, rows = flat_field.shape
    slab_count = total // cols
    vmem = pl.BlockSpec(memory_space=pltpu.VMEM)
    out_shape = (slab_count * own_cols, rows)
    return pl.pallas_call(
        functools.partial(ensemble_kernel, levels, cols),
        name="ensemble",
        in_specs=[vmem] * 4 + [pl.BlockSpec(memory_space=pl.ANY)],
        out_specs=[vmem, vmem],
        out_shape=[jax.ShapeDtypeStruct(out_shape, BF16), jax.ShapeDtypeStruct(out_shape, F32)],
        scratch_shapes=[pltpu.VMEM((2 * own_cols, padded(slab_count), rows), F32)] * 3,
        compiler_params=pltpu.CompilerParams(vmem_limit_bytes=VMEM),
        cost_estimate=pl.CostEstimate(flops=5 * 10**8, bytes_accessed=8 * MIB, transcendentals=0),
    )(loc, flat_field, mine, other, after)


def tables_kernel(levels, own_cols, col_dev, slabs, table_ref, entries_ref, vert_ref, after_ref, mat_ref, coef_ref, vert_out):
    first = lax.axis_index("tile") * col_dev + lax.axis_index("mem") * own_cols
    count = 2 * own_cols
    alphas = [table_ref[entries_ref[var, first + col]] for var in range(2) for col in range(own_cols)]
    by_lane = jnp.zeros((1, 128), F32)
    by_row = jnp.zeros((count, 1), F32)
    for k, alpha in enumerate(alphas):
        by_lane = jnp.where(iota((1, 128), 1) == k, alpha, by_lane)
        by_row = jnp.where(iota((count, 1), 0) == k, alpha, by_row)

    def series(alpha, number):
        alpha = jnp.broadcast_to(alpha, number.shape)
        total, unit = jnp.zeros(number.shape, F32), jnp.ones(number.shape, F32)
        single, power, both = alpha, alpha * alpha, jnp.ones(number.shape, F32)
        for bit in range(BLOCK.bit_length()):
            here = ((number >> bit) & 1) == 1
            total = jnp.where(here, unit + power * total, total)
            both = jnp.where(here, both * single, both)
            unit, single, power = unit * (1.0 + power), single * single, power * power
        return total, both

    down, _ = series(by_lane, BLOCK - iota((BLOCK, 128), 0))
    place = iota((count, BLOCK), 1)
    across, right = series(by_row, BLOCK - place)
    _, left = series(by_row, place + 1)
    coef_ref[0] = left * across
    coef_ref[1] = right
    coef_ref[2] = jnp.broadcast_to(right[:, 0:1], right.shape)
    coef_ref[3] = jnp.broadcast_to(left[:, 0:1] * across[:, 0:1], right.shape)
    far = jnp.abs(iota((BLOCK, BLOCK), 0) - iota((BLOCK, BLOCK), 1)).astype(F32)
    for k in range(count):
        alpha = by_row[k : k + 1]
        decay = jnp.exp(far * jnp.log(jnp.maximum(alpha, 1e-30)))
        reach = jnp.minimum(down[:, k : k + 1], across[k : k + 1])
        mat_ref[k] = (gain_of(alpha) * decay * reach).astype(BF16)
    shape = vert_out.shape
    (row_slab, row_col), (col_col, col_slab) = split(iota(shape, 0), own_cols), split(iota(shape, 1), slabs)
    vert_out[...] = spread(vert_ref[...], levels, row_slab, row_col, col_slab, col_col)


def tables_call(table, entries, vert, after, levels, own_cols, col_dev, slabs):
    count = 2 * own_cols
    smem = pl.BlockSpec(memory_space=pltpu.SMEM)
    return pl.pallas_call(
        functools.partial(tables_kernel, levels, own_cols, col_dev, slabs),
        name="tables",
        in_specs=[smem, smem, pl.BlockSpec(memory_space=pltpu.VMEM), pl.BlockSpec(memory_space=pl.ANY)],
        out_specs=[pl.BlockSpec(memory_space=pltpu.VMEM)] * 3,
        out_shape=[
            jax.ShapeDtypeStruct((count, BLOCK, BLOCK), BF16),
            jax.ShapeDtypeStruct((4, count, BLOCK), F32),
            jax.ShapeDtypeStruct((own_cols * slabs, own_cols * slabs), BF16),
        ],
        compiler_params=pltpu.CompilerParams(vmem_limit_bytes=VMEM),
        cost_estimate=pl.CostEstimate(flops=10**8, bytes_accessed=2 * MIB, transcendentals=0),
    )(table, entries, vert, after)


def along_rows(lines, matrix, coef):
    count, rows = lines.shape
    blocks = rows // BLOCK
    parts = jnp.concatenate([lines[:, b * BLOCK : (b + 1) * BLOCK] for b in range(blocks)], 0)
    local = dot(parts.astype(BF16), matrix)
    local = [local[b * count : (b + 1) * count] for b in range(blocks)]
    into, right, decay, turn = coef[0:1], coef[1:2], coef[2:3, 0:1], coef[3:4, 0:1]
    forward, state = [None], None
    for b in range(blocks - 1):
        end = local[b][:, BLOCK - 1 : BLOCK]
        state = end if state is None else decay * state + end
        forward.append(state)
    out, state = [None] * blocks, None
    for b in range(blocks - 1, -1, -1):
        piece = local[b]
        if forward[b] is not None:
            piece = piece + into * forward[b]
        if state is not None:
            piece = piece + right * state
        out[b] = piece
        if b:
            start = local[b][:, 0:1] + turn * forward[b]
            state = start if state is None else decay * state + start
    return out


def final_kernel(
    levels, scale, own_ref, coef_ref, part_0_ref, part_1_ref, last_0_ref, last_1_ref, mat_ref, row_coef_ref, vert_ref,
    keep_ref, came_ref, out_ref, carry, last, smooth, filt
):
    own_cols, slabs, rows = own_ref.shape
    cols = coef_ref.shape[1] - 1
    mem = lax.axis_index("mem")
    subs = slabs // CORES
    core = mem & (CORES - 1)
    for flip, part_ref, last_ref in ((0, part_0_ref, last_0_ref), (1, part_1_ref, last_1_ref)):
        share = pl.ds(pl.multiple_of((core ^ flip) * subs, subs), subs)
        carry[:, share, :] = part_ref[...].astype(F32)
        last[share, :] = last_ref[...].astype(F32)
    top = levels // 8 * 8
    is_level = iota((8, rows), 0) < levels - top
    for side in range(2):
        old = carry[side, top : top + 8]
        carry[side] = carry[side] + coef_ref[side, cols, 0:1] * last[...]
        other = old + coef_ref[side, cols, 1:2] * last[top : top + 8]
        carry[side, top : top + 8] = jnp.where(is_level, carry[side, top : top + 8], other)
    for col in range(own_cols):
        pair = coef_ref[:, mem * own_cols + col]
        smooth[col] = own_ref[col] + pair[0, 0:1] * carry[0] + pair[1, 0:1] * carry[1]
        end = slice(top, top + 8)
        other = own_ref[col, end] + pair[0, 1:2] * carry[0, end] + pair[1, 1:2] * carry[1, end]
        smooth[col, end] = jnp.where(is_level, smooth[col, end], other)
    for col in range(own_cols):
        lines = smooth[col]
        main = along_rows(lines, mat_ref[col], row_coef_ref[:, col])
        last = along_rows(lines[top : top + 8], mat_ref[own_cols + col], row_coef_ref[:, own_cols + col])
        for b, (piece, extra) in enumerate(zip(main, last)):
            place = slice(b * BLOCK, (b + 1) * BLOCK)
            filt[col * slabs : col * slabs + slabs, place] = piece
            filt[col * slabs + top : col * slabs + top + 8, place] = jnp.where(
                iota((8, BLOCK), 0) < levels - top, piece[top : top + 8], extra
            )
    count = out_ref.shape[0]
    for start in range(0, rows, BLOCK):
        part = slice(start, start + BLOCK)
        static = filt[:, part]
        high = static.astype(BF16)
        low = (static - high.astype(F32)).astype(BF16)
        total = dot(vert_ref[...], high) + dot(vert_ref[...], low)
        ens = keep_ref[:, part] + came_ref[:, part].astype(F32)
        total = total[: count * own_cols] + ens * scale
        out_ref[:, :, part] = total.reshape(count, own_cols, BLOCK).astype(BF16)


def final_call(slab_count, levels, scale, args):
    own_cols, slabs, rows = args[0].shape
    vmem = pl.BlockSpec(memory_space=pltpu.VMEM)
    return pl.pallas_call(
        functools.partial(final_kernel, levels, scale),
        name="final",
        in_specs=[vmem] * len(args),
        out_specs=vmem,
        out_shape=jax.ShapeDtypeStruct((slab_count, own_cols, rows), BF16),
        scratch_shapes=[
            pltpu.VMEM((2, slabs, rows), F32),
            pltpu.VMEM((slabs, rows), F32),
            pltpu.VMEM((own_cols, slabs, rows), F32),
            pltpu.VMEM((own_cols * slabs, rows), F32),
        ],
        compiler_params=pltpu.CompilerParams(vmem_limit_bytes=VMEM),
        cost_estimate=pl.CostEstimate(flops=10**9, bytes_accessed=6 * MIB, transcendentals=0),
    )(*args)


def merge_kernel(levels, cols, step, last, after_count, *refs):
    table_ref, entries_ref = refs[:2]
    pairs = refs[2 : 4 + 2 * step]
    out_ref, *part_ref = refs[4 + 2 * step + after_count :]
    _, subs, rows = pairs[0].shape
    tile, mem = lax.axis_index("tile"), lax.axis_index("mem")
    decay, turn = line_coefs(lookup(table_ref, entries_ref[...]), cols)
    is_level = iota((subs, rows), 0) + (mem & (CORES - 1)) * subs < levels
    decay = jnp.where(is_level, decay[0:1], decay[1:2])
    turn = jnp.where(is_level, turn[0:1], turn[1:2])
    from_left, from_right, turned, left, right = 1.0, 1.0, 0.0, 0.0, 0.0
    for level in range(step + 1):
        second = ((tile >> level) & 1) == 1
        if last or level == step:
            mine, came = (pairs[2 * level + k][...].astype(F32) for k in range(2))
            lower = jnp.where(second, came, mine)
            upper = jnp.where(second, mine, came)
            bent = turn * lower[0] + upper[1]
        if last:
            left = left + jnp.where(second, from_left * lower[0], 0.0)
            right = right + jnp.where(second, turned * lower[0], from_right * bent)
            turned = jnp.where(second, turned * decay, turned + from_right * turn * decay)
            from_left = jnp.where(second, from_left * decay, from_left)
            from_right = jnp.where(second, from_right, from_right * decay)
        if level == step:
            block = decay * lower[0] + upper[0], lower[1] + decay * bent
        turn = turn * (1.0 + decay * decay)
        decay = decay * decay
    if last:
        second = ((tile >> (step + 1)) & 1) == 1
        out_ref[...] = jnp.where(second, block[1], block[0]).astype(BF16)
        part_ref[0][0] = left.astype(BF16)
        part_ref[0][1] = jnp.where(second, right, right + from_right * turn * block[0]).astype(BF16)
    else:
        out_ref[0] = block[0].astype(BF16)
        out_ref[1] = block[1].astype(BF16)


def merge_call(table, entries, pairs, after, levels, cols, last):
    step = len(pairs) // 2 - 1
    whole = jax.ShapeDtypeStruct(pairs[0].shape, BF16)
    outs = [jax.ShapeDtypeStruct(whole.shape[1:], BF16), whole] if last else [whole]
    vmem, smem = pl.BlockSpec(memory_space=pltpu.VMEM), pl.BlockSpec(memory_space=pltpu.SMEM)
    held = [pl.BlockSpec(memory_space=pl.ANY)] * len(after)
    return pl.pallas_call(
        functools.partial(merge_kernel, levels, cols, step, last, len(after)),
        name="merge",
        in_specs=[smem] + [vmem] * (1 + len(pairs)) + held,
        out_specs=[vmem] * len(outs) + held,
        out_shape=outs + [jax.ShapeDtypeStruct(array.shape, array.dtype) for array in after],
        input_output_aliases={2 + len(pairs) + k: len(outs) + k for k in range(len(after))},
        compiler_params=pltpu.CompilerParams(vmem_limit_bytes=VMEM),
        cost_estimate=pl.CostEstimate(flops=10**6, bytes_accessed=MIB // 4, transcendentals=0),
    )(table, entries, *pairs, *after)


def body(field, vert_filter, loc_filter, alpha_table, xscale_idx, yscale_idx, members):
    tile_count, mem_count = lax.axis_size("tile"), lax.axis_size("mem")
    slab_count, cols, rows = field.shape
    levels = vert_filter.shape[1]
    own_cols = cols // mem_count
    slabs = padded(slab_count)
    steps = tile_count.bit_length() - 1

    def swap(array, flip, axis="mem"):
        return lax.ppermute(array, axis, [(i, i ^ flip) for i in range(lax.axis_size(axis))])

    def merge(pairs, after):
        last = len(pairs) == 2 * (steps - 1)
        return merge_call(alpha_table, xscale_idx, pairs, after, levels, cols, last)

    full_field = field.reshape(slab_count * cols, rows)
    flat_field = pltpu.with_memory_space_constraint(full_field, pltpu.HBM)
    mine = members.reshape(slab_count * cols, rows)
    other = swap(mine, 1)
    core = (lax.axis_index("mem") & (CORES - 1)).astype(jnp.int32).reshape(1)
    alpha_table = pltpu.with_memory_space_constraint(alpha_table, pltpu.HBM)
    xscale_idx = pltpu.with_memory_space_constraint(xscale_idx, pltpu.HBM)
    block = ends_call(core, alpha_table, xscale_idx, flat_field, levels, cols)

    pairs = [block, swap(block, 1, "tile")]
    own, coef = local_call(alpha_table, xscale_idx, full_field, block, levels, steps, cols, own_cols)
    send, keep = ensemble_call(loc_filter[0], full_field, mine, other, own, levels, cols, own_cols)
    block, send = merge(pairs, [send])
    came = swap(send, 2)
    pairs += [block, swap(block, 2, "tile")]
    mats, row_coef, vert = tables_call(alpha_table, yscale_idx, vert_filter[0], block, levels, own_cols, cols, slabs)
    held = [mats]
    for step in range(2, steps):
        block, *rest = merge(pairs, held)
        if held:
            mats, held = rest.pop(), []
        if step < steps - 1:
            pairs += [block, swap(block, 1 << step, "tile")]
    last = swap(block, tile_count // 2, "tile")
    shares = [rest[0], swap(rest[0], 1), last, swap(last, 1)]
    scale = 1.0 / (mem_count * members.shape[0] - 1)
    return final_call(slab_count, levels, scale, [own, coef, *shares, mats, row_coef, vert, keep, came])


def solution(mesh):
    return jax.shard_map(
        body,
        mesh=mesh,
        in_specs=(P(None, "tile", None), P(), P(), P(), P(), P(), P("mem", None, "tile", None)),
        out_specs=P(None, ("tile", "mem"), None),
        check_vma=False,
    )
```

time: 32.9 us -> 28.8 us (0.88)
  Pallas kernels: 16.6 us -> 13.5 us
  starting transfers between devices: 11.3 us -> 8.83 us
  waiting for transfers between devices: 4.54 us -> 5.99 us
    ppermute x9 -> x7, starting transfers between devices: 11.3 us -> 8.83 us  [swap(): lax.ppermute(array, axis, [(i, i ^ flip) for i in range(lax.axis_size(axi...]
    pallas_call x2 -> x1, Pallas kernels: 6.44 us -> 4.05 us  [ensemble_call(): pl.pallas_call(functools.partial(ensemble_kernel, levels, cols), name='en...]
    ppermute x9 -> x7, waiting for transfers between devices: 4.54 us -> 5.99 us  [swap(): lax.ppermute(array, axis, [(i, i ^ flip) for i in range(lax.axis_size(axi...]
    pallas_call x4 -> x3, Pallas kernels: 4.66 us -> 3.9 us  [the longest x1 2.13 us: local_call(): pl.pallas_call(functools.partial(local_kernel, levels, steps), name='loca...]
    pallas_call x1, Pallas kernels: 1.63 us -> 2.09 us  [ends_call(): pl.pallas_call(functools.partial(ends_kernel, levels, total // cols), nam...]
    pallas_call x1, Pallas kernels: 1.89 us -> 1.54 us  [tables_call(): pl.pallas_call(functools.partial(tables_kernel, levels, own_cols, col_dev...]
  transfers between devices with their start and end apart: 9 -> 7, of which waited for: 3 -> 3; matrix products, arithmetic and copies ran while one was open for 0% -> 0% of each run, Pallas kernels for 43% -> 38%
where the time goes in v4:
time: 28.8 us; the launch traced here: 28.5 us
  Pallas kernels  13.5 us (47%)
  starting transfers between devices  8.83 us (31%)
  waiting for transfers between devices  5.99 us (21%)
    ppermute x7, starting transfers between devices, swap(): lax.ppermute(array, axis, [(i, i ^ flip) for i in range(lax.axis_size(axi...  8.83 us
    ppermute x7, waiting for transfers between devices, swap(): lax.ppermute(array, axis, [(i, i ^ flip) for i in range(lax.axis_size(axi...  5.99 us
    pallas_call x1, Pallas kernels, ensemble_call(): pl.pallas_call(functools.partial(ensemble_kernel, levels, cols), name='en...  4.05 us
    pallas_call x1, Pallas kernels, local_call(): pl.pallas_call(functools.partial(local_kernel, levels, steps), name='loca...  2.13 us
    pallas_call x1, Pallas kernels, ends_call(): pl.pallas_call(functools.partial(ends_kernel, levels, total // cols), nam...  2.09 us
    pallas_call x1, Pallas kernels, final_call(): pl.pallas_call(functools.partial(final_kernel, levels, scale), name='fina...  1.94 us
    pallas_call x2, Pallas kernels, merge_call(): pl.pallas_call(functools.partial(merge_kernel, levels, cols, step, last,...  1.78 us
    pallas_call x1, Pallas kernels, tables_call(): pl.pallas_call(functools.partial(tables_kernel, levels, own_cols, col_dev...  1.54 us
  transfers between devices with their start and end apart: 7, of which 3 were waited for; matrix products, arithmetic and copies ran while one was open for 0% of the time, Pallas kernels for 38%

profile of v4, /device:TPU:0, one launch (start us, length us, event | category | flops | bytes accessed | tf_op | source)
XLA Modules:
  0.0 28.5 jit_solution(5771917767518693270)
XLA Ops:
  0.0 0.0 copy-start
  0.0 0.5 %collective-permute-start.1 = (bf16[976,1024]{1,0:T(8,128)(2,1)}, bf16[976,1024]{1,0:T(8,128)(2,1)}, u32[]{:S(2)}, u32[]{:S(2)}) collective-permute-start(bf16[976,1024]{1,0:T(8,128)(2,1)} %bitcast.8), channel_id=1, source_target_pairs={{0,1},{1,0},{2,3},{3,2},{4,5},{5,4},{6,7},{7,6},{8,9},{9,8},{10,11... | collective-permute-start | bytes 5996552 | tf_op jit(solution)/shard_map/ppermute | solution.py:459
  0.5 0.0 copy-start.1
  0.5 0.0 copy-start.2
  0.5 2.1 %ends.1.after_ref.refs_2_ = bf16[2,32,1024]{2,1,0:T(8,128)(2,1)S(1)} custom-call(s32[1]{0:T(128)} %bitcast.1.core_ref, f32[16]{0:T(128)} %refs_0_.3, s32[2,1024]{1,0:T(2,128)} %refs_1_.3, bf16[976,1024]{1,0:T(8,128)(2,1)} %bitcast.5), custom_call_target="tpu_custom_call" | custom-call | flops 100000000 | bytes 2097152 | tf_op jit(solution)/shard_map/ends/pallas_call | solution.py:94
  2.6 2.6 %collective-permute-start = (bf16[2,32,1024]{2,1,0:T(8,128)(2,1)S(1)}, bf16[2,32,1024]{2,1,0:T(8,128)(2,1)S(1)}, u32[]{:S(2)}, u32[]{:S(2)}) collective-permute-start(bf16[2,32,1024]{2,1,0:T(8,128)(2,1)S(1)} %ends.1.after_ref.refs_2_), channel_id=1, source_target_pairs={{0,4},{4,0},{8,12},{12,8},{16,20},{20,16},{24,28},{28,24},{1,5},{5... | collective-permute-start | bytes 393224 | tf_op jit(solution)/shard_map/ppermute | solution.py:459
  5.1 0.0 copy-done
  5.1 2.1 %local.1 = (f32[4,64,1024]{2,1,0:T(8,128)S(1)}, f32[2,17,2,1024]{3,2,1,0:T(2,128)S(1)}) custom-call(f32[16]{0:T(128)} %refs_0_.3, s32[2,1024]{1,0:T(2,128)} %refs_1_.3, bf16[976,1024]{1,0:T(8,128)(2,1)S(1)} %bitcast.6, bf16[2,32,1024]{2,1,0:T(8,128)(2,1)S(1)} %ends.1.after_ref.refs_2_), custom_call_target="tpu_custom_call" | custom-call | flops 500000000 | bytes 4194304 | tf_op jit(solution)/shard_map/local/pallas_call | solution.py:164
  7.3 0.0 collective-permute-done.1.other_ref
  7.3 0.0 copy-done.1
  7.3 0.0 copy-done.2
  7.3 0.0 copy-start.3
  7.3 0.0 copy-start.4
  7.3 4.0 %ensemble.1 = (bf16[244,1024]{1,0:T(8,128)(2,1)S(1)}, f32[244,1024]{1,0:T(8,128)S(1)}) custom-call(bf16[60,60]{1,0:T(8,128)(2,1)S(1)} %bitcast.10, bf16[976,1024]{1,0:T(8,128)(2,1)S(1)} %bitcast.7, bf16[976,1024]{1,0:T(8,128)(2,1)S(1)} %bitcast.9, bf16[976,1024]{1,0:T(8,128)(2,1)} %collective-permute-done.1.other_ref, ...), custom_call_target="tpu_custom_call" | custom-call | flops 500000000 | bytes 8388608 | tf_op jit(solution)/shard_map/ensemble/pallas_call | solution.py:230
  11.4 0.0 collective-permute-done.refs_3_
  11.4 0.8 %merge.2 = (bf16[2,32,1024]{2,1,0:T(8,128)(2,1)S(1)}, bf16[244,1024]{1,0:T(8,128)(2,1)S(1)}) custom-call(f32[16]{0:T(128)} %refs_0_.3, s32[2,1024]{1,0:T(2,128)} %refs_1_.3, bf16[2,32,1024]{2,1,0:T(8,128)(2,1)S(1)} %ends.1.after_ref.refs_2_, bf16[2,32,1024]{2,1,0:T(8,128)(2,1)S(1)} %collective-permute-done.refs_3_, ...), custom_call_target="tpu_custom_call", output_to_operand_aliasing={{1}: (4, {})} | custom-call | flops 1000000 | bytes 262144 | tf_op jit(solution)/shard_map/merge/pallas_call | solution.py:438
  12.2 1.6 %collective-permute-start.6 = (bf16[244,1024]{1,0:T(8,128)(2,1)S(1)}, bf16[244,1024]{1,0:T(8,128)(2,1)S(1)}, u32[]{:S(2)}, u32[]{:S(2)}) collective-permute-start(bf16[244,1024]{1,0:T(8,128)(2,1)S(1)} %get-tuple-element.28), channel_id=1, source_target_pairs={{0,2},{1,3},{2,0},{3,1},{4,6},{5,7},{6,4},{7,5},{8,10},{9,11},{10,... | collective-permute-start | bytes 1499144 | tf_op jit(solution)/shard_map/ppermute | solution.py:459
  13.8 1.6 %collective-permute-start.2 = (bf16[2,32,1024]{2,1,0:T(8,128)(2,1)S(1)}, bf16[2,32,1024]{2,1,0:T(8,128)(2,1)S(1)}, u32[]{:S(2)}, u32[]{:S(2)}) collective-permute-start(bf16[2,32,1024]{2,1,0:T(8,128)(2,1)S(1)} %get-tuple-element.20.after_ref.refs_4_), channel_id=1, source_target_pairs={{0,8},{4,12},{8,0},{12,4},{16,24},{20,28},{24,16},{28,20},{1,9},{5... | collective-permute-start | bytes 393224 | tf_op jit(solution)/shard_map/ppermute | solution.py:459
  15.3 0.0 copy-done.3
  15.3 0.0 copy-done.4
  15.4 1.5 %tables.1 = (bf16[8,256,256]{2,1,0:T(8,128)(2,1)S(1)}, f32[4,8,256]{2,1,0:T(8,128)S(1)}, bf16[256,256]{1,0:T(8,128)(2,1)S(1)}) custom-call(f32[16]{0:T(128)} %refs_0_.3, s32[2,128]{1,0:T(2,128)S(1)} %copy-done.4, bf16[60,60]{1,0:T(8,128)(2,1)S(1)} %bitcast.11, bf16[2,32,1024]{2,1,0:T(8,128)(2,1)S(1)} %get-tuple-element.20.after_ref.refs_4_), custom_call_target="tpu_custom_call" | custom-call | flops 100000000 | bytes 2097152 | tf_op jit(solution)/shard_map/tables/pallas_call | solution.py:285
  16.9 2.2 %collective-permute-done.2.refs_5_ = bf16[2,32,1024]{2,1,0:T(8,128)(2,1)S(1)} collective-permute-done((bf16[2,32,1024]{2,1,0:T(8,128)(2,1)S(1)}, bf16[2,32,1024]{2,1,0:T(8,128)(2,1)S(1)}, u32[]{:S(2)}, u32[]{:S(2)}) %collective-permute-start.2) | collective-permute-done | bytes 131104 | tf_op jit(solution)/shard_map/ppermute | solution.py:459
  19.1 1.0 %merge.3 = (bf16[32,1024]{1,0:T(8,128)(2,1)S(1)}, bf16[2,32,1024]{2,1,0:T(8,128)(2,1)S(1)}, bf16[8,256,256]{2,1,0:T(8,128)(2,1)S(1)}) custom-call(f32[16]{0:T(128)} %refs_0_.3, s32[2,1024]{1,0:T(2,128)} %refs_1_.3, bf16[2,32,1024]{2,1,0:T(8,128)(2,1)S(1)} %ends.1.after_ref.refs_2_, ...), custom_call_target="tpu_custom_call", output_to_operand_aliasing={{2}: (6, {})} | custom-call | flops 1000000 | bytes 262144 | tf_op jit(solution)/shard_map/merge/pallas_call | solution.py:438
  20.0 2.7 %collective-permute-start.4 = (bf16[32,1024]{1,0:T(8,128)(2,1)S(1)}, bf16[32,1024]{1,0:T(8,128)(2,1)S(1)}, u32[]{:S(2)}, u32[]{:S(2)}) collective-permute-start(bf16[32,1024]{1,0:T(8,128)(2,1)S(1)} %get-tuple-element.23), channel_id=1, source_target_pairs={{0,16},{4,20},{8,24},{12,28},{16,0},{20,4},{24,8},{28,12},{1,17},{... | collective-permute-start | bytes 196616 | tf_op jit(solution)/shard_map/ppermute | solution.py:459
  22.7 0.0 collective-permute-start.3
  22.7 2.6 %collective-permute-done.4.last_0_ref = bf16[32,1024]{1,0:T(8,128)(2,1)S(1)} collective-permute-done((bf16[32,1024]{1,0:T(8,128)(2,1)S(1)}, bf16[32,1024]{1,0:T(8,128)(2,1)S(1)}, u32[]{:S(2)}, u32[]{:S(2)}) %collective-permute-start.4) | collective-permute-done | bytes 65568 | tf_op jit(solution)/shard_map/ppermute | solution.py:459
  25.3 0.0 collective-permute-start.5
  25.3 1.3 %collective-permute-done.5.last_1_ref = bf16[32,1024]{1,0:T(8,128)(2,1)S(1)} collective-permute-done((bf16[32,1024]{1,0:T(8,128)(2,1)S(1)}, bf16[32,1024]{1,0:T(8,128)(2,1)S(1)}, u32[]{:S(2)}, u32[]{:S(2)}) %collective-permute-start.5) | collective-permute-done | bytes 65568 | tf_op jit(solution)/shard_map/ppermute | solution.py:459
  26.5 0.0 collective-permute-done.3.part_1_ref
  26.5 0.0 collective-permute-done.6.came_ref
  26.5 1.9 %final.1 = bf16[61,4,1024]{2,1,0:T(4,128)(2,1)} custom-call(f32[4,64,1024]{2,1,0:T(8,128)S(1)} %get-tuple-element.17.after_ref.own_ref, f32[2,17,2,1024]{3,2,1,0:T(2,128)S(1)} %get-tuple-element.18.coef_ref, bf16[2,32,1024]{2,1,0:T(8,128)(2,1)S(1)} %get-tuple-element.22.part_0_ref, bf16[2,32,1024]{2,1,0:T(8,128)(2,1)S(1)} %collective-permute-done.3.part_1_ref, ...), custom_call_target="tpu_custom_call" | custom-call | flops 1000000000 | bytes 6291456 | tf_op jit(solution)/shard_map/final/pallas_call | solution.py:377
Async XLA Ops:
  0.0 5.1 %copy-start = (bf16[61,16,1024]{2,1,0:T(8,128)(2,1)S(1)}, bf16[61,16,1024]{2,1,0:T(8,128)(2,1)}, u32[]{:S(2)}) copy-start(bf16[61,16,1024]{2,1,0:T(8,128)(2,1)} %param.7) | copy-start | bytes 5996548
  0.0 7.3 %collective-permute-start.1 = (bf16[976,1024]{1,0:T(8,128)(2,1)}, bf16[976,1024]{1,0:T(8,128)(2,1)}, u32[]{:S(2)}, u32[]{:S(2)}) collective-permute-start(bf16[976,1024]{1,0:T(8,128)(2,1)} %bitcast.8), channel_id=1, source_target_pairs={{0,1},{1,0},{2,3},{3,2},{4,5},{5,4},{6,7},{7,6},{8,9},{9,8},{10,11... | collective-permute-start | bytes 5996552 | tf_op jit(solution)/shard_map/ppermute | solution.py:459
  0.5 6.8 %copy-start.1 = (bf16[1,61,16,1024]{3,2,1,0:T(8,128)(2,1)S(1)}, bf16[1,61,16,1024]{3,2,1,0:T(8,128)(2,1)}, u32[]{:S(2)}) copy-start(bf16[1,61,16,1024]{3,2,1,0:T(8,128)(2,1)} %param.13) | copy-start | bytes 5996548
  0.5 6.8 %copy-start.2 = (bf16[1,60,60]{2,1,0:T(8,128)(2,1)S(1)}, bf16[1,60,60]{2,1,0:T(8,128)(2,1)}, u32[]{:S(2)}) copy-start(bf16[1,60,60]{2,1,0:T(8,128)(2,1)} %param.9) | copy-start | bytes 21604
  2.6 8.8 %collective-permute-start = (bf16[2,32,1024]{2,1,0:T(8,128)(2,1)S(1)}, bf16[2,32,1024]{2,1,0:T(8,128)(2,1)S(1)}, u32[]{:S(2)}, u32[]{:S(2)}) collective-permute-start(bf16[2,32,1024]{2,1,0:T(8,128)(2,1)S(1)} %ends.1.after_ref.refs_2_), channel_id=1, source_target_pairs={{0,4},{4,0},{8,12},{12,8},{16,20},{20,16},{24,28},{28,24},{1,5},{5... | collective-permute-start | bytes 393224 | tf_op jit(solution)/shard_map/ppermute | solution.py:459
  7.3 8.0 %copy-start.3 = (bf16[1,60,60]{2,1,0:T(8,128)(2,1)S(1)}, bf16[1,60,60]{2,1,0:T(8,128)(2,1)}, u32[]{:S(2)}) copy-start(bf16[1,60,60]{2,1,0:T(8,128)(2,1)} %param.8) | copy-start | bytes 21604
  7.3 8.0 %copy-start.4 = (s32[2,128]{1,0:T(2,128)S(1)}, s32[2,128]{1,0:T(2,128)}, u32[]{:S(2)}) copy-start(s32[2,128]{1,0:T(2,128)} %entries_ref.5) | copy-start | bytes 3076
  12.2 14.3 %collective-permute-start.6 = (bf16[244,1024]{1,0:T(8,128)(2,1)S(1)}, bf16[244,1024]{1,0:T(8,128)(2,1)S(1)}, u32[]{:S(2)}, u32[]{:S(2)}) collective-permute-start(bf16[244,1024]{1,0:T(8,128)(2,1)S(1)} %get-tuple-element.28), channel_id=1, source_target_pairs={{0,2},{1,3},{2,0},{3,1},{4,6},{5,7},{6,4},{7,5},{8,10},{9,11},{10,... | collective-permute-start | bytes 1499144 | tf_op jit(solution)/shard_map/ppermute | solution.py:459
  13.8 5.3 %collective-permute-start.2 = (bf16[2,32,1024]{2,1,0:T(8,128)(2,1)S(1)}, bf16[2,32,1024]{2,1,0:T(8,128)(2,1)S(1)}, u32[]{:S(2)}, u32[]{:S(2)}) collective-permute-start(bf16[2,32,1024]{2,1,0:T(8,128)(2,1)S(1)} %get-tuple-element.20.after_ref.refs_4_), channel_id=1, source_target_pairs={{0,8},{4,12},{8,0},{12,4},{16,24},{20,28},{24,16},{28,20},{1,9},{5... | collective-permute-start | bytes 393224 | tf_op jit(solution)/shard_map/ppermute | solution.py:459
  20.0 5.2 %collective-permute-start.4 = (bf16[32,1024]{1,0:T(8,128)(2,1)S(1)}, bf16[32,1024]{1,0:T(8,128)(2,1)S(1)}, u32[]{:S(2)}, u32[]{:S(2)}) collective-permute-start(bf16[32,1024]{1,0:T(8,128)(2,1)S(1)} %get-tuple-element.23), channel_id=1, source_target_pairs={{0,16},{4,20},{8,24},{12,28},{16,0},{20,4},{24,8},{28,12},{1,17},{... | collective-permute-start | bytes 196616 | tf_op jit(solution)/shard_map/ppermute | solution.py:459
  22.7 3.8 %collective-permute-start.3 = (bf16[2,32,1024]{2,1,0:T(8,128)(2,1)S(1)}, bf16[2,32,1024]{2,1,0:T(8,128)(2,1)S(1)}, u32[]{:S(2)}, u32[]{:S(2)}) collective-permute-start(bf16[2,32,1024]{2,1,0:T(8,128)(2,1)S(1)} %get-tuple-element.22.part_0_ref), channel_id=1, source_target_pairs={{0,1},{1,0},{2,3},{3,2},{4,5},{5,4},{6,7},{7,6},{8,9},{9,8},{10,11... | collective-permute-start | bytes 393224 | tf_op jit(solution)/shard_map/ppermute | solution.py:459
  25.3 1.3 %collective-permute-start.5 = (bf16[32,1024]{1,0:T(8,128)(2,1)S(1)}, bf16[32,1024]{1,0:T(8,128)(2,1)S(1)}, u32[]{:S(2)}, u32[]{:S(2)}) collective-permute-start(bf16[32,1024]{1,0:T(8,128)(2,1)S(1)} %collective-permute-done.4.last_0_ref), channel_id=1, source_target_pairs={{0,1},{1,0},{2,3},{3,2},{4,5},{5,4},{6,7},{7,6},{8,9},{9,8},{10,11... | collective-permute-start | bytes 196616 | tf_op jit(solution)/shard_map/ppermute | solution.py:459

commit v5 on v4

--- a/solution.py
+++ b/solution.py
@@ -20,6 +20,10 @@
     return lax.broadcasted_iota(jnp.int32, shape, dim)
 
 
+def taking(microseconds):
+    return pl.CostEstimate(flops=int(microseconds * 1.15e9), bytes_accessed=MIB // 4, transcendentals=0)
+
+
 def split(number, size):
     assert size & (size - 1) == 0
     return number >> (size.bit_length() - 1), number & (size - 1)
@@ -52,7 +56,7 @@
     for chunk in range(out_ref.shape[1] // SUB):
         depth = min(step, total - chunk * step)
         moved = dot(perm[:, :depth], flat[chunk * step : chunk * step + depth])
-        out_ref[:, chunk * SUB : (chunk + 1) * SUB, :] = moved.reshape(wanted, SUB, -1)
+        out_ref[:, chunk * SUB : (chunk + 1) * SUB, :] = moved.reshape(wanted, SUB, -1).astype(out_ref.dtype)
 
 
 def sweep(work, alpha):
@@ -72,27 +76,54 @@
     return ((out_slab == in_slab) & (out_col == in_col)).astype(BF16)
 
 
-def ends_kernel(levels, slab_count, core_ref, table_ref, entries_ref, field_ref, ends_ref, work):
+def line_coefs(pair, cols):
+    decay, turn = pair, pair
+    while cols > 1:
+        turn = turn * (1.0 + decay * decay)
+        decay = decay * decay
+        cols //= 2
+    return decay, turn
+
+
+def reflected(decay, turn, tile, steps):
+    behind = (1 << steps) - 1 - tile
+    total, power = jnp.zeros_like(turn), jnp.ones_like(turn)
+    for level in range(steps):
+        here = ((behind >> level) & 1) == 1
+        total = jnp.where(here, total + power * power * turn, total)
+        power = jnp.where(here, power * decay, power)
+        turn = turn * (1.0 + decay * decay)
+        decay = decay * decay
+    return total
+
+
+def ends_kernel(levels, steps, slab_count, core_ref, table_ref, entries_ref, field_ref, ends_ref, work):
     _, cols, subs, lanes = work.shape
     first = core_ref[0] * subs
+    tile = lax.axis_index("tile")
     perm = transposer(cols)
     for chunk in range(work.shape[0]):
         part = slice(chunk * lanes, (chunk + 1) * lanes)
         held = jnp.where(iota((cols * subs, lanes), 0) < (slab_count - first) * cols, field_ref[:, part], 0)
         to_columns(perm, held, work.at[chunk], cols)
         pair = lookup(table_ref, entries_ref[:, part])
-        alpha = jnp.where(iota((subs, lanes), 0) + first < levels, pair[0:1], pair[1:2])
+        is_level = iota((subs, lanes), 0) + first < levels
+        alpha = jnp.where(is_level, pair[0:1], pair[1:2])
         sweep(work.at[chunk], alpha)
         gain = gain_of(alpha)
-        ends_ref[0, :, part] = (gain * work[chunk, cols - 1]).astype(BF16)
-        ends_ref[1, :, part] = (gain * work[chunk, 0]).astype(BF16)
-
-
-def ends_call(core, table, entries, flat_field, levels, cols):
+        decay, turn = line_coefs(pair, cols)
+        behind = decay * reflected(decay, turn, tile, steps)
+        behind = jnp.where(is_level, behind[0:1], behind[1:2])
+        forward = gain * work[chunk, cols - 1]
+        ends_ref[0, :, part] = forward.astype(BF16)
+        ends_ref[1, :, part] = (gain * work[chunk, 0] + behind * forward).astype(BF16)
+
+
+def ends_call(core, table, entries, flat_field, levels, steps, cols):
     total, rows = flat_field.shape
     subs = padded(total // cols) // CORES
     return pl.pallas_call(
-        functools.partial(ends_kernel, levels, total // cols),
+        functools.partial(ends_kernel, levels, steps, total // cols),
         name="ends",
         grid_spec=pltpu.PrefetchScalarGridSpec(
             num_scalar_prefetch=1,
@@ -107,17 +138,8 @@
         ),
         out_shape=jax.ShapeDtypeStruct((2, subs, rows), BF16),
         compiler_params=pltpu.CompilerParams(vmem_limit_bytes=VMEM),
-        cost_estimate=pl.CostEstimate(flops=10**8, bytes_accessed=2 * MIB, transcendentals=0),
+        cost_estimate=taking(2.1),
     )(core, table, entries, flat_field)
-
-
-def line_coefs(pair, cols):
-    decay, turn = pair, pair
-    while cols > 1:
-        turn = turn * (1.0 + decay * decay)
-        decay = decay * decay
-        cols //= 2
-    return decay, turn
 
 
 def local_kernel(levels, steps, table_ref, entries_ref, field_ref, after_ref, own_ref, coef_ref, work):
@@ -144,17 +166,19 @@
         coef_ref[0, col] = rights[col] * geometric[cols - 1 - col]
         coef_ref[1, col] = rights[cols - 1 - col]
     decay, turn = line_coefs(pair, cols)
-    from_left, from_right, turned = jnp.ones_like(pair), jnp.ones_like(pair), jnp.zeros_like(pair)
-    for level in range(steps - 1):
+    behind = decay * reflected(decay, turn, tile, steps)
+    from_left, from_right = jnp.ones_like(pair), jnp.ones_like(pair)
+    for level in range(steps - 2):
         second = ((tile >> level) & 1) == 1
-        turned = jnp.where(second, turned * decay, turned + from_right * turn * decay)
         from_left = jnp.where(second, from_left * decay, from_left)
         from_right = jnp.where(second, from_right, from_right * decay)
-        turn = turn * (1.0 + decay * decay)
         decay = decay * decay
-    second = ((tile >> (steps - 1)) & 1) == 1
-    coef_ref[0, cols] = jnp.where(second, from_left, 0.0)
-    coef_ref[1, cols] = jnp.where(second, turned, from_right)
+    quarter = tile >> (steps - 2)
+    outer = (quarter == 0) | (quarter == 3)
+    for flip, weight in ((1, 1.0), (2, decay), (3, jnp.where(outer, decay * decay, 1.0))):
+        upper = (quarter ^ flip) < quarter
+        coef_ref[0, cols + flip - 1] = jnp.where(upper, from_left * weight, 0.0)
+        coef_ref[1, cols + flip - 1] = weight * jnp.where(upper, behind * from_left, from_right)
 
 
 def local_call(table, entries, flat_field, after, levels, steps, cols, own_cols):
@@ -168,11 +192,11 @@
         out_specs=[vmem, vmem],
         out_shape=[
             jax.ShapeDtypeStruct((own_cols, slabs, rows), F32),
-            jax.ShapeDtypeStruct((2, cols + 1, 2, rows), F32),
+            jax.ShapeDtypeStruct((2, cols + 3, 2, rows), F32),
         ],
         scratch_shapes=[pltpu.VMEM((rows // LANES, cols, slabs, LANES), F32)],
         compiler_params=pltpu.CompilerParams(vmem_limit_bytes=VMEM),
-        cost_estimate=pl.CostEstimate(flops=5 * 10**8, bytes_accessed=4 * MIB, transcendentals=0),
+        cost_estimate=taking(2.1),
     )(table, entries, flat_field, after)
 
 
@@ -187,56 +211,82 @@
     return jnp.where(row_col == col_col, full, 0.0).astype(BF16)
 
 
-def ensemble_kernel(levels, cols, loc_ref, field_ref, mine_ref, other_ref, after_ref, send_ref, keep_ref, *work):
-    own_cols, count = work[0].shape[0] // 2, keep_ref.shape[0]
-    _, slabs, lanes = work[0].shape
-    mem = lax.axis_index("mem")
-    chip, core = split(mem, 2)
-    shape = (2 * own_cols * SUB, cols * SUB)
-    (slot, out_slab), (in_slab, in_col) = split(iota(shape, 0), SUB), split(iota(shape, 1), cols)
+def member_term(local, member_w, field_w, part):
+    cols, slabs, rows = field_w[part].shape
+    member = member_w[part]
+    scaled = (member * field_w[part].astype(F32)).astype(BF16).reshape(cols * slabs, rows)
+    return member * dot(local, scaled).reshape(cols, slabs, rows)
+
+
+def mine_kernel(
+    levels, cols, loc_ref, field_ref, mine_ref, after_ref, perm_ref, local_ref, order_ref, field_out, total_out, member_w
+):
+    own_cols = field_out.shape[0] // 2
+    slabs = field_out.shape[1]
+    chip, core = split(lax.axis_index("mem"), 2)
+    (slot, out_slab), (in_slab, in_col) = split(iota(perm_ref.shape, 0), SUB), split(iota(perm_ref.shape, 1), cols)
     first = jnp.where(slot < own_cols, (2 * (1 - chip) + core) * own_cols, (2 * chip + core) * own_cols)
     hit = (out_slab == in_slab) & (first + (slot & (own_cols - 1)) == in_col)
     perm = hit.astype(BF16)
-    for ref, out in zip((field_ref, mine_ref, other_ref), work):
-        to_columns(perm, ref, out, cols)
-    side = own_cols * slabs
-    row, col = iota((side, side), 0), iota((side, side), 1)
+    perm_ref[...] = perm
+    row, col = iota(local_ref.shape, 0), iota(local_ref.shape, 1)
     (row_col, row_slab), (col_col, col_slab) = split(row, slabs), split(col, slabs)
     local = spread(loc_ref[...], levels, row_slab, row_col, col_slab, col_col)
+    local_ref[...] = local
     row_slab, row_col = split(row, own_cols)
-    order = ((row_slab == col_slab) & (row_col == col_col)).astype(BF16)
-    for half, out_ref in enumerate((send_ref, keep_ref)):
-        part = slice(half * own_cols, (half + 1) * own_cols)
-        field = work[0][part]
-        total = None
-        for member_w in work[1:]:
-            member = member_w[part]
-            scaled = (member * field).astype(BF16).reshape(side, lanes)
-            term = member * dot(local, scaled).reshape(own_cols, slabs, lanes)
-            total = term if total is None else total + term
-        total = total.reshape(side, lanes)
+    order_ref[...] = ((row_slab == col_slab) & (row_col == col_col)).astype(BF16)
+    to_columns(perm, field_ref, field_out, cols)
+    to_columns(perm, mine_ref, member_w, cols)
+    for part in (slice(0, own_cols), slice(own_cols, 2 * own_cols)):
+        total_out[part] = member_term(local, member_w, field_out, part)
+
+
+def other_kernel(cols, perm_ref, local_ref, order_ref, field_w, total_ref, other_ref, send_ref, keep_ref, member_w):
+    own_cols, count = field_w.shape[0] // 2, keep_ref.shape[0]
+    to_columns(perm_ref[...], other_ref, member_w, cols)
+    for part, out_ref in ((slice(0, own_cols), send_ref), (slice(own_cols, 2 * own_cols), keep_ref)):
+        total = total_ref[part] + member_term(local_ref[...], member_w, field_w, part)
+        total = total.reshape(order_ref.shape[0], -1)
         high = total.astype(BF16)
-        ordered = dot(order, high)
+        ordered = dot(order_ref[...], high)
         if out_ref is keep_ref:
-            ordered = ordered + dot(order, (total - high.astype(F32)).astype(BF16))
+            ordered = ordered + dot(order_ref[...], (total - high.astype(F32)).astype(BF16))
         out_ref[...] = ordered[:count].astype(out_ref.dtype)
 
 
-def ensemble_call(loc, flat_field, mine, other, after, levels, cols, own_cols):
+def ensemble_calls(loc, flat_field, mine, other, after, levels, cols, own_cols):
     total, rows = flat_field.shape
     slab_count = total // cols
+    slabs, side = padded(slab_count), own_cols * padded(slab_count)
     vmem = pl.BlockSpec(memory_space=pltpu.VMEM)
+    work = (2 * own_cols, slabs, rows)
+    held = pl.pallas_call(
+        functools.partial(mine_kernel, levels, cols),
+        name="mine",
+        in_specs=[vmem] * 3 + [pl.BlockSpec(memory_space=pl.ANY)],
+        out_specs=[vmem] * 5,
+        out_shape=[
+            jax.ShapeDtypeStruct((2 * own_cols * SUB, cols * SUB), BF16),
+            jax.ShapeDtypeStruct((side, side), BF16),
+            jax.ShapeDtypeStruct((side, side), BF16),
+            jax.ShapeDtypeStruct(work, BF16),
+            jax.ShapeDtypeStruct(work, F32),
+        ],
+        scratch_shapes=[pltpu.VMEM(work, F32)],
+        compiler_params=pltpu.CompilerParams(vmem_limit_bytes=VMEM),
+        cost_estimate=taking(1.8),
+    )(loc, flat_field, mine, after)
     out_shape = (slab_count * own_cols, rows)
     return pl.pallas_call(
-        functools.partial(ensemble_kernel, levels, cols),
-        name="ensemble",
-        in_specs=[vmem] * 4 + [pl.BlockSpec(memory_space=pl.ANY)],
+        functools.partial(other_kernel, cols),
+        name="other",
+        in_specs=[vmem] * 6,
         out_specs=[vmem, vmem],
         out_shape=[jax.ShapeDtypeStruct(out_shape, BF16), jax.ShapeDtypeStruct(out_shape, F32)],
-        scratch_shapes=[pltpu.VMEM((2 * own_cols, padded(slab_count), rows), F32)] * 3,
-        compiler_params=pltpu.CompilerParams(vmem_limit_bytes=VMEM),
-        cost_estimate=pl.CostEstimate(flops=5 * 10**8, bytes_accessed=8 * MIB, transcendentals=0),
-    )(loc, flat_field, mine, other, after)
+        scratch_shapes=[pltpu.VMEM(work, F32)],
+        compiler_params=pltpu.CompilerParams(vmem_limit_bytes=VMEM),
+        cost_estimate=taking(2.0),
+    )(*held, other)
 
 
 def tables_kernel(levels, own_cols, col_dev, slabs, table_ref, entries_ref, vert_ref, after_ref, mat_ref, coef_ref, vert_out):
@@ -293,7 +343,7 @@
             jax.ShapeDtypeStruct((own_cols * slabs, own_cols * slabs), BF16),
         ],
         compiler_params=pltpu.CompilerParams(vmem_limit_bytes=VMEM),
-        cost_estimate=pl.CostEstimate(flops=10**8, bytes_accessed=2 * MIB, transcendentals=0),
+        cost_estimate=taking(1.5),
     )(table, entries, vert, after)
 
 
@@ -324,25 +374,28 @@
 
 
 def final_kernel(
-    levels, scale, own_ref, coef_ref, part_0_ref, part_1_ref, last_0_ref, last_1_ref, mat_ref, row_coef_ref, vert_ref,
-    keep_ref, came_ref, out_ref, carry, last, smooth, filt
+    levels, scale, own_ref, coef_ref, mat_ref, row_coef_ref, vert_ref, keep_ref, came_ref, *refs
 ):
     own_cols, slabs, rows = own_ref.shape
-    cols = coef_ref.shape[1] - 1
+    cols = coef_ref.shape[1] - 3
+    mine, others, (out_ref, carry, last, smooth, filt) = refs[:4], refs[4:8], refs[8:]
     mem = lax.axis_index("mem")
     subs = slabs // CORES
     core = mem & (CORES - 1)
-    for flip, part_ref, last_ref in ((0, part_0_ref, last_0_ref), (1, part_1_ref, last_1_ref)):
+    for flip, (part_ref, *last_refs) in enumerate((mine, others)):
         share = pl.ds(pl.multiple_of((core ^ flip) * subs, subs), subs)
         carry[:, share, :] = part_ref[...].astype(F32)
-        last[share, :] = last_ref[...].astype(F32)
+        for k, last_ref in enumerate(last_refs):
+            last[k, share, :] = last_ref[...].astype(F32)
     top = levels // 8 * 8
     is_level = iota((8, rows), 0) < levels - top
     for side in range(2):
-        old = carry[side, top : top + 8]
-        carry[side] = carry[side] + coef_ref[side, cols, 0:1] * last[...]
-        other = old + coef_ref[side, cols, 1:2] * last[top : top + 8]
-        carry[side, top : top + 8] = jnp.where(is_level, carry[side, top : top + 8], other)
+        value, end = carry[side], carry[side, top : top + 8]
+        for k in range(3):
+            value = value + coef_ref[side, cols + k, 0:1] * last[k]
+            end = end + coef_ref[side, cols + k, 1:2] * last[k, top : top + 8]
+        carry[side] = value
+        carry[side, top : top + 8] = jnp.where(is_level, carry[side, top : top + 8], end)
     for col in range(own_cols):
         pair = coef_ref[:, mem * own_cols + col]
         smooth[col] = own_ref[col] + pair[0, 0:1] * carry[0] + pair[1, 0:1] * carry[1]
@@ -382,69 +435,66 @@
         out_shape=jax.ShapeDtypeStruct((slab_count, own_cols, rows), BF16),
         scratch_shapes=[
             pltpu.VMEM((2, slabs, rows), F32),
-            pltpu.VMEM((slabs, rows), F32),
+            pltpu.VMEM((3, slabs, rows), F32),
             pltpu.VMEM((own_cols, slabs, rows), F32),
             pltpu.VMEM((own_cols * slabs, rows), F32),
         ],
         compiler_params=pltpu.CompilerParams(vmem_limit_bytes=VMEM),
-        cost_estimate=pl.CostEstimate(flops=10**9, bytes_accessed=6 * MIB, transcendentals=0),
+        cost_estimate=taking(2.0),
     )(*args)
 
 
-def merge_kernel(levels, cols, step, last, after_count, *refs):
-    table_ref, entries_ref = refs[:2]
-    pairs = refs[2 : 4 + 2 * step]
-    out_ref, *part_ref = refs[4 + 2 * step + after_count :]
-    _, subs, rows = pairs[0].shape
+def merge_kernel(levels, cols, steps, step, last, after_count, *refs):
+    table_ref, entries_ref, ends_ref = refs[:3]
+    came_refs, outs = refs[3 : 3 + step], refs[3 + step + after_count :]
+    _, subs, rows = ends_ref.shape
     tile, mem = lax.axis_index("tile"), lax.axis_index("mem")
     decay, turn = line_coefs(lookup(table_ref, entries_ref[...]), cols)
     is_level = iota((subs, rows), 0) + (mem & (CORES - 1)) * subs < levels
+    behind = reflected(decay, turn, tile, steps)
     decay = jnp.where(is_level, decay[0:1], decay[1:2])
-    turn = jnp.where(is_level, turn[0:1], turn[1:2])
-    from_left, from_right, turned, left, right = 1.0, 1.0, 0.0, 0.0, 0.0
-    for level in range(step + 1):
+    behind = jnp.where(is_level, behind[0:1], behind[1:2])
+    turned = behind * decay
+    right, left = ends_ref[0].astype(F32), ends_ref[1].astype(F32)
+    into_right, into_left, from_left, from_right = 0.0, behind * right, 1.0, 1.0
+    for level, came_ref in enumerate(came_refs):
         second = ((tile >> level) & 1) == 1
-        if last or level == step:
-            mine, came = (pairs[2 * level + k][...].astype(F32) for k in range(2))
-            lower = jnp.where(second, came, mine)
-            upper = jnp.where(second, mine, came)
-            bent = turn * lower[0] + upper[1]
-        if last:
-            left = left + jnp.where(second, from_left * lower[0], 0.0)
-            right = right + jnp.where(second, turned * lower[0], from_right * bent)
-            turned = jnp.where(second, turned * decay, turned + from_right * turn * decay)
-            from_left = jnp.where(second, from_left * decay, from_left)
-            from_right = jnp.where(second, from_right, from_right * decay)
-        if level == step:
-            block = decay * lower[0] + upper[0], lower[1] + decay * bent
-        turn = turn * (1.0 + decay * decay)
+        came_right, came_left = came_ref[0].astype(F32), came_ref[1].astype(F32)
+        into_right = into_right + jnp.where(second, from_left * came_right, 0.0)
+        into_left = into_left + jnp.where(second, 0.0, from_right * came_left)
+        right = jnp.where(second, decay * came_right + right, decay * right + came_right)
+        left = jnp.where(second, came_left + decay * left, left + decay * came_left)
+        from_left = jnp.where(second, from_left * decay, from_left)
+        from_right = jnp.where(second, from_right, from_right * decay)
         decay = decay * decay
     if last:
-        second = ((tile >> (step + 1)) & 1) == 1
-        out_ref[...] = jnp.where(second, block[1], block[0]).astype(BF16)
-        part_ref[0][0] = left.astype(BF16)
-        part_ref[0][1] = jnp.where(second, right, right + from_right * turn * block[0]).astype(BF16)
+        quarter = tile >> (steps - 2)
+        outs[0][...] = jnp.where((quarter & 1) == 1, left, right).astype(BF16)
+        outs[1][...] = jnp.where(quarter >= 2, left, right).astype(BF16)
+        outs[2][0] = into_right.astype(BF16)
+        outs[2][1] = (into_left + turned * into_right).astype(BF16)
     else:
-        out_ref[0] = block[0].astype(BF16)
-        out_ref[1] = block[1].astype(BF16)
-
-
-def merge_call(table, entries, pairs, after, levels, cols, last):
-    step = len(pairs) // 2 - 1
-    whole = jax.ShapeDtypeStruct(pairs[0].shape, BF16)
-    outs = [jax.ShapeDtypeStruct(whole.shape[1:], BF16), whole] if last else [whole]
+        outs[0][0] = right.astype(BF16)
+        outs[0][1] = left.astype(BF16)
+
+
+def merge_call(table, entries, ends, came, after, levels, cols, steps):
+    last = len(came) == steps - 2
+    whole = jax.ShapeDtypeStruct(ends.shape, BF16)
+    one = jax.ShapeDtypeStruct(ends.shape[1:], BF16)
+    outs = [one, one, whole] if last else [whole]
     vmem, smem = pl.BlockSpec(memory_space=pltpu.VMEM), pl.BlockSpec(memory_space=pltpu.SMEM)
     held = [pl.BlockSpec(memory_space=pl.ANY)] * len(after)
     return pl.pallas_call(
-        functools.partial(merge_kernel, levels, cols, step, last, len(after)),
+        functools.partial(merge_kernel, levels, cols, steps, len(came), last, len(after)),
         name="merge",
-        in_specs=[smem] + [vmem] * (1 + len(pairs)) + held,
+        in_specs=[smem] + [vmem] * (2 + len(came)) + held,
         out_specs=[vmem] * len(outs) + held,
         out_shape=outs + [jax.ShapeDtypeStruct(array.shape, array.dtype) for array in after],
-        input_output_aliases={2 + len(pairs) + k: len(outs) + k for k in range(len(after))},
-        compiler_params=pltpu.CompilerParams(vmem_limit_bytes=VMEM),
-        cost_estimate=pl.CostEstimate(flops=10**6, bytes_accessed=MIB // 4, transcendentals=0),
-    )(table, entries, *pairs, *after)
+        input_output_aliases={3 + len(came) + k: len(outs) + k for k in range(len(after))},
+        compiler_params=pltpu.CompilerParams(vmem_limit_bytes=VMEM),
+        cost_estimate=taking(0.8),
+    )(table, entries, ends, *came, *after)
 
 
 def body(field, vert_filter, loc_filter, alpha_table, xscale_idx, yscale_idx, members):
@@ -458,10 +508,6 @@
     def swap(array, flip, axis="mem"):
         return lax.ppermute(array, axis, [(i, i ^ flip) for i in range(lax.axis_size(axis))])
 
-    def merge(pairs, after):
-        last = len(pairs) == 2 * (steps - 1)
-        return merge_call(alpha_table, xscale_idx, pairs, after, levels, cols, last)
-
     full_field = field.reshape(slab_count * cols, rows)
     flat_field = pltpu.with_memory_space_constraint(full_field, pltpu.HBM)
     mine = members.reshape(slab_count * cols, rows)
@@ -469,26 +515,21 @@
     core = (lax.axis_index("mem") & (CORES - 1)).astype(jnp.int32).reshape(1)
     alpha_table = pltpu.with_memory_space_constraint(alpha_table, pltpu.HBM)
     xscale_idx = pltpu.with_memory_space_constraint(xscale_idx, pltpu.HBM)
-    block = ends_call(core, alpha_table, xscale_idx, flat_field, levels, cols)
-
-    pairs = [block, swap(block, 1, "tile")]
-    own, coef = local_call(alpha_table, xscale_idx, full_field, block, levels, steps, cols, own_cols)
-    send, keep = ensemble_call(loc_filter[0], full_field, mine, other, own, levels, cols, own_cols)
-    block, send = merge(pairs, [send])
-    came = swap(send, 2)
-    pairs += [block, swap(block, 2, "tile")]
-    mats, row_coef, vert = tables_call(alpha_table, yscale_idx, vert_filter[0], block, levels, own_cols, cols, slabs)
-    held = [mats]
-    for step in range(2, steps):
-        block, *rest = merge(pairs, held)
-        if held:
-            mats, held = rest.pop(), []
-        if step < steps - 1:
-            pairs += [block, swap(block, 1 << step, "tile")]
-    last = swap(block, tile_count // 2, "tile")
-    shares = [rest[0], swap(rest[0], 1), last, swap(last, 1)]
+    ends = ends_call(core, alpha_table, xscale_idx, flat_field, levels, steps, cols)
+    blocks, came = [ends], []
+    send, keep = ensemble_calls(loc_filter[0], full_field, mine, other, ends, levels, cols, own_cols)
+    over = swap(send, 2)
+    own, coef = local_call(alpha_table, xscale_idx, full_field, send, levels, steps, cols, own_cols)
+    for level in range(steps - 2):
+        came.append(swap(blocks[0], 1 << level, "tile"))
+        *blocks, own = merge_call(alpha_table, xscale_idx, ends, came, [own], levels, cols, steps)
+    near, far, part = blocks
+    last = {flip: swap(near if flip == 1 else far, flip << (steps - 2), "tile") for flip in (2, 3, 1)}
+    mats, row_coef, vert = tables_call(alpha_table, yscale_idx, vert_filter[0], part, levels, own_cols, cols, slabs)
+    shares = [part, last[1], last[2], last[3]]
+    shares += [swap(share, 1) for share in shares]
     scale = 1.0 / (mem_count * members.shape[0] - 1)
-    return final_call(slab_count, levels, scale, [own, coef, *shares, mats, row_coef, vert, keep, came])
+    return final_call(slab_count, levels, scale, [own, coef, mats, row_coef, vert, keep, over, *shares])
 
 
 def solution(mesh):

time: 28.8 us -> 26.8 us (0.931)
  Pallas kernels: 13.5 us -> 11.4 us
  starting transfers between devices: 8.83 us -> 9.57 us
  waiting for transfers between devices: 5.99 us -> 5.41 us
    pallas_call x4, Pallas kernels: 7.92 us -> 5.67 us  [the longest x1 2.13 us: ends_call(): pl.pallas_call(functools.partial(ends_kernel, levels, steps, total // col...]
    ppermute x7 -> x10, starting transfers between devices: 8.83 us -> 9.57 us  [swap(): lax.ppermute(array, axis, [(i, i ^ flip) for i in range(lax.axis_size(axi...]
    ppermute x7 -> x10, waiting for transfers between devices: 5.99 us -> 5.41 us  [swap(): lax.ppermute(array, axis, [(i, i ^ flip) for i in range(lax.axis_size(axi...]
  transfers between devices with their start and end apart: 7 -> 10, of which waited for: 3 -> 2; matrix products, arithmetic and copies ran while one was open for 0% -> 0% of each run, Pallas kernels for 38% -> 35%
where the time goes in v5:
time: 26.8 us; the launch traced here: 26.5 us
  Pallas kernels  11.4 us (43%)
  starting transfers between devices  9.57 us (36%)
  waiting for transfers between devices  5.41 us (20%)
    ppermute x10, starting transfers between devices, swap(): lax.ppermute(array, axis, [(i, i ^ flip) for i in range(lax.axis_size(axi...  9.57 us
    ppermute x10, waiting for transfers between devices, swap(): lax.ppermute(array, axis, [(i, i ^ flip) for i in range(lax.axis_size(axi...  5.41 us
    pallas_call x1, Pallas kernels, local_call(): pl.pallas_call(functools.partial(local_kernel, levels, steps), name='loca...  2.15 us
    pallas_call x1, Pallas kernels, ends_call(): pl.pallas_call(functools.partial(ends_kernel, levels, steps, total // col...  2.13 us
    pallas_call x1, Pallas kernels, final_call(): pl.pallas_call(functools.partial(final_kernel, levels, scale), name='fina...  2.05 us
    pallas_call x1, Pallas kernels, tables_call(): pl.pallas_call(functools.partial(tables_kernel, levels, own_cols, col_dev...  1.54 us
    pallas_call x1, Pallas kernels, ensemble_calls(): pl.pallas_call(functools.partial(other_kernel, cols), name='other', in_sp...  1.44 us
    pallas_call x1, Pallas kernels, ensemble_calls(): pl.pallas_call(functools.partial(mine_kernel, levels, cols), name='mine',...  1.23 us
  transfers between devices with their start and end apart: 10, of which 2 were waited for; matrix products, arithmetic and copies ran while one was open for 0% of the time, Pallas kernels for 35%

profile of v5, /device:TPU:0, one launch (start us, length us, event | category | flops | bytes accessed | tf_op | source)
XLA Modules:
  0.0 26.5 jit_solution(11346199173733737827)
XLA Ops:
  0.0 0.5 %collective-permute-start.1 = (bf16[976,1024]{1,0:T(8,128)(2,1)}, bf16[976,1024]{1,0:T(8,128)(2,1)S(1)}, u32[]{:S(2)}, u32[]{:S(2)}) collective-permute-start(bf16[976,1024]{1,0:T(8,128)(2,1)} %bitcast.5), channel_id=1, source_target_pairs={{0,1},{1,0},{2,3},{3,2},{4,5},{5,4},{6,7},{7,6},{8,9},{9,8},{10,11... | collective-permute-start | bytes 5996552 | tf_op jit(solution)/shard_map/ppermute | solution.py:509
  0.5 0.0 copy-start
  0.5 0.0 copy-start.1
  0.5 0.0 copy-start.2
  0.5 2.1 %ends.1.after_ref.refs_2_ = bf16[2,32,1024]{2,1,0:T(8,128)(2,1)S(1)} custom-call(s32[1]{0:T(128)} %bitcast.core_ref, f32[16]{0:T(128)} %table_ref.5, s32[2,1024]{1,0:T(2,128)} %refs_1_.1, bf16[976,1024]{1,0:T(8,128)(2,1)} %bitcast.7), custom_call_target="tpu_custom_call" | custom-call | flops 2415000064 | bytes 262144 | tf_op jit(solution)/shard_map/ends/pallas_call | solution.py:125
  2.6 2.6 %collective-permute-start = (bf16[2,32,1024]{2,1,0:T(8,128)(2,1)S(1)}, bf16[2,32,1024]{2,1,0:T(8,128)(2,1)S(1)}, u32[]{:S(2)}, u32[]{:S(2)}) collective-permute-start(bf16[2,32,1024]{2,1,0:T(8,128)(2,1)S(1)} %ends.1.after_ref.refs_2_), channel_id=1, source_target_pairs={{0,4},{4,0},{8,12},{12,8},{16,20},{20,16},{24,28},{28,24},{1,5},{5... | collective-permute-start | bytes 393224 | tf_op jit(solution)/shard_map/ppermute | solution.py:509
  5.2 0.0 copy-done
  5.2 0.0 copy-done.1
  5.2 0.0 copy-done.2
  5.2 1.2 %mine.1 = (bf16[128,256]{1,0:T(8,128)(2,1)S(1)}, bf16[256,256]{1,0:T(8,128)(2,1)S(1)}, bf16[256,256]{1,0:T(8,128)(2,1)S(1)}, bf16[8,64,1024]{2,1,0:T(8,128)(2,1)S(1)}, f32[8,64,1024]{2,1,0:T(8,128)S(1)}) custom-call(bf16[60,60]{1,0:T(8,128)(2,1)S(1)} %bitcast.10, bf16[976,1024]{1,0:T(8,128)(2,1)S(1)} %bitcast.8, bf16[976,1024]{1,0:T(8,128)(2,1)S(1)} %bitcast.6, ...), custom_call_target="tpu_custom_call" | custom-call | flops 2070000000 | bytes 262144 | tf_op jit(solution)/shard_map/mine/pallas_call | solution.py:263
  6.4 0.0 collective-permute-done.1.other_ref
  6.4 1.4 %other.1 = (bf16[244,1024]{1,0:T(8,128)(2,1)S(1)}, f32[244,1024]{1,0:T(8,128)S(1)}) custom-call(bf16[128,256]{1,0:T(8,128)(2,1)S(1)} %get-tuple-element.21.perm_ref, bf16[256,256]{1,0:T(8,128)(2,1)S(1)} %get-tuple-element.22.local_ref, bf16[256,256]{1,0:T(8,128)(2,1)S(1)} %get-tuple-element.23.order_ref, bf16[8,64,1024]{2,1,0:T(8,128)(2,1)S(1)} %get-tuple-element.24.field_w, ...), custom_call_target="tpu_custom_call" | custom-call | flops 2300000000 | bytes 262144 | tf_op jit(solution)/shard_map/other/pallas_call | solution.py:280
  7.9 1.6 %collective-permute-start.2 = (bf16[244,1024]{1,0:T(8,128)(2,1)S(1)}, bf16[244,1024]{1,0:T(8,128)(2,1)S(1)}, u32[]{:S(2)}, u32[]{:S(2)}) collective-permute-start(bf16[244,1024]{1,0:T(8,128)(2,1)S(1)} %get-tuple-element.26.after_ref), channel_id=1, source_target_pairs={{0,2},{1,3},{2,0},{3,1},{4,6},{5,7},{6,4},{7,5},{8,10},{9,11},{10,... | collective-permute-start | bytes 1499144 | tf_op jit(solution)/shard_map/ppermute | solution.py:509
  9.4 2.1 %local.1 = (f32[4,64,1024]{2,1,0:T(8,128)S(1)}, f32[2,19,2,1024]{3,2,1,0:T(2,128)S(1)}) custom-call(f32[16]{0:T(128)} %table_ref.5, s32[2,1024]{1,0:T(2,128)} %refs_1_.1, bf16[976,1024]{1,0:T(8,128)(2,1)S(1)} %bitcast.9, bf16[244,1024]{1,0:T(8,128)(2,1)S(1)} %get-tuple-element.26.after_ref), custom_call_target="tpu_custom_call" | custom-call | flops 2415000064 | bytes 262144 | tf_op jit(solution)/shard_map/local/pallas_call | solution.py:188
  11.6 0.0 copy-start.3
  11.6 0.0 copy-start.4
  11.6 0.0 collective-permute-done.refs_3_
  11.6 0.9 %merge.1 = (bf16[32,1024]{1,0:T(8,128)(2,1)S(1)}, bf16[32,1024]{1,0:T(8,128)(2,1)S(1)}, bf16[2,32,1024]{2,1,0:T(8,128)(2,1)S(1)}, f32[4,64,1024]{2,1,0:T(8,128)S(1)}) custom-call(f32[16]{0:T(128)} %table_ref.5, s32[2,1024]{1,0:T(2,128)} %refs_1_.1, bf16[2,32,1024]{2,1,0:T(8,128)(2,1)S(1)} %ends.1.after_ref.refs_2_, ...), custom_call_target="tpu_custom_call", output_to_operand_aliasing={{3}: (4, {})} | custom-call | flops 920000000 | bytes 262144 | tf_op jit(solution)/shard_map/merge/pallas_call | solution.py:488
  12.5 1.6 %collective-permute-start.3 = (bf16[32,1024]{1,0:T(8,128)(2,1)S(1)}, bf16[32,1024]{1,0:T(8,128)(2,1)S(1)}, u32[]{:S(2)}, u32[]{:S(2)}) collective-permute-start(bf16[32,1024]{1,0:T(8,128)(2,1)S(1)} %get-tuple-element.35), channel_id=1, source_target_pairs={{0,8},{4,12},{8,0},{12,4},{16,24},{20,28},{24,16},{28,20},{1,9},{5... | collective-permute-start | bytes 196616 | tf_op jit(solution)/shard_map/ppermute | solution.py:509
  14.1 2.6 %collective-permute-start.4 = (bf16[32,1024]{1,0:T(8,128)(2,1)S(1)}, bf16[32,1024]{1,0:T(8,128)(2,1)S(1)}, u32[]{:S(2)}, u32[]{:S(2)}) collective-permute-start(bf16[32,1024]{1,0:T(8,128)(2,1)S(1)} %get-tuple-element.36), channel_id=1, source_target_pairs={{0,16},{4,20},{8,24},{12,28},{16,0},{20,4},{24,8},{28,12},{1,17},{... | collective-permute-start | bytes 196616 | tf_op jit(solution)/shard_map/ppermute | solution.py:509
  16.7 0.2 collective-permute-start.5
  17.0 0.0 collective-permute-start.6
  17.0 0.0 collective-permute-done.3.refs_1_
  17.0 0.5 %collective-permute-start.7 = (bf16[32,1024]{1,0:T(8,128)(2,1)S(1)}, bf16[32,1024]{1,0:T(8,128)(2,1)S(1)}, u32[]{:S(2)}, u32[]{:S(2)}) collective-permute-start(bf16[32,1024]{1,0:T(8,128)(2,1)S(1)} %collective-permute-done.3.refs_1_), channel_id=1, source_target_pairs={{0,1},{1,0},{2,3},{3,2},{4,5},{5,4},{6,7},{7,6},{8,9},{9,8},{10,11... | collective-permute-start | bytes 196616 | tf_op jit(solution)/shard_map/ppermute | solution.py:509
  17.5 4.0 %collective-permute-done.4.refs_2_ = bf16[32,1024]{1,0:T(8,128)(2,1)S(1)} collective-permute-done((bf16[32,1024]{1,0:T(8,128)(2,1)S(1)}, bf16[32,1024]{1,0:T(8,128)(2,1)S(1)}, u32[]{:S(2)}, u32[]{:S(2)}) %collective-permute-start.4) | collective-permute-done | bytes 65568 | tf_op jit(solution)/shard_map/ppermute | solution.py:509
  21.5 0.0 collective-permute-start.8
  21.5 1.4 %collective-permute-done.5.refs_3_ = bf16[32,1024]{1,0:T(8,128)(2,1)S(1)} collective-permute-done((bf16[32,1024]{1,0:T(8,128)(2,1)S(1)}, bf16[32,1024]{1,0:T(8,128)(2,1)S(1)}, u32[]{:S(2)}, u32[]{:S(2)}) %collective-permute-start.5) | collective-permute-done | bytes 65568 | tf_op jit(solution)/shard_map/ppermute | solution.py:509
  22.9 0.0 collective-permute-start.9
  22.9 0.0 copy-done.3
  22.9 0.0 copy-done.4
  22.9 1.5 %tables.1 = (bf16[8,256,256]{2,1,0:T(8,128)(2,1)S(1)}, f32[4,8,256]{2,1,0:T(8,128)S(1)}, bf16[256,256]{1,0:T(8,128)(2,1)S(1)}) custom-call(f32[16]{0:T(128)} %table_ref.5, s32[2,128]{1,0:T(2,128)S(1)} %copy-done.4, bf16[60,60]{1,0:T(8,128)(2,1)S(1)} %bitcast.11, bf16[2,32,1024]{2,1,0:T(8,128)(2,1)S(1)} %get-tuple-element.30.after_ref.refs_0_), custom_call_target="tpu_custom_call" | custom-call | flops 1724999936 | bytes 262144 | tf_op jit(solution)/shard_map/tables/pallas_call | solution.py:335
  24.4 0.0 collective-permute-done.7.refs_5_
  24.4 0.0 collective-permute-done.8.refs_6_
  24.4 0.0 collective-permute-done.9.refs_7_
  24.4 0.0 collective-permute-done.6.refs_4_
  24.5 0.0 collective-permute-done.2.came_ref
  24.5 2.1 %final.1 = bf16[61,4,1024]{2,1,0:T(4,128)(2,1)} custom-call(f32[4,64,1024]{2,1,0:T(8,128)S(1)} %get-tuple-element.28.own_ref, f32[2,19,2,1024]{3,2,1,0:T(2,128)S(1)} %get-tuple-element.29.coef_ref, bf16[8,256,256]{2,1,0:T(8,128)(2,1)S(1)} %get-tuple-element.31.mat_ref, f32[4,8,256]{2,1,0:T(8,128)S(1)} %get-tuple-element.32.row_coef_ref, ...), custom_call_target="tpu_custom_call" | custom-call | flops 2300000000 | bytes 262144 | tf_op jit(solution)/shard_map/final/pallas_call | solution.py:430
Async XLA Ops:
  0.0 6.4 %collective-permute-start.1 = (bf16[976,1024]{1,0:T(8,128)(2,1)}, bf16[976,1024]{1,0:T(8,128)(2,1)S(1)}, u32[]{:S(2)}, u32[]{:S(2)}) collective-permute-start(bf16[976,1024]{1,0:T(8,128)(2,1)} %bitcast.5), channel_id=1, source_target_pairs={{0,1},{1,0},{2,3},{3,2},{4,5},{5,4},{6,7},{7,6},{8,9},{9,8},{10,11... | collective-permute-start | bytes 5996552 | tf_op jit(solution)/shard_map/ppermute | solution.py:509
  0.5 4.7 %copy-start = (bf16[1,61,16,1024]{3,2,1,0:T(8,128)(2,1)S(1)}, bf16[1,61,16,1024]{3,2,1,0:T(8,128)(2,1)}, u32[]{:S(2)}) copy-start(bf16[1,61,16,1024]{3,2,1,0:T(8,128)(2,1)} %param.13) | copy-start | bytes 5996548
  0.5 4.7 %copy-start.1 = (bf16[61,16,1024]{2,1,0:T(8,128)(2,1)S(1)}, bf16[61,16,1024]{2,1,0:T(8,128)(2,1)}, u32[]{:S(2)}) copy-start(bf16[61,16,1024]{2,1,0:T(8,128)(2,1)} %param.7) | copy-start | bytes 5996548
  0.5 4.7 %copy-start.2 = (bf16[1,60,60]{2,1,0:T(8,128)(2,1)S(1)}, bf16[1,60,60]{2,1,0:T(8,128)(2,1)}, u32[]{:S(2)}) copy-start(bf16[1,60,60]{2,1,0:T(8,128)(2,1)} %param.9) | copy-start | bytes 21604
  2.6 9.0 %collective-permute-start = (bf16[2,32,1024]{2,1,0:T(8,128)(2,1)S(1)}, bf16[2,32,1024]{2,1,0:T(8,128)(2,1)S(1)}, u32[]{:S(2)}, u32[]{:S(2)}) collective-permute-start(bf16[2,32,1024]{2,1,0:T(8,128)(2,1)S(1)} %ends.1.after_ref.refs_2_), channel_id=1, source_target_pairs={{0,4},{4,0},{8,12},{12,8},{16,20},{20,16},{24,28},{28,24},{1,5},{5... | collective-permute-start | bytes 393224 | tf_op jit(solution)/shard_map/ppermute | solution.py:509
  7.9 16.6 %collective-permute-start.2 = (bf16[244,1024]{1,0:T(8,128)(2,1)S(1)}, bf16[244,1024]{1,0:T(8,128)(2,1)S(1)}, u32[]{:S(2)}, u32[]{:S(2)}) collective-permute-start(bf16[244,1024]{1,0:T(8,128)(2,1)S(1)} %get-tuple-element.26.after_ref), channel_id=1, source_target_pairs={{0,2},{1,3},{2,0},{3,1},{4,6},{5,7},{6,4},{7,5},{8,10},{9,11},{10,... | collective-permute-start | bytes 1499144 | tf_op jit(solution)/shard_map/ppermute | solution.py:509
  11.6 11.3 %copy-start.3 = (bf16[1,60,60]{2,1,0:T(8,128)(2,1)S(1)}, bf16[1,60,60]{2,1,0:T(8,128)(2,1)}, u32[]{:S(2)}) copy-start(bf16[1,60,60]{2,1,0:T(8,128)(2,1)} %param.8) | copy-start | bytes 21604
  11.6 11.3 %copy-start.4 = (s32[2,128]{1,0:T(2,128)S(1)}, s32[2,128]{1,0:T(2,128)}, u32[]{:S(2)}) copy-start(s32[2,128]{1,0:T(2,128)} %entries_ref.5) | copy-start | bytes 3076
  12.5 4.5 %collective-permute-start.3 = (bf16[32,1024]{1,0:T(8,128)(2,1)S(1)}, bf16[32,1024]{1,0:T(8,128)(2,1)S(1)}, u32[]{:S(2)}, u32[]{:S(2)}) collective-permute-start(bf16[32,1024]{1,0:T(8,128)(2,1)S(1)} %get-tuple-element.35), channel_id=1, source_target_pairs={{0,8},{4,12},{8,0},{12,4},{16,24},{20,28},{24,16},{28,20},{1,9},{5... | collective-permute-start | bytes 196616 | tf_op jit(solution)/shard_map/ppermute | solution.py:509
  14.1 7.3 %collective-permute-start.4 = (bf16[32,1024]{1,0:T(8,128)(2,1)S(1)}, bf16[32,1024]{1,0:T(8,128)(2,1)S(1)}, u32[]{:S(2)}, u32[]{:S(2)}) collective-permute-start(bf16[32,1024]{1,0:T(8,128)(2,1)S(1)} %get-tuple-element.36), channel_id=1, source_target_pairs={{0,16},{4,20},{8,24},{12,28},{16,0},{20,4},{24,8},{28,12},{1,17},{... | collective-permute-start | bytes 196616 | tf_op jit(solution)/shard_map/ppermute | solution.py:509
  16.7 6.1 %collective-permute-start.5 = (bf16[32,1024]{1,0:T(8,128)(2,1)S(1)}, bf16[32,1024]{1,0:T(8,128)(2,1)S(1)}, u32[]{:S(2)}, u32[]{:S(2)}) collective-permute-start(bf16[32,1024]{1,0:T(8,128)(2,1)S(1)} %get-tuple-element.36), channel_id=1, source_target_pairs={{0,24},{4,28},{8,16},{12,20},{16,8},{20,12},{24,0},{28,4},{1,25},{... | collective-permute-start | bytes 196616 | tf_op jit(solution)/shard_map/ppermute | solution.py:509
  17.0 7.5 %collective-permute-start.6 = (bf16[2,32,1024]{2,1,0:T(8,128)(2,1)S(1)}, bf16[2,32,1024]{2,1,0:T(8,128)(2,1)S(1)}, u32[]{:S(2)}, u32[]{:S(2)}) collective-permute-start(bf16[2,32,1024]{2,1,0:T(8,128)(2,1)S(1)} %get-tuple-element.30.after_ref.refs_0_), channel_id=1, source_target_pairs={{0,1},{1,0},{2,3},{3,2},{4,5},{5,4},{6,7},{7,6},{8,9},{9,8},{10,11... | collective-permute-start | bytes 393224 | tf_op jit(solution)/shard_map/ppermute | solution.py:509
  17.0 7.5 %collective-permute-start.7 = (bf16[32,1024]{1,0:T(8,128)(2,1)S(1)}, bf16[32,1024]{1,0:T(8,128)(2,1)S(1)}, u32[]{:S(2)}, u32[]{:S(2)}) collective-permute-start(bf16[32,1024]{1,0:T(8,128)(2,1)S(1)} %collective-permute-done.3.refs_1_), channel_id=1, source_target_pairs={{0,1},{1,0},{2,3},{3,2},{4,5},{5,4},{6,7},{7,6},{8,9},{9,8},{10,11... | collective-permute-start | bytes 196616 | tf_op jit(solution)/shard_map/ppermute | solution.py:509
  21.5 3.0 %collective-permute-start.8 = (bf16[32,1024]{1,0:T(8,128)(2,1)S(1)}, bf16[32,1024]{1,0:T(8,128)(2,1)S(1)}, u32[]{:S(2)}, u32[]{:S(2)}) collective-permute-start(bf16[32,1024]{1,0:T(8,128)(2,1)S(1)} %collective-permute-done.4.refs_2_), channel_id=1, source_target_pairs={{0,1},{1,0},{2,3},{3,2},{4,5},{5,4},{6,7},{7,6},{8,9},{9,8},{10,11... | collective-permute-start | bytes 196616 | tf_op jit(solution)/shard_map/ppermute | solution.py:509
  22.9 1.6 %collective-permute-start.9 = (bf16[32,1024]{1,0:T(8,128)(2,1)S(1)}, bf16[32,1024]{1,0:T(8,128)(2,1)S(1)}, u32[]{:S(2)}, u32[]{:S(2)}) collective-permute-start(bf16[32,1024]{1,0:T(8,128)(2,1)S(1)} %collective-permute-done.5.refs_3_), channel_id=1, source_target_pairs={{0,1},{1,0},{2,3},{3,2},{4,5},{5,4},{6,7},{7,6},{8,9},{9,8},{10,11... | collective-permute-start | bytes 196616 | tf_op jit(solution)/shard_map/ppermute | solution.py:509

commit v6 on v5

--- a/solution.py
+++ b/solution.py
@@ -74,6 +74,71 @@
     shape = (SUB * cols, SUB * cols)
     (out_col, out_slab), (in_slab, in_col) = split(iota(shape, 0), SUB), split(iota(shape, 1), cols)
     return ((out_slab == in_slab) & (out_col == in_col)).astype(BF16)
+
+
+def share_rows(total, cols, subs, share):
+    return slice(share * subs * cols, min((share + 1) * subs * cols, total))
+
+
+def sweep_share(levels, slab_count, share, alpha, held, work):
+    cols, subs, lanes = work.shape
+    first = share * subs
+    held = jnp.where(iota(held.shape, 0) < (slab_count - first) * cols, held, 0)
+    to_columns(transposer(cols), held, work, cols)
+    is_level = iota((subs, lanes), 0) + first < levels
+    alpha = jnp.where(is_level, alpha[0:1], alpha[1:2])
+    sweep(work, alpha)
+    return gain_of(alpha), is_level
+
+
+def ends_kernel(
+    levels, steps, slab_count, share_ref, table_ref, entries_ref, field_ref, ends_ref, own_ref, lines_ref, work
+):
+    pieces, cols, subs, lanes = work.shape
+    own_cols = own_ref.shape[0]
+    tile, mem = lax.axis_index("tile"), lax.axis_index("mem")
+    share = share_ref[0]
+    pair = lookup(table_ref, entries_ref[...])
+    decay, turn = line_coefs(pair, cols)
+    behind = reflected(decay, turn, tile, steps)
+    lines_ref[0], lines_ref[1], lines_ref[2] = pair, decay, behind
+    for piece in range(pieces):
+        part = slice(piece * lanes, (piece + 1) * lanes)
+        gain, is_level = sweep_share(levels, slab_count, share, pair[:, part], field_ref[:, part], work.at[piece])
+        turned = (decay * behind)[:, part]
+        turned = jnp.where(is_level, turned[0:1], turned[1:2])
+        forward = gain * work[piece, cols - 1]
+        ends_ref[0, :, part] = forward.astype(BF16)
+        ends_ref[1, :, part] = (gain * work[piece, 0] + turned * forward).astype(BF16)
+        own_ref[:, :, part] = work[piece, pl.ds(mem * own_cols, own_cols)] * gain[None]
+
+
+def ends_call(share, table, entries, flat_field, levels, steps, cols, own_cols):
+    total, rows = flat_field.shape
+    subs = padded(total // cols) // CORES
+    vmem, smem = pl.BlockSpec(memory_space=pltpu.VMEM), pl.BlockSpec(memory_space=pltpu.SMEM)
+    return pl.pallas_call(
+        functools.partial(ends_kernel, levels, steps, total // cols),
+        name="ends",
+        grid_spec=pltpu.PrefetchScalarGridSpec(
+            num_scalar_prefetch=1,
+            grid=(1,),
+            in_specs=[
+                smem,
+                pl.BlockSpec(entries.shape, lambda i, share: (0, 0)),
+                pl.BlockSpec((subs * cols, rows), lambda i, share: (share[0], 0)),
+            ],
+            out_specs=[vmem] * 3,
+            scratch_shapes=[pltpu.VMEM((rows // LANES, cols, subs, LANES), F32)],
+        ),
+        out_shape=[
+            jax.ShapeDtypeStruct((2, subs, rows), BF16),
+            jax.ShapeDtypeStruct((own_cols, subs, rows), F32),
+            jax.ShapeDtypeStruct((3, 2, rows), F32),
+        ],
+        compiler_params=pltpu.CompilerParams(vmem_limit_bytes=VMEM),
+        cost_estimate=taking(2.1),
+    )(share, table, entries, flat_field)
 
 
 def line_coefs(pair, cols):
@@ -97,64 +162,23 @@
     return total
 
 
-def ends_kernel(levels, steps, slab_count, core_ref, table_ref, entries_ref, field_ref, ends_ref, work):
-    _, cols, subs, lanes = work.shape
-    first = core_ref[0] * subs
-    tile = lax.axis_index("tile")
-    perm = transposer(cols)
-    for chunk in range(work.shape[0]):
-        part = slice(chunk * lanes, (chunk + 1) * lanes)
-        held = jnp.where(iota((cols * subs, lanes), 0) < (slab_count - first) * cols, field_ref[:, part], 0)
-        to_columns(perm, held, work.at[chunk], cols)
-        pair = lookup(table_ref, entries_ref[:, part])
-        is_level = iota((subs, lanes), 0) + first < levels
-        alpha = jnp.where(is_level, pair[0:1], pair[1:2])
-        sweep(work.at[chunk], alpha)
-        gain = gain_of(alpha)
-        decay, turn = line_coefs(pair, cols)
-        behind = decay * reflected(decay, turn, tile, steps)
-        behind = jnp.where(is_level, behind[0:1], behind[1:2])
-        forward = gain * work[chunk, cols - 1]
-        ends_ref[0, :, part] = forward.astype(BF16)
-        ends_ref[1, :, part] = (gain * work[chunk, 0] + behind * forward).astype(BF16)
-
-
-def ends_call(core, table, entries, flat_field, levels, steps, cols):
-    total, rows = flat_field.shape
-    subs = padded(total // cols) // CORES
-    return pl.pallas_call(
-        functools.partial(ends_kernel, levels, steps, total // cols),
-        name="ends",
-        grid_spec=pltpu.PrefetchScalarGridSpec(
-            num_scalar_prefetch=1,
-            grid=(1,),
-            in_specs=[
-                pl.BlockSpec(memory_space=pltpu.SMEM),
-                pl.BlockSpec(entries.shape, lambda i, core: (0, 0)),
-                pl.BlockSpec((subs * cols, rows), lambda i, core: (core[0], 0)),
-            ],
-            out_specs=pl.BlockSpec((2, subs, rows), lambda i, core: (0, 0, 0)),
-            scratch_shapes=[pltpu.VMEM((rows // LANES, cols, subs, LANES), F32)],
-        ),
-        out_shape=jax.ShapeDtypeStruct((2, subs, rows), BF16),
-        compiler_params=pltpu.CompilerParams(vmem_limit_bytes=VMEM),
-        cost_estimate=taking(2.1),
-    )(core, table, entries, flat_field)
-
-
-def local_kernel(levels, steps, table_ref, entries_ref, field_ref, after_ref, own_ref, coef_ref, work):
-    _, cols, slabs, lanes = work.shape
+def local_kernel(levels, steps, slab_count, lines_ref, field_ref, after_ref, own_ref, coef_ref, held_ref, work):
+    pieces, cols, subs, lanes = work.shape
     own_cols = own_ref.shape[0]
     tile, mem = lax.axis_index("tile"), lax.axis_index("mem")
-    perm = transposer(cols)
-    for chunk in range(work.shape[0]):
-        part = slice(chunk * lanes, (chunk + 1) * lanes)
-        to_columns(perm, field_ref.at[:, part], work.at[chunk], cols)
-        pair = lookup(table_ref, entries_ref[:, part])
-        alpha = jnp.where(iota((slabs, lanes), 0) < levels, pair[0:1], pair[1:2])
-        sweep(work.at[chunk], alpha)
-        own_ref[:, :, part] = work[chunk, pl.ds(mem * own_cols, own_cols)] * gain_of(alpha)[None]
-    pair = lookup(table_ref, entries_ref[...])
+    share = (mem & (CORES - 1)) ^ 1
+    for core in range(CORES):
+        rows = share_rows(slab_count * cols, cols, subs, core)
+
+        @pl.when(share == core)
+        def _():
+            held_ref[0 : rows.stop - rows.start, :] = field_ref[rows, :]
+
+    pair, decay, behind = lines_ref[0], lines_ref[1], lines_ref[2]
+    for piece in range(pieces):
+        part = slice(piece * lanes, (piece + 1) * lanes)
+        gain, _ = sweep_share(levels, slab_count, share, pair[:, part], held_ref[:, part], work.at[piece])
+        own_ref[:, :, part] = work[piece, pl.ds(mem * own_cols, own_cols)] * gain[None]
     square = pair * pair
     power, sums = jnp.ones_like(pair), jnp.zeros_like(pair)
     rights, geometric = [], []
@@ -165,8 +189,7 @@
     for col in range(cols):
         coef_ref[0, col] = rights[col] * geometric[cols - 1 - col]
         coef_ref[1, col] = rights[cols - 1 - col]
-    decay, turn = line_coefs(pair, cols)
-    behind = decay * reflected(decay, turn, tile, steps)
+    turned = decay * behind
     from_left, from_right = jnp.ones_like(pair), jnp.ones_like(pair)
     for level in range(steps - 2):
         second = ((tile >> level) & 1) == 1
@@ -178,26 +201,29 @@
     for flip, weight in ((1, 1.0), (2, decay), (3, jnp.where(outer, decay * decay, 1.0))):
         upper = (quarter ^ flip) < quarter
         coef_ref[0, cols + flip - 1] = jnp.where(upper, from_left * weight, 0.0)
-        coef_ref[1, cols + flip - 1] = weight * jnp.where(upper, behind * from_left, from_right)
-
-
-def local_call(table, entries, flat_field, after, levels, steps, cols, own_cols):
+        coef_ref[1, cols + flip - 1] = weight * jnp.where(upper, turned * from_left, from_right)
+
+
+def local_call(lines, flat_field, after, levels, steps, cols, own_cols):
     total, rows = flat_field.shape
-    slabs = padded(total // cols)
-    vmem, smem = pl.BlockSpec(memory_space=pltpu.VMEM), pl.BlockSpec(memory_space=pltpu.SMEM)
-    return pl.pallas_call(
-        functools.partial(local_kernel, levels, steps),
+    subs = padded(total // cols) // CORES
+    vmem = pl.BlockSpec(memory_space=pltpu.VMEM)
+    return pl.pallas_call(
+        functools.partial(local_kernel, levels, steps, total // cols),
         name="local",
-        in_specs=[smem, vmem, vmem, pl.BlockSpec(memory_space=pl.ANY)],
+        in_specs=[vmem, vmem, pl.BlockSpec(memory_space=pl.ANY)],
         out_specs=[vmem, vmem],
         out_shape=[
-            jax.ShapeDtypeStruct((own_cols, slabs, rows), F32),
+            jax.ShapeDtypeStruct((own_cols, subs, rows), F32),
             jax.ShapeDtypeStruct((2, cols + 3, 2, rows), F32),
         ],
-        scratch_shapes=[pltpu.VMEM((rows // LANES, cols, slabs, LANES), F32)],
-        compiler_params=pltpu.CompilerParams(vmem_limit_bytes=VMEM),
-        cost_estimate=taking(2.1),
-    )(table, entries, flat_field, after)
+        scratch_shapes=[
+            pltpu.VMEM((subs * cols, rows), BF16),
+            pltpu.VMEM((rows // LANES, cols, subs, LANES), F32),
+        ],
+        compiler_params=pltpu.CompilerParams(vmem_limit_bytes=VMEM),
+        cost_estimate=taking(3.0),
+    )(lines, flat_field, after)
 
 
 def spread(matrix, levels, row_slab, row_col, col_slab, col_col):
@@ -292,12 +318,15 @@
 def tables_kernel(levels, own_cols, col_dev, slabs, table_ref, entries_ref, vert_ref, after_ref, mat_ref, coef_ref, vert_out):
     first = lax.axis_index("tile") * col_dev + lax.axis_index("mem") * own_cols
     count = 2 * own_cols
-    alphas = [table_ref[entries_ref[var, first + col]] for var in range(2) for col in range(own_cols)]
-    by_lane = jnp.zeros((1, 128), F32)
     by_row = jnp.zeros((count, 1), F32)
-    for k, alpha in enumerate(alphas):
-        by_lane = jnp.where(iota((1, 128), 1) == k, alpha, by_lane)
-        by_row = jnp.where(iota((count, 1), 0) == k, alpha, by_row)
+    every, found = entries_ref[...], jnp.zeros(entries_ref.shape, F32)
+    for entry in range(table_ref.shape[1]):
+        found = jnp.where(every == entry, table_ref[0:1, entry : entry + 1], found)
+    for col in range(own_cols):
+        here = iota(found.shape, 1) == first + col
+        alphas = jnp.sum(jnp.where(here, found, 0.0), axis=1, keepdims=True)
+        for var in range(2):
+            by_row = jnp.where(iota((count, 1), 0) == var * own_cols + col, alphas[var : var + 1], by_row)
 
     def series(alpha, number):
         alpha = jnp.broadcast_to(alpha, number.shape)
@@ -310,9 +339,9 @@
             unit, single, power = unit * (1.0 + power), single * single, power * power
         return total, both
 
-    down, _ = series(by_lane, BLOCK - iota((BLOCK, 128), 0))
     place = iota((count, BLOCK), 1)
     across, right = series(by_row, BLOCK - place)
+    down = jnp.concatenate([across, jnp.zeros((128 - count, BLOCK), F32)], 0).T
     _, left = series(by_row, place + 1)
     coef_ref[0] = left * across
     coef_ref[1] = right
@@ -331,11 +360,10 @@
 
 def tables_call(table, entries, vert, after, levels, own_cols, col_dev, slabs):
     count = 2 * own_cols
-    smem = pl.BlockSpec(memory_space=pltpu.SMEM)
     return pl.pallas_call(
         functools.partial(tables_kernel, levels, own_cols, col_dev, slabs),
         name="tables",
-        in_specs=[smem, smem, pl.BlockSpec(memory_space=pltpu.VMEM), pl.BlockSpec(memory_space=pl.ANY)],
+        in_specs=[pl.BlockSpec(memory_space=pltpu.VMEM)] * 3 + [pl.BlockSpec(memory_space=pl.ANY)],
         out_specs=[pl.BlockSpec(memory_space=pltpu.VMEM)] * 3,
         out_shape=[
             jax.ShapeDtypeStruct((count, BLOCK, BLOCK), BF16),
@@ -343,8 +371,8 @@
             jax.ShapeDtypeStruct((own_cols * slabs, own_cols * slabs), BF16),
         ],
         compiler_params=pltpu.CompilerParams(vmem_limit_bytes=VMEM),
-        cost_estimate=taking(1.5),
-    )(table, entries, vert, after)
+        cost_estimate=taking(1.0),
+    )(table[None], entries, vert, after)
 
 
 def along_rows(lines, matrix, coef):
@@ -373,87 +401,114 @@
     return out
 
 
-def final_kernel(
-    levels, scale, own_ref, coef_ref, mat_ref, row_coef_ref, vert_ref, keep_ref, came_ref, *refs
-):
-    own_cols, slabs, rows = own_ref.shape
+def filter_share(levels, share, own_ref, coef_ref, mat_ref, row_coef_ref, part_ref, last_refs, out_ref):
+    own_cols, subs, rows = own_ref.shape
     cols = coef_ref.shape[1] - 3
-    mine, others, (out_ref, carry, last, smooth, filt) = refs[:4], refs[4:8], refs[8:]
     mem = lax.axis_index("mem")
-    subs = slabs // CORES
-    core = mem & (CORES - 1)
-    for flip, (part_ref, *last_refs) in enumerate((mine, others)):
-        share = pl.ds(pl.multiple_of((core ^ flip) * subs, subs), subs)
-        carry[:, share, :] = part_ref[...].astype(F32)
-        for k, last_ref in enumerate(last_refs):
-            last[k, share, :] = last_ref[...].astype(F32)
-    top = levels // 8 * 8
-    is_level = iota((8, rows), 0) < levels - top
+    end = slice(subs - 8, subs)
+    is_level = iota((8, rows), 0) + share * subs + subs - 8 < levels
+    lasts = [ref[...].astype(F32) for ref in last_refs]
+    carry, carry_end = [], []
     for side in range(2):
-        value, end = carry[side], carry[side, top : top + 8]
-        for k in range(3):
-            value = value + coef_ref[side, cols + k, 0:1] * last[k]
-            end = end + coef_ref[side, cols + k, 1:2] * last[k, top : top + 8]
-        carry[side] = value
-        carry[side, top : top + 8] = jnp.where(is_level, carry[side, top : top + 8], end)
+        value = part_ref[side].astype(F32)
+        other = value[end]
+        for k, last in enumerate(lasts):
+            value = value + coef_ref[side, cols + k, 0:1] * last
+            other = other + coef_ref[side, cols + k, 1:2] * last[end]
+        carry.append(value)
+        carry_end.append(other)
     for col in range(own_cols):
         pair = coef_ref[:, mem * own_cols + col]
-        smooth[col] = own_ref[col] + pair[0, 0:1] * carry[0] + pair[1, 0:1] * carry[1]
-        end = slice(top, top + 8)
-        other = own_ref[col, end] + pair[0, 1:2] * carry[0, end] + pair[1, 1:2] * carry[1, end]
-        smooth[col, end] = jnp.where(is_level, smooth[col, end], other)
-    for col in range(own_cols):
-        lines = smooth[col]
+        own = own_ref[col]
+        lines = own + pair[0, 0:1] * carry[0] + pair[1, 0:1] * carry[1]
+        last_lines = own[end] + pair[0, 1:2] * carry_end[0] + pair[1, 1:2] * carry_end[1]
         main = along_rows(lines, mat_ref[col], row_coef_ref[:, col])
-        last = along_rows(lines[top : top + 8], mat_ref[own_cols + col], row_coef_ref[:, own_cols + col])
+        last = along_rows(last_lines, mat_ref[own_cols + col], row_coef_ref[:, own_cols + col])
         for b, (piece, extra) in enumerate(zip(main, last)):
             place = slice(b * BLOCK, (b + 1) * BLOCK)
-            filt[col * slabs : col * slabs + slabs, place] = piece
-            filt[col * slabs + top : col * slabs + top + 8, place] = jnp.where(
-                iota((8, BLOCK), 0) < levels - top, piece[top : top + 8], extra
-            )
+            out_ref[col, 0 : subs - 8, place] = piece[0 : subs - 8]
+            out_ref[col, end, place] = jnp.where(is_level[:, place], piece[end], extra)
+
+
+def rows_kernel(levels, own_ref, coef_ref, mat_ref, row_coef_ref, part_ref, *refs):
+    share = lax.axis_index("mem") & (CORES - 1)
+    filter_share(levels, share, own_ref, coef_ref, mat_ref, row_coef_ref, part_ref, refs[:3], refs[3])
+
+
+def rows_call(levels, own, coef, mats, row_coef, shares):
+    vmem = pl.BlockSpec(memory_space=pltpu.VMEM)
+    args = [own, coef, mats, row_coef, *shares]
+    return pl.pallas_call(
+        functools.partial(rows_kernel, levels),
+        name="rows",
+        in_specs=[vmem] * len(args),
+        out_specs=vmem,
+        out_shape=jax.ShapeDtypeStruct(own.shape, F32),
+        compiler_params=pltpu.CompilerParams(vmem_limit_bytes=VMEM),
+        cost_estimate=taking(0.7),
+    )(*args)
+
+
+def final_kernel(
+    levels, scale, done_ref, own_ref, coef_ref, mat_ref, row_coef_ref, part_ref, last_1_ref, last_2_ref, last_3_ref,
+    vert_ref, keep_ref, came_ref, out_hbm, filt, out_ref, sent
+):
+    own_cols, subs, rows = own_ref.shape
+    share = lax.axis_index("mem") & (CORES - 1)
+    filt[:, pl.ds(pl.multiple_of(share * subs, subs), subs), :] = done_ref[...]
+    other = 1 - share
+    place = pl.ds(pl.multiple_of(other * subs, subs), subs)
+    last_refs = last_1_ref, last_2_ref, last_3_ref
+    filter_share(
+        levels, other, own_ref, coef_ref, mat_ref, row_coef_ref, part_ref, last_refs, filt.at[:, place, :]
+    )
     count = out_ref.shape[0]
+    copies = []
     for start in range(0, rows, BLOCK):
         part = slice(start, start + BLOCK)
-        static = filt[:, part]
+        static = filt[:, :, part].reshape(vert_ref.shape[1], BLOCK)
         high = static.astype(BF16)
         low = (static - high.astype(F32)).astype(BF16)
         total = dot(vert_ref[...], high) + dot(vert_ref[...], low)
         ens = keep_ref[:, part] + came_ref[:, part].astype(F32)
         total = total[: count * own_cols] + ens * scale
         out_ref[:, :, part] = total.reshape(count, own_cols, BLOCK).astype(BF16)
-
-
-def final_call(slab_count, levels, scale, args):
-    own_cols, slabs, rows = args[0].shape
+        copy = pltpu.make_async_copy(out_ref.at[:, :, part], out_hbm.at[:, :, part], sent.at[start // BLOCK])
+        copy.start()
+        copies.append(copy)
+    for copy in copies:
+        copy.wait()
+
+
+def final_call(slab_count, levels, scale, done, own, coef, mats, row_coef, shares, vert, keep, came):
+    own_cols, subs, rows = own.shape
     vmem = pl.BlockSpec(memory_space=pltpu.VMEM)
+    args = [done, own, coef, mats, row_coef, *shares, vert, keep, came]
+    out_shape = (slab_count, own_cols, rows)
     return pl.pallas_call(
         functools.partial(final_kernel, levels, scale),
         name="final",
         in_specs=[vmem] * len(args),
-        out_specs=vmem,
-        out_shape=jax.ShapeDtypeStruct((slab_count, own_cols, rows), BF16),
+        out_specs=pl.BlockSpec(memory_space=pl.ANY),
+        out_shape=jax.ShapeDtypeStruct(out_shape, BF16),
         scratch_shapes=[
-            pltpu.VMEM((2, slabs, rows), F32),
-            pltpu.VMEM((3, slabs, rows), F32),
-            pltpu.VMEM((own_cols, slabs, rows), F32),
-            pltpu.VMEM((own_cols * slabs, rows), F32),
+            pltpu.VMEM((own_cols, CORES * subs, rows), F32),
+            pltpu.VMEM(out_shape, BF16),
+            pltpu.SemaphoreType.DMA((rows // BLOCK,)),
         ],
         compiler_params=pltpu.CompilerParams(vmem_limit_bytes=VMEM),
-        cost_estimate=taking(2.0),
+        cost_estimate=taking(1.5),
     )(*args)
 
 
-def merge_kernel(levels, cols, steps, step, last, after_count, *refs):
-    table_ref, entries_ref, ends_ref = refs[:3]
-    came_refs, outs = refs[3 : 3 + step], refs[3 + step + after_count :]
+def merge_kernel(levels, steps, step, last, after_count, *refs):
+    lines_ref, ends_ref = refs[:2]
+    came_refs, outs = refs[2 : 2 + step], refs[2 + step + after_count :]
     _, subs, rows = ends_ref.shape
     tile, mem = lax.axis_index("tile"), lax.axis_index("mem")
-    decay, turn = line_coefs(lookup(table_ref, entries_ref[...]), cols)
     is_level = iota((subs, rows), 0) + (mem & (CORES - 1)) * subs < levels
-    behind = reflected(decay, turn, tile, steps)
-    decay = jnp.where(is_level, decay[0:1], decay[1:2])
-    behind = jnp.where(is_level, behind[0:1], behind[1:2])
+    decay = jnp.where(is_level, lines_ref[1, 0:1], lines_ref[1, 1:2])
+    behind = jnp.where(is_level, lines_ref[2, 0:1], lines_ref[2, 1:2])
     turned = behind * decay
     right, left = ends_ref[0].astype(F32), ends_ref[1].astype(F32)
     into_right, into_left, from_left, from_right = 0.0, behind * right, 1.0, 1.0
@@ -478,23 +533,23 @@
         outs[0][1] = left.astype(BF16)
 
 
-def merge_call(table, entries, ends, came, after, levels, cols, steps):
+def merge_call(lines, ends, came, after, levels, steps):
     last = len(came) == steps - 2
     whole = jax.ShapeDtypeStruct(ends.shape, BF16)
     one = jax.ShapeDtypeStruct(ends.shape[1:], BF16)
     outs = [one, one, whole] if last else [whole]
-    vmem, smem = pl.BlockSpec(memory_space=pltpu.VMEM), pl.BlockSpec(memory_space=pltpu.SMEM)
+    vmem = pl.BlockSpec(memory_space=pltpu.VMEM)
     held = [pl.BlockSpec(memory_space=pl.ANY)] * len(after)
     return pl.pallas_call(
-        functools.partial(merge_kernel, levels, cols, steps, len(came), last, len(after)),
+        functools.partial(merge_kernel, levels, steps, len(came), last, len(after)),
         name="merge",
-        in_specs=[smem] + [vmem] * (2 + len(came)) + held,
+        in_specs=[vmem] * (2 + len(came)) + held,
         out_specs=[vmem] * len(outs) + held,
         out_shape=outs + [jax.ShapeDtypeStruct(array.shape, array.dtype) for array in after],
-        input_output_aliases={3 + len(came) + k: len(outs) + k for k in range(len(after))},
+        input_output_aliases={2 + len(came) + k: len(outs) + k for k in range(len(after))},
         compiler_params=pltpu.CompilerParams(vmem_limit_bytes=VMEM),
         cost_estimate=taking(0.8),
-    )(table, entries, ends, *came, *after)
+    )(lines, ends, *came, *after)
 
 
 def body(field, vert_filter, loc_filter, alpha_table, xscale_idx, yscale_idx, members):
@@ -512,24 +567,25 @@
     flat_field = pltpu.with_memory_space_constraint(full_field, pltpu.HBM)
     mine = members.reshape(slab_count * cols, rows)
     other = swap(mine, 1)
-    core = (lax.axis_index("mem") & (CORES - 1)).astype(jnp.int32).reshape(1)
-    alpha_table = pltpu.with_memory_space_constraint(alpha_table, pltpu.HBM)
-    xscale_idx = pltpu.with_memory_space_constraint(xscale_idx, pltpu.HBM)
-    ends = ends_call(core, alpha_table, xscale_idx, flat_field, levels, steps, cols)
+    line_table = pltpu.with_memory_space_constraint(alpha_table, pltpu.HBM)
+    line_entries = pltpu.with_memory_space_constraint(xscale_idx, pltpu.HBM)
+    share = (lax.axis_index("mem") & (CORES - 1)).astype(jnp.int32).reshape(1)
+    ends, own_0, lines = ends_call(share, line_table, line_entries, flat_field, levels, steps, cols, own_cols)
     blocks, came = [ends], []
     send, keep = ensemble_calls(loc_filter[0], full_field, mine, other, ends, levels, cols, own_cols)
     over = swap(send, 2)
-    own, coef = local_call(alpha_table, xscale_idx, full_field, send, levels, steps, cols, own_cols)
+    own_1, coef = local_call(lines, full_field, send, levels, steps, cols, own_cols)
+    mats, row_coef, vert = tables_call(alpha_table, yscale_idx, vert_filter[0], own_1, levels, own_cols, cols, slabs)
     for level in range(steps - 2):
         came.append(swap(blocks[0], 1 << level, "tile"))
-        *blocks, own = merge_call(alpha_table, xscale_idx, ends, came, [own], levels, cols, steps)
+        *blocks, mats = merge_call(lines, ends, came, [mats], levels, steps)
     near, far, part = blocks
     last = {flip: swap(near if flip == 1 else far, flip << (steps - 2), "tile") for flip in (2, 3, 1)}
-    mats, row_coef, vert = tables_call(alpha_table, yscale_idx, vert_filter[0], part, levels, own_cols, cols, slabs)
     shares = [part, last[1], last[2], last[3]]
-    shares += [swap(share, 1) for share in shares]
+    others = [swap(share, 1) for share in shares]
+    done = rows_call(levels, own_0, coef, mats, row_coef, shares)
     scale = 1.0 / (mem_count * members.shape[0] - 1)
-    return final_call(slab_count, levels, scale, [own, coef, mats, row_coef, vert, keep, over, *shares])
+    return final_call(slab_count, levels, scale, done, own_1, coef, mats, row_coef, others, vert, keep, over)
 
 
 def solution(mesh):

time: 26.8 us -> 25.2 us (0.940)
  Pallas kernels: 11.4 us -> 9.28 us
  waiting for transfers between devices: 5.41 us -> 6.1 us
    pallas_call x2 -> x3, Pallas kernels: 3.02 us -> 1.67 us  [the longest x1 0.99 us: local_call(): pl.pallas_call(functools.partial(local_kernel, levels, steps, total // co...]
    pallas_call x1, Pallas kernels: 1.54 us -> 0.79 us  [tables_call(): pl.pallas_call(functools.partial(tables_kernel, levels, own_cols, col_dev...]
    ppermute x10, waiting for transfers between devices: 5.41 us -> 6.1 us  [swap(): lax.ppermute(array, axis, [(i, i ^ flip) for i in range(lax.axis_size(axi...]
  transfers between devices with their start and end apart: 10 -> 10, of which waited for: 2 -> 3; matrix products, arithmetic and copies ran while one was open for 0% -> 0% of each run, Pallas kernels for 35% -> 30%
where the time goes in v6:
time: 25.2 us; the launch traced here: 25.1 us
  starting transfers between devices  9.58 us (38%)
  Pallas kernels  9.28 us (37%)
  waiting for transfers between devices  6.1 us (24%)
    ppermute x10, starting transfers between devices, swap(): lax.ppermute(array, axis, [(i, i ^ flip) for i in range(lax.axis_size(axi...  9.58 us
    ppermute x10, waiting for transfers between devices, swap(): lax.ppermute(array, axis, [(i, i ^ flip) for i in range(lax.axis_size(axi...  6.1 us
    pallas_call x1, Pallas kernels, ends_call(): pl.pallas_call(functools.partial(ends_kernel, levels, steps, total // col...  2.35 us
    pallas_call x1, Pallas kernels, final_call(): pl.pallas_call(functools.partial(final_kernel, levels, scale), name='fina...  1.81 us
    pallas_call x1, Pallas kernels, ensemble_calls(): pl.pallas_call(functools.partial(other_kernel, cols), name='other', in_sp...  1.43 us
    pallas_call x1, Pallas kernels, ensemble_calls(): pl.pallas_call(functools.partial(mine_kernel, levels, cols), name='mine',...  1.23 us
    pallas_call x1, Pallas kernels, local_call(): pl.pallas_call(functools.partial(local_kernel, levels, steps, total // co...  0.99 us
    pallas_call x1, Pallas kernels, tables_call(): pl.pallas_call(functools.partial(tables_kernel, levels, own_cols, col_dev...  0.79 us
  transfers between devices with their start and end apart: 10, of which 3 were waited for; matrix products, arithmetic and copies ran while one was open for 0% of the time, Pallas kernels for 30%

profile of v6, /device:TPU:0, one launch (start us, length us, event | category | flops | bytes accessed | tf_op | source)
XLA Modules:
  0.0 25.1 jit_solution(8988436909931334755)
XLA Ops:
  0.0 0.5 %collective-permute-start = (bf16[976,1024]{1,0:T(8,128)(2,1)}, bf16[976,1024]{1,0:T(8,128)(2,1)S(1)}, u32[]{:S(2)}, u32[]{:S(2)}) collective-permute-start(bf16[976,1024]{1,0:T(8,128)(2,1)} %bitcast.6), channel_id=1, source_target_pairs={{0,1},{1,0},{2,3},{3,2},{4,5},{5,4},{6,7},{7,6},{8,9},{9,8},{10,11... | collective-permute-start | bytes 5996552 | tf_op jit(solution)/shard_map/ppermute | solution.py:564
  0.5 0.0 copy-start
  0.5 0.0 copy-start.1
  0.5 0.0 copy-start.2
  0.5 2.4 %ends.1 = (bf16[2,32,1024]{2,1,0:T(8,128)(2,1)S(1)}, f32[4,32,1024]{2,1,0:T(8,128)S(1)}, f32[3,2,1024]{2,1,0:T(2,128)S(1)}) custom-call(s32[1]{0:T(128)} %bitcast.share_ref, f32[16]{0:T(128)} %table_ref.1, s32[2,1024]{1,0:T(2,128)} %entries_ref.2, bf16[976,1024]{1,0:T(8,128)(2,1)} %bitcast.8), custom_call_target="tpu_custom_call" | custom-call | flops 2415000064 | bytes 262144 | tf_op jit(solution)/shard_map/ends/pallas_call | solution.py:120
  2.8 2.6 %collective-permute-start.1 = (bf16[2,32,1024]{2,1,0:T(8,128)(2,1)S(1)}, bf16[2,32,1024]{2,1,0:T(8,128)(2,1)S(1)}, u32[]{:S(2)}, u32[]{:S(2)}) collective-permute-start(bf16[2,32,1024]{2,1,0:T(8,128)(2,1)S(1)} %get-tuple-element.26.after_ref.refs_1_), channel_id=1, source_target_pairs={{0,4},{4,0},{8,12},{12,8},{16,20},{20,16},{24,28},{28,24},{1,5},{5... | collective-permute-start | bytes 393224 | tf_op jit(solution)/shard_map/ppermute | solution.py:564
  5.4 0.0 copy-done
  5.4 0.0 copy-done.1
  5.4 0.0 copy-done.2
  5.4 1.2 %mine.1 = (bf16[128,256]{1,0:T(8,128)(2,1)S(1)}, bf16[256,256]{1,0:T(8,128)(2,1)S(1)}, bf16[256,256]{1,0:T(8,128)(2,1)S(1)}, bf16[8,64,1024]{2,1,0:T(8,128)(2,1)S(1)}, f32[8,64,1024]{2,1,0:T(8,128)S(1)}) custom-call(bf16[60,60]{1,0:T(8,128)(2,1)S(1)} %bitcast.11, bf16[976,1024]{1,0:T(8,128)(2,1)S(1)} %bitcast.9, bf16[976,1024]{1,0:T(8,128)(2,1)S(1)} %bitcast.7, ...), custom_call_target="tpu_custom_call" | custom-call | flops 2070000000 | bytes 262144 | tf_op jit(solution)/shard_map/mine/pallas_call | solution.py:289
  6.7 0.0 collective-permute-done.other_ref
  6.7 1.4 %other.1 = (bf16[244,1024]{1,0:T(8,128)(2,1)S(1)}, f32[244,1024]{1,0:T(8,128)S(1)}) custom-call(bf16[128,256]{1,0:T(8,128)(2,1)S(1)} %get-tuple-element.27.perm_ref, bf16[256,256]{1,0:T(8,128)(2,1)S(1)} %get-tuple-element.28.local_ref, bf16[256,256]{1,0:T(8,128)(2,1)S(1)} %get-tuple-element.29.order_ref, bf16[8,64,1024]{2,1,0:T(8,128)(2,1)S(1)} %get-tuple-element.30.field_w, ...), custom_call_target="tpu_custom_call" | custom-call | flops 2300000000 | bytes 262144 | tf_op jit(solution)/shard_map/other/pallas_call | solution.py:306
  8.1 1.6 %collective-permute-start.9 = (bf16[244,1024]{1,0:T(8,128)(2,1)S(1)}, bf16[244,1024]{1,0:T(8,128)(2,1)S(1)}, u32[]{:S(2)}, u32[]{:S(2)}) collective-permute-start(bf16[244,1024]{1,0:T(8,128)(2,1)S(1)} %get-tuple-element.32.after_ref), channel_id=1, source_target_pairs={{0,2},{1,3},{2,0},{3,1},{4,6},{5,7},{6,4},{7,5},{8,10},{9,11},{10,... | collective-permute-start | bytes 1499144 | tf_op jit(solution)/shard_map/ppermute | solution.py:564
  9.7 0.0 copy-start.3
  9.7 0.0 copy-start.4
  9.7 0.0 copy-start.5
  9.7 1.0 %local.1 = (f32[4,32,1024]{2,1,0:T(8,128)S(1)}, f32[2,19,2,1024]{3,2,1,0:T(2,128)S(1)}) custom-call(f32[3,2,1024]{2,1,0:T(2,128)S(1)} %get-tuple-element.25.lines_ref.refs_0_, bf16[976,1024]{1,0:T(8,128)(2,1)S(1)} %bitcast.10, bf16[244,1024]{1,0:T(8,128)(2,1)S(1)} %get-tuple-element.32.after_ref), custom_call_target="tpu_custom_call" | custom-call | flops 3449999872 | bytes 262144 | tf_op jit(solution)/shard_map/local/pallas_call | solution.py:211
  10.6 0.0 copy-done.3
  10.7 0.0 copy-done.4
  10.7 0.0 copy-done.5
  10.7 0.8 %tables.1 = (bf16[8,256,256]{2,1,0:T(8,128)(2,1)S(1)}, f32[4,8,256]{2,1,0:T(8,128)S(1)}, bf16[256,256]{1,0:T(8,128)(2,1)S(1)}) custom-call(f32[1,16]{1,0:T(1,128)S(1)} %bitcast.13, s32[2,128]{1,0:T(2,128)S(1)} %copy-done.4, bf16[60,60]{1,0:T(8,128)(2,1)S(1)} %bitcast.12, f32[4,32,1024]{2,1,0:T(8,128)S(1)} %get-tuple-element.34.after_ref.own_ref), custom_call_target="tpu_custom_call" | custom-call | flops 1150000000 | bytes 262144 | tf_op jit(solution)/shard_map/tables/pallas_call | solution.py:363
  11.5 0.0 collective-permute-done.1.refs_2_
  11.5 0.1 merge.1
  11.6 1.6 %collective-permute-start.2 = (bf16[32,1024]{1,0:T(8,128)(2,1)S(1)}, bf16[32,1024]{1,0:T(8,128)(2,1)S(1)}, u32[]{:S(2)}, u32[]{:S(2)}) collective-permute-start(bf16[32,1024]{1,0:T(8,128)(2,1)S(1)} %get-tuple-element.39), channel_id=1, source_target_pairs={{0,8},{4,12},{8,0},{12,4},{16,24},{20,28},{24,16},{28,20},{1,9},{5... | collective-permute-start | bytes 196616 | tf_op jit(solution)/shard_map/ppermute | solution.py:564
  13.3 2.6 %collective-permute-start.3 = (bf16[32,1024]{1,0:T(8,128)(2,1)S(1)}, bf16[32,1024]{1,0:T(8,128)(2,1)S(1)}, u32[]{:S(2)}, u32[]{:S(2)}) collective-permute-start(bf16[32,1024]{1,0:T(8,128)(2,1)S(1)} %get-tuple-element.40), channel_id=1, source_target_pairs={{0,16},{4,20},{8,24},{12,28},{16,0},{20,4},{24,8},{28,12},{1,17},{... | collective-permute-start | bytes 196616 | tf_op jit(solution)/shard_map/ppermute | solution.py:564
  15.9 0.2 collective-permute-start.4
  16.1 0.0 collective-permute-start.5
  16.1 0.0 collective-permute-done.2.refs_0_
  16.1 0.5 %collective-permute-start.6 = (bf16[32,1024]{1,0:T(8,128)(2,1)S(1)}, bf16[32,1024]{1,0:T(8,128)(2,1)S(1)}, u32[]{:S(2)}, u32[]{:S(2)}) collective-permute-start(bf16[32,1024]{1,0:T(8,128)(2,1)S(1)} %collective-permute-done.2.refs_0_), channel_id=1, source_target_pairs={{0,1},{1,0},{2,3},{3,2},{4,5},{5,4},{6,7},{7,6},{8,9},{9,8},{10,11... | collective-permute-start | bytes 196616 | tf_op jit(solution)/shard_map/ppermute | solution.py:564
  16.6 4.0 %collective-permute-done.3.refs_1_ = bf16[32,1024]{1,0:T(8,128)(2,1)S(1)} collective-permute-done((bf16[32,1024]{1,0:T(8,128)(2,1)S(1)}, bf16[32,1024]{1,0:T(8,128)(2,1)S(1)}, u32[]{:S(2)}, u32[]{:S(2)}) %collective-permute-start.3) | collective-permute-done | bytes 65568 | tf_op jit(solution)/shard_map/ppermute | solution.py:564
  20.6 0.0 collective-permute-start.7
  20.6 1.4 %collective-permute-done.4.refs_2_ = bf16[32,1024]{1,0:T(8,128)(2,1)S(1)} collective-permute-done((bf16[32,1024]{1,0:T(8,128)(2,1)S(1)}, bf16[32,1024]{1,0:T(8,128)(2,1)S(1)}, u32[]{:S(2)}, u32[]{:S(2)}) %collective-permute-start.4) | collective-permute-done | bytes 65568 | tf_op jit(solution)/shard_map/ppermute | solution.py:564
  22.0 0.0 collective-permute-start.8
  22.0 0.5 %rows.1.done_ref = f32[4,32,1024]{2,1,0:T(8,128)S(1)} custom-call(f32[4,32,1024]{2,1,0:T(8,128)S(1)} %get-tuple-element.24.own_ref, f32[2,19,2,1024]{3,2,1,0:T(2,128)S(1)} %get-tuple-element.33.coef_ref, bf16[8,256,256]{2,1,0:T(8,128)(2,1)S(1)} %get-tuple-element.36.mat_ref, f32[4,8,256]{2,1,0:T(8,128)S(1)} %get-tuple-element.37.row_coef_ref, ...), custom_call_target="tpu_custom_call" | custom-call | flops 805000000 | bytes 262144 | tf_op jit(solution)/shard_map/rows/pallas_call | solution.py:441
  22.6 0.0 collective-permute-done.5.part_ref
  22.6 0.0 collective-permute-done.6.last_1_ref
  22.6 0.0 collective-permute-done.7.last_2_ref
  22.6 0.7 %collective-permute-done.8.last_3_ref = bf16[32,1024]{1,0:T(8,128)(2,1)S(1)} collective-permute-done((bf16[32,1024]{1,0:T(8,128)(2,1)S(1)}, bf16[32,1024]{1,0:T(8,128)(2,1)S(1)}, u32[]{:S(2)}, u32[]{:S(2)}) %collective-permute-start.8) | collective-permute-done | bytes 65568 | tf_op jit(solution)/shard_map/ppermute | solution.py:564
  23.3 0.0 collective-permute-done.9.came_ref
  23.3 1.8 %final.1 = bf16[61,4,1024]{2,1,0:T(4,128)(2,1)} custom-call(f32[4,32,1024]{2,1,0:T(8,128)S(1)} %rows.1.done_ref, f32[4,32,1024]{2,1,0:T(8,128)S(1)} %get-tuple-element.34.after_ref.own_ref, f32[2,19,2,1024]{3,2,1,0:T(2,128)S(1)} %get-tuple-element.33.coef_ref, bf16[8,256,256]{2,1,0:T(8,128)(2,1)S(1)} %get-tuple-element.36.mat_ref, ...), custom_call_target="tpu_custom_call" | custom-call | flops 1724999936 | bytes 262144 | tf_op jit(solution)/shard_map/final/pallas_call | solution.py:488
Async XLA Ops:
  0.0 6.7 %collective-permute-start = (bf16[976,1024]{1,0:T(8,128)(2,1)}, bf16[976,1024]{1,0:T(8,128)(2,1)S(1)}, u32[]{:S(2)}, u32[]{:S(2)}) collective-permute-start(bf16[976,1024]{1,0:T(8,128)(2,1)} %bitcast.6), channel_id=1, source_target_pairs={{0,1},{1,0},{2,3},{3,2},{4,5},{5,4},{6,7},{7,6},{8,9},{9,8},{10,11... | collective-permute-start | bytes 5996552 | tf_op jit(solution)/shard_map/ppermute | solution.py:564
  0.5 5.0 %copy-start = (bf16[1,61,16,1024]{3,2,1,0:T(8,128)(2,1)S(1)}, bf16[1,61,16,1024]{3,2,1,0:T(8,128)(2,1)}, u32[]{:S(2)}) copy-start(bf16[1,61,16,1024]{3,2,1,0:T(8,128)(2,1)} %param.13) | copy-start | bytes 5996548
  0.5 5.0 %copy-start.1 = (bf16[61,16,1024]{2,1,0:T(8,128)(2,1)S(1)}, bf16[61,16,1024]{2,1,0:T(8,128)(2,1)}, u32[]{:S(2)}) copy-start(bf16[61,16,1024]{2,1,0:T(8,128)(2,1)} %param.7) | copy-start | bytes 5996548
  0.5 5.0 %copy-start.2 = (bf16[1,60,60]{2,1,0:T(8,128)(2,1)S(1)}, bf16[1,60,60]{2,1,0:T(8,128)(2,1)}, u32[]{:S(2)}) copy-start(bf16[1,60,60]{2,1,0:T(8,128)(2,1)} %param.9) | copy-start | bytes 21604
  2.8 8.7 %collective-permute-start.1 = (bf16[2,32,1024]{2,1,0:T(8,128)(2,1)S(1)}, bf16[2,32,1024]{2,1,0:T(8,128)(2,1)S(1)}, u32[]{:S(2)}, u32[]{:S(2)}) collective-permute-start(bf16[2,32,1024]{2,1,0:T(8,128)(2,1)S(1)} %get-tuple-element.26.after_ref.refs_1_), channel_id=1, source_target_pairs={{0,4},{4,0},{8,12},{12,8},{16,20},{20,16},{24,28},{28,24},{1,5},{5... | collective-permute-start | bytes 393224 | tf_op jit(solution)/shard_map/ppermute | solution.py:564
  8.1 15.2 %collective-permute-start.9 = (bf16[244,1024]{1,0:T(8,128)(2,1)S(1)}, bf16[244,1024]{1,0:T(8,128)(2,1)S(1)}, u32[]{:S(2)}, u32[]{:S(2)}) collective-permute-start(bf16[244,1024]{1,0:T(8,128)(2,1)S(1)} %get-tuple-element.32.after_ref), channel_id=1, source_target_pairs={{0,2},{1,3},{2,0},{3,1},{4,6},{5,7},{6,4},{7,5},{8,10},{9,11},{10,... | collective-permute-start | bytes 1499144 | tf_op jit(solution)/shard_map/ppermute | solution.py:564
  9.7 1.0 %copy-start.3 = (bf16[1,60,60]{2,1,0:T(8,128)(2,1)S(1)}, bf16[1,60,60]{2,1,0:T(8,128)(2,1)}, u32[]{:S(2)}) copy-start(bf16[1,60,60]{2,1,0:T(8,128)(2,1)} %param.8) | copy-start | bytes 21604
  9.7 1.0 %copy-start.4 = (s32[2,128]{1,0:T(2,128)S(1)}, s32[2,128]{1,0:T(2,128)}, u32[]{:S(2)}) copy-start(s32[2,128]{1,0:T(2,128)} %entries_ref.3) | copy-start | bytes 3076
  9.7 1.0 %copy-start.5 = (f32[16]{0:T(128)S(1)}, f32[16]{0:T(128)}, u32[]{:S(2)}) copy-start(f32[16]{0:T(128)} %table_ref.1) | copy-start | bytes 196
  11.6 4.5 %collective-permute-start.2 = (bf16[32,1024]{1,0:T(8,128)(2,1)S(1)}, bf16[32,1024]{1,0:T(8,128)(2,1)S(1)}, u32[]{:S(2)}, u32[]{:S(2)}) collective-permute-start(bf16[32,1024]{1,0:T(8,128)(2,1)S(1)} %get-tuple-element.39), channel_id=1, source_target_pairs={{0,8},{4,12},{8,0},{12,4},{16,24},{20,28},{24,16},{28,20},{1,9},{5... | collective-permute-start | bytes 196616 | tf_op jit(solution)/shard_map/ppermute | solution.py:564
  13.3 7.3 %collective-permute-start.3 = (bf16[32,1024]{1,0:T(8,128)(2,1)S(1)}, bf16[32,1024]{1,0:T(8,128)(2,1)S(1)}, u32[]{:S(2)}, u32[]{:S(2)}) collective-permute-start(bf16[32,1024]{1,0:T(8,128)(2,1)S(1)} %get-tuple-element.40), channel_id=1, source_target_pairs={{0,16},{4,20},{8,24},{12,28},{16,0},{20,4},{24,8},{28,12},{1,17},{... | collective-permute-start | bytes 196616 | tf_op jit(solution)/shard_map/ppermute | solution.py:564
  15.9 6.2 %collective-permute-start.4 = (bf16[32,1024]{1,0:T(8,128)(2,1)S(1)}, bf16[32,1024]{1,0:T(8,128)(2,1)S(1)}, u32[]{:S(2)}, u32[]{:S(2)}) collective-permute-start(bf16[32,1024]{1,0:T(8,128)(2,1)S(1)} %get-tuple-element.40), channel_id=1, source_target_pairs={{0,24},{4,28},{8,16},{12,20},{16,8},{20,12},{24,0},{28,4},{1,25},{... | collective-permute-start | bytes 196616 | tf_op jit(solution)/shard_map/ppermute | solution.py:564
  16.1 6.5 %collective-permute-start.5 = (bf16[2,32,1024]{2,1,0:T(8,128)(2,1)S(1)}, bf16[2,32,1024]{2,1,0:T(8,128)(2,1)S(1)}, u32[]{:S(2)}, u32[]{:S(2)}) collective-permute-start(bf16[2,32,1024]{2,1,0:T(8,128)(2,1)S(1)} %get-tuple-element.38.part_ref), channel_id=1, source_target_pairs={{0,1},{1,0},{2,3},{3,2},{4,5},{5,4},{6,7},{7,6},{8,9},{9,8},{10,11... | collective-permute-start | bytes 393224 | tf_op jit(solution)/shard_map/ppermute | solution.py:564
  16.1 6.5 %collective-permute-start.6 = (bf16[32,1024]{1,0:T(8,128)(2,1)S(1)}, bf16[32,1024]{1,0:T(8,128)(2,1)S(1)}, u32[]{:S(2)}, u32[]{:S(2)}) collective-permute-start(bf16[32,1024]{1,0:T(8,128)(2,1)S(1)} %collective-permute-done.2.refs_0_), channel_id=1, source_target_pairs={{0,1},{1,0},{2,3},{3,2},{4,5},{5,4},{6,7},{7,6},{8,9},{9,8},{10,11... | collective-permute-start | bytes 196616 | tf_op jit(solution)/shard_map/ppermute | solution.py:564
  20.6 2.0 %collective-permute-start.7 = (bf16[32,1024]{1,0:T(8,128)(2,1)S(1)}, bf16[32,1024]{1,0:T(8,128)(2,1)S(1)}, u32[]{:S(2)}, u32[]{:S(2)}) collective-permute-start(bf16[32,1024]{1,0:T(8,128)(2,1)S(1)} %collective-permute-done.3.refs_1_), channel_id=1, source_target_pairs={{0,1},{1,0},{2,3},{3,2},{4,5},{5,4},{6,7},{7,6},{8,9},{9,8},{10,11... | collective-permute-start | bytes 196616 | tf_op jit(solution)/shard_map/ppermute | solution.py:564
  22.0 1.3 %collective-permute-start.8 = (bf16[32,1024]{1,0:T(8,128)(2,1)S(1)}, bf16[32,1024]{1,0:T(8,128)(2,1)S(1)}, u32[]{:S(2)}, u32[]{:S(2)}) collective-permute-start(bf16[32,1024]{1,0:T(8,128)(2,1)S(1)} %collective-permute-done.4.refs_2_), channel_id=1, source_target_pairs={{0,1},{1,0},{2,3},{3,2},{4,5},{5,4},{6,7},{7,6},{8,9},{9,8},{10,11... | collective-permute-start | bytes 196616 | tf_op jit(solution)/shard_map/ppermute | solution.py:564

commit v7 on v6

--- a/solution.py
+++ b/solution.py
@@ -80,11 +80,11 @@
     return slice(share * subs * cols, min((share + 1) * subs * cols, total))
 
 
-def sweep_share(levels, slab_count, share, alpha, held, work):
+def sweep_share(levels, slab_count, share, perm, alpha, held, work):
     cols, subs, lanes = work.shape
     first = share * subs
     held = jnp.where(iota(held.shape, 0) < (slab_count - first) * cols, held, 0)
-    to_columns(transposer(cols), held, work, cols)
+    to_columns(perm, held, work, cols)
     is_level = iota((subs, lanes), 0) + first < levels
     alpha = jnp.where(is_level, alpha[0:1], alpha[1:2])
     sweep(work, alpha)
@@ -97,14 +97,14 @@
     pieces, cols, subs, lanes = work.shape
     own_cols = own_ref.shape[0]
     tile, mem = lax.axis_index("tile"), lax.axis_index("mem")
-    share = share_ref[0]
+    share, perm = share_ref[0], transposer(cols)
     pair = lookup(table_ref, entries_ref[...])
     decay, turn = line_coefs(pair, cols)
     behind = reflected(decay, turn, tile, steps)
     lines_ref[0], lines_ref[1], lines_ref[2] = pair, decay, behind
     for piece in range(pieces):
         part = slice(piece * lanes, (piece + 1) * lanes)
-        gain, is_level = sweep_share(levels, slab_count, share, pair[:, part], field_ref[:, part], work.at[piece])
+        gain, is_level = sweep_share(levels, slab_count, share, perm, pair[:, part], field_ref[:, part], work.at[piece])
         turned = (decay * behind)[:, part]
         turned = jnp.where(is_level, turned[0:1], turned[1:2])
         forward = gain * work[piece, cols - 1]
@@ -175,9 +175,10 @@
             held_ref[0 : rows.stop - rows.start, :] = field_ref[rows, :]
 
     pair, decay, behind = lines_ref[0], lines_ref[1], lines_ref[2]
+    perm = transposer(cols)
     for piece in range(pieces):
         part = slice(piece * lanes, (piece + 1) * lanes)
-        gain, _ = sweep_share(levels, slab_count, share, pair[:, part], held_ref[:, part], work.at[piece])
+        gain, _ = sweep_share(levels, slab_count, share, perm, pair[:, part], held_ref[:, part], work.at[piece])
         own_ref[:, :, part] = work[piece, pl.ds(mem * own_cols, own_cols)] * gain[None]
     square = pair * pair
     power, sums = jnp.ones_like(pair), jnp.zeros_like(pair)
@@ -222,7 +223,7 @@
             pltpu.VMEM((rows // LANES, cols, subs, LANES), F32),
         ],
         compiler_params=pltpu.CompilerParams(vmem_limit_bytes=VMEM),
-        cost_estimate=taking(3.0),
+        cost_estimate=taking(0.5),
     )(lines, flat_field, after)
 
 
@@ -238,8 +239,8 @@
 
 
 def member_term(local, member_w, field_w, part):
-    cols, slabs, rows = field_w[part].shape
     member = member_w[part]
+    cols, slabs, rows = member.shape
     scaled = (member * field_w[part].astype(F32)).astype(BF16).reshape(cols * slabs, rows)
     return member * dot(local, scaled).reshape(cols, slabs, rows)
 
@@ -267,17 +268,17 @@
         total_out[part] = member_term(local, member_w, field_out, part)
 
 
-def other_kernel(cols, perm_ref, local_ref, order_ref, field_w, total_ref, other_ref, send_ref, keep_ref, member_w):
-    own_cols, count = field_w.shape[0] // 2, keep_ref.shape[0]
-    to_columns(perm_ref[...], other_ref, member_w, cols)
-    for part, out_ref in ((slice(0, own_cols), send_ref), (slice(own_cols, 2 * own_cols), keep_ref)):
-        total = total_ref[part] + member_term(local_ref[...], member_w, field_w, part)
-        total = total.reshape(order_ref.shape[0], -1)
-        high = total.astype(BF16)
-        ordered = dot(order_ref[...], high)
-        if out_ref is keep_ref:
-            ordered = ordered + dot(order_ref[...], (total - high.astype(F32)).astype(BF16))
-        out_ref[...] = ordered[:count].astype(out_ref.dtype)
+def other_kernel(half, cols, perm_ref, local_ref, order_ref, field_w, total_ref, other_ref, after_ref, out_ref, member_w):
+    own_cols, count = member_w.shape[0], out_ref.shape[0]
+    part = slice(half * own_cols, (half + 1) * own_cols)
+    to_columns(perm_ref[half * own_cols * SUB : (half + 1) * own_cols * SUB, :], other_ref, member_w, cols)
+    total = total_ref[part] + member_term(local_ref[...], member_w, field_w.at[part], slice(0, own_cols))
+    total = total.reshape(order_ref.shape[0], -1)
+    high = total.astype(BF16)
+    ordered = dot(order_ref[...], high)
+    if out_ref.dtype == F32:
+        ordered = ordered + dot(order_ref[...], (total - high.astype(F32)).astype(BF16))
+    out_ref[...] = ordered[:count].astype(out_ref.dtype)
 
 
 def ensemble_calls(loc, flat_field, mine, other, after, levels, cols, own_cols):
@@ -302,17 +303,20 @@
         compiler_params=pltpu.CompilerParams(vmem_limit_bytes=VMEM),
         cost_estimate=taking(1.8),
     )(loc, flat_field, mine, after)
-    out_shape = (slab_count * own_cols, rows)
-    return pl.pallas_call(
-        functools.partial(other_kernel, cols),
-        name="other",
-        in_specs=[vmem] * 6,
-        out_specs=[vmem, vmem],
-        out_shape=[jax.ShapeDtypeStruct(out_shape, BF16), jax.ShapeDtypeStruct(out_shape, F32)],
-        scratch_shapes=[pltpu.VMEM(work, F32)],
-        compiler_params=pltpu.CompilerParams(vmem_limit_bytes=VMEM),
-        cost_estimate=taking(2.0),
-    )(*held, other)
+    after, outs = other, []
+    for half, dtype in enumerate((BF16, F32)):
+        after = pl.pallas_call(
+            functools.partial(other_kernel, half, cols),
+            name=("send", "keep")[half],
+            in_specs=[vmem] * 6 + [pl.BlockSpec(memory_space=pl.ANY)],
+            out_specs=vmem,
+            out_shape=jax.ShapeDtypeStruct((slab_count * own_cols, rows), dtype),
+            scratch_shapes=[pltpu.VMEM((own_cols, slabs, rows), F32)],
+            compiler_params=pltpu.CompilerParams(vmem_limit_bytes=VMEM),
+            cost_estimate=taking((0.8, 4.0)[half]),
+        )(*held, other, after)
+        outs.append(after)
+    return outs
 
 
 def tables_kernel(levels, own_cols, col_dev, slabs, table_ref, entries_ref, vert_ref, after_ref, mat_ref, coef_ref, vert_out):
@@ -371,7 +375,7 @@
             jax.ShapeDtypeStruct((own_cols * slabs, own_cols * slabs), BF16),
         ],
         compiler_params=pltpu.CompilerParams(vmem_limit_bytes=VMEM),
-        cost_estimate=taking(1.0),
+        cost_estimate=taking(0.4),
     )(table[None], entries, vert, after)
 
 
@@ -445,7 +449,7 @@
         out_specs=vmem,
         out_shape=jax.ShapeDtypeStruct(own.shape, F32),
         compiler_params=pltpu.CompilerParams(vmem_limit_bytes=VMEM),
-        cost_estimate=taking(0.7),
+        cost_estimate=taking(0.9),
     )(*args)
 
 
@@ -574,13 +578,13 @@
     blocks, came = [ends], []
     send, keep = ensemble_calls(loc_filter[0], full_field, mine, other, ends, levels, cols, own_cols)
     over = swap(send, 2)
-    own_1, coef = local_call(lines, full_field, send, levels, steps, cols, own_cols)
-    mats, row_coef, vert = tables_call(alpha_table, yscale_idx, vert_filter[0], own_1, levels, own_cols, cols, slabs)
     for level in range(steps - 2):
         came.append(swap(blocks[0], 1 << level, "tile"))
-        *blocks, mats = merge_call(lines, ends, came, [mats], levels, steps)
+        *blocks, keep = merge_call(lines, ends, came, [keep], levels, steps)
     near, far, part = blocks
     last = {flip: swap(near if flip == 1 else far, flip << (steps - 2), "tile") for flip in (2, 3, 1)}
+    own_1, coef = local_call(lines, full_field, near, levels, steps, cols, own_cols)
+    mats, row_coef, vert = tables_call(alpha_table, yscale_idx, vert_filter[0], own_1, levels, own_cols, cols, slabs)
     shares = [part, last[1], last[2], last[3]]
     others = [swap(share, 1) for share in shares]
     done = rows_call(levels, own_0, coef, mats, row_coef, shares)

time: 25.2 us -> 23.3 us (0.925)
  waiting for transfers between devices: 6.1 us -> 3.61 us
  Pallas kernels: 9.28 us -> 9.9 us
    ppermute x10, waiting for transfers between devices: 6.1 us -> 3.61 us  [swap(): lax.ppermute(array, axis, [(i, i ^ flip) for i in range(lax.axis_size(axi...]
    pallas_call x1 -> x2, Pallas kernels: 1.43 us -> 2.06 us  [ensemble_calls(): pl.pallas_call(functools.partial(other_kernel, half, cols), name=('send',...]
  transfers between devices with their start and end apart: 10 -> 10, of which waited for: 3 -> 4; matrix products, arithmetic and copies ran while one was open for 0% -> 0% of each run, Pallas kernels for 30% -> 31%
where the time goes in v7:
time: 23.3 us; the launch traced here: 23.2 us
  Pallas kernels  9.9 us (42%)
  starting transfers between devices  9.48 us (41%)
  waiting for transfers between devices  3.61 us (15%)
    ppermute x10, starting transfers between devices, swap(): lax.ppermute(array, axis, [(i, i ^ flip) for i in range(lax.axis_size(axi...  9.48 us
    ppermute x10, waiting for transfers between devices, swap(): lax.ppermute(array, axis, [(i, i ^ flip) for i in range(lax.axis_size(axi...  3.61 us
    pallas_call x1, Pallas kernels, ends_call(): pl.pallas_call(functools.partial(ends_kernel, levels, steps, total // col...  2.35 us
    pallas_call x2, Pallas kernels, ensemble_calls(): pl.pallas_call(functools.partial(other_kernel, half, cols), name=('send',...  2.06 us
    pallas_call x1, Pallas kernels, final_call(): pl.pallas_call(functools.partial(final_kernel, levels, scale), name='fina...  1.81 us
    pallas_call x1, Pallas kernels, ensemble_calls(): pl.pallas_call(functools.partial(mine_kernel, levels, cols), name='mine',...  1.22 us
    pallas_call x1, Pallas kernels, local_call(): pl.pallas_call(functools.partial(local_kernel, levels, steps, total // co...  0.97 us
    pallas_call x1, Pallas kernels, tables_call(): pl.pallas_call(functools.partial(tables_kernel, levels, own_cols, col_dev...  0.79 us
  transfers between devices with their start and end apart: 10, of which 4 were waited for; matrix products, arithmetic and copies ran while one was open for 0% of the time, Pallas kernels for 31%

profile of v7, /device:TPU:0, one launch (start us, length us, event | category | flops | bytes accessed | tf_op | source)
XLA Modules:
  0.0 23.2 jit_solution(6374335129735393610)
XLA Ops:
  0.0 0.5 %collective-permute-start.1 = (bf16[976,1024]{1,0:T(8,128)(2,1)}, bf16[976,1024]{1,0:T(8,128)(2,1)S(1)}, u32[]{:S(2)}, u32[]{:S(2)}) collective-permute-start(bf16[976,1024]{1,0:T(8,128)(2,1)} %bitcast.6), channel_id=1, source_target_pairs={{0,1},{1,0},{2,3},{3,2},{4,5},{5,4},{6,7},{7,6},{8,9},{9,8},{10,11... | collective-permute-start | bytes 5996552 | tf_op jit(solution)/shard_map/ppermute | solution.py:568
  0.5 0.0 copy-start
  0.5 0.0 copy-start.1
  0.5 0.0 copy-start.2
  0.5 2.3 %ends.1 = (bf16[2,32,1024]{2,1,0:T(8,128)(2,1)S(1)}, f32[4,32,1024]{2,1,0:T(8,128)S(1)}, f32[3,2,1024]{2,1,0:T(2,128)S(1)}) custom-call(s32[1]{0:T(128)} %bitcast.share_ref, f32[16]{0:T(128)} %table_ref.1, s32[2,1024]{1,0:T(2,128)} %entries_ref.2, bf16[976,1024]{1,0:T(8,128)(2,1)} %bitcast.8), custom_call_target="tpu_custom_call" | custom-call | flops 2415000064 | bytes 262144 | tf_op jit(solution)/shard_map/ends/pallas_call | solution.py:120
  2.8 2.6 %collective-permute-start = (bf16[2,32,1024]{2,1,0:T(8,128)(2,1)S(1)}, bf16[2,32,1024]{2,1,0:T(8,128)(2,1)S(1)}, u32[]{:S(2)}, u32[]{:S(2)}) collective-permute-start(bf16[2,32,1024]{2,1,0:T(8,128)(2,1)S(1)} %get-tuple-element.24.after_ref.refs_1_), channel_id=1, source_target_pairs={{0,4},{4,0},{8,12},{12,8},{16,20},{20,16},{24,28},{28,24},{1,5},{5... | collective-permute-start | bytes 393224 | tf_op jit(solution)/shard_map/ppermute | solution.py:568
  5.4 0.0 copy-done
  5.4 0.0 copy-done.1
  5.4 0.0 copy-done.2
  5.4 1.2 %mine.1 = (bf16[128,256]{1,0:T(8,128)(2,1)S(1)}, bf16[256,256]{1,0:T(8,128)(2,1)S(1)}, bf16[256,256]{1,0:T(8,128)(2,1)S(1)}, bf16[8,64,1024]{2,1,0:T(8,128)(2,1)S(1)}, f32[8,64,1024]{2,1,0:T(8,128)S(1)}) custom-call(bf16[60,60]{1,0:T(8,128)(2,1)S(1)} %bitcast.11, bf16[976,1024]{1,0:T(8,128)(2,1)S(1)} %bitcast.9, bf16[976,1024]{1,0:T(8,128)(2,1)S(1)} %bitcast.7, ...), custom_call_target="tpu_custom_call" | custom-call | flops 2070000000 | bytes 262144 | tf_op jit(solution)/shard_map/mine/pallas_call | solution.py:290
  6.6 0.0 collective-permute-done.1.other_ref.after_ref
  6.7 0.9 %send.1.after_ref = bf16[244,1024]{1,0:T(8,128)(2,1)S(1)} custom-call(bf16[128,256]{1,0:T(8,128)(2,1)S(1)} %get-tuple-element.25.perm_ref, bf16[256,256]{1,0:T(8,128)(2,1)S(1)} %get-tuple-element.26.local_ref, bf16[256,256]{1,0:T(8,128)(2,1)S(1)} %get-tuple-element.27.order_ref, bf16[8,64,1024]{2,1,0:T(8,128)(2,1)S(1)} %get-tuple-element.28.field_w, ...), custom_call_target="tpu_custom_call" | custom-call | flops 920000000 | bytes 262144 | tf_op jit(solution)/shard_map/send/pallas_call | solution.py:308
  7.6 1.5 %collective-permute-start.9 = (bf16[244,1024]{1,0:T(8,128)(2,1)S(1)}, bf16[244,1024]{1,0:T(8,128)(2,1)S(1)}, u32[]{:S(2)}, u32[]{:S(2)}) collective-permute-start(bf16[244,1024]{1,0:T(8,128)(2,1)S(1)} %send.1.after_ref), channel_id=1, source_target_pairs={{0,2},{1,3},{2,0},{3,1},{4,6},{5,7},{6,4},{7,5},{8,10},{9,11},{10,... | collective-permute-start | bytes 1499144 | tf_op jit(solution)/shard_map/ppermute | solution.py:568
  9.2 1.1 %keep.1.refs_3_ = f32[244,1024]{1,0:T(8,128)S(1)} custom-call(bf16[128,256]{1,0:T(8,128)(2,1)S(1)} %get-tuple-element.25.perm_ref, bf16[256,256]{1,0:T(8,128)(2,1)S(1)} %get-tuple-element.26.local_ref, bf16[256,256]{1,0:T(8,128)(2,1)S(1)} %get-tuple-element.27.order_ref, bf16[8,64,1024]{2,1,0:T(8,128)(2,1)S(1)} %get-tuple-element.28.field_w, ...), custom_call_target="tpu_custom_call" | custom-call | flops 4600000000 | bytes 262144 | tf_op jit(solution)/shard_map/keep/pallas_call | solution.py:308
  10.3 0.0 collective-permute-done.refs_2_
  10.3 0.0 copy-start.3
  10.3 0.0 copy-start.4
  10.3 0.0 copy-start.5
  10.3 0.1 merge.1
  10.5 2.7 %collective-permute-start.3 = (bf16[32,1024]{1,0:T(8,128)(2,1)S(1)}, bf16[32,1024]{1,0:T(8,128)(2,1)S(1)}, u32[]{:S(2)}, u32[]{:S(2)}) collective-permute-start(bf16[32,1024]{1,0:T(8,128)(2,1)S(1)} %get-tuple-element.36), channel_id=1, source_target_pairs={{0,16},{4,20},{8,24},{12,28},{16,0},{20,4},{24,8},{28,12},{1,17},{... | collective-permute-start | bytes 196616 | tf_op jit(solution)/shard_map/ppermute | solution.py:568
  13.1 1.3 %collective-permute-start.4 = (bf16[32,1024]{1,0:T(8,128)(2,1)S(1)}, bf16[32,1024]{1,0:T(8,128)(2,1)S(1)}, u32[]{:S(2)}, u32[]{:S(2)}) collective-permute-start(bf16[32,1024]{1,0:T(8,128)(2,1)S(1)} %get-tuple-element.36), channel_id=1, source_target_pairs={{0,24},{4,28},{8,16},{12,20},{16,8},{20,12},{24,0},{28,4},{1,25},{... | collective-permute-start | bytes 196616 | tf_op jit(solution)/shard_map/ppermute | solution.py:568
  14.5 0.2 %collective-permute-start.2 = (bf16[32,1024]{1,0:T(8,128)(2,1)S(1)}, bf16[32,1024]{1,0:T(8,128)(2,1)S(1)}, u32[]{:S(2)}, u32[]{:S(2)}) collective-permute-start(bf16[32,1024]{1,0:T(8,128)(2,1)S(1)} %get-tuple-element.30.after_ref), channel_id=1, source_target_pairs={{0,8},{4,12},{8,0},{12,4},{16,24},{20,28},{24,16},{28,20},{1,9},{5... | collective-permute-start | bytes 196616 | tf_op jit(solution)/shard_map/ppermute | solution.py:568
  14.7 1.0 %local.1 = (f32[4,32,1024]{2,1,0:T(8,128)S(1)}, f32[2,19,2,1024]{3,2,1,0:T(2,128)S(1)}) custom-call(f32[3,2,1024]{2,1,0:T(2,128)S(1)} %get-tuple-element.23.refs_0_.lines_ref, bf16[976,1024]{1,0:T(8,128)(2,1)S(1)} %bitcast.10, bf16[32,1024]{1,0:T(8,128)(2,1)S(1)} %get-tuple-element.30.after_ref), custom_call_target="tpu_custom_call" | custom-call | flops 575000000 | bytes 262144 | tf_op jit(solution)/shard_map/local/pallas_call | solution.py:212
  15.7 0.1 collective-permute-start.5
  15.8 0.0 copy-done.3
  15.8 0.0 copy-done.4
  15.8 0.0 copy-done.5
  15.8 0.8 %tables.1 = (bf16[8,256,256]{2,1,0:T(8,128)(2,1)S(1)}, f32[4,8,256]{2,1,0:T(8,128)S(1)}, bf16[256,256]{1,0:T(8,128)(2,1)S(1)}) custom-call(f32[1,16]{1,0:T(1,128)S(1)} %bitcast.13, s32[2,128]{1,0:T(2,128)S(1)} %copy-done.4, bf16[60,60]{1,0:T(8,128)(2,1)S(1)} %bitcast.12, f32[4,32,1024]{2,1,0:T(8,128)S(1)} %get-tuple-element.32.after_ref.own_ref), custom_call_target="tpu_custom_call" | custom-call | flops 460000000 | bytes 262144 | tf_op jit(solution)/shard_map/tables/pallas_call | solution.py:367
  16.6 3.0 %collective-permute-done.2.refs_0_ = bf16[32,1024]{1,0:T(8,128)(2,1)S(1)} collective-permute-done((bf16[32,1024]{1,0:T(8,128)(2,1)S(1)}, bf16[32,1024]{1,0:T(8,128)(2,1)S(1)}, u32[]{:S(2)}, u32[]{:S(2)}) %collective-permute-start.2) | collective-permute-done | bytes 65568 | tf_op jit(solution)/shard_map/ppermute | solution.py:568
  19.6 0.0 collective-permute-start.6
  19.6 0.0 collective-permute-done.3.refs_1_
  19.6 0.5 %collective-permute-start.7 = (bf16[32,1024]{1,0:T(8,128)(2,1)S(1)}, bf16[32,1024]{1,0:T(8,128)(2,1)S(1)}, u32[]{:S(2)}, u32[]{:S(2)}) collective-permute-start(bf16[32,1024]{1,0:T(8,128)(2,1)S(1)} %collective-permute-done.3.refs_1_), channel_id=1, source_target_pairs={{0,1},{1,0},{2,3},{3,2},{4,5},{5,4},{6,7},{7,6},{8,9},{9,8},{10,11... | collective-permute-start | bytes 196616 | tf_op jit(solution)/shard_map/ppermute | solution.py:568
  20.1 0.0 collective-permute-done.4.refs_2_
  20.1 0.1 collective-permute-start.8
  20.1 0.6 %rows.1.done_ref = f32[4,32,1024]{2,1,0:T(8,128)S(1)} custom-call(f32[4,32,1024]{2,1,0:T(8,128)S(1)} %get-tuple-element.22.own_ref, f32[2,19,2,1024]{3,2,1,0:T(2,128)S(1)} %get-tuple-element.31.coef_ref, bf16[8,256,256]{2,1,0:T(8,128)(2,1)S(1)} %get-tuple-element.33.mat_ref, f32[4,8,256]{2,1,0:T(8,128)S(1)} %get-tuple-element.34.row_coef_ref, ...), custom_call_target="tpu_custom_call" | custom-call | flops 1035000000 | bytes 262144 | tf_op jit(solution)/shard_map/rows/pallas_call | solution.py:445
  20.7 0.1 collective-permute-done.6.last_1_ref
  20.8 0.2 collective-permute-done.7.last_2_ref
  21.0 0.4 %collective-permute-done.8.last_3_ref = bf16[32,1024]{1,0:T(8,128)(2,1)S(1)} collective-permute-done((bf16[32,1024]{1,0:T(8,128)(2,1)S(1)}, bf16[32,1024]{1,0:T(8,128)(2,1)S(1)}, u32[]{:S(2)}, u32[]{:S(2)}) %collective-permute-start.8) | collective-permute-done | bytes 65568 | tf_op jit(solution)/shard_map/ppermute | solution.py:568
  21.3 0.0 collective-permute-done.5.part_ref
  21.3 0.0 collective-permute-done.9.came_ref
  21.3 1.8 %final.1 = bf16[61,4,1024]{2,1,0:T(4,128)(2,1)} custom-call(f32[4,32,1024]{2,1,0:T(8,128)S(1)} %rows.1.done_ref, f32[4,32,1024]{2,1,0:T(8,128)S(1)} %get-tuple-element.32.after_ref.own_ref, f32[2,19,2,1024]{3,2,1,0:T(2,128)S(1)} %get-tuple-element.31.coef_ref, bf16[8,256,256]{2,1,0:T(8,128)(2,1)S(1)} %get-tuple-element.33.mat_ref, ...), custom_call_target="tpu_custom_call" | custom-call | flops 1724999936 | bytes 262144 | tf_op jit(solution)/shard_map/final/pallas_call | solution.py:492
Async XLA Ops:
  0.0 6.6 %collective-permute-start.1 = (bf16[976,1024]{1,0:T(8,128)(2,1)}, bf16[976,1024]{1,0:T(8,128)(2,1)S(1)}, u32[]{:S(2)}, u32[]{:S(2)}) collective-permute-start(bf16[976,1024]{1,0:T(8,128)(2,1)} %bitcast.6), channel_id=1, source_target_pairs={{0,1},{1,0},{2,3},{3,2},{4,5},{5,4},{6,7},{7,6},{8,9},{9,8},{10,11... | collective-permute-start | bytes 5996552 | tf_op jit(solution)/shard_map/ppermute | solution.py:568
  0.5 5.0 %copy-start = (bf16[1,61,16,1024]{3,2,1,0:T(8,128)(2,1)S(1)}, bf16[1,61,16,1024]{3,2,1,0:T(8,128)(2,1)}, u32[]{:S(2)}) copy-start(bf16[1,61,16,1024]{3,2,1,0:T(8,128)(2,1)} %param.13) | copy-start | bytes 5996548
  0.5 5.0 %copy-start.1 = (bf16[61,16,1024]{2,1,0:T(8,128)(2,1)S(1)}, bf16[61,16,1024]{2,1,0:T(8,128)(2,1)}, u32[]{:S(2)}) copy-start(bf16[61,16,1024]{2,1,0:T(8,128)(2,1)} %param.7) | copy-start | bytes 5996548
  0.5 5.0 %copy-start.2 = (bf16[1,60,60]{2,1,0:T(8,128)(2,1)S(1)}, bf16[1,60,60]{2,1,0:T(8,128)(2,1)}, u32[]{:S(2)}) copy-start(bf16[1,60,60]{2,1,0:T(8,128)(2,1)} %param.9) | copy-start | bytes 21604
  2.8 7.5 %collective-permute-start = (bf16[2,32,1024]{2,1,0:T(8,128)(2,1)S(1)}, bf16[2,32,1024]{2,1,0:T(8,128)(2,1)S(1)}, u32[]{:S(2)}, u32[]{:S(2)}) collective-permute-start(bf16[2,32,1024]{2,1,0:T(8,128)(2,1)S(1)} %get-tuple-element.24.after_ref.refs_1_), channel_id=1, source_target_pairs={{0,4},{4,0},{8,12},{12,8},{16,20},{20,16},{24,28},{28,24},{1,5},{5... | collective-permute-start | bytes 393224 | tf_op jit(solution)/shard_map/ppermute | solution.py:568
  7.6 13.7 %collective-permute-start.9 = (bf16[244,1024]{1,0:T(8,128)(2,1)S(1)}, bf16[244,1024]{1,0:T(8,128)(2,1)S(1)}, u32[]{:S(2)}, u32[]{:S(2)}) collective-permute-start(bf16[244,1024]{1,0:T(8,128)(2,1)S(1)} %send.1.after_ref), channel_id=1, source_target_pairs={{0,2},{1,3},{2,0},{3,1},{4,6},{5,7},{6,4},{7,5},{8,10},{9,11},{10,... | collective-permute-start | bytes 1499144 | tf_op jit(solution)/shard_map/ppermute | solution.py:568
  10.3 5.5 %copy-start.3 = (bf16[1,60,60]{2,1,0:T(8,128)(2,1)S(1)}, bf16[1,60,60]{2,1,0:T(8,128)(2,1)}, u32[]{:S(2)}) copy-start(bf16[1,60,60]{2,1,0:T(8,128)(2,1)} %param.8) | copy-start | bytes 21604
  10.3 5.5 %copy-start.4 = (s32[2,128]{1,0:T(2,128)S(1)}, s32[2,128]{1,0:T(2,128)}, u32[]{:S(2)}) copy-start(s32[2,128]{1,0:T(2,128)} %entries_ref.3) | copy-start | bytes 3076
  10.3 5.5 %copy-start.5 = (f32[16]{0:T(128)S(1)}, f32[16]{0:T(128)}, u32[]{:S(2)}) copy-start(f32[16]{0:T(128)} %table_ref.1) | copy-start | bytes 196
  10.5 9.1 %collective-permute-start.3 = (bf16[32,1024]{1,0:T(8,128)(2,1)S(1)}, bf16[32,1024]{1,0:T(8,128)(2,1)S(1)}, u32[]{:S(2)}, u32[]{:S(2)}) collective-permute-start(bf16[32,1024]{1,0:T(8,128)(2,1)S(1)} %get-tuple-element.36), channel_id=1, source_target_pairs={{0,16},{4,20},{8,24},{12,28},{16,0},{20,4},{24,8},{28,12},{1,17},{... | collective-permute-start | bytes 196616 | tf_op jit(solution)/shard_map/ppermute | solution.py:568
  13.1 7.0 %collective-permute-start.4 = (bf16[32,1024]{1,0:T(8,128)(2,1)S(1)}, bf16[32,1024]{1,0:T(8,128)(2,1)S(1)}, u32[]{:S(2)}, u32[]{:S(2)}) collective-permute-start(bf16[32,1024]{1,0:T(8,128)(2,1)S(1)} %get-tuple-element.36), channel_id=1, source_target_pairs={{0,24},{4,28},{8,16},{12,20},{16,8},{20,12},{24,0},{28,4},{1,25},{... | collective-permute-start | bytes 196616 | tf_op jit(solution)/shard_map/ppermute | solution.py:568
  14.5 5.1 %collective-permute-start.2 = (bf16[32,1024]{1,0:T(8,128)(2,1)S(1)}, bf16[32,1024]{1,0:T(8,128)(2,1)S(1)}, u32[]{:S(2)}, u32[]{:S(2)}) collective-permute-start(bf16[32,1024]{1,0:T(8,128)(2,1)S(1)} %get-tuple-element.30.after_ref), channel_id=1, source_target_pairs={{0,8},{4,12},{8,0},{12,4},{16,24},{20,28},{24,16},{28,20},{1,9},{5... | collective-permute-start | bytes 196616 | tf_op jit(solution)/shard_map/ppermute | solution.py:568
  15.7 5.7 %collective-permute-start.5 = (bf16[2,32,1024]{2,1,0:T(8,128)(2,1)S(1)}, bf16[2,32,1024]{2,1,0:T(8,128)(2,1)S(1)}, u32[]{:S(2)}, u32[]{:S(2)}) collective-permute-start(bf16[2,32,1024]{2,1,0:T(8,128)(2,1)S(1)} %get-tuple-element.35.part_ref), channel_id=1, source_target_pairs={{0,1},{1,0},{2,3},{3,2},{4,5},{5,4},{6,7},{7,6},{8,9},{9,8},{10,11... | collective-permute-start | bytes 393224 | tf_op jit(solution)/shard_map/ppermute | solution.py:568
  19.6 1.3 %collective-permute-start.6 = (bf16[32,1024]{1,0:T(8,128)(2,1)S(1)}, bf16[32,1024]{1,0:T(8,128)(2,1)S(1)}, u32[]{:S(2)}, u32[]{:S(2)}) collective-permute-start(bf16[32,1024]{1,0:T(8,128)(2,1)S(1)} %collective-permute-done.2.refs_0_), channel_id=1, source_target_pairs={{0,1},{1,0},{2,3},{3,2},{4,5},{5,4},{6,7},{7,6},{8,9},{9,8},{10,11... | collective-permute-start | bytes 196616 | tf_op jit(solution)/shard_map/ppermute | solution.py:568
  19.6 1.4 %collective-permute-start.7 = (bf16[32,1024]{1,0:T(8,128)(2,1)S(1)}, bf16[32,1024]{1,0:T(8,128)(2,1)S(1)}, u32[]{:S(2)}, u32[]{:S(2)}) collective-permute-start(bf16[32,1024]{1,0:T(8,128)(2,1)S(1)} %collective-permute-done.3.refs_1_), channel_id=1, source_target_pairs={{0,1},{1,0},{2,3},{3,2},{4,5},{5,4},{6,7},{7,6},{8,9},{9,8},{10,11... | collective-permute-start | bytes 196616 | tf_op jit(solution)/shard_map/ppermute | solution.py:568
  20.1 1.3 %collective-permute-start.8 = (bf16[32,1024]{1,0:T(8,128)(2,1)S(1)}, bf16[32,1024]{1,0:T(8,128)(2,1)S(1)}, u32[]{:S(2)}, u32[]{:S(2)}) collective-permute-start(bf16[32,1024]{1,0:T(8,128)(2,1)S(1)} %collective-permute-done.4.refs_2_), channel_id=1, source_target_pairs={{0,1},{1,0},{2,3},{3,2},{4,5},{5,4},{6,7},{7,6},{8,9},{9,8},{10,11... | collective-permute-start | bytes 196616 | tf_op jit(solution)/shard_map/ppermute | solution.py:568

commit v8 on v7

--- a/solution.py
+++ b/solution.py
@@ -162,10 +162,10 @@
     return total
 
 
-def local_kernel(levels, steps, slab_count, lines_ref, field_ref, after_ref, own_ref, coef_ref, held_ref, work):
+def local_kernel(levels, slab_count, lines_ref, field_ref, after_ref, own_ref, held_ref, work):
     pieces, cols, subs, lanes = work.shape
     own_cols = own_ref.shape[0]
-    tile, mem = lax.axis_index("tile"), lax.axis_index("mem")
+    mem = lax.axis_index("mem")
     share = (mem & (CORES - 1)) ^ 1
     for core in range(CORES):
         rows = share_rows(slab_count * cols, cols, subs, core)
@@ -174,12 +174,36 @@
         def _():
             held_ref[0 : rows.stop - rows.start, :] = field_ref[rows, :]
 
-    pair, decay, behind = lines_ref[0], lines_ref[1], lines_ref[2]
-    perm = transposer(cols)
+    pair, perm = lines_ref[0], transposer(cols)
     for piece in range(pieces):
         part = slice(piece * lanes, (piece + 1) * lanes)
         gain, _ = sweep_share(levels, slab_count, share, perm, pair[:, part], held_ref[:, part], work.at[piece])
         own_ref[:, :, part] = work[piece, pl.ds(mem * own_cols, own_cols)] * gain[None]
+
+
+def local_call(lines, flat_field, after, levels, cols, own_cols):
+    total, rows = flat_field.shape
+    subs = padded(total // cols) // CORES
+    vmem = pl.BlockSpec(memory_space=pltpu.VMEM)
+    return pl.pallas_call(
+        functools.partial(local_kernel, levels, total // cols),
+        name="local",
+        in_specs=[vmem, vmem, pl.BlockSpec(memory_space=pl.ANY)],
+        out_specs=vmem,
+        out_shape=jax.ShapeDtypeStruct((own_cols, subs, rows), F32),
+        scratch_shapes=[
+            pltpu.VMEM((subs * cols, rows), BF16),
+            pltpu.VMEM((rows // LANES, cols, subs, LANES), F32),
+        ],
+        compiler_params=pltpu.CompilerParams(vmem_limit_bytes=VMEM),
+        cost_estimate=taking(0.5),
+    )(lines, flat_field, after)
+
+
+def coefs_kernel(steps, lines_ref, after_ref, coef_ref):
+    cols = coef_ref.shape[1] - 3
+    tile = lax.axis_index("tile")
+    pair, decay, behind = lines_ref[0], lines_ref[1], lines_ref[2]
     square = pair * pair
     power, sums = jnp.ones_like(pair), jnp.zeros_like(pair)
     rights, geometric = [], []
@@ -205,26 +229,17 @@
         coef_ref[1, cols + flip - 1] = weight * jnp.where(upper, turned * from_left, from_right)
 
 
-def local_call(lines, flat_field, after, levels, steps, cols, own_cols):
-    total, rows = flat_field.shape
-    subs = padded(total // cols) // CORES
-    vmem = pl.BlockSpec(memory_space=pltpu.VMEM)
-    return pl.pallas_call(
-        functools.partial(local_kernel, levels, steps, total // cols),
-        name="local",
-        in_specs=[vmem, vmem, pl.BlockSpec(memory_space=pl.ANY)],
-        out_specs=[vmem, vmem],
-        out_shape=[
-            jax.ShapeDtypeStruct((own_cols, subs, rows), F32),
-            jax.ShapeDtypeStruct((2, cols + 3, 2, rows), F32),
-        ],
-        scratch_shapes=[
-            pltpu.VMEM((subs * cols, rows), BF16),
-            pltpu.VMEM((rows // LANES, cols, subs, LANES), F32),
-        ],
-        compiler_params=pltpu.CompilerParams(vmem_limit_bytes=VMEM),
-        cost_estimate=taking(0.5),
-    )(lines, flat_field, after)
+def coefs_call(lines, after, steps, cols):
+    vmem = pl.BlockSpec(memory_space=pltpu.VMEM)
+    return pl.pallas_call(
+        functools.partial(coefs_kernel, steps),
+        name="coefs",
+        in_specs=[vmem, pl.BlockSpec(memory_space=pl.ANY)],
+        out_specs=vmem,
+        out_shape=jax.ShapeDtypeStruct((2, cols + 3, *lines.shape[1:]), F32),
+        compiler_params=pltpu.CompilerParams(vmem_limit_bytes=VMEM),
+        cost_estimate=taking(4.0),
+    )(lines, after)
 
 
 def spread(matrix, levels, row_slab, row_col, col_slab, col_col):
@@ -238,62 +253,66 @@
     return jnp.where(row_col == col_col, full, 0.0).astype(BF16)
 
 
-def member_term(local, member_w, field_w, part):
-    member = member_w[part]
-    cols, slabs, rows = member.shape
-    scaled = (member * field_w[part].astype(F32)).astype(BF16).reshape(cols * slabs, rows)
-    return member * dot(local, scaled).reshape(cols, slabs, rows)
+def selection(block, shape, own_cols, cols):
+    (slot, out_slab), (in_slab, in_col) = split(iota(shape, 0), SUB), split(iota(shape, 1), cols)
+    return ((out_slab == in_slab) & (block * own_cols + slot == in_col)).astype(BF16)
+
+
+def member_term(local, member, field):
+    scaled = (member * field.astype(F32)).astype(BF16).reshape(local.shape[0], -1)
+    return member * dot(local, scaled).reshape(member.shape)
 
 
 def mine_kernel(
     levels, cols, loc_ref, field_ref, mine_ref, after_ref, perm_ref, local_ref, order_ref, field_out, total_out, member_w
 ):
-    own_cols = field_out.shape[0] // 2
-    slabs = field_out.shape[1]
+    own_cols, slabs, _ = field_out.shape
     chip, core = split(lax.axis_index("mem"), 2)
-    (slot, out_slab), (in_slab, in_col) = split(iota(perm_ref.shape, 0), SUB), split(iota(perm_ref.shape, 1), cols)
-    first = jnp.where(slot < own_cols, (2 * (1 - chip) + core) * own_cols, (2 * chip + core) * own_cols)
-    hit = (out_slab == in_slab) & (first + (slot & (own_cols - 1)) == in_col)
-    perm = hit.astype(BF16)
+    perm = selection(2 * (1 - chip) + core, perm_ref.shape, own_cols, cols)
     perm_ref[...] = perm
+    to_columns(perm, field_ref, field_out, cols)
+    to_columns(perm, mine_ref, member_w, cols)
     row, col = iota(local_ref.shape, 0), iota(local_ref.shape, 1)
     (row_col, row_slab), (col_col, col_slab) = split(row, slabs), split(col, slabs)
     local = spread(loc_ref[...], levels, row_slab, row_col, col_slab, col_col)
     local_ref[...] = local
     row_slab, row_col = split(row, own_cols)
     order_ref[...] = ((row_slab == col_slab) & (row_col == col_col)).astype(BF16)
-    to_columns(perm, field_ref, field_out, cols)
-    to_columns(perm, mine_ref, member_w, cols)
-    for part in (slice(0, own_cols), slice(own_cols, 2 * own_cols)):
-        total_out[part] = member_term(local, member_w, field_out, part)
-
-
-def other_kernel(half, cols, perm_ref, local_ref, order_ref, field_w, total_ref, other_ref, after_ref, out_ref, member_w):
-    own_cols, count = member_w.shape[0], out_ref.shape[0]
-    part = slice(half * own_cols, (half + 1) * own_cols)
-    to_columns(perm_ref[half * own_cols * SUB : (half + 1) * own_cols * SUB, :], other_ref, member_w, cols)
-    total = total_ref[part] + member_term(local_ref[...], member_w, field_w.at[part], slice(0, own_cols))
+    total_out[...] = member_term(local, member_w[...], field_out[...])
+
+
+def send_kernel(cols, perm_ref, local_ref, order_ref, field_w, total_ref, other_ref, send_ref, member_w):
+    to_columns(perm_ref[...], other_ref, member_w, cols)
+    total = total_ref[...] + member_term(local_ref[...], member_w[...], field_w[...])
+    total = total.reshape(order_ref.shape[0], -1).astype(BF16)
+    send_ref[...] = dot(order_ref[...], total)[: send_ref.shape[0]].astype(BF16)
+
+
+def keep_kernel(cols, local_ref, order_ref, field_ref, mine_ref, other_ref, after_ref, keep_ref, field_w, mine_w, other_w):
+    own_cols = field_w.shape[0]
+    perm = selection(lax.axis_index("mem"), (own_cols * SUB, cols * SUB), own_cols, cols)
+    for ref, out in ((field_ref, field_w), (mine_ref, mine_w), (other_ref, other_w)):
+        to_columns(perm, ref, out, cols)
+    field, local = field_w[...], local_ref[...]
+    total = member_term(local, mine_w[...], field) + member_term(local, other_w[...], field)
     total = total.reshape(order_ref.shape[0], -1)
     high = total.astype(BF16)
-    ordered = dot(order_ref[...], high)
-    if out_ref.dtype == F32:
-        ordered = ordered + dot(order_ref[...], (total - high.astype(F32)).astype(BF16))
-    out_ref[...] = ordered[:count].astype(out_ref.dtype)
-
-
-def ensemble_calls(loc, flat_field, mine, other, after, levels, cols, own_cols):
+    ordered = dot(order_ref[...], high) + dot(order_ref[...], (total - high.astype(F32)).astype(BF16))
+    keep_ref[...] = ordered[: keep_ref.shape[0]]
+
+
+def mine_call(loc, flat_field, mine, after, levels, cols, own_cols):
     total, rows = flat_field.shape
-    slab_count = total // cols
-    slabs, side = padded(slab_count), own_cols * padded(slab_count)
-    vmem = pl.BlockSpec(memory_space=pltpu.VMEM)
-    work = (2 * own_cols, slabs, rows)
-    held = pl.pallas_call(
+    slabs = padded(total // cols)
+    vmem = pl.BlockSpec(memory_space=pltpu.VMEM)
+    work, side = (own_cols, slabs, rows), own_cols * slabs
+    return pl.pallas_call(
         functools.partial(mine_kernel, levels, cols),
         name="mine",
         in_specs=[vmem] * 3 + [pl.BlockSpec(memory_space=pl.ANY)],
         out_specs=[vmem] * 5,
         out_shape=[
-            jax.ShapeDtypeStruct((2 * own_cols * SUB, cols * SUB), BF16),
+            jax.ShapeDtypeStruct((own_cols * SUB, cols * SUB), BF16),
             jax.ShapeDtypeStruct((side, side), BF16),
             jax.ShapeDtypeStruct((side, side), BF16),
             jax.ShapeDtypeStruct(work, BF16),
@@ -303,20 +322,36 @@
         compiler_params=pltpu.CompilerParams(vmem_limit_bytes=VMEM),
         cost_estimate=taking(1.8),
     )(loc, flat_field, mine, after)
-    after, outs = other, []
-    for half, dtype in enumerate((BF16, F32)):
-        after = pl.pallas_call(
-            functools.partial(other_kernel, half, cols),
-            name=("send", "keep")[half],
-            in_specs=[vmem] * 6 + [pl.BlockSpec(memory_space=pl.ANY)],
-            out_specs=vmem,
-            out_shape=jax.ShapeDtypeStruct((slab_count * own_cols, rows), dtype),
-            scratch_shapes=[pltpu.VMEM((own_cols, slabs, rows), F32)],
-            compiler_params=pltpu.CompilerParams(vmem_limit_bytes=VMEM),
-            cost_estimate=taking((0.8, 4.0)[half]),
-        )(*held, other, after)
-        outs.append(after)
-    return outs
+
+
+def send_call(held, other, cols):
+    own_cols, _, rows = held[3].shape
+    vmem = pl.BlockSpec(memory_space=pltpu.VMEM)
+    return pl.pallas_call(
+        functools.partial(send_kernel, cols),
+        name="send",
+        in_specs=[vmem] * 6,
+        out_specs=vmem,
+        out_shape=jax.ShapeDtypeStruct((other.shape[0] // cols * own_cols, rows), BF16),
+        scratch_shapes=[pltpu.VMEM(held[4].shape, F32)],
+        compiler_params=pltpu.CompilerParams(vmem_limit_bytes=VMEM),
+        cost_estimate=taking(0.8),
+    )(*held, other)
+
+
+def keep_call(held, flat_field, mine, other, after, cols):
+    own_cols, _, rows = held[3].shape
+    vmem = pl.BlockSpec(memory_space=pltpu.VMEM)
+    return pl.pallas_call(
+        functools.partial(keep_kernel, cols),
+        name="keep",
+        in_specs=[vmem] * 5 + [pl.BlockSpec(memory_space=pl.ANY)],
+        out_specs=vmem,
+        out_shape=jax.ShapeDtypeStruct((other.shape[0] // cols * own_cols, rows), F32),
+        scratch_shapes=[pltpu.VMEM(held[4].shape, F32)] * 3,
+        compiler_params=pltpu.CompilerParams(vmem_limit_bytes=VMEM),
+        cost_estimate=taking(0.6),
+    )(held[1], held[2], flat_field, mine, other, after)
 
 
 def tables_kernel(levels, own_cols, col_dev, slabs, table_ref, entries_ref, vert_ref, after_ref, mat_ref, coef_ref, vert_out):
@@ -357,9 +392,11 @@
         decay = jnp.exp(far * jnp.log(jnp.maximum(alpha, 1e-30)))
         reach = jnp.minimum(down[:, k : k + 1], across[k : k + 1])
         mat_ref[k] = (gain_of(alpha) * decay * reach).astype(BF16)
-    shape = vert_out.shape
-    (row_slab, row_col), (col_col, col_slab) = split(iota(shape, 0), own_cols), split(iota(shape, 1), slabs)
-    vert_out[...] = spread(vert_ref[...], levels, row_slab, row_col, col_slab, col_col)
+    shape = vert_out.shape[1:]
+    (row_slab, row_col), (col_col, col_slab) = split(iota(shape, 0), own_cols), split(iota(shape, 1), slabs // CORES)
+    for share in range(CORES):
+        first = share * (slabs // CORES)
+        vert_out[share] = spread(vert_ref[...], levels, row_slab, row_col, col_slab + first, col_col)
 
 
 def tables_call(table, entries, vert, after, levels, own_cols, col_dev, slabs):
@@ -372,7 +409,7 @@
         out_shape=[
             jax.ShapeDtypeStruct((count, BLOCK, BLOCK), BF16),
             jax.ShapeDtypeStruct((4, count, BLOCK), F32),
-            jax.ShapeDtypeStruct((own_cols * slabs, own_cols * slabs), BF16),
+            jax.ShapeDtypeStruct((CORES, own_cols * slabs, own_cols * slabs // CORES), BF16),
         ],
         compiler_params=pltpu.CompilerParams(vmem_limit_bytes=VMEM),
         cost_estimate=taking(0.4),
@@ -434,75 +471,88 @@
             out_ref[col, end, place] = jnp.where(is_level[:, place], piece[end], extra)
 
 
-def rows_kernel(levels, own_ref, coef_ref, mat_ref, row_coef_ref, part_ref, *refs):
+def mixed(vert, static):
+    high = static.astype(BF16)
+    return dot(vert, high) + dot(vert, (static - high.astype(F32)).astype(BF16))
+
+
+def rows_kernel(levels, scale, own_ref, coef_ref, mat_ref, row_coef_ref, part_ref, *refs):
+    *last_refs, vert_ref, keep_ref, base_ref, filt = refs
     share = lax.axis_index("mem") & (CORES - 1)
-    filter_share(levels, share, own_ref, coef_ref, mat_ref, row_coef_ref, part_ref, refs[:3], refs[3])
-
-
-def rows_call(levels, own, coef, mats, row_coef, shares):
-    vmem = pl.BlockSpec(memory_space=pltpu.VMEM)
-    args = [own, coef, mats, row_coef, *shares]
-    return pl.pallas_call(
-        functools.partial(rows_kernel, levels),
+    filter_share(levels, share, own_ref, coef_ref, mat_ref, row_coef_ref, part_ref, last_refs, filt)
+    total = mixed(vert_ref[share], filt[...].reshape(vert_ref.shape[2], -1))
+    base_ref[...] = total[: base_ref.shape[0]] + keep_ref[...] * scale
+
+
+def rows_call(levels, scale, own, coef, mats, row_coef, shares, vert, keep):
+    vmem = pl.BlockSpec(memory_space=pltpu.VMEM)
+    args = [own, coef, mats, row_coef, *shares, vert, keep]
+    return pl.pallas_call(
+        functools.partial(rows_kernel, levels, scale),
         name="rows",
         in_specs=[vmem] * len(args),
         out_specs=vmem,
-        out_shape=jax.ShapeDtypeStruct(own.shape, F32),
-        compiler_params=pltpu.CompilerParams(vmem_limit_bytes=VMEM),
-        cost_estimate=taking(0.9),
+        out_shape=jax.ShapeDtypeStruct(keep.shape, F32),
+        scratch_shapes=[pltpu.VMEM(own.shape, F32)],
+        compiler_params=pltpu.CompilerParams(vmem_limit_bytes=VMEM),
+        cost_estimate=taking(1.2),
     )(*args)
 
 
-def final_kernel(
-    levels, scale, done_ref, own_ref, coef_ref, mat_ref, row_coef_ref, part_ref, last_1_ref, last_2_ref, last_3_ref,
-    vert_ref, keep_ref, came_ref, out_hbm, filt, out_ref, sent
+def join_kernel(
+    levels, own_ref, coef_ref, mat_ref, row_coef_ref, part_ref, last_1_ref, last_2_ref, last_3_ref, vert_ref, base_ref,
+    total_ref, filt
 ):
-    own_cols, subs, rows = own_ref.shape
-    share = lax.axis_index("mem") & (CORES - 1)
-    filt[:, pl.ds(pl.multiple_of(share * subs, subs), subs), :] = done_ref[...]
-    other = 1 - share
-    place = pl.ds(pl.multiple_of(other * subs, subs), subs)
+    other = 1 - (lax.axis_index("mem") & (CORES - 1))
     last_refs = last_1_ref, last_2_ref, last_3_ref
-    filter_share(
-        levels, other, own_ref, coef_ref, mat_ref, row_coef_ref, part_ref, last_refs, filt.at[:, place, :]
-    )
-    count = out_ref.shape[0]
+    filter_share(levels, other, own_ref, coef_ref, mat_ref, row_coef_ref, part_ref, last_refs, filt)
+    total = mixed(vert_ref[other], filt[...].reshape(vert_ref.shape[2], -1))
+    total_ref[...] = total[: base_ref.shape[0]] + base_ref[...]
+
+
+def join_call(levels, own, coef, mats, row_coef, shares, vert, base):
+    vmem = pl.BlockSpec(memory_space=pltpu.VMEM)
+    args = [own, coef, mats, row_coef, *shares, vert, base]
+    return pl.pallas_call(
+        functools.partial(join_kernel, levels),
+        name="join",
+        in_specs=[vmem] * len(args),
+        out_specs=vmem,
+        out_shape=jax.ShapeDtypeStruct(base.shape, F32),
+        scratch_shapes=[pltpu.VMEM(own.shape, F32)],
+        compiler_params=pltpu.CompilerParams(vmem_limit_bytes=VMEM),
+        cost_estimate=taking(0.8),
+    )(*args)
+
+
+def final_kernel(scale, total_ref, came_ref, out_hbm, out_ref, sent):
+    count, own_cols, rows = out_ref.shape
     copies = []
-    for start in range(0, rows, BLOCK):
-        part = slice(start, start + BLOCK)
-        static = filt[:, :, part].reshape(vert_ref.shape[1], BLOCK)
-        high = static.astype(BF16)
-        low = (static - high.astype(F32)).astype(BF16)
-        total = dot(vert_ref[...], high) + dot(vert_ref[...], low)
-        ens = keep_ref[:, part] + came_ref[:, part].astype(F32)
-        total = total[: count * own_cols] + ens * scale
-        out_ref[:, :, part] = total.reshape(count, own_cols, BLOCK).astype(BF16)
-        copy = pltpu.make_async_copy(out_ref.at[:, :, part], out_hbm.at[:, :, part], sent.at[start // BLOCK])
-        copy.start()
-        copies.append(copy)
+    for piece, first in enumerate(range(0, count, SUB)):
+        place = slice(first, min(first + SUB, count))
+        wide = slice(place.start * own_cols, place.stop * own_cols)
+        total = total_ref[wide] + came_ref[wide].astype(F32) * scale
+        out_ref[place] = total.reshape(place.stop - place.start, own_cols, rows).astype(BF16)
+        copies.append(pltpu.make_async_copy(out_ref.at[place], out_hbm.at[place], sent.at[piece]))
+        copies[-1].start()
     for copy in copies:
         copy.wait()
 
 
-def final_call(slab_count, levels, scale, done, own, coef, mats, row_coef, shares, vert, keep, came):
-    own_cols, subs, rows = own.shape
-    vmem = pl.BlockSpec(memory_space=pltpu.VMEM)
-    args = [done, own, coef, mats, row_coef, *shares, vert, keep, came]
+def final_call(slab_count, own_cols, scale, total, came):
+    rows = total.shape[1]
+    vmem = pl.BlockSpec(memory_space=pltpu.VMEM)
     out_shape = (slab_count, own_cols, rows)
     return pl.pallas_call(
-        functools.partial(final_kernel, levels, scale),
+        functools.partial(final_kernel, scale),
         name="final",
-        in_specs=[vmem] * len(args),
+        in_specs=[vmem] * 2,
         out_specs=pl.BlockSpec(memory_space=pl.ANY),
         out_shape=jax.ShapeDtypeStruct(out_shape, BF16),
-        scratch_shapes=[
-            pltpu.VMEM((own_cols, CORES * subs, rows), F32),
-            pltpu.VMEM(out_shape, BF16),
-            pltpu.SemaphoreType.DMA((rows // BLOCK,)),
-        ],
-        compiler_params=pltpu.CompilerParams(vmem_limit_bytes=VMEM),
-        cost_estimate=taking(1.5),
-    )(*args)
+        scratch_shapes=[pltpu.VMEM(out_shape, BF16), pltpu.SemaphoreType.DMA((-(-slab_count // SUB),))],
+        compiler_params=pltpu.CompilerParams(vmem_limit_bytes=VMEM),
+        cost_estimate=taking(0.8),
+    )(total, came)
 
 
 def merge_kernel(levels, steps, step, last, after_count, *refs):
@@ -576,20 +626,24 @@
     share = (lax.axis_index("mem") & (CORES - 1)).astype(jnp.int32).reshape(1)
     ends, own_0, lines = ends_call(share, line_table, line_entries, flat_field, levels, steps, cols, own_cols)
     blocks, came = [ends], []
-    send, keep = ensemble_calls(loc_filter[0], full_field, mine, other, ends, levels, cols, own_cols)
+    held = mine_call(loc_filter[0], full_field, mine, ends, levels, cols, own_cols)
+    send = send_call(held, other, cols)
     over = swap(send, 2)
+    coef = coefs_call(lines, send, steps, cols)
     for level in range(steps - 2):
         came.append(swap(blocks[0], 1 << level, "tile"))
-        *blocks, keep = merge_call(lines, ends, came, [keep], levels, steps)
+        *blocks, coef = merge_call(lines, ends, came, [coef], levels, steps)
     near, far, part = blocks
     last = {flip: swap(near if flip == 1 else far, flip << (steps - 2), "tile") for flip in (2, 3, 1)}
-    own_1, coef = local_call(lines, full_field, near, levels, steps, cols, own_cols)
+    keep = keep_call(held, full_field, mine, other, near, cols)
+    own_1 = local_call(lines, full_field, near, levels, cols, own_cols)
     mats, row_coef, vert = tables_call(alpha_table, yscale_idx, vert_filter[0], own_1, levels, own_cols, cols, slabs)
     shares = [part, last[1], last[2], last[3]]
     others = [swap(share, 1) for share in shares]
-    done = rows_call(levels, own_0, coef, mats, row_coef, shares)
     scale = 1.0 / (mem_count * members.shape[0] - 1)
-    return final_call(slab_count, levels, scale, done, own_1, coef, mats, row_coef, others, vert, keep, over)
+    base = rows_call(levels, scale, own_0, coef, mats, row_coef, shares, vert, keep)
+    total = join_call(levels, own_1, coef, mats, row_coef, others, vert, base)
+    return final_call(slab_count, own_cols, scale, total, over)
 
 
 def solution(mesh):

time: 23.3 us -> 22.6 us (0.970)
  waiting for transfers between devices: 3.61 us -> 1.53 us
  Pallas kernels: 9.9 us -> 11.2 us
    ppermute x10, waiting for transfers between devices: 3.61 us -> 1.53 us  [swap(): lax.ppermute(array, axis, [(i, i ^ flip) for i in range(lax.axis_size(axi...]
    pallas_call x6 -> x8, Pallas kernels: 6.62 us -> 7.91 us  [the longest x1 1.91 us: keep_call(): pl.pallas_call(functools.partial(keep_kernel, cols), name='keep', in_spec...]
  transfers between devices with their start and end apart: 10 -> 10, of which waited for: 4 -> 3; matrix products, arithmetic and copies ran while one was open for 0% -> 0% of each run, Pallas kernels for 31% -> 41%
where the time goes in v8:
time: 22.6 us; the launch traced here: 22.5 us
  Pallas kernels  11.2 us (50%)
  starting transfers between devices  9.63 us (43%)
  waiting for transfers between devices  1.53 us (7%)
    ppermute x10, starting transfers between devices, swap(): lax.ppermute(array, axis, [(i, i ^ flip) for i in range(lax.axis_size(axi...  9.63 us
    pallas_call x1, Pallas kernels, ends_call(): pl.pallas_call(functools.partial(ends_kernel, levels, steps, total // col...  2.34 us
    pallas_call x1, Pallas kernels, keep_call(): pl.pallas_call(functools.partial(keep_kernel, cols), name='keep', in_spec...  1.91 us
    ppermute x10, waiting for transfers between devices, swap(): lax.ppermute(array, axis, [(i, i ^ flip) for i in range(lax.axis_size(axi...  1.53 us
    pallas_call x1, Pallas kernels, mine_call(): pl.pallas_call(functools.partial(mine_kernel, levels, cols), name='mine',...  1.27 us
    pallas_call x1, Pallas kernels, local_call(): pl.pallas_call(functools.partial(local_kernel, levels, total // cols), na...  0.98 us
    pallas_call x1, Pallas kernels, send_call(): pl.pallas_call(functools.partial(send_kernel, cols), name='send', in_spec...  0.94 us
    pallas_call x1, Pallas kernels, final_call(): pl.pallas_call(functools.partial(final_kernel, scale), name='final', in_s...  0.93 us
  transfers between devices with their start and end apart: 10, of which 3 were waited for; matrix products, arithmetic and copies ran while one was open for 0% of the time, Pallas kernels for 41%

profile of v8, /device:TPU:0, one launch (start us, length us, event | category | flops | bytes accessed | tf_op | source)
XLA Modules:
  0.0 22.5 jit_solution(995748204506045756)
XLA Ops:
  0.0 0.5 %collective-permute-start.1 = (bf16[976,1024]{1,0:T(8,128)(2,1)}, bf16[976,1024]{1,0:T(8,128)(2,1)S(1)}, u32[]{:S(2)}, u32[]{:S(2)}) collective-permute-start(bf16[976,1024]{1,0:T(8,128)(2,1)} %bitcast.10), channel_id=1, source_target_pairs={{0,1},{1,0},{2,3},{3,2},{4,5},{5,4},{6,7},{7,6},{8,9},{9,8},{10,11... | collective-permute-start | bytes 5996552 | tf_op jit(solution)/shard_map/ppermute | solution.py:618
  0.5 0.0 copy-start
  0.5 0.0 copy-start.1
  0.5 0.0 copy-start.2
  0.5 2.3 %ends.1 = (bf16[2,32,1024]{2,1,0:T(8,128)(2,1)S(1)}, f32[4,32,1024]{2,1,0:T(8,128)S(1)}, f32[3,2,1024]{2,1,0:T(2,128)S(1)}) custom-call(s32[1]{0:T(128)} %bitcast.share_ref, f32[16]{0:T(128)} %table_ref.1, s32[2,1024]{1,0:T(2,128)} %entries_ref.2, bf16[976,1024]{1,0:T(8,128)(2,1)} %bitcast.6), custom_call_target="tpu_custom_call" | custom-call | flops 2415000064 | bytes 262144 | tf_op jit(solution)/shard_map/ends/pallas_call | solution.py:120
  2.8 2.6 %collective-permute-start = (bf16[2,32,1024]{2,1,0:T(8,128)(2,1)S(1)}, bf16[2,32,1024]{2,1,0:T(8,128)(2,1)S(1)}, u32[]{:S(2)}, u32[]{:S(2)}) collective-permute-start(bf16[2,32,1024]{2,1,0:T(8,128)(2,1)S(1)} %get-tuple-element.21.after_ref.refs_1_), channel_id=1, source_target_pairs={{0,4},{4,0},{8,12},{12,8},{16,20},{20,16},{24,28},{28,24},{1,5},{5... | collective-permute-start | bytes 393224 | tf_op jit(solution)/shard_map/ppermute | solution.py:618
  5.4 0.0 copy-done
  5.4 0.0 copy-done.1
  5.4 0.0 copy-done.2
  5.4 1.3 %mine.1 = (bf16[64,256]{1,0:T(8,128)(2,1)S(1)}, bf16[256,256]{1,0:T(8,128)(2,1)S(1)}, bf16[256,256]{1,0:T(8,128)(2,1)S(1)}, bf16[4,64,1024]{2,1,0:T(8,128)(2,1)S(1)}, f32[4,64,1024]{2,1,0:T(8,128)S(1)}) custom-call(bf16[60,60]{1,0:T(8,128)(2,1)S(1)} %bitcast.13, bf16[976,1024]{1,0:T(8,128)(2,1)S(1)} %bitcast.7, bf16[976,1024]{1,0:T(8,128)(2,1)S(1)} %bitcast.11, ...), custom_call_target="tpu_custom_call" | custom-call | flops 2070000000 | bytes 262144 | tf_op jit(solution)/shard_map/mine/pallas_call | solution.py:309
  6.7 0.0 collective-permute-done.1.other_ref
  6.7 0.9 %send.1.after_ref = bf16[244,1024]{1,0:T(8,128)(2,1)S(1)} custom-call(bf16[64,256]{1,0:T(8,128)(2,1)S(1)} %get-tuple-element.22.perm_ref, bf16[256,256]{1,0:T(8,128)(2,1)S(1)} %get-tuple-element.23.local_ref, bf16[256,256]{1,0:T(8,128)(2,1)S(1)} %get-tuple-element.24.order_ref, bf16[4,64,1024]{2,1,0:T(8,128)(2,1)S(1)} %get-tuple-element.25.field_w, ...), custom_call_target="tpu_custom_call" | custom-call | flops 920000000 | bytes 262144 | tf_op jit(solution)/shard_map/send/pallas_call | solution.py:330
  7.7 1.5 %collective-permute-start.9 = (bf16[244,1024]{1,0:T(8,128)(2,1)S(1)}, bf16[244,1024]{1,0:T(8,128)(2,1)S(1)}, u32[]{:S(2)}, u32[]{:S(2)}) collective-permute-start(bf16[244,1024]{1,0:T(8,128)(2,1)S(1)} %send.1.after_ref), channel_id=1, source_target_pairs={{0,2},{1,3},{2,0},{3,1},{4,6},{5,7},{6,4},{7,5},{8,10},{9,11},{10,... | collective-permute-start | bytes 1499144 | tf_op jit(solution)/shard_map/ppermute | solution.py:618
  9.2 0.3 %collective-permute-done.refs_2_ = bf16[2,32,1024]{2,1,0:T(8,128)(2,1)S(1)} collective-permute-done((bf16[2,32,1024]{2,1,0:T(8,128)(2,1)S(1)}, bf16[2,32,1024]{2,1,0:T(8,128)(2,1)S(1)}, u32[]{:S(2)}, u32[]{:S(2)}) %collective-permute-start) | collective-permute-done | bytes 131104 | tf_op jit(solution)/shard_map/ppermute | solution.py:618
  9.5 0.1 merge.1
  9.7 2.9 %collective-permute-start.5 = (bf16[32,1024]{1,0:T(8,128)(2,1)S(1)}, bf16[32,1024]{1,0:T(8,128)(2,1)S(1)}, u32[]{:S(2)}, u32[]{:S(2)}) collective-permute-start(bf16[32,1024]{1,0:T(8,128)(2,1)S(1)} %get-tuple-element.32), channel_id=1, source_target_pairs={{0,16},{4,20},{8,24},{12,28},{16,0},{20,4},{24,8},{28,12},{1,17},{... | collective-permute-start | bytes 196616 | tf_op jit(solution)/shard_map/ppermute | solution.py:618
  12.5 1.3 %collective-permute-start.7 = (bf16[32,1024]{1,0:T(8,128)(2,1)S(1)}, bf16[32,1024]{1,0:T(8,128)(2,1)S(1)}, u32[]{:S(2)}, u32[]{:S(2)}) collective-permute-start(bf16[32,1024]{1,0:T(8,128)(2,1)S(1)} %get-tuple-element.32), channel_id=1, source_target_pairs={{0,24},{4,28},{8,16},{12,20},{16,8},{20,12},{24,0},{28,4},{1,25},{... | collective-permute-start | bytes 196616 | tf_op jit(solution)/shard_map/ppermute | solution.py:618
  13.9 0.2 %collective-permute-start.3 = (bf16[32,1024]{1,0:T(8,128)(2,1)S(1)}, bf16[32,1024]{1,0:T(8,128)(2,1)S(1)}, u32[]{:S(2)}, u32[]{:S(2)}) collective-permute-start(bf16[32,1024]{1,0:T(8,128)(2,1)S(1)} %get-tuple-element.27.after_ref), channel_id=1, source_target_pairs={{0,8},{4,12},{8,0},{12,4},{16,24},{20,28},{24,16},{28,20},{1,9},{5... | collective-permute-start | bytes 196616 | tf_op jit(solution)/shard_map/ppermute | solution.py:618
  14.1 0.0 collective-permute-start.2
  14.1 1.9 %keep.1.refs_4_ = f32[244,1024]{1,0:T(8,128)S(1)} custom-call(bf16[256,256]{1,0:T(8,128)(2,1)S(1)} %get-tuple-element.23.local_ref, bf16[256,256]{1,0:T(8,128)(2,1)S(1)} %get-tuple-element.24.order_ref, bf16[976,1024]{1,0:T(8,128)(2,1)S(1)} %bitcast.8, bf16[976,1024]{1,0:T(8,128)(2,1)S(1)} %bitcast.12, ...), custom_call_target="tpu_custom_call" | custom-call | flops 690000000 | bytes 262144 | tf_op jit(solution)/shard_map/keep/pallas_call | solution.py:345
  16.0 0.0 copy-start.3
  16.0 0.0 copy-start.4
  16.1 0.0 copy-start.5
  16.1 1.0 %local.1.after_ref.own_ref = f32[4,32,1024]{2,1,0:T(8,128)S(1)} custom-call(f32[3,2,1024]{2,1,0:T(2,128)S(1)} %get-tuple-element.20.lines_ref.refs_0_, bf16[976,1024]{1,0:T(8,128)(2,1)S(1)} %bitcast.9, bf16[32,1024]{1,0:T(8,128)(2,1)S(1)} %get-tuple-element.27.after_ref), custom_call_target="tpu_custom_call" | custom-call | flops 575000000 | bytes 262144 | tf_op jit(solution)/shard_map/local/pallas_call | solution.py:188
  17.0 0.0 copy-done.3
  17.1 0.0 copy-done.4
  17.1 0.0 copy-done.5
  17.1 0.8 %tables.1 = (bf16[8,256,256]{2,1,0:T(8,128)(2,1)S(1)}, f32[4,8,256]{2,1,0:T(8,128)S(1)}, bf16[2,256,128]{2,1,0:T(8,128)(2,1)S(1)}) custom-call(f32[1,16]{1,0:T(1,128)S(1)} %bitcast.15, s32[2,128]{1,0:T(2,128)S(1)} %copy-done.4, bf16[60,60]{1,0:T(8,128)(2,1)S(1)} %bitcast.14, f32[4,32,1024]{2,1,0:T(8,128)S(1)} %local.1.after_ref.own_ref), custom_call_target="tpu_custom_call" | custom-call | flops 460000000 | bytes 262144 | tf_op jit(solution)/shard_map/tables/pallas_call | solution.py:404
  17.9 1.0 %collective-permute-done.3.refs_0_ = bf16[32,1024]{1,0:T(8,128)(2,1)S(1)} collective-permute-done((bf16[32,1024]{1,0:T(8,128)(2,1)S(1)}, bf16[32,1024]{1,0:T(8,128)(2,1)S(1)}, u32[]{:S(2)}, u32[]{:S(2)}) %collective-permute-start.3) | collective-permute-done | bytes 65568 | tf_op jit(solution)/shard_map/ppermute | solution.py:618
  18.8 0.0 collective-permute-start.4
  18.9 0.0 collective-permute-done.5.refs_1_
  18.9 0.5 %collective-permute-start.6 = (bf16[32,1024]{1,0:T(8,128)(2,1)S(1)}, bf16[32,1024]{1,0:T(8,128)(2,1)S(1)}, u32[]{:S(2)}, u32[]{:S(2)}) collective-permute-start(bf16[32,1024]{1,0:T(8,128)(2,1)S(1)} %collective-permute-done.5.refs_1_), channel_id=1, source_target_pairs={{0,1},{1,0},{2,3},{3,2},{4,5},{5,4},{6,7},{7,6},{8,9},{9,8},{10,11... | collective-permute-start | bytes 196616 | tf_op jit(solution)/shard_map/ppermute | solution.py:618
  19.4 0.0 collective-permute-done.7.refs_2_
  19.4 0.1 collective-permute-start.8
  19.4 0.9 %rows.1.base_ref = f32[244,1024]{1,0:T(8,128)S(1)} custom-call(f32[4,32,1024]{2,1,0:T(8,128)S(1)} %get-tuple-element.34.own_ref, f32[2,19,2,1024]{3,2,1,0:T(2,128)S(1)} %get-tuple-element.28.coef_ref, bf16[8,256,256]{2,1,0:T(8,128)(2,1)S(1)} %get-tuple-element.29.mat_ref, f32[4,8,256]{2,1,0:T(8,128)S(1)} %get-tuple-element.30.row_coef_ref, ...), custom_call_target="tpu_custom_call" | custom-call | flops 1380000000 | bytes 262144 | tf_op jit(solution)/shard_map/rows/pallas_call | solution.py:490
  20.4 0.0 collective-permute-done.4.last_1_ref
  20.4 0.0 collective-permute-done.6.last_2_ref
  20.4 0.2 %collective-permute-done.8.last_3_ref = bf16[32,1024]{1,0:T(8,128)(2,1)S(1)} collective-permute-done((bf16[32,1024]{1,0:T(8,128)(2,1)S(1)}, bf16[32,1024]{1,0:T(8,128)(2,1)S(1)}, u32[]{:S(2)}, u32[]{:S(2)}) %collective-permute-start.8) | collective-permute-done | bytes 65568 | tf_op jit(solution)/shard_map/ppermute | solution.py:618
  20.6 0.0 collective-permute-done.2.part_ref
  20.6 0.9 %join.1.total_ref = f32[244,1024]{1,0:T(8,128)S(1)} custom-call(f32[4,32,1024]{2,1,0:T(8,128)S(1)} %local.1.after_ref.own_ref, f32[2,19,2,1024]{3,2,1,0:T(2,128)S(1)} %get-tuple-element.28.coef_ref, bf16[8,256,256]{2,1,0:T(8,128)(2,1)S(1)} %get-tuple-element.29.mat_ref, f32[4,8,256]{2,1,0:T(8,128)S(1)} %get-tuple-element.30.row_coef_ref, ...), custom_call_target="tpu_custom_call" | custom-call | flops 920000000 | bytes 262144 | tf_op jit(solution)/shard_map/join/pallas_call | solution.py:516
  21.6 0.0 collective-permute-done.9.came_ref
  21.6 0.9 %final.1 = bf16[61,4,1024]{2,1,0:T(4,128)(2,1)} custom-call(f32[244,1024]{1,0:T(8,128)S(1)} %join.1.total_ref, bf16[244,1024]{1,0:T(8,128)(2,1)S(1)} %collective-permute-done.9.came_ref), custom_call_target="tpu_custom_call" | custom-call | flops 920000000 | bytes 262144 | tf_op jit(solution)/shard_map/final/pallas_call | solution.py:546
  (1 shorter events, 0.0 us)
Async XLA Ops:
  0.0 6.7 %collective-permute-start.1 = (bf16[976,1024]{1,0:T(8,128)(2,1)}, bf16[976,1024]{1,0:T(8,128)(2,1)S(1)}, u32[]{:S(2)}, u32[]{:S(2)}) collective-permute-start(bf16[976,1024]{1,0:T(8,128)(2,1)} %bitcast.10), channel_id=1, source_target_pairs={{0,1},{1,0},{2,3},{3,2},{4,5},{5,4},{6,7},{7,6},{8,9},{9,8},{10,11... | collective-permute-start | bytes 5996552 | tf_op jit(solution)/shard_map/ppermute | solution.py:618
  0.5 5.0 %copy-start = (bf16[61,16,1024]{2,1,0:T(8,128)(2,1)S(1)}, bf16[61,16,1024]{2,1,0:T(8,128)(2,1)}, u32[]{:S(2)}) copy-start(bf16[61,16,1024]{2,1,0:T(8,128)(2,1)} %param.7) | copy-start | bytes 5996548
  0.5 5.0 %copy-start.1 = (bf16[1,61,16,1024]{3,2,1,0:T(8,128)(2,1)S(1)}, bf16[1,61,16,1024]{3,2,1,0:T(8,128)(2,1)}, u32[]{:S(2)}) copy-start(bf16[1,61,16,1024]{3,2,1,0:T(8,128)(2,1)} %param.13) | copy-start | bytes 5996548
  0.5 5.0 %copy-start.2 = (bf16[1,60,60]{2,1,0:T(8,128)(2,1)S(1)}, bf16[1,60,60]{2,1,0:T(8,128)(2,1)}, u32[]{:S(2)}) copy-start(bf16[1,60,60]{2,1,0:T(8,128)(2,1)} %param.9) | copy-start | bytes 21604
  2.8 6.7 %collective-permute-start = (bf16[2,32,1024]{2,1,0:T(8,128)(2,1)S(1)}, bf16[2,32,1024]{2,1,0:T(8,128)(2,1)S(1)}, u32[]{:S(2)}, u32[]{:S(2)}) collective-permute-start(bf16[2,32,1024]{2,1,0:T(8,128)(2,1)S(1)} %get-tuple-element.21.after_ref.refs_1_), channel_id=1, source_target_pairs={{0,4},{4,0},{8,12},{12,8},{16,20},{20,16},{24,28},{28,24},{1,5},{5... | collective-permute-start | bytes 393224 | tf_op jit(solution)/shard_map/ppermute | solution.py:618
  7.7 13.9 %collective-permute-start.9 = (bf16[244,1024]{1,0:T(8,128)(2,1)S(1)}, bf16[244,1024]{1,0:T(8,128)(2,1)S(1)}, u32[]{:S(2)}, u32[]{:S(2)}) collective-permute-start(bf16[244,1024]{1,0:T(8,128)(2,1)S(1)} %send.1.after_ref), channel_id=1, source_target_pairs={{0,2},{1,3},{2,0},{3,1},{4,6},{5,7},{6,4},{7,5},{8,10},{9,11},{10,... | collective-permute-start | bytes 1499144 | tf_op jit(solution)/shard_map/ppermute | solution.py:618
  9.7 9.2 %collective-permute-start.5 = (bf16[32,1024]{1,0:T(8,128)(2,1)S(1)}, bf16[32,1024]{1,0:T(8,128)(2,1)S(1)}, u32[]{:S(2)}, u32[]{:S(2)}) collective-permute-start(bf16[32,1024]{1,0:T(8,128)(2,1)S(1)} %get-tuple-element.32), channel_id=1, source_target_pairs={{0,16},{4,20},{8,24},{12,28},{16,0},{20,4},{24,8},{28,12},{1,17},{... | collective-permute-start | bytes 196616 | tf_op jit(solution)/shard_map/ppermute | solution.py:618
  12.5 6.8 %collective-permute-start.7 = (bf16[32,1024]{1,0:T(8,128)(2,1)S(1)}, bf16[32,1024]{1,0:T(8,128)(2,1)S(1)}, u32[]{:S(2)}, u32[]{:S(2)}) collective-permute-start(bf16[32,1024]{1,0:T(8,128)(2,1)S(1)} %get-tuple-element.32), channel_id=1, source_target_pairs={{0,24},{4,28},{8,16},{12,20},{16,8},{20,12},{24,0},{28,4},{1,25},{... | collective-permute-start | bytes 196616 | tf_op jit(solution)/shard_map/ppermute | solution.py:618
  13.9 5.0 %collective-permute-start.3 = (bf16[32,1024]{1,0:T(8,128)(2,1)S(1)}, bf16[32,1024]{1,0:T(8,128)(2,1)S(1)}, u32[]{:S(2)}, u32[]{:S(2)}) collective-permute-start(bf16[32,1024]{1,0:T(8,128)(2,1)S(1)} %get-tuple-element.27.after_ref), channel_id=1, source_target_pairs={{0,8},{4,12},{8,0},{12,4},{16,24},{20,28},{24,16},{28,20},{1,9},{5... | collective-permute-start | bytes 196616 | tf_op jit(solution)/shard_map/ppermute | solution.py:618
  14.1 6.5 %collective-permute-start.2 = (bf16[2,32,1024]{2,1,0:T(8,128)(2,1)S(1)}, bf16[2,32,1024]{2,1,0:T(8,128)(2,1)S(1)}, u32[]{:S(2)}, u32[]{:S(2)}) collective-permute-start(bf16[2,32,1024]{2,1,0:T(8,128)(2,1)S(1)} %get-tuple-element.31.part_ref), channel_id=1, source_target_pairs={{0,1},{1,0},{2,3},{3,2},{4,5},{5,4},{6,7},{7,6},{8,9},{9,8},{10,11... | collective-permute-start | bytes 393224 | tf_op jit(solution)/shard_map/ppermute | solution.py:618
  16.0 1.0 %copy-start.3 = (bf16[1,60,60]{2,1,0:T(8,128)(2,1)S(1)}, bf16[1,60,60]{2,1,0:T(8,128)(2,1)}, u32[]{:S(2)}) copy-start(bf16[1,60,60]{2,1,0:T(8,128)(2,1)} %param.8) | copy-start | bytes 21604
  16.0 1.0 %copy-start.4 = (s32[2,128]{1,0:T(2,128)S(1)}, s32[2,128]{1,0:T(2,128)}, u32[]{:S(2)}) copy-start(s32[2,128]{1,0:T(2,128)} %entries_ref.3) | copy-start | bytes 3076
  16.1 1.0 %copy-start.5 = (f32[16]{0:T(128)S(1)}, f32[16]{0:T(128)}, u32[]{:S(2)}) copy-start(f32[16]{0:T(128)} %table_ref.1) | copy-start | bytes 196
  18.8 1.5 %collective-permute-start.4 = (bf16[32,1024]{1,0:T(8,128)(2,1)S(1)}, bf16[32,1024]{1,0:T(8,128)(2,1)S(1)}, u32[]{:S(2)}, u32[]{:S(2)}) collective-permute-start(bf16[32,1024]{1,0:T(8,128)(2,1)S(1)} %collective-permute-done.3.refs_0_), channel_id=1, source_target_pairs={{0,1},{1,0},{2,3},{3,2},{4,5},{5,4},{6,7},{7,6},{8,9},{9,8},{10,11... | collective-permute-start | bytes 196616 | tf_op jit(solution)/shard_map/ppermute | solution.py:618
  18.9 1.5 %collective-permute-start.6 = (bf16[32,1024]{1,0:T(8,128)(2,1)S(1)}, bf16[32,1024]{1,0:T(8,128)(2,1)S(1)}, u32[]{:S(2)}, u32[]{:S(2)}) collective-permute-start(bf16[32,1024]{1,0:T(8,128)(2,1)S(1)} %collective-permute-done.5.refs_1_), channel_id=1, source_target_pairs={{0,1},{1,0},{2,3},{3,2},{4,5},{5,4},{6,7},{7,6},{8,9},{9,8},{10,11... | collective-permute-start | bytes 196616 | tf_op jit(solution)/shard_map/ppermute | solution.py:618
  19.4 1.3 %collective-permute-start.8 = (bf16[32,1024]{1,0:T(8,128)(2,1)S(1)}, bf16[32,1024]{1,0:T(8,128)(2,1)S(1)}, u32[]{:S(2)}, u32[]{:S(2)}) collective-permute-start(bf16[32,1024]{1,0:T(8,128)(2,1)S(1)} %collective-permute-done.7.refs_2_), channel_id=1, source_target_pairs={{0,1},{1,0},{2,3},{3,2},{4,5},{5,4},{6,7},{7,6},{8,9},{9,8},{10,11... | collective-permute-start | bytes 196616 | tf_op jit(solution)/shard_map/ppermute | solution.py:618

commit v9 on v8

--- a/solution.py
+++ b/solution.py
@@ -11,6 +11,8 @@
 SUB = 16
 CORES = 2
 LANES = 256
+ORDER = (2, 3, 1)
+FETCHES = 1
 BLOCK = 256
 MIB = 1 << 20
 VMEM = 32 * MIB
@@ -80,31 +82,77 @@
     return slice(share * subs * cols, min((share + 1) * subs * cols, total))
 
 
-def sweep_share(levels, slab_count, share, perm, alpha, held, work):
+def clear_rest(held_ref, rows):
+    first = rows.stop - rows.start
+    if first < held_ref.shape[0]:
+        held_ref[first:, :] = jnp.zeros((held_ref.shape[0] - first, held_ref.shape[1]), BF16)
+
+
+def sweep_share(levels, share, perm, alpha, held, work):
     cols, subs, lanes = work.shape
-    first = share * subs
-    held = jnp.where(iota(held.shape, 0) < (slab_count - first) * cols, held, 0)
     to_columns(perm, held, work, cols)
-    is_level = iota((subs, lanes), 0) + first < levels
+    is_level = iota((subs, lanes), 0) + share * subs < levels
     alpha = jnp.where(is_level, alpha[0:1], alpha[1:2])
     sweep(work, alpha)
     return gain_of(alpha), is_level
 
 
 def ends_kernel(
-    levels, steps, slab_count, share_ref, table_ref, entries_ref, field_ref, ends_ref, own_ref, lines_ref, work
+    levels, steps, slab_count, table_hbm, entries_hbm, loc_hbm, field_hbm, ends_ref, own_ref, lines_ref, perm_ref,
+    local_ref, order_ref, table_ref, entries_ref, loc_ref, held_ref, work, small, arrived
 ):
     pieces, cols, subs, lanes = work.shape
     own_cols = own_ref.shape[0]
+    slabs, rows = CORES * subs, held_ref.shape[1]
     tile, mem = lax.axis_index("tile"), lax.axis_index("mem")
-    share, perm = share_ref[0], transposer(cols)
+    chip, share = split(mem, CORES)
+    parts = arrived.shape[0]
+
+    def fetch(part, begin):
+        width = rows // parts
+        place = pl.ds(part * width, width)
+        for core in range(CORES):
+            held = share_rows(slab_count * cols, cols, subs, core)
+
+            @pl.when(share == core)
+            def _():
+                copy = pltpu.make_async_copy(
+                    field_hbm.at[held, place], held_ref.at[0 : held.stop - held.start, place], arrived.at[part]
+                )
+                if begin:
+                    copy.start()
+                    clear_rest(held_ref, held)
+                else:
+                    copy.wait()
+
+    for part in range(parts):
+        fetch(part, True)
+    given = [
+        pltpu.make_async_copy(source, target, small.at[k])
+        for k, (source, target) in enumerate(
+            ((table_hbm, table_ref), (entries_hbm, entries_ref), (loc_hbm, loc_ref))
+        )
+    ]
+    for copy in given:
+        copy.start()
+    perm_ref[...] = selection(2 * (1 - chip) + share, perm_ref.shape, own_cols, cols)
+    row, col = iota(local_ref.shape, 0), iota(local_ref.shape, 1)
+    (row_col, row_slab), (col_col, col_slab) = split(row, slabs), split(col, slabs)
+    order_slab, order_col = split(row, own_cols)
+    order_ref[...] = ((order_slab == col_slab) & (order_col == col_col)).astype(BF16)
+    perm = transposer(cols)
+    for copy in given:
+        copy.wait()
+    local_ref[...] = spread(loc_ref[...], levels, row_slab, row_col, col_slab, col_col)
     pair = lookup(table_ref, entries_ref[...])
     decay, turn = line_coefs(pair, cols)
     behind = reflected(decay, turn, tile, steps)
     lines_ref[0], lines_ref[1], lines_ref[2] = pair, decay, behind
     for piece in range(pieces):
+        if piece % (pieces // parts) == 0:
+            fetch(piece // (pieces // parts), False)
         part = slice(piece * lanes, (piece + 1) * lanes)
-        gain, is_level = sweep_share(levels, slab_count, share, perm, pair[:, part], field_ref[:, part], work.at[piece])
+        gain, is_level = sweep_share(levels, share, perm, pair[:, part], held_ref[:, part], work.at[piece])
         turned = (decay * behind)[:, part]
         turned = jnp.where(is_level, turned[0:1], turned[1:2])
         forward = gain * work[piece, cols - 1]
@@ -113,32 +161,36 @@
         own_ref[:, :, part] = work[piece, pl.ds(mem * own_cols, own_cols)] * gain[None]
 
 
-def ends_call(share, table, entries, flat_field, levels, steps, cols, own_cols):
+def ends_call(table, entries, loc, flat_field, levels, steps, cols, own_cols):
     total, rows = flat_field.shape
     subs = padded(total // cols) // CORES
-    vmem, smem = pl.BlockSpec(memory_space=pltpu.VMEM), pl.BlockSpec(memory_space=pltpu.SMEM)
+    side = own_cols * CORES * subs
+    vmem = pl.BlockSpec(memory_space=pltpu.VMEM)
     return pl.pallas_call(
         functools.partial(ends_kernel, levels, steps, total // cols),
         name="ends",
-        grid_spec=pltpu.PrefetchScalarGridSpec(
-            num_scalar_prefetch=1,
-            grid=(1,),
-            in_specs=[
-                smem,
-                pl.BlockSpec(entries.shape, lambda i, share: (0, 0)),
-                pl.BlockSpec((subs * cols, rows), lambda i, share: (share[0], 0)),
-            ],
-            out_specs=[vmem] * 3,
-            scratch_shapes=[pltpu.VMEM((rows // LANES, cols, subs, LANES), F32)],
-        ),
+        in_specs=[pl.BlockSpec(memory_space=pl.ANY)] * 4,
+        out_specs=[vmem] * 6,
         out_shape=[
             jax.ShapeDtypeStruct((2, subs, rows), BF16),
             jax.ShapeDtypeStruct((own_cols, subs, rows), F32),
             jax.ShapeDtypeStruct((3, 2, rows), F32),
+            jax.ShapeDtypeStruct((own_cols * SUB, cols * SUB), BF16),
+            jax.ShapeDtypeStruct((side, side), BF16),
+            jax.ShapeDtypeStruct((side, side), BF16),
         ],
+        scratch_shapes=[
+            pltpu.SMEM(table.shape, F32),
+            pltpu.VMEM(entries.shape, jnp.int32),
+            pltpu.VMEM(loc.shape, BF16),
+            pltpu.VMEM((subs * cols, rows), BF16),
+            pltpu.VMEM((rows // LANES, cols, subs, LANES), F32),
+            pltpu.SemaphoreType.DMA((3,)),
+            pltpu.SemaphoreType.DMA((FETCHES,)),
+        ],
         compiler_params=pltpu.CompilerParams(vmem_limit_bytes=VMEM),
         cost_estimate=taking(2.1),
-    )(share, table, entries, flat_field)
+    )(table, entries, loc, flat_field)
 
 
 def line_coefs(pair, cols):
@@ -173,11 +225,12 @@
         @pl.when(share == core)
         def _():
             held_ref[0 : rows.stop - rows.start, :] = field_ref[rows, :]
+            clear_rest(held_ref, rows)
 
     pair, perm = lines_ref[0], transposer(cols)
     for piece in range(pieces):
         part = slice(piece * lanes, (piece + 1) * lanes)
-        gain, _ = sweep_share(levels, slab_count, share, perm, pair[:, part], held_ref[:, part], work.at[piece])
+        gain, _ = sweep_share(levels, share, perm, pair[:, part], held_ref[:, part], work.at[piece])
         own_ref[:, :, part] = work[piece, pl.ds(mem * own_cols, own_cols)] * gain[None]
 
 
@@ -225,8 +278,8 @@
     outer = (quarter == 0) | (quarter == 3)
     for flip, weight in ((1, 1.0), (2, decay), (3, jnp.where(outer, decay * decay, 1.0))):
         upper = (quarter ^ flip) < quarter
-        coef_ref[0, cols + flip - 1] = jnp.where(upper, from_left * weight, 0.0)
-        coef_ref[1, cols + flip - 1] = weight * jnp.where(upper, turned * from_left, from_right)
+        coef_ref[0, cols + ORDER.index(flip)] = jnp.where(upper, from_left * weight, 0.0)
+        coef_ref[1, cols + ORDER.index(flip)] = weight * jnp.where(upper, turned * from_left, from_right)
 
 
 def coefs_call(lines, after, steps, cols):
@@ -263,22 +316,10 @@
     return member * dot(local, scaled).reshape(member.shape)
 
 
-def mine_kernel(
-    levels, cols, loc_ref, field_ref, mine_ref, after_ref, perm_ref, local_ref, order_ref, field_out, total_out, member_w
-):
-    own_cols, slabs, _ = field_out.shape
-    chip, core = split(lax.axis_index("mem"), 2)
-    perm = selection(2 * (1 - chip) + core, perm_ref.shape, own_cols, cols)
-    perm_ref[...] = perm
-    to_columns(perm, field_ref, field_out, cols)
-    to_columns(perm, mine_ref, member_w, cols)
-    row, col = iota(local_ref.shape, 0), iota(local_ref.shape, 1)
-    (row_col, row_slab), (col_col, col_slab) = split(row, slabs), split(col, slabs)
-    local = spread(loc_ref[...], levels, row_slab, row_col, col_slab, col_col)
-    local_ref[...] = local
-    row_slab, row_col = split(row, own_cols)
-    order_ref[...] = ((row_slab == col_slab) & (row_col == col_col)).astype(BF16)
-    total_out[...] = member_term(local, member_w[...], field_out[...])
+def mine_kernel(cols, perm_ref, local_ref, field_ref, mine_ref, after_ref, field_out, total_out, member_w):
+    to_columns(perm_ref[...], field_ref, field_out, cols)
+    to_columns(perm_ref[...], mine_ref, member_w, cols)
+    total_out[...] = member_term(local_ref[...], member_w[...], field_out[...])
 
 
 def send_kernel(cols, perm_ref, local_ref, order_ref, field_w, total_ref, other_ref, send_ref, member_w):
@@ -301,27 +342,20 @@
     keep_ref[...] = ordered[: keep_ref.shape[0]]
 
 
-def mine_call(loc, flat_field, mine, after, levels, cols, own_cols):
+def mine_call(perm, local, flat_field, mine, after, cols, own_cols):
     total, rows = flat_field.shape
-    slabs = padded(total // cols)
-    vmem = pl.BlockSpec(memory_space=pltpu.VMEM)
-    work, side = (own_cols, slabs, rows), own_cols * slabs
-    return pl.pallas_call(
-        functools.partial(mine_kernel, levels, cols),
+    work = (own_cols, padded(total // cols), rows)
+    vmem = pl.BlockSpec(memory_space=pltpu.VMEM)
+    return pl.pallas_call(
+        functools.partial(mine_kernel, cols),
         name="mine",
-        in_specs=[vmem] * 3 + [pl.BlockSpec(memory_space=pl.ANY)],
-        out_specs=[vmem] * 5,
-        out_shape=[
-            jax.ShapeDtypeStruct((own_cols * SUB, cols * SUB), BF16),
-            jax.ShapeDtypeStruct((side, side), BF16),
-            jax.ShapeDtypeStruct((side, side), BF16),
-            jax.ShapeDtypeStruct(work, BF16),
-            jax.ShapeDtypeStruct(work, F32),
-        ],
+        in_specs=[vmem] * 4 + [pl.BlockSpec(memory_space=pl.ANY)],
+        out_specs=[vmem] * 2,
+        out_shape=[jax.ShapeDtypeStruct(work, BF16), jax.ShapeDtypeStruct(work, F32)],
         scratch_shapes=[pltpu.VMEM(work, F32)],
         compiler_params=pltpu.CompilerParams(vmem_limit_bytes=VMEM),
         cost_estimate=taking(1.8),
-    )(loc, flat_field, mine, after)
+    )(perm, local, flat_field, mine, after)
 
 
 def send_call(held, other, cols):
@@ -472,8 +506,7 @@
 
 
 def mixed(vert, static):
-    high = static.astype(BF16)
-    return dot(vert, high) + dot(vert, (static - high.astype(F32)).astype(BF16))
+    return dot(vert, static.astype(BF16))
 
 
 def rows_kernel(levels, scale, own_ref, coef_ref, mat_ref, row_coef_ref, part_ref, *refs):
@@ -623,10 +656,12 @@
     other = swap(mine, 1)
     line_table = pltpu.with_memory_space_constraint(alpha_table, pltpu.HBM)
     line_entries = pltpu.with_memory_space_constraint(xscale_idx, pltpu.HBM)
-    share = (lax.axis_index("mem") & (CORES - 1)).astype(jnp.int32).reshape(1)
-    ends, own_0, lines = ends_call(share, line_table, line_entries, flat_field, levels, steps, cols, own_cols)
+    line_loc = pltpu.with_memory_space_constraint(loc_filter[0], pltpu.HBM)
+    ends, own_0, lines, *matrices = ends_call(
+        line_table, line_entries, line_loc, flat_field, levels, steps, cols, own_cols
+    )
     blocks, came = [ends], []
-    held = mine_call(loc_filter[0], full_field, mine, ends, levels, cols, own_cols)
+    held = [*matrices, *mine_call(*matrices[:2], full_field, mine, ends, cols, own_cols)]
     send = send_call(held, other, cols)
     over = swap(send, 2)
     coef = coefs_call(lines, send, steps, cols)
@@ -634,11 +669,11 @@
         came.append(swap(blocks[0], 1 << level, "tile"))
         *blocks, coef = merge_call(lines, ends, came, [coef], levels, steps)
     near, far, part = blocks
-    last = {flip: swap(near if flip == 1 else far, flip << (steps - 2), "tile") for flip in (2, 3, 1)}
+    last = {flip: swap(near if flip == 1 else far, flip << (steps - 2), "tile") for flip in ORDER}
     keep = keep_call(held, full_field, mine, other, near, cols)
     own_1 = local_call(lines, full_field, near, levels, cols, own_cols)
     mats, row_coef, vert = tables_call(alpha_table, yscale_idx, vert_filter[0], own_1, levels, own_cols, cols, slabs)
-    shares = [part, last[1], last[2], last[3]]
+    shares = [part] + [last[flip] for flip in ORDER]
     others = [swap(share, 1) for share in shares]
     scale = 1.0 / (mem_count * members.shape[0] - 1)
     base = rows_call(levels, scale, own_0, coef, mats, row_coef, shares, vert, keep)

time: 22.6 us -> 22.4 us (level)
  Pallas kernels: 11.2 us -> 10.7 us
  starting transfers between devices: 9.63 us -> 10.1 us
  waiting for transfers between devices: 1.53 us -> 1.25 us
    ppermute x10, starting transfers between devices: 9.63 us -> 10.1 us  [swap(): lax.ppermute(array, axis, [(i, i ^ flip) for i in range(lax.axis_size(axi...]
    ppermute x10, waiting for transfers between devices: 1.53 us -> 1.25 us  [swap(): lax.ppermute(array, axis, [(i, i ^ flip) for i in range(lax.axis_size(axi...]
  transfers between devices with their start and end apart: 10 -> 10, of which waited for: 3 -> 5; matrix products, arithmetic and copies ran while one was open for 0% -> 0% of each run, Pallas kernels for 41% -> 40%
where the time goes in v9:
time: 22.4 us; the launch traced here: 22.2 us
  Pallas kernels  10.7 us (48%)
  starting transfers between devices  10.1 us (45%)
  waiting for transfers between devices  1.25 us (6%)
    ppermute x10, starting transfers between devices, swap(): lax.ppermute(array, axis, [(i, i ^ flip) for i in range(lax.axis_size(axi...  10.1 us
    pallas_call x1, Pallas kernels, ends_call(): pl.pallas_call(functools.partial(ends_kernel, levels, steps, total // col...  2.39 us
    pallas_call x1, Pallas kernels, keep_call(): pl.pallas_call(functools.partial(keep_kernel, cols), name='keep', in_spec...  1.9 us
    ppermute x10, waiting for transfers between devices, swap(): lax.ppermute(array, axis, [(i, i ^ flip) for i in range(lax.axis_size(axi...  1.25 us
    pallas_call x1, Pallas kernels, mine_call(): pl.pallas_call(functools.partial(mine_kernel, cols), name='mine', in_spec...  1.09 us
    pallas_call x1, Pallas kernels, send_call(): pl.pallas_call(functools.partial(send_kernel, cols), name='send', in_spec...  0.95 us
    pallas_call x1, Pallas kernels, final_call(): pl.pallas_call(functools.partial(final_kernel, scale), name='final', in_s...  0.93 us
    pallas_call x1, Pallas kernels, local_call(): pl.pallas_call(functools.partial(local_kernel, levels, total // cols), na...  0.89 us
  transfers between devices with their start and end apart: 10, of which 5 were waited for; matrix products, arithmetic and copies ran while one was open for 0% of the time, Pallas kernels for 40%

profile of v9, /device:TPU:0, one launch (start us, length us, event | category | flops | bytes accessed | tf_op | source)
XLA Modules:
  0.0 22.2 jit_solution(10902845408984885361)
XLA Ops:
  0.0 0.5 %collective-permute-start.1 = (bf16[976,1024]{1,0:T(8,128)(2,1)}, bf16[976,1024]{1,0:T(8,128)(2,1)S(1)}, u32[]{:S(2)}, u32[]{:S(2)}) collective-permute-start(bf16[976,1024]{1,0:T(8,128)(2,1)} %bitcast.9), channel_id=1, source_target_pairs={{0,1},{1,0},{2,3},{3,2},{4,5},{5,4},{6,7},{7,6},{8,9},{9,8},{10,11... | collective-permute-start | bytes 5996552 | tf_op jit(solution)/shard_map/ppermute | solution.py:651
  0.5 0.0 copy-start
  0.5 0.0 copy-start.1
  0.5 2.4 %ends.1 = (bf16[2,32,1024]{2,1,0:T(8,128)(2,1)S(1)}, f32[4,32,1024]{2,1,0:T(8,128)S(1)}, f32[3,2,1024]{2,1,0:T(2,128)S(1)}, bf16[64,256]{1,0:T(8,128)(2,1)S(1)},...) custom-call(f32[16]{0:T(128)} %table_hbm.1, s32[2,1024]{1,0:T(2,128)} %entries_hbm.1, ...), custom_call_target="tpu_custom_call" | custom-call | flops 2415000064 | bytes 262144 | tf_op jit(solution)/shard_map/ends/pallas_call | solution.py:169
  2.9 2.6 %collective-permute-start = (bf16[2,32,1024]{2,1,0:T(8,128)(2,1)S(1)}, bf16[2,32,1024]{2,1,0:T(8,128)(2,1)S(1)}, u32[]{:S(2)}, u32[]{:S(2)}) collective-permute-start(bf16[2,32,1024]{2,1,0:T(8,128)(2,1)S(1)} %get-tuple-element.21.after_ref.refs_1_), channel_id=1, source_target_pairs={{0,4},{4,0},{8,12},{12,8},{16,20},{20,16},{24,28},{28,24},{1,5},{5... | collective-permute-start | bytes 393224 | tf_op jit(solution)/shard_map/ppermute | solution.py:651
  5.5 0.0 copy-done
  5.5 0.0 copy-done.1
  5.5 1.1 %mine.1 = (bf16[4,64,1024]{2,1,0:T(8,128)(2,1)S(1)}, f32[4,64,1024]{2,1,0:T(8,128)S(1)}) custom-call(bf16[64,256]{1,0:T(8,128)(2,1)S(1)} %get-tuple-element.22.perm_ref, bf16[256,256]{1,0:T(8,128)(2,1)S(1)} %get-tuple-element.23.local_ref, bf16[976,1024]{1,0:T(8,128)(2,1)S(1)} %bitcast.6, bf16[976,1024]{1,0:T(8,128)(2,1)S(1)} %bitcast.10, ...), custom_call_target="tpu_custom_call" | custom-call | flops 2070000000 | bytes 262144 | tf_op jit(solution)/shard_map/mine/pallas_call | solution.py:349
  6.6 0.0 collective-permute-done.1.other_ref
  6.6 0.9 %send.1.after_ref = bf16[244,1024]{1,0:T(8,128)(2,1)S(1)} custom-call(bf16[64,256]{1,0:T(8,128)(2,1)S(1)} %get-tuple-element.22.perm_ref, bf16[256,256]{1,0:T(8,128)(2,1)S(1)} %get-tuple-element.23.local_ref, bf16[256,256]{1,0:T(8,128)(2,1)S(1)} %get-tuple-element.24.order_ref, bf16[4,64,1024]{2,1,0:T(8,128)(2,1)S(1)} %get-tuple-element.25.field_w, ...), custom_call_target="tpu_custom_call" | custom-call | flops 920000000 | bytes 262144 | tf_op jit(solution)/shard_map/send/pallas_call | solution.py:364
  7.5 1.5 %collective-permute-start.9 = (bf16[244,1024]{1,0:T(8,128)(2,1)S(1)}, bf16[244,1024]{1,0:T(8,128)(2,1)S(1)}, u32[]{:S(2)}, u32[]{:S(2)}) collective-permute-start(bf16[244,1024]{1,0:T(8,128)(2,1)S(1)} %send.1.after_ref), channel_id=1, source_target_pairs={{0,2},{1,3},{2,0},{3,1},{4,6},{5,7},{6,4},{7,5},{8,10},{9,11},{10,... | collective-permute-start | bytes 1499144 | tf_op jit(solution)/shard_map/ppermute | solution.py:651
  9.1 0.5 %collective-permute-done.refs_2_ = bf16[2,32,1024]{2,1,0:T(8,128)(2,1)S(1)} collective-permute-done((bf16[2,32,1024]{2,1,0:T(8,128)(2,1)S(1)}, bf16[2,32,1024]{2,1,0:T(8,128)(2,1)S(1)}, u32[]{:S(2)}, u32[]{:S(2)}) %collective-permute-start) | collective-permute-done | bytes 131104 | tf_op jit(solution)/shard_map/ppermute | solution.py:651
  9.6 0.1 merge.1
  9.7 2.9 %collective-permute-start.3 = (bf16[32,1024]{1,0:T(8,128)(2,1)S(1)}, bf16[32,1024]{1,0:T(8,128)(2,1)S(1)}, u32[]{:S(2)}, u32[]{:S(2)}) collective-permute-start(bf16[32,1024]{1,0:T(8,128)(2,1)S(1)} %get-tuple-element.32), channel_id=1, source_target_pairs={{0,16},{4,20},{8,24},{12,28},{16,0},{20,4},{24,8},{28,12},{1,17},{... | collective-permute-start | bytes 196616 | tf_op jit(solution)/shard_map/ppermute | solution.py:651
  12.6 1.3 %collective-permute-start.5 = (bf16[32,1024]{1,0:T(8,128)(2,1)S(1)}, bf16[32,1024]{1,0:T(8,128)(2,1)S(1)}, u32[]{:S(2)}, u32[]{:S(2)}) collective-permute-start(bf16[32,1024]{1,0:T(8,128)(2,1)S(1)} %get-tuple-element.32), channel_id=1, source_target_pairs={{0,24},{4,28},{8,16},{12,20},{16,8},{20,12},{24,0},{28,4},{1,25},{... | collective-permute-start | bytes 196616 | tf_op jit(solution)/shard_map/ppermute | solution.py:651
  13.9 0.2 %collective-permute-start.7 = (bf16[32,1024]{1,0:T(8,128)(2,1)S(1)}, bf16[32,1024]{1,0:T(8,128)(2,1)S(1)}, u32[]{:S(2)}, u32[]{:S(2)}) collective-permute-start(bf16[32,1024]{1,0:T(8,128)(2,1)S(1)} %get-tuple-element.27.after_ref), channel_id=1, source_target_pairs={{0,8},{4,12},{8,0},{12,4},{16,24},{20,28},{24,16},{28,20},{1,9},{5... | collective-permute-start | bytes 196616 | tf_op jit(solution)/shard_map/ppermute | solution.py:651
  14.2 0.0 collective-permute-start.2
  14.2 1.9 %keep.1.refs_4_ = f32[244,1024]{1,0:T(8,128)S(1)} custom-call(bf16[256,256]{1,0:T(8,128)(2,1)S(1)} %get-tuple-element.23.local_ref, bf16[256,256]{1,0:T(8,128)(2,1)S(1)} %get-tuple-element.24.order_ref, bf16[976,1024]{1,0:T(8,128)(2,1)S(1)} %bitcast.7, bf16[976,1024]{1,0:T(8,128)(2,1)S(1)} %bitcast.11, ...), custom_call_target="tpu_custom_call" | custom-call | flops 690000000 | bytes 262144 | tf_op jit(solution)/shard_map/keep/pallas_call | solution.py:379
  16.1 0.0 copy-start.2
  16.1 0.0 copy-start.3
  16.1 0.0 copy-start.4
  16.1 0.9 %local.1.after_ref.own_ref = f32[4,32,1024]{2,1,0:T(8,128)S(1)} custom-call(f32[3,2,1024]{2,1,0:T(2,128)S(1)} %get-tuple-element.20.lines_ref.refs_0_, bf16[976,1024]{1,0:T(8,128)(2,1)S(1)} %bitcast.8, bf16[32,1024]{1,0:T(8,128)(2,1)S(1)} %get-tuple-element.27.after_ref), custom_call_target="tpu_custom_call" | custom-call | flops 575000000 | bytes 262144 | tf_op jit(solution)/shard_map/local/pallas_call | solution.py:241
  17.0 0.0 copy-done.2
  17.0 0.0 copy-done.3
  17.0 0.0 copy-done.4
  17.1 0.8 %tables.1 = (bf16[8,256,256]{2,1,0:T(8,128)(2,1)S(1)}, f32[4,8,256]{2,1,0:T(8,128)S(1)}, bf16[2,256,128]{2,1,0:T(8,128)(2,1)S(1)}) custom-call(f32[1,16]{1,0:T(1,128)S(1)} %bitcast.13, s32[2,128]{1,0:T(2,128)S(1)} %copy-done.3, bf16[60,60]{1,0:T(8,128)(2,1)S(1)} %bitcast.12, f32[4,32,1024]{2,1,0:T(8,128)S(1)} %local.1.after_ref.own_ref), custom_call_target="tpu_custom_call" | custom-call | flops 460000000 | bytes 262144 | tf_op jit(solution)/shard_map/tables/pallas_call | solution.py:438
  17.8 0.0 collective-permute-done.3.refs_0_
  17.8 0.6 %collective-permute-start.4 = (bf16[32,1024]{1,0:T(8,128)(2,1)S(1)}, bf16[32,1024]{1,0:T(8,128)(2,1)S(1)}, u32[]{:S(2)}, u32[]{:S(2)}) collective-permute-start(bf16[32,1024]{1,0:T(8,128)(2,1)S(1)} %collective-permute-done.3.refs_0_), channel_id=1, source_target_pairs={{0,1},{1,0},{2,3},{3,2},{4,5},{5,4},{6,7},{7,6},{8,9},{9,8},{10,11... | collective-permute-start | bytes 196616 | tf_op jit(solution)/shard_map/ppermute | solution.py:651
  18.4 0.4 %collective-permute-done.5.refs_1_ = bf16[32,1024]{1,0:T(8,128)(2,1)S(1)} collective-permute-done((bf16[32,1024]{1,0:T(8,128)(2,1)S(1)}, bf16[32,1024]{1,0:T(8,128)(2,1)S(1)}, u32[]{:S(2)}, u32[]{:S(2)}) %collective-permute-start.5) | collective-permute-done | bytes 65568 | tf_op jit(solution)/shard_map/ppermute | solution.py:651
  18.8 0.0 collective-permute-start.6
  18.8 0.1 collective-permute-done.7.refs_2_
  18.9 0.4 %collective-permute-start.8 = (bf16[32,1024]{1,0:T(8,128)(2,1)S(1)}, bf16[32,1024]{1,0:T(8,128)(2,1)S(1)}, u32[]{:S(2)}, u32[]{:S(2)}) collective-permute-start(bf16[32,1024]{1,0:T(8,128)(2,1)S(1)} %collective-permute-done.7.refs_2_), channel_id=1, source_target_pairs={{0,1},{1,0},{2,3},{3,2},{4,5},{5,4},{6,7},{7,6},{8,9},{9,8},{10,11... | collective-permute-start | bytes 196616 | tf_op jit(solution)/shard_map/ppermute | solution.py:651
  19.3 0.8 %rows.1.base_ref = f32[244,1024]{1,0:T(8,128)S(1)} custom-call(f32[4,32,1024]{2,1,0:T(8,128)S(1)} %get-tuple-element.34.own_ref, f32[2,19,2,1024]{3,2,1,0:T(2,128)S(1)} %get-tuple-element.28.coef_ref, bf16[8,256,256]{2,1,0:T(8,128)(2,1)S(1)} %get-tuple-element.29.mat_ref, f32[4,8,256]{2,1,0:T(8,128)S(1)} %get-tuple-element.30.row_coef_ref, ...), custom_call_target="tpu_custom_call" | custom-call | flops 1380000000 | bytes 262144 | tf_op jit(solution)/shard_map/rows/pallas_call | solution.py:523
  20.1 0.0 collective-permute-done.4.last_1_ref
  20.1 0.0 collective-permute-done.6.last_2_ref
  20.2 0.1 collective-permute-done.8.last_3_ref
  20.2 0.0 collective-permute-done.2.part_ref
  20.2 0.8 %join.1.total_ref = f32[244,1024]{1,0:T(8,128)S(1)} custom-call(f32[4,32,1024]{2,1,0:T(8,128)S(1)} %local.1.after_ref.own_ref, f32[2,19,2,1024]{3,2,1,0:T(2,128)S(1)} %get-tuple-element.28.coef_ref, bf16[8,256,256]{2,1,0:T(8,128)(2,1)S(1)} %get-tuple-element.29.mat_ref, f32[4,8,256]{2,1,0:T(8,128)S(1)} %get-tuple-element.30.row_coef_ref, ...), custom_call_target="tpu_custom_call" | custom-call | flops 920000000 | bytes 262144 | tf_op jit(solution)/shard_map/join/pallas_call | solution.py:549
  21.0 0.2 collective-permute-done.9.came_ref
  21.3 0.9 %final.1 = bf16[61,4,1024]{2,1,0:T(4,128)(2,1)} custom-call(f32[244,1024]{1,0:T(8,128)S(1)} %join.1.total_ref, bf16[244,1024]{1,0:T(8,128)(2,1)S(1)} %collective-permute-done.9.came_ref), custom_call_target="tpu_custom_call" | custom-call | flops 920000000 | bytes 262144 | tf_op jit(solution)/shard_map/final/pallas_call | solution.py:579
  (1 shorter events, 0.0 us)
Async XLA Ops:
  0.0 6.6 %collective-permute-start.1 = (bf16[976,1024]{1,0:T(8,128)(2,1)}, bf16[976,1024]{1,0:T(8,128)(2,1)S(1)}, u32[]{:S(2)}, u32[]{:S(2)}) collective-permute-start(bf16[976,1024]{1,0:T(8,128)(2,1)} %bitcast.9), channel_id=1, source_target_pairs={{0,1},{1,0},{2,3},{3,2},{4,5},{5,4},{6,7},{7,6},{8,9},{9,8},{10,11... | collective-permute-start | bytes 5996552 | tf_op jit(solution)/shard_map/ppermute | solution.py:651
  0.5 5.0 %copy-start = (bf16[61,16,1024]{2,1,0:T(8,128)(2,1)S(1)}, bf16[61,16,1024]{2,1,0:T(8,128)(2,1)}, u32[]{:S(2)}) copy-start(bf16[61,16,1024]{2,1,0:T(8,128)(2,1)} %param.7) | copy-start | bytes 5996548
  0.5 5.0 %copy-start.1 = (bf16[1,61,16,1024]{3,2,1,0:T(8,128)(2,1)S(1)}, bf16[1,61,16,1024]{3,2,1,0:T(8,128)(2,1)}, u32[]{:S(2)}) copy-start(bf16[1,61,16,1024]{3,2,1,0:T(8,128)(2,1)} %param.13) | copy-start | bytes 5996548
  2.9 6.7 %collective-permute-start = (bf16[2,32,1024]{2,1,0:T(8,128)(2,1)S(1)}, bf16[2,32,1024]{2,1,0:T(8,128)(2,1)S(1)}, u32[]{:S(2)}, u32[]{:S(2)}) collective-permute-start(bf16[2,32,1024]{2,1,0:T(8,128)(2,1)S(1)} %get-tuple-element.21.after_ref.refs_1_), channel_id=1, source_target_pairs={{0,4},{4,0},{8,12},{12,8},{16,20},{20,16},{24,28},{28,24},{1,5},{5... | collective-permute-start | bytes 393224 | tf_op jit(solution)/shard_map/ppermute | solution.py:651
  7.5 13.7 %collective-permute-start.9 = (bf16[244,1024]{1,0:T(8,128)(2,1)S(1)}, bf16[244,1024]{1,0:T(8,128)(2,1)S(1)}, u32[]{:S(2)}, u32[]{:S(2)}) collective-permute-start(bf16[244,1024]{1,0:T(8,128)(2,1)S(1)} %send.1.after_ref), channel_id=1, source_target_pairs={{0,2},{1,3},{2,0},{3,1},{4,6},{5,7},{6,4},{7,5},{8,10},{9,11},{10,... | collective-permute-start | bytes 1499144 | tf_op jit(solution)/shard_map/ppermute | solution.py:651
  9.7 8.1 %collective-permute-start.3 = (bf16[32,1024]{1,0:T(8,128)(2,1)S(1)}, bf16[32,1024]{1,0:T(8,128)(2,1)S(1)}, u32[]{:S(2)}, u32[]{:S(2)}) collective-permute-start(bf16[32,1024]{1,0:T(8,128)(2,1)S(1)} %get-tuple-element.32), channel_id=1, source_target_pairs={{0,16},{4,20},{8,24},{12,28},{16,0},{20,4},{24,8},{28,12},{1,17},{... | collective-permute-start | bytes 196616 | tf_op jit(solution)/shard_map/ppermute | solution.py:651
  12.6 6.2 %collective-permute-start.5 = (bf16[32,1024]{1,0:T(8,128)(2,1)S(1)}, bf16[32,1024]{1,0:T(8,128)(2,1)S(1)}, u32[]{:S(2)}, u32[]{:S(2)}) collective-permute-start(bf16[32,1024]{1,0:T(8,128)(2,1)S(1)} %get-tuple-element.32), channel_id=1, source_target_pairs={{0,24},{4,28},{8,16},{12,20},{16,8},{20,12},{24,0},{28,4},{1,25},{... | collective-permute-start | bytes 196616 | tf_op jit(solution)/shard_map/ppermute | solution.py:651
  13.9 5.0 %collective-permute-start.7 = (bf16[32,1024]{1,0:T(8,128)(2,1)S(1)}, bf16[32,1024]{1,0:T(8,128)(2,1)S(1)}, u32[]{:S(2)}, u32[]{:S(2)}) collective-permute-start(bf16[32,1024]{1,0:T(8,128)(2,1)S(1)} %get-tuple-element.27.after_ref), channel_id=1, source_target_pairs={{0,8},{4,12},{8,0},{12,4},{16,24},{20,28},{24,16},{28,20},{1,9},{5... | collective-permute-start | bytes 196616 | tf_op jit(solution)/shard_map/ppermute | solution.py:651
  14.2 6.1 %collective-permute-start.2 = (bf16[2,32,1024]{2,1,0:T(8,128)(2,1)S(1)}, bf16[2,32,1024]{2,1,0:T(8,128)(2,1)S(1)}, u32[]{:S(2)}, u32[]{:S(2)}) collective-permute-start(bf16[2,32,1024]{2,1,0:T(8,128)(2,1)S(1)} %get-tuple-element.31.part_ref), channel_id=1, source_target_pairs={{0,1},{1,0},{2,3},{3,2},{4,5},{5,4},{6,7},{7,6},{8,9},{9,8},{10,11... | collective-permute-start | bytes 393224 | tf_op jit(solution)/shard_map/ppermute | solution.py:651
  16.1 0.9 %copy-start.2 = (bf16[1,60,60]{2,1,0:T(8,128)(2,1)S(1)}, bf16[1,60,60]{2,1,0:T(8,128)(2,1)}, u32[]{:S(2)}) copy-start(bf16[1,60,60]{2,1,0:T(8,128)(2,1)} %param.8) | copy-start | bytes 21604
  16.1 0.9 %copy-start.3 = (s32[2,128]{1,0:T(2,128)S(1)}, s32[2,128]{1,0:T(2,128)}, u32[]{:S(2)}) copy-start(s32[2,128]{1,0:T(2,128)} %entries_ref.1) | copy-start | bytes 3076
  16.1 0.9 %copy-start.4 = (f32[16]{0:T(128)S(1)}, f32[16]{0:T(128)}, u32[]{:S(2)}) copy-start(f32[16]{0:T(128)} %table_hbm.1) | copy-start | bytes 196
  17.8 2.3 %collective-permute-start.4 = (bf16[32,1024]{1,0:T(8,128)(2,1)S(1)}, bf16[32,1024]{1,0:T(8,128)(2,1)S(1)}, u32[]{:S(2)}, u32[]{:S(2)}) collective-permute-start(bf16[32,1024]{1,0:T(8,128)(2,1)S(1)} %collective-permute-done.3.refs_0_), channel_id=1, source_target_pairs={{0,1},{1,0},{2,3},{3,2},{4,5},{5,4},{6,7},{7,6},{8,9},{9,8},{10,11... | collective-permute-start | bytes 196616 | tf_op jit(solution)/shard_map/ppermute | solution.py:651
  18.8 1.3 %collective-permute-start.6 = (bf16[32,1024]{1,0:T(8,128)(2,1)S(1)}, bf16[32,1024]{1,0:T(8,128)(2,1)S(1)}, u32[]{:S(2)}, u32[]{:S(2)}) collective-permute-start(bf16[32,1024]{1,0:T(8,128)(2,1)S(1)} %collective-permute-done.5.refs_1_), channel_id=1, source_target_pairs={{0,1},{1,0},{2,3},{3,2},{4,5},{5,4},{6,7},{7,6},{8,9},{9,8},{10,11... | collective-permute-start | bytes 196616 | tf_op jit(solution)/shard_map/ppermute | solution.py:651
  18.9 1.3 %collective-permute-start.8 = (bf16[32,1024]{1,0:T(8,128)(2,1)S(1)}, bf16[32,1024]{1,0:T(8,128)(2,1)S(1)}, u32[]{:S(2)}, u32[]{:S(2)}) collective-permute-start(bf16[32,1024]{1,0:T(8,128)(2,1)S(1)} %collective-permute-done.7.refs_2_), channel_id=1, source_target_pairs={{0,1},{1,0},{2,3},{3,2},{4,5},{5,4},{6,7},{7,6},{8,9},{9,8},{10,11... | collective-permute-start | bytes 196616 | tf_op jit(solution)/shard_map/ppermute | solution.py:651

commit v10 on v9

--- a/solution.py
+++ b/solution.py
@@ -98,11 +98,10 @@
 
 
 def ends_kernel(
-    levels, steps, slab_count, table_hbm, entries_hbm, loc_hbm, field_hbm, ends_ref, own_ref, lines_ref, perm_ref,
-    local_ref, order_ref, table_ref, entries_ref, loc_ref, held_ref, work, small, arrived
+    levels, steps, slab_count, own_cols, table_hbm, entries_hbm, loc_hbm, field_hbm, ends_ref, work, lines_ref, perm_ref,
+    local_ref, order_ref, table_ref, entries_ref, loc_ref, held_ref, small, arrived
 ):
     pieces, cols, subs, lanes = work.shape
-    own_cols = own_ref.shape[0]
     slabs, rows = CORES * subs, held_ref.shape[1]
     tile, mem = lax.axis_index("tile"), lax.axis_index("mem")
     chip, share = split(mem, CORES)
@@ -158,7 +157,6 @@
         forward = gain * work[piece, cols - 1]
         ends_ref[0, :, part] = forward.astype(BF16)
         ends_ref[1, :, part] = (gain * work[piece, 0] + turned * forward).astype(BF16)
-        own_ref[:, :, part] = work[piece, pl.ds(mem * own_cols, own_cols)] * gain[None]
 
 
 def ends_call(table, entries, loc, flat_field, levels, steps, cols, own_cols):
@@ -167,13 +165,13 @@
     side = own_cols * CORES * subs
     vmem = pl.BlockSpec(memory_space=pltpu.VMEM)
     return pl.pallas_call(
-        functools.partial(ends_kernel, levels, steps, total // cols),
+        functools.partial(ends_kernel, levels, steps, total // cols, own_cols),
         name="ends",
         in_specs=[pl.BlockSpec(memory_space=pl.ANY)] * 4,
         out_specs=[vmem] * 6,
         out_shape=[
             jax.ShapeDtypeStruct((2, subs, rows), BF16),
-            jax.ShapeDtypeStruct((own_cols, subs, rows), F32),
+            jax.ShapeDtypeStruct((rows // LANES, cols, subs, LANES), F32),
             jax.ShapeDtypeStruct((3, 2, rows), F32),
             jax.ShapeDtypeStruct((own_cols * SUB, cols * SUB), BF16),
             jax.ShapeDtypeStruct((side, side), BF16),
@@ -184,7 +182,6 @@
             pltpu.VMEM(entries.shape, jnp.int32),
             pltpu.VMEM(loc.shape, BF16),
             pltpu.VMEM((subs * cols, rows), BF16),
-            pltpu.VMEM((rows // LANES, cols, subs, LANES), F32),
             pltpu.SemaphoreType.DMA((3,)),
             pltpu.SemaphoreType.DMA((FETCHES,)),
         ],
@@ -214,7 +211,7 @@
     return total
 
 
-def local_kernel(levels, slab_count, lines_ref, field_ref, after_ref, own_ref, held_ref, work):
+def local_kernel(levels, slab_count, lines_ref, states_ref, field_ref, after_ref, mine_ref, own_ref, held_ref, work):
     pieces, cols, subs, lanes = work.shape
     own_cols = own_ref.shape[0]
     mem = lax.axis_index("mem")
@@ -231,26 +228,30 @@
     for piece in range(pieces):
         part = slice(piece * lanes, (piece + 1) * lanes)
         gain, _ = sweep_share(levels, share, perm, pair[:, part], held_ref[:, part], work.at[piece])
-        own_ref[:, :, part] = work[piece, pl.ds(mem * own_cols, own_cols)] * gain[None]
-
-
-def local_call(lines, flat_field, after, levels, cols, own_cols):
+        wanted = pl.ds(mem * own_cols, own_cols)
+        own_ref[:, :, part] = work[piece, wanted] * gain[None]
+        is_level = iota((subs, lanes), 0) + (1 - share) * subs < levels
+        gain = gain_of(jnp.where(is_level, pair[0:1, part], pair[1:2, part]))
+        mine_ref[:, :, part] = states_ref[piece, wanted] * gain[None]
+
+
+def local_call(lines, states, flat_field, after, levels, cols, own_cols):
     total, rows = flat_field.shape
     subs = padded(total // cols) // CORES
     vmem = pl.BlockSpec(memory_space=pltpu.VMEM)
     return pl.pallas_call(
         functools.partial(local_kernel, levels, total // cols),
         name="local",
-        in_specs=[vmem, vmem, pl.BlockSpec(memory_space=pl.ANY)],
-        out_specs=vmem,
-        out_shape=jax.ShapeDtypeStruct((own_cols, subs, rows), F32),
+        in_specs=[vmem] * 3 + [pl.BlockSpec(memory_space=pl.ANY)],
+        out_specs=[vmem] * 2,
+        out_shape=[jax.ShapeDtypeStruct((own_cols, subs, rows), F32)] * 2,
         scratch_shapes=[
             pltpu.VMEM((subs * cols, rows), BF16),
             pltpu.VMEM((rows // LANES, cols, subs, LANES), F32),
         ],
         compiler_params=pltpu.CompilerParams(vmem_limit_bytes=VMEM),
         cost_estimate=taking(0.5),
-    )(lines, flat_field, after)
+    )(lines, states, flat_field, after)
 
 
 def coefs_kernel(steps, lines_ref, after_ref, coef_ref):
@@ -657,7 +658,7 @@
     line_table = pltpu.with_memory_space_constraint(alpha_table, pltpu.HBM)
     line_entries = pltpu.with_memory_space_constraint(xscale_idx, pltpu.HBM)
     line_loc = pltpu.with_memory_space_constraint(loc_filter[0], pltpu.HBM)
-    ends, own_0, lines, *matrices = ends_call(
+    ends, states, lines, *matrices = ends_call(
         line_table, line_entries, line_loc, flat_field, levels, steps, cols, own_cols
     )
     blocks, came = [ends], []
@@ -671,7 +672,7 @@
     near, far, part = blocks
     last = {flip: swap(near if flip == 1 else far, flip << (steps - 2), "tile") for flip in ORDER}
     keep = keep_call(held, full_field, mine, other, near, cols)
-    own_1 = local_call(lines, full_field, near, levels, cols, own_cols)
+    own_0, own_1 = local_call(lines, states, full_field, near, levels, cols, own_cols)
     mats, row_coef, vert = tables_call(alpha_table, yscale_idx, vert_filter[0], own_1, levels, own_cols, cols, slabs)
     shares = [part] + [last[flip] for flip in ORDER]
     others = [swap(share, 1) for share in shares]

time: 22.4 us -> 22.2 us (level)
  no operation moved by 1% of the time
where the time goes in v10:
time: 22.2 us; the launch traced here: 22 us
  Pallas kernels  10.6 us (48%)
  starting transfers between devices  10.1 us (45%)
  waiting for transfers between devices  1.15 us (5%)
    ppermute x10, starting transfers between devices, swap(): lax.ppermute(array, axis, [(i, i ^ flip) for i in range(lax.axis_size(axi...  10.1 us
    pallas_call x1, Pallas kernels, ends_call(): pl.pallas_call(functools.partial(ends_kernel, levels, steps, total // col...  2.2 us
    pallas_call x1, Pallas kernels, keep_call(): pl.pallas_call(functools.partial(keep_kernel, cols), name='keep', in_spec...  1.9 us
    ppermute x10, waiting for transfers between devices, swap(): lax.ppermute(array, axis, [(i, i ^ flip) for i in range(lax.axis_size(axi...  1.15 us
    pallas_call x1, Pallas kernels, mine_call(): pl.pallas_call(functools.partial(mine_kernel, cols), name='mine', in_spec...  1.09 us
    pallas_call x1, Pallas kernels, local_call(): pl.pallas_call(functools.partial(local_kernel, levels, total // cols), na...  1.02 us
    pallas_call x1, Pallas kernels, send_call(): pl.pallas_call(functools.partial(send_kernel, cols), name='send', in_spec...  0.94 us
    pallas_call x1, Pallas kernels, final_call(): pl.pallas_call(functools.partial(final_kernel, scale), name='final', in_s...  0.93 us
  transfers between devices with their start and end apart: 10, of which 5 were waited for; matrix products, arithmetic and copies ran while one was open for 0% of the time, Pallas kernels for 40%

profile of v10, /device:TPU:0, one launch (start us, length us, event | category | flops | bytes accessed | tf_op | source)
XLA Modules:
  0.0 22.0 jit_solution(15942522283247481239)
XLA Ops:
  0.0 0.5 %collective-permute-start.1 = (bf16[976,1024]{1,0:T(8,128)(2,1)}, bf16[976,1024]{1,0:T(8,128)(2,1)S(1)}, u32[]{:S(2)}, u32[]{:S(2)}) collective-permute-start(bf16[976,1024]{1,0:T(8,128)(2,1)} %bitcast.9), channel_id=1, source_target_pairs={{0,1},{1,0},{2,3},{3,2},{4,5},{5,4},{6,7},{7,6},{8,9},{9,8},{10,11... | collective-permute-start | bytes 5996552 | tf_op jit(solution)/shard_map/ppermute | solution.py:652
  0.5 0.0 copy-start
  0.5 0.0 copy-start.1
  0.5 2.2 %ends.1 = (bf16[2,32,1024]{2,1,0:T(8,128)(2,1)S(1)}, f32[4,16,32,256]{3,2,1,0:T(8,128)S(1)}, f32[3,2,1024]{2,1,0:T(2,128)S(1)}, bf16[64,256]{1,0:T(8,128)(2,1)S(...) custom-call(f32[16]{0:T(128)} %table_hbm.1, s32[2,1024]{1,0:T(2,128)} %entries_hbm.1, ...), custom_call_target="tpu_custom_call" | custom-call | flops 2415000064 | bytes 262144 | tf_op jit(solution)/shard_map/ends/pallas_call | solution.py:167
  2.7 2.6 %collective-permute-start = (bf16[2,32,1024]{2,1,0:T(8,128)(2,1)S(1)}, bf16[2,32,1024]{2,1,0:T(8,128)(2,1)S(1)}, u32[]{:S(2)}, u32[]{:S(2)}) collective-permute-start(bf16[2,32,1024]{2,1,0:T(8,128)(2,1)S(1)} %get-tuple-element.24.after_ref.refs_1_), channel_id=1, source_target_pairs={{0,4},{4,0},{8,12},{12,8},{16,20},{20,16},{24,28},{28,24},{1,5},{5... | collective-permute-start | bytes 393224 | tf_op jit(solution)/shard_map/ppermute | solution.py:652
  5.3 0.0 copy-done
  5.3 0.0 copy-done.1
  5.3 1.1 %mine.1 = (bf16[4,64,1024]{2,1,0:T(8,128)(2,1)S(1)}, f32[4,64,1024]{2,1,0:T(8,128)S(1)}) custom-call(bf16[64,256]{1,0:T(8,128)(2,1)S(1)} %get-tuple-element.25.perm_ref, bf16[256,256]{1,0:T(8,128)(2,1)S(1)} %get-tuple-element.26.local_ref, bf16[976,1024]{1,0:T(8,128)(2,1)S(1)} %bitcast.6, bf16[976,1024]{1,0:T(8,128)(2,1)S(1)} %bitcast.10, ...), custom_call_target="tpu_custom_call" | custom-call | flops 2070000000 | bytes 262144 | tf_op jit(solution)/shard_map/mine/pallas_call | solution.py:350
  6.4 0.0 collective-permute-done.1.other_ref
  6.4 0.9 %send.1.after_ref = bf16[244,1024]{1,0:T(8,128)(2,1)S(1)} custom-call(bf16[64,256]{1,0:T(8,128)(2,1)S(1)} %get-tuple-element.25.perm_ref, bf16[256,256]{1,0:T(8,128)(2,1)S(1)} %get-tuple-element.26.local_ref, bf16[256,256]{1,0:T(8,128)(2,1)S(1)} %get-tuple-element.27.order_ref, bf16[4,64,1024]{2,1,0:T(8,128)(2,1)S(1)} %get-tuple-element.28.field_w, ...), custom_call_target="tpu_custom_call" | custom-call | flops 920000000 | bytes 262144 | tf_op jit(solution)/shard_map/send/pallas_call | solution.py:365
  7.3 1.6 %collective-permute-start.9 = (bf16[244,1024]{1,0:T(8,128)(2,1)S(1)}, bf16[244,1024]{1,0:T(8,128)(2,1)S(1)}, u32[]{:S(2)}, u32[]{:S(2)}) collective-permute-start(bf16[244,1024]{1,0:T(8,128)(2,1)S(1)} %send.1.after_ref), channel_id=1, source_target_pairs={{0,2},{1,3},{2,0},{3,1},{4,6},{5,7},{6,4},{7,5},{8,10},{9,11},{10,... | collective-permute-start | bytes 1499144 | tf_op jit(solution)/shard_map/ppermute | solution.py:652
  8.9 0.5 %collective-permute-done.refs_2_ = bf16[2,32,1024]{2,1,0:T(8,128)(2,1)S(1)} collective-permute-done((bf16[2,32,1024]{2,1,0:T(8,128)(2,1)S(1)}, bf16[2,32,1024]{2,1,0:T(8,128)(2,1)S(1)}, u32[]{:S(2)}, u32[]{:S(2)}) %collective-permute-start) | collective-permute-done | bytes 131104 | tf_op jit(solution)/shard_map/ppermute | solution.py:652
  9.4 0.1 merge.1
  9.5 2.9 %collective-permute-start.3 = (bf16[32,1024]{1,0:T(8,128)(2,1)S(1)}, bf16[32,1024]{1,0:T(8,128)(2,1)S(1)}, u32[]{:S(2)}, u32[]{:S(2)}) collective-permute-start(bf16[32,1024]{1,0:T(8,128)(2,1)S(1)} %get-tuple-element.36), channel_id=1, source_target_pairs={{0,16},{4,20},{8,24},{12,28},{16,0},{20,4},{24,8},{28,12},{1,17},{... | collective-permute-start | bytes 196616 | tf_op jit(solution)/shard_map/ppermute | solution.py:652
  12.4 1.3 %collective-permute-start.5 = (bf16[32,1024]{1,0:T(8,128)(2,1)S(1)}, bf16[32,1024]{1,0:T(8,128)(2,1)S(1)}, u32[]{:S(2)}, u32[]{:S(2)}) collective-permute-start(bf16[32,1024]{1,0:T(8,128)(2,1)S(1)} %get-tuple-element.36), channel_id=1, source_target_pairs={{0,24},{4,28},{8,16},{12,20},{16,8},{20,12},{24,0},{28,4},{1,25},{... | collective-permute-start | bytes 196616 | tf_op jit(solution)/shard_map/ppermute | solution.py:652
  13.8 0.2 %collective-permute-start.7 = (bf16[32,1024]{1,0:T(8,128)(2,1)S(1)}, bf16[32,1024]{1,0:T(8,128)(2,1)S(1)}, u32[]{:S(2)}, u32[]{:S(2)}) collective-permute-start(bf16[32,1024]{1,0:T(8,128)(2,1)S(1)} %get-tuple-element.30.after_ref), channel_id=1, source_target_pairs={{0,8},{4,12},{8,0},{12,4},{16,24},{20,28},{24,16},{28,20},{1,9},{5... | collective-permute-start | bytes 196616 | tf_op jit(solution)/shard_map/ppermute | solution.py:652
  14.0 0.0 collective-permute-start.2
  14.0 1.9 %keep.1.refs_4_ = f32[244,1024]{1,0:T(8,128)S(1)} custom-call(bf16[256,256]{1,0:T(8,128)(2,1)S(1)} %get-tuple-element.26.local_ref, bf16[256,256]{1,0:T(8,128)(2,1)S(1)} %get-tuple-element.27.order_ref, bf16[976,1024]{1,0:T(8,128)(2,1)S(1)} %bitcast.7, bf16[976,1024]{1,0:T(8,128)(2,1)S(1)} %bitcast.11, ...), custom_call_target="tpu_custom_call" | custom-call | flops 690000000 | bytes 262144 | tf_op jit(solution)/shard_map/keep/pallas_call | solution.py:380
  15.9 0.0 copy-start.2
  15.9 0.0 copy-start.3
  15.9 0.0 copy-start.4
  15.9 1.0 %local.1 = (f32[4,32,1024]{2,1,0:T(8,128)S(1)}, f32[4,32,1024]{2,1,0:T(8,128)S(1)}) custom-call(f32[3,2,1024]{2,1,0:T(2,128)S(1)} %get-tuple-element.22.lines_ref.refs_0_, f32[4,16,32,256]{3,2,1,0:T(8,128)S(1)} %get-tuple-element.23.states_ref, bf16[976,1024]{1,0:T(8,128)(2,1)S(1)} %bitcast.8, bf16[32,1024]{1,0:T(8,128)(2,1)S(1)} %get-tuple-element.30.after_ref), custom_call_target="tpu_custom_call" | custom-call | flops 575000000 | bytes 262144 | tf_op jit(solution)/shard_map/local/pallas_call | solution.py:242
  17.0 0.0 copy-done.2
  17.0 0.0 copy-done.3
  17.0 0.0 copy-done.4
  17.0 0.8 %tables.1 = (bf16[8,256,256]{2,1,0:T(8,128)(2,1)S(1)}, f32[4,8,256]{2,1,0:T(8,128)S(1)}, bf16[2,256,128]{2,1,0:T(8,128)(2,1)S(1)}) custom-call(f32[1,16]{1,0:T(1,128)S(1)} %bitcast.13, s32[2,128]{1,0:T(2,128)S(1)} %copy-done.3, bf16[60,60]{1,0:T(8,128)(2,1)S(1)} %bitcast.12, f32[4,32,1024]{2,1,0:T(8,128)S(1)} %get-tuple-element.31.after_ref.own_ref), custom_call_target="tpu_custom_call" | custom-call | flops 460000000 | bytes 262144 | tf_op jit(solution)/shard_map/tables/pallas_call | solution.py:439
  17.8 0.0 collective-permute-done.3.refs_0_
  17.8 0.6 %collective-permute-start.4 = (bf16[32,1024]{1,0:T(8,128)(2,1)S(1)}, bf16[32,1024]{1,0:T(8,128)(2,1)S(1)}, u32[]{:S(2)}, u32[]{:S(2)}) collective-permute-start(bf16[32,1024]{1,0:T(8,128)(2,1)S(1)} %collective-permute-done.3.refs_0_), channel_id=1, source_target_pairs={{0,1},{1,0},{2,3},{3,2},{4,5},{5,4},{6,7},{7,6},{8,9},{9,8},{10,11... | collective-permute-start | bytes 196616 | tf_op jit(solution)/shard_map/ppermute | solution.py:652
  18.3 0.3 %collective-permute-done.5.refs_1_ = bf16[32,1024]{1,0:T(8,128)(2,1)S(1)} collective-permute-done((bf16[32,1024]{1,0:T(8,128)(2,1)S(1)}, bf16[32,1024]{1,0:T(8,128)(2,1)S(1)}, u32[]{:S(2)}, u32[]{:S(2)}) %collective-permute-start.5) | collective-permute-done | bytes 65568 | tf_op jit(solution)/shard_map/ppermute | solution.py:652
  18.6 0.0 collective-permute-start.6
  18.6 0.1 collective-permute-done.7.refs_2_
  18.7 0.4 %collective-permute-start.8 = (bf16[32,1024]{1,0:T(8,128)(2,1)S(1)}, bf16[32,1024]{1,0:T(8,128)(2,1)S(1)}, u32[]{:S(2)}, u32[]{:S(2)}) collective-permute-start(bf16[32,1024]{1,0:T(8,128)(2,1)S(1)} %collective-permute-done.7.refs_2_), channel_id=1, source_target_pairs={{0,1},{1,0},{2,3},{3,2},{4,5},{5,4},{6,7},{7,6},{8,9},{9,8},{10,11... | collective-permute-start | bytes 196616 | tf_op jit(solution)/shard_map/ppermute | solution.py:652
  19.1 0.8 %rows.1.base_ref = f32[244,1024]{1,0:T(8,128)S(1)} custom-call(f32[4,32,1024]{2,1,0:T(8,128)S(1)} %get-tuple-element.38.own_ref, f32[2,19,2,1024]{3,2,1,0:T(2,128)S(1)} %get-tuple-element.32.coef_ref, bf16[8,256,256]{2,1,0:T(8,128)(2,1)S(1)} %get-tuple-element.33.mat_ref, f32[4,8,256]{2,1,0:T(8,128)S(1)} %get-tuple-element.34.row_coef_ref, ...), custom_call_target="tpu_custom_call" | custom-call | flops 1380000000 | bytes 262144 | tf_op jit(solution)/shard_map/rows/pallas_call | solution.py:524
  19.9 0.0 collective-permute-done.4.last_1_ref
  19.9 0.0 collective-permute-done.6.last_2_ref
  20.0 0.1 collective-permute-done.8.last_3_ref
  20.0 0.0 collective-permute-done.2.part_ref
  20.0 0.8 %join.1.total_ref = f32[244,1024]{1,0:T(8,128)S(1)} custom-call(f32[4,32,1024]{2,1,0:T(8,128)S(1)} %get-tuple-element.31.after_ref.own_ref, f32[2,19,2,1024]{3,2,1,0:T(2,128)S(1)} %get-tuple-element.32.coef_ref, bf16[8,256,256]{2,1,0:T(8,128)(2,1)S(1)} %get-tuple-element.33.mat_ref, f32[4,8,256]{2,1,0:T(8,128)S(1)} %get-tuple-element.34.row_coef_ref, ...), custom_call_target="tpu_custom_call" | custom-call | flops 920000000 | bytes 262144 | tf_op jit(solution)/shard_map/join/pallas_call | solution.py:550
  20.8 0.2 collective-permute-done.9.came_ref
  21.1 0.9 %final.1 = bf16[61,4,1024]{2,1,0:T(4,128)(2,1)} custom-call(f32[244,1024]{1,0:T(8,128)S(1)} %join.1.total_ref, bf16[244,1024]{1,0:T(8,128)(2,1)S(1)} %collective-permute-done.9.came_ref), custom_call_target="tpu_custom_call" | custom-call | flops 920000000 | bytes 262144 | tf_op jit(solution)/shard_map/final/pallas_call | solution.py:580
  (1 shorter events, 0.0 us)
Async XLA Ops:
  0.0 6.4 %collective-permute-start.1 = (bf16[976,1024]{1,0:T(8,128)(2,1)}, bf16[976,1024]{1,0:T(8,128)(2,1)S(1)}, u32[]{:S(2)}, u32[]{:S(2)}) collective-permute-start(bf16[976,1024]{1,0:T(8,128)(2,1)} %bitcast.9), channel_id=1, source_target_pairs={{0,1},{1,0},{2,3},{3,2},{4,5},{5,4},{6,7},{7,6},{8,9},{9,8},{10,11... | collective-permute-start | bytes 5996552 | tf_op jit(solution)/shard_map/ppermute | solution.py:652
  0.5 4.8 %copy-start = (bf16[61,16,1024]{2,1,0:T(8,128)(2,1)S(1)}, bf16[61,16,1024]{2,1,0:T(8,128)(2,1)}, u32[]{:S(2)}) copy-start(bf16[61,16,1024]{2,1,0:T(8,128)(2,1)} %param.7) | copy-start | bytes 5996548
  0.5 4.8 %copy-start.1 = (bf16[1,61,16,1024]{3,2,1,0:T(8,128)(2,1)S(1)}, bf16[1,61,16,1024]{3,2,1,0:T(8,128)(2,1)}, u32[]{:S(2)}) copy-start(bf16[1,61,16,1024]{3,2,1,0:T(8,128)(2,1)} %param.13) | copy-start | bytes 5996548
  2.7 6.7 %collective-permute-start = (bf16[2,32,1024]{2,1,0:T(8,128)(2,1)S(1)}, bf16[2,32,1024]{2,1,0:T(8,128)(2,1)S(1)}, u32[]{:S(2)}, u32[]{:S(2)}) collective-permute-start(bf16[2,32,1024]{2,1,0:T(8,128)(2,1)S(1)} %get-tuple-element.24.after_ref.refs_1_), channel_id=1, source_target_pairs={{0,4},{4,0},{8,12},{12,8},{16,20},{20,16},{24,28},{28,24},{1,5},{5... | collective-permute-start | bytes 393224 | tf_op jit(solution)/shard_map/ppermute | solution.py:652
  7.3 13.7 %collective-permute-start.9 = (bf16[244,1024]{1,0:T(8,128)(2,1)S(1)}, bf16[244,1024]{1,0:T(8,128)(2,1)S(1)}, u32[]{:S(2)}, u32[]{:S(2)}) collective-permute-start(bf16[244,1024]{1,0:T(8,128)(2,1)S(1)} %send.1.after_ref), channel_id=1, source_target_pairs={{0,2},{1,3},{2,0},{3,1},{4,6},{5,7},{6,4},{7,5},{8,10},{9,11},{10,... | collective-permute-start | bytes 1499144 | tf_op jit(solution)/shard_map/ppermute | solution.py:652
  9.5 8.2 %collective-permute-start.3 = (bf16[32,1024]{1,0:T(8,128)(2,1)S(1)}, bf16[32,1024]{1,0:T(8,128)(2,1)S(1)}, u32[]{:S(2)}, u32[]{:S(2)}) collective-permute-start(bf16[32,1024]{1,0:T(8,128)(2,1)S(1)} %get-tuple-element.36), channel_id=1, source_target_pairs={{0,16},{4,20},{8,24},{12,28},{16,0},{20,4},{24,8},{28,12},{1,17},{... | collective-permute-start | bytes 196616 | tf_op jit(solution)/shard_map/ppermute | solution.py:652
  12.4 6.2 %collective-permute-start.5 = (bf16[32,1024]{1,0:T(8,128)(2,1)S(1)}, bf16[32,1024]{1,0:T(8,128)(2,1)S(1)}, u32[]{:S(2)}, u32[]{:S(2)}) collective-permute-start(bf16[32,1024]{1,0:T(8,128)(2,1)S(1)} %get-tuple-element.36), channel_id=1, source_target_pairs={{0,24},{4,28},{8,16},{12,20},{16,8},{20,12},{24,0},{28,4},{1,25},{... | collective-permute-start | bytes 196616 | tf_op jit(solution)/shard_map/ppermute | solution.py:652
  13.8 5.0 %collective-permute-start.7 = (bf16[32,1024]{1,0:T(8,128)(2,1)S(1)}, bf16[32,1024]{1,0:T(8,128)(2,1)S(1)}, u32[]{:S(2)}, u32[]{:S(2)}) collective-permute-start(bf16[32,1024]{1,0:T(8,128)(2,1)S(1)} %get-tuple-element.30.after_ref), channel_id=1, source_target_pairs={{0,8},{4,12},{8,0},{12,4},{16,24},{20,28},{24,16},{28,20},{1,9},{5... | collective-permute-start | bytes 196616 | tf_op jit(solution)/shard_map/ppermute | solution.py:652
  14.0 6.1 %collective-permute-start.2 = (bf16[2,32,1024]{2,1,0:T(8,128)(2,1)S(1)}, bf16[2,32,1024]{2,1,0:T(8,128)(2,1)S(1)}, u32[]{:S(2)}, u32[]{:S(2)}) collective-permute-start(bf16[2,32,1024]{2,1,0:T(8,128)(2,1)S(1)} %get-tuple-element.35.part_ref), channel_id=1, source_target_pairs={{0,1},{1,0},{2,3},{3,2},{4,5},{5,4},{6,7},{7,6},{8,9},{9,8},{10,11... | collective-permute-start | bytes 393224 | tf_op jit(solution)/shard_map/ppermute | solution.py:652
  15.9 1.1 %copy-start.2 = (bf16[1,60,60]{2,1,0:T(8,128)(2,1)S(1)}, bf16[1,60,60]{2,1,0:T(8,128)(2,1)}, u32[]{:S(2)}) copy-start(bf16[1,60,60]{2,1,0:T(8,128)(2,1)} %param.8) | copy-start | bytes 21604
  15.9 1.1 %copy-start.3 = (s32[2,128]{1,0:T(2,128)S(1)}, s32[2,128]{1,0:T(2,128)}, u32[]{:S(2)}) copy-start(s32[2,128]{1,0:T(2,128)} %entries_ref.1) | copy-start | bytes 3076
  15.9 1.1 %copy-start.4 = (f32[16]{0:T(128)S(1)}, f32[16]{0:T(128)}, u32[]{:S(2)}) copy-start(f32[16]{0:T(128)} %table_hbm.1) | copy-start | bytes 196
  17.8 2.2 %collective-permute-start.4 = (bf16[32,1024]{1,0:T(8,128)(2,1)S(1)}, bf16[32,1024]{1,0:T(8,128)(2,1)S(1)}, u32[]{:S(2)}, u32[]{:S(2)}) collective-permute-start(bf16[32,1024]{1,0:T(8,128)(2,1)S(1)} %collective-permute-done.3.refs_0_), channel_id=1, source_target_pairs={{0,1},{1,0},{2,3},{3,2},{4,5},{5,4},{6,7},{7,6},{8,9},{9,8},{10,11... | collective-permute-start | bytes 196616 | tf_op jit(solution)/shard_map/ppermute | solution.py:652
  18.6 1.3 %collective-permute-start.6 = (bf16[32,1024]{1,0:T(8,128)(2,1)S(1)}, bf16[32,1024]{1,0:T(8,128)(2,1)S(1)}, u32[]{:S(2)}, u32[]{:S(2)}) collective-permute-start(bf16[32,1024]{1,0:T(8,128)(2,1)S(1)} %collective-permute-done.5.refs_1_), channel_id=1, source_target_pairs={{0,1},{1,0},{2,3},{3,2},{4,5},{5,4},{6,7},{7,6},{8,9},{9,8},{10,11... | collective-permute-start | bytes 196616 | tf_op jit(solution)/shard_map/ppermute | solution.py:652
  18.7 1.3 %collective-permute-start.8 = (bf16[32,1024]{1,0:T(8,128)(2,1)S(1)}, bf16[32,1024]{1,0:T(8,128)(2,1)S(1)}, u32[]{:S(2)}, u32[]{:S(2)}) collective-permute-start(bf16[32,1024]{1,0:T(8,128)(2,1)S(1)} %collective-permute-done.7.refs_2_), channel_id=1, source_target_pairs={{0,1},{1,0},{2,3},{3,2},{4,5},{5,4},{6,7},{7,6},{8,9},{9,8},{10,11... | collective-permute-start | bytes 196616 | tf_op jit(solution)/shard_map/ppermute | solution.py:652

commit v11 on v10

--- a/solution.py
+++ b/solution.py
@@ -11,7 +11,7 @@
 SUB = 16
 CORES = 2
 LANES = 256
-ORDER = (2, 3, 1)
+ORDER = (1, 3, 2)
 FETCHES = 1
 BLOCK = 256
 MIB = 1 << 20
@@ -317,15 +317,13 @@
     return member * dot(local, scaled).reshape(member.shape)
 
 
-def mine_kernel(cols, perm_ref, local_ref, field_ref, mine_ref, after_ref, field_out, total_out, member_w):
-    to_columns(perm_ref[...], field_ref, field_out, cols)
-    to_columns(perm_ref[...], mine_ref, member_w, cols)
-    total_out[...] = member_term(local_ref[...], member_w[...], field_out[...])
-
-
-def send_kernel(cols, perm_ref, local_ref, order_ref, field_w, total_ref, other_ref, send_ref, member_w):
-    to_columns(perm_ref[...], other_ref, member_w, cols)
-    total = total_ref[...] + member_term(local_ref[...], member_w[...], field_w[...])
+def send_kernel(
+    cols, perm_ref, local_ref, order_ref, field_ref, mine_ref, other_ref, after_ref, send_ref, field_w, mine_w, other_w
+):
+    for ref, out in ((field_ref, field_w), (mine_ref, mine_w), (other_ref, other_w)):
+        to_columns(perm_ref[...], ref, out, cols)
+    field, local = field_w[...], local_ref[...]
+    total = member_term(local, mine_w[...], field) + member_term(local, other_w[...], field)
     total = total.reshape(order_ref.shape[0], -1).astype(BF16)
     send_ref[...] = dot(order_ref[...], total)[: send_ref.shape[0]].astype(BF16)
 
@@ -343,50 +341,36 @@
     keep_ref[...] = ordered[: keep_ref.shape[0]]
 
 
-def mine_call(perm, local, flat_field, mine, after, cols, own_cols):
-    total, rows = flat_field.shape
-    work = (own_cols, padded(total // cols), rows)
-    vmem = pl.BlockSpec(memory_space=pltpu.VMEM)
-    return pl.pallas_call(
-        functools.partial(mine_kernel, cols),
-        name="mine",
-        in_specs=[vmem] * 4 + [pl.BlockSpec(memory_space=pl.ANY)],
-        out_specs=[vmem] * 2,
-        out_shape=[jax.ShapeDtypeStruct(work, BF16), jax.ShapeDtypeStruct(work, F32)],
-        scratch_shapes=[pltpu.VMEM(work, F32)],
-        compiler_params=pltpu.CompilerParams(vmem_limit_bytes=VMEM),
-        cost_estimate=taking(1.8),
-    )(perm, local, flat_field, mine, after)
-
-
-def send_call(held, other, cols):
-    own_cols, _, rows = held[3].shape
+def send_call(matrices, flat_field, mine, other, after, cols, own_cols):
+    total, rows = other.shape
+    work = pltpu.VMEM((own_cols, padded(total // cols), rows), F32)
     vmem = pl.BlockSpec(memory_space=pltpu.VMEM)
     return pl.pallas_call(
         functools.partial(send_kernel, cols),
         name="send",
-        in_specs=[vmem] * 6,
+        in_specs=[vmem] * 6 + [pl.BlockSpec(memory_space=pl.ANY)],
         out_specs=vmem,
-        out_shape=jax.ShapeDtypeStruct((other.shape[0] // cols * own_cols, rows), BF16),
-        scratch_shapes=[pltpu.VMEM(held[4].shape, F32)],
-        compiler_params=pltpu.CompilerParams(vmem_limit_bytes=VMEM),
-        cost_estimate=taking(0.8),
-    )(*held, other)
-
-
-def keep_call(held, flat_field, mine, other, after, cols):
-    own_cols, _, rows = held[3].shape
+        out_shape=jax.ShapeDtypeStruct((total // cols * own_cols, rows), BF16),
+        scratch_shapes=[work] * 3,
+        compiler_params=pltpu.CompilerParams(vmem_limit_bytes=VMEM),
+        cost_estimate=taking(2.6),
+    )(*matrices, flat_field, mine, other, after)
+
+
+def keep_call(matrices, flat_field, mine, other, after, cols, own_cols):
+    total, rows = other.shape
+    work = pltpu.VMEM((own_cols, padded(total // cols), rows), F32)
     vmem = pl.BlockSpec(memory_space=pltpu.VMEM)
     return pl.pallas_call(
         functools.partial(keep_kernel, cols),
         name="keep",
         in_specs=[vmem] * 5 + [pl.BlockSpec(memory_space=pl.ANY)],
         out_specs=vmem,
-        out_shape=jax.ShapeDtypeStruct((other.shape[0] // cols * own_cols, rows), F32),
-        scratch_shapes=[pltpu.VMEM(held[4].shape, F32)] * 3,
+        out_shape=jax.ShapeDtypeStruct((total // cols * own_cols, rows), F32),
+        scratch_shapes=[work] * 3,
         compiler_params=pltpu.CompilerParams(vmem_limit_bytes=VMEM),
         cost_estimate=taking(0.6),
-    )(held[1], held[2], flat_field, mine, other, after)
+    )(*matrices[1:], flat_field, mine, other, after)
 
 
 def tables_kernel(levels, own_cols, col_dev, slabs, table_ref, entries_ref, vert_ref, after_ref, mat_ref, coef_ref, vert_out):
@@ -662,8 +646,7 @@
         line_table, line_entries, line_loc, flat_field, levels, steps, cols, own_cols
     )
     blocks, came = [ends], []
-    held = [*matrices, *mine_call(*matrices[:2], full_field, mine, ends, cols, own_cols)]
-    send = send_call(held, other, cols)
+    send = send_call(matrices, full_field, mine, other, ends, cols, own_cols)
     over = swap(send, 2)
     coef = coefs_call(lines, send, steps, cols)
     for level in range(steps - 2):
@@ -671,7 +654,7 @@
         *blocks, coef = merge_call(lines, ends, came, [coef], levels, steps)
     near, far, part = blocks
     last = {flip: swap(near if flip == 1 else far, flip << (steps - 2), "tile") for flip in ORDER}
-    keep = keep_call(held, full_field, mine, other, near, cols)
+    keep = keep_call(matrices, full_field, mine, other, near, cols, own_cols)
     own_0, own_1 = local_call(lines, states, full_field, near, levels, cols, own_cols)
     mats, row_coef, vert = tables_call(alpha_table, yscale_idx, vert_filter[0], own_1, levels, own_cols, cols, slabs)
     shares = [part] + [last[flip] for flip in ORDER]

time: 22.2 us -> 22.1 us (level)
  starting transfers between devices: 10.1 us -> 10.5 us
  waiting for transfers between devices: 1.15 us -> 0.79 us
    pallas_call x1 -> x0, Pallas kernels: 1.09 us -> none  [mine_call(): pl.pallas_call(functools.partial(mine_kernel, cols), name='mine', in_spec...]
    pallas_call x1, Pallas kernels: 0.94 us -> 1.77 us  [send_call(): pl.pallas_call(functools.partial(send_kernel, cols), name='send', in_spec...]
    ppermute x10, starting transfers between devices: 10.1 us -> 10.5 us  [swap(): lax.ppermute(array, axis, [(i, i ^ flip) for i in range(lax.axis_size(axi...]
    ppermute x10, waiting for transfers between devices: 1.15 us -> 0.79 us  [swap(): lax.ppermute(array, axis, [(i, i ^ flip) for i in range(lax.axis_size(axi...]
  transfers between devices with their start and end apart: 10 -> 10, of which waited for: 5 -> 4; matrix products, arithmetic and copies ran while one was open for 0% -> 0% of each run, Pallas kernels for 40% -> 35%
where the time goes in v11:
time: 22.1 us; the launch traced here: 21.8 us
  starting transfers between devices  10.5 us (48%)
  Pallas kernels  10.4 us (47%)
  waiting for transfers between devices  0.79 us (4%)
    ppermute x10, starting transfers between devices, swap(): lax.ppermute(array, axis, [(i, i ^ flip) for i in range(lax.axis_size(axi...  10.5 us
    pallas_call x1, Pallas kernels, ends_call(): pl.pallas_call(functools.partial(ends_kernel, levels, steps, total // col...  2.2 us
    pallas_call x1, Pallas kernels, keep_call(): pl.pallas_call(functools.partial(keep_kernel, cols), name='keep', in_spec...  1.93 us
    pallas_call x1, Pallas kernels, send_call(): pl.pallas_call(functools.partial(send_kernel, cols), name='send', in_spec...  1.77 us
    pallas_call x1, Pallas kernels, local_call(): pl.pallas_call(functools.partial(local_kernel, levels, total // cols), na...  1.01 us
    pallas_call x1, Pallas kernels, final_call(): pl.pallas_call(functools.partial(final_kernel, scale), name='final', in_s...  0.93 us
    pallas_call x1, Pallas kernels, rows_call(): pl.pallas_call(functools.partial(rows_kernel, levels, scale), name='rows'...  0.8 us
    pallas_call x1, Pallas kernels, join_call(): pl.pallas_call(functools.partial(join_kernel, levels), name='join', in_sp...  0.8 us
  transfers between devices with their start and end apart: 10, of which 4 were waited for; matrix products, arithmetic and copies ran while one was open for 0% of the time, Pallas kernels for 35%

profile of v11, /device:TPU:0, one launch (start us, length us, event | category | flops | bytes accessed | tf_op | source)
XLA Modules:
  0.0 21.8 jit_solution(1286734234030929647)
XLA Ops:
  0.0 0.5 %collective-permute-start.1 = (bf16[976,1024]{1,0:T(8,128)(2,1)}, bf16[976,1024]{1,0:T(8,128)(2,1)S(1)}, u32[]{:S(2)}, u32[]{:S(2)}) collective-permute-start(bf16[976,1024]{1,0:T(8,128)(2,1)} %bitcast.9), channel_id=1, source_target_pairs={{0,1},{1,0},{2,3},{3,2},{4,5},{5,4},{6,7},{7,6},{8,9},{9,8},{10,11... | collective-permute-start | bytes 5996552 | tf_op jit(solution)/shard_map/ppermute | solution.py:636
  0.5 0.0 copy-start
  0.5 0.0 copy-start.1
  0.5 2.2 %ends.1 = (bf16[2,32,1024]{2,1,0:T(8,128)(2,1)S(1)}, f32[4,16,32,256]{3,2,1,0:T(8,128)S(1)}, f32[3,2,1024]{2,1,0:T(2,128)S(1)}, bf16[64,256]{1,0:T(8,128)(2,1)S(...) custom-call(f32[16]{0:T(128)} %table_hbm.1, s32[2,1024]{1,0:T(2,128)} %entries_hbm.1, ...), custom_call_target="tpu_custom_call" | custom-call | flops 2415000064 | bytes 262144 | tf_op jit(solution)/shard_map/ends/pallas_call | solution.py:167
  2.7 2.6 %collective-permute-start = (bf16[2,32,1024]{2,1,0:T(8,128)(2,1)S(1)}, bf16[2,32,1024]{2,1,0:T(8,128)(2,1)S(1)}, u32[]{:S(2)}, u32[]{:S(2)}) collective-permute-start(bf16[2,32,1024]{2,1,0:T(8,128)(2,1)S(1)} %get-tuple-element.22.after_ref.refs_1_), channel_id=1, source_target_pairs={{0,4},{4,0},{8,12},{12,8},{16,20},{20,16},{24,28},{28,24},{1,5},{5... | collective-permute-start | bytes 393224 | tf_op jit(solution)/shard_map/ppermute | solution.py:636
  5.3 0.0 collective-permute-done.1.other_ref
  5.3 0.0 copy-done
  5.3 0.0 copy-done.1
  5.3 1.8 %send.1.after_ref = bf16[244,1024]{1,0:T(8,128)(2,1)S(1)} custom-call(bf16[64,256]{1,0:T(8,128)(2,1)S(1)} %get-tuple-element.23.perm_ref, bf16[256,256]{1,0:T(8,128)(2,1)S(1)} %get-tuple-element.24.local_ref, bf16[256,256]{1,0:T(8,128)(2,1)S(1)} %get-tuple-element.25.order_ref, bf16[976,1024]{1,0:T(8,128)(2,1)S(1)} %bitcast.6, ...), custom_call_target="tpu_custom_call" | custom-call | flops 2990000128 | bytes 262144 | tf_op jit(solution)/shard_map/send/pallas_call | solution.py:348
  7.1 2.0 %collective-permute-start.9 = (bf16[244,1024]{1,0:T(8,128)(2,1)S(1)}, bf16[244,1024]{1,0:T(8,128)(2,1)S(1)}, u32[]{:S(2)}, u32[]{:S(2)}) collective-permute-start(bf16[244,1024]{1,0:T(8,128)(2,1)S(1)} %send.1.after_ref), channel_id=1, source_target_pairs={{0,2},{1,3},{2,0},{3,1},{4,6},{5,7},{6,4},{7,5},{8,10},{9,11},{10,... | collective-permute-start | bytes 1499144 | tf_op jit(solution)/shard_map/ppermute | solution.py:636
  9.1 0.3 %collective-permute-done.refs_2_ = bf16[2,32,1024]{2,1,0:T(8,128)(2,1)S(1)} collective-permute-done((bf16[2,32,1024]{2,1,0:T(8,128)(2,1)S(1)}, bf16[2,32,1024]{2,1,0:T(8,128)(2,1)S(1)}, u32[]{:S(2)}, u32[]{:S(2)}) %collective-permute-start) | collective-permute-done | bytes 131104 | tf_op jit(solution)/shard_map/ppermute | solution.py:636
  9.4 0.1 merge.1
  9.5 2.9 %collective-permute-start.7 = (bf16[32,1024]{1,0:T(8,128)(2,1)S(1)}, bf16[32,1024]{1,0:T(8,128)(2,1)S(1)}, u32[]{:S(2)}, u32[]{:S(2)}) collective-permute-start(bf16[32,1024]{1,0:T(8,128)(2,1)S(1)} %get-tuple-element.32), channel_id=1, source_target_pairs={{0,16},{4,20},{8,24},{12,28},{16,0},{20,4},{24,8},{28,12},{1,17},{... | collective-permute-start | bytes 196616 | tf_op jit(solution)/shard_map/ppermute | solution.py:636
  12.4 1.3 %collective-permute-start.5 = (bf16[32,1024]{1,0:T(8,128)(2,1)S(1)}, bf16[32,1024]{1,0:T(8,128)(2,1)S(1)}, u32[]{:S(2)}, u32[]{:S(2)}) collective-permute-start(bf16[32,1024]{1,0:T(8,128)(2,1)S(1)} %get-tuple-element.32), channel_id=1, source_target_pairs={{0,24},{4,28},{8,16},{12,20},{16,8},{20,12},{24,0},{28,4},{1,25},{... | collective-permute-start | bytes 196616 | tf_op jit(solution)/shard_map/ppermute | solution.py:636
  13.8 0.2 %collective-permute-start.3 = (bf16[32,1024]{1,0:T(8,128)(2,1)S(1)}, bf16[32,1024]{1,0:T(8,128)(2,1)S(1)}, u32[]{:S(2)}, u32[]{:S(2)}) collective-permute-start(bf16[32,1024]{1,0:T(8,128)(2,1)S(1)} %get-tuple-element.26.after_ref), channel_id=1, source_target_pairs={{0,8},{4,12},{8,0},{12,4},{16,24},{20,28},{24,16},{28,20},{1,9},{5... | collective-permute-start | bytes 196616 | tf_op jit(solution)/shard_map/ppermute | solution.py:636
  14.0 0.0 collective-permute-start.2
  14.0 1.9 %keep.1.refs_4_ = f32[244,1024]{1,0:T(8,128)S(1)} custom-call(bf16[256,256]{1,0:T(8,128)(2,1)S(1)} %get-tuple-element.24.local_ref, bf16[256,256]{1,0:T(8,128)(2,1)S(1)} %get-tuple-element.25.order_ref, bf16[976,1024]{1,0:T(8,128)(2,1)S(1)} %bitcast.7, bf16[976,1024]{1,0:T(8,128)(2,1)S(1)} %bitcast.11, ...), custom_call_target="tpu_custom_call" | custom-call | flops 690000000 | bytes 262144 | tf_op jit(solution)/shard_map/keep/pallas_call | solution.py:364
  15.9 0.0 copy-start.2
  15.9 0.0 copy-start.3
  15.9 0.0 copy-start.4
  16.0 1.0 %local.1 = (f32[4,32,1024]{2,1,0:T(8,128)S(1)}, f32[4,32,1024]{2,1,0:T(8,128)S(1)}) custom-call(f32[3,2,1024]{2,1,0:T(2,128)S(1)} %get-tuple-element.20.lines_ref.refs_0_, f32[4,16,32,256]{3,2,1,0:T(8,128)S(1)} %get-tuple-element.21.states_ref, bf16[976,1024]{1,0:T(8,128)(2,1)S(1)} %bitcast.8, bf16[32,1024]{1,0:T(8,128)(2,1)S(1)} %get-tuple-element.26.after_ref), custom_call_target="tpu_custom_call" | custom-call | flops 575000000 | bytes 262144 | tf_op jit(solution)/shard_map/local/pallas_call | solution.py:242
  17.0 0.0 copy-done.2
  17.0 0.0 copy-done.3
  17.0 0.0 copy-done.4
  17.0 0.8 %tables.1 = (bf16[8,256,256]{2,1,0:T(8,128)(2,1)S(1)}, f32[4,8,256]{2,1,0:T(8,128)S(1)}, bf16[2,256,128]{2,1,0:T(8,128)(2,1)S(1)}) custom-call(f32[1,16]{1,0:T(1,128)S(1)} %bitcast.13, s32[2,128]{1,0:T(2,128)S(1)} %copy-done.3, bf16[60,60]{1,0:T(8,128)(2,1)S(1)} %bitcast.12, f32[4,32,1024]{2,1,0:T(8,128)S(1)} %get-tuple-element.27.after_ref.own_ref), custom_call_target="tpu_custom_call" | custom-call | flops 460000000 | bytes 262144 | tf_op jit(solution)/shard_map/tables/pallas_call | solution.py:423
  17.8 0.0 collective-permute-done.7.refs_2_
  17.8 0.6 %collective-permute-start.8 = (bf16[32,1024]{1,0:T(8,128)(2,1)S(1)}, bf16[32,1024]{1,0:T(8,128)(2,1)S(1)}, u32[]{:S(2)}, u32[]{:S(2)}) collective-permute-start(bf16[32,1024]{1,0:T(8,128)(2,1)S(1)} %collective-permute-done.7.refs_2_), channel_id=1, source_target_pairs={{0,1},{1,0},{2,3},{3,2},{4,5},{5,4},{6,7},{7,6},{8,9},{9,8},{10,11... | collective-permute-start | bytes 196616 | tf_op jit(solution)/shard_map/ppermute | solution.py:636
  18.4 0.2 %collective-permute-done.5.refs_1_ = bf16[32,1024]{1,0:T(8,128)(2,1)S(1)} collective-permute-done((bf16[32,1024]{1,0:T(8,128)(2,1)S(1)}, bf16[32,1024]{1,0:T(8,128)(2,1)S(1)}, u32[]{:S(2)}, u32[]{:S(2)}) %collective-permute-start.5) | collective-permute-done | bytes 65568 | tf_op jit(solution)/shard_map/ppermute | solution.py:636
  18.6 0.0 collective-permute-start.6
  18.6 0.1 collective-permute-done.3.refs_0_
  18.7 0.4 %collective-permute-start.4 = (bf16[32,1024]{1,0:T(8,128)(2,1)S(1)}, bf16[32,1024]{1,0:T(8,128)(2,1)S(1)}, u32[]{:S(2)}, u32[]{:S(2)}) collective-permute-start(bf16[32,1024]{1,0:T(8,128)(2,1)S(1)} %collective-permute-done.3.refs_0_), channel_id=1, source_target_pairs={{0,1},{1,0},{2,3},{3,2},{4,5},{5,4},{6,7},{7,6},{8,9},{9,8},{10,11... | collective-permute-start | bytes 196616 | tf_op jit(solution)/shard_map/ppermute | solution.py:636
  19.1 0.8 %rows.1.base_ref = f32[244,1024]{1,0:T(8,128)S(1)} custom-call(f32[4,32,1024]{2,1,0:T(8,128)S(1)} %get-tuple-element.34.own_ref, f32[2,19,2,1024]{3,2,1,0:T(2,128)S(1)} %get-tuple-element.28.coef_ref, bf16[8,256,256]{2,1,0:T(8,128)(2,1)S(1)} %get-tuple-element.29.mat_ref, f32[4,8,256]{2,1,0:T(8,128)S(1)} %get-tuple-element.30.row_coef_ref, ...), custom_call_target="tpu_custom_call" | custom-call | flops 1380000000 | bytes 262144 | tf_op jit(solution)/shard_map/rows/pallas_call | solution.py:508
  19.9 0.0 collective-permute-done.8.last_3_ref
  20.0 0.0 collective-permute-done.6.last_2_ref
  20.0 0.1 collective-permute-done.4.last_1_ref
  20.0 0.0 collective-permute-done.2.part_ref
  20.0 0.8 %join.1.total_ref = f32[244,1024]{1,0:T(8,128)S(1)} custom-call(f32[4,32,1024]{2,1,0:T(8,128)S(1)} %get-tuple-element.27.after_ref.own_ref, f32[2,19,2,1024]{3,2,1,0:T(2,128)S(1)} %get-tuple-element.28.coef_ref, bf16[8,256,256]{2,1,0:T(8,128)(2,1)S(1)} %get-tuple-element.29.mat_ref, f32[4,8,256]{2,1,0:T(8,128)S(1)} %get-tuple-element.30.row_coef_ref, ...), custom_call_target="tpu_custom_call" | custom-call | flops 920000000 | bytes 262144 | tf_op jit(solution)/shard_map/join/pallas_call | solution.py:534
  20.9 0.0 collective-permute-done.9.came_ref
  20.9 0.9 %final.1 = bf16[61,4,1024]{2,1,0:T(4,128)(2,1)} custom-call(f32[244,1024]{1,0:T(8,128)S(1)} %join.1.total_ref, bf16[244,1024]{1,0:T(8,128)(2,1)S(1)} %collective-permute-done.9.came_ref), custom_call_target="tpu_custom_call" | custom-call | flops 920000000 | bytes 262144 | tf_op jit(solution)/shard_map/final/pallas_call | solution.py:564
  (1 shorter events, 0.0 us)
Async XLA Ops:
  0.0 5.3 %collective-permute-start.1 = (bf16[976,1024]{1,0:T(8,128)(2,1)}, bf16[976,1024]{1,0:T(8,128)(2,1)S(1)}, u32[]{:S(2)}, u32[]{:S(2)}) collective-permute-start(bf16[976,1024]{1,0:T(8,128)(2,1)} %bitcast.9), channel_id=1, source_target_pairs={{0,1},{1,0},{2,3},{3,2},{4,5},{5,4},{6,7},{7,6},{8,9},{9,8},{10,11... | collective-permute-start | bytes 5996552 | tf_op jit(solution)/shard_map/ppermute | solution.py:636
  0.5 4.8 %copy-start = (bf16[61,16,1024]{2,1,0:T(8,128)(2,1)S(1)}, bf16[61,16,1024]{2,1,0:T(8,128)(2,1)}, u32[]{:S(2)}) copy-start(bf16[61,16,1024]{2,1,0:T(8,128)(2,1)} %param.7) | copy-start | bytes 5996548
  0.5 4.8 %copy-start.1 = (bf16[1,61,16,1024]{3,2,1,0:T(8,128)(2,1)S(1)}, bf16[1,61,16,1024]{3,2,1,0:T(8,128)(2,1)}, u32[]{:S(2)}) copy-start(bf16[1,61,16,1024]{3,2,1,0:T(8,128)(2,1)} %param.13) | copy-start | bytes 5996548
  2.7 6.7 %collective-permute-start = (bf16[2,32,1024]{2,1,0:T(8,128)(2,1)S(1)}, bf16[2,32,1024]{2,1,0:T(8,128)(2,1)S(1)}, u32[]{:S(2)}, u32[]{:S(2)}) collective-permute-start(bf16[2,32,1024]{2,1,0:T(8,128)(2,1)S(1)} %get-tuple-element.22.after_ref.refs_1_), channel_id=1, source_target_pairs={{0,4},{4,0},{8,12},{12,8},{16,20},{20,16},{24,28},{28,24},{1,5},{5... | collective-permute-start | bytes 393224 | tf_op jit(solution)/shard_map/ppermute | solution.py:636
  7.1 13.8 %collective-permute-start.9 = (bf16[244,1024]{1,0:T(8,128)(2,1)S(1)}, bf16[244,1024]{1,0:T(8,128)(2,1)S(1)}, u32[]{:S(2)}, u32[]{:S(2)}) collective-permute-start(bf16[244,1024]{1,0:T(8,128)(2,1)S(1)} %send.1.after_ref), channel_id=1, source_target_pairs={{0,2},{1,3},{2,0},{3,1},{4,6},{5,7},{6,4},{7,5},{8,10},{9,11},{10,... | collective-permute-start | bytes 1499144 | tf_op jit(solution)/shard_map/ppermute | solution.py:636
  9.5 8.3 %collective-permute-start.7 = (bf16[32,1024]{1,0:T(8,128)(2,1)S(1)}, bf16[32,1024]{1,0:T(8,128)(2,1)S(1)}, u32[]{:S(2)}, u32[]{:S(2)}) collective-permute-start(bf16[32,1024]{1,0:T(8,128)(2,1)S(1)} %get-tuple-element.32), channel_id=1, source_target_pairs={{0,16},{4,20},{8,24},{12,28},{16,0},{20,4},{24,8},{28,12},{1,17},{... | collective-permute-start | bytes 196616 | tf_op jit(solution)/shard_map/ppermute | solution.py:636
  12.4 6.2 %collective-permute-start.5 = (bf16[32,1024]{1,0:T(8,128)(2,1)S(1)}, bf16[32,1024]{1,0:T(8,128)(2,1)S(1)}, u32[]{:S(2)}, u32[]{:S(2)}) collective-permute-start(bf16[32,1024]{1,0:T(8,128)(2,1)S(1)} %get-tuple-element.32), channel_id=1, source_target_pairs={{0,24},{4,28},{8,16},{12,20},{16,8},{20,12},{24,0},{28,4},{1,25},{... | collective-permute-start | bytes 196616 | tf_op jit(solution)/shard_map/ppermute | solution.py:636
  13.8 5.0 %collective-permute-start.3 = (bf16[32,1024]{1,0:T(8,128)(2,1)S(1)}, bf16[32,1024]{1,0:T(8,128)(2,1)S(1)}, u32[]{:S(2)}, u32[]{:S(2)}) collective-permute-start(bf16[32,1024]{1,0:T(8,128)(2,1)S(1)} %get-tuple-element.26.after_ref), channel_id=1, source_target_pairs={{0,8},{4,12},{8,0},{12,4},{16,24},{20,28},{24,16},{28,20},{1,9},{5... | collective-permute-start | bytes 196616 | tf_op jit(solution)/shard_map/ppermute | solution.py:636
  14.0 6.1 %collective-permute-start.2 = (bf16[2,32,1024]{2,1,0:T(8,128)(2,1)S(1)}, bf16[2,32,1024]{2,1,0:T(8,128)(2,1)S(1)}, u32[]{:S(2)}, u32[]{:S(2)}) collective-permute-start(bf16[2,32,1024]{2,1,0:T(8,128)(2,1)S(1)} %get-tuple-element.31.part_ref), channel_id=1, source_target_pairs={{0,1},{1,0},{2,3},{3,2},{4,5},{5,4},{6,7},{7,6},{8,9},{9,8},{10,11... | collective-permute-start | bytes 393224 | tf_op jit(solution)/shard_map/ppermute | solution.py:636
  15.9 1.1 %copy-start.2 = (bf16[1,60,60]{2,1,0:T(8,128)(2,1)S(1)}, bf16[1,60,60]{2,1,0:T(8,128)(2,1)}, u32[]{:S(2)}) copy-start(bf16[1,60,60]{2,1,0:T(8,128)(2,1)} %param.8) | copy-start | bytes 21604
  15.9 1.0 %copy-start.3 = (s32[2,128]{1,0:T(2,128)S(1)}, s32[2,128]{1,0:T(2,128)}, u32[]{:S(2)}) copy-start(s32[2,128]{1,0:T(2,128)} %entries_ref.1) | copy-start | bytes 3076
  15.9 1.0 %copy-start.4 = (f32[16]{0:T(128)S(1)}, f32[16]{0:T(128)}, u32[]{:S(2)}) copy-start(f32[16]{0:T(128)} %table_hbm.1) | copy-start | bytes 196
  17.8 2.2 %collective-permute-start.8 = (bf16[32,1024]{1,0:T(8,128)(2,1)S(1)}, bf16[32,1024]{1,0:T(8,128)(2,1)S(1)}, u32[]{:S(2)}, u32[]{:S(2)}) collective-permute-start(bf16[32,1024]{1,0:T(8,128)(2,1)S(1)} %collective-permute-done.7.refs_2_), channel_id=1, source_target_pairs={{0,1},{1,0},{2,3},{3,2},{4,5},{5,4},{6,7},{7,6},{8,9},{9,8},{10,11... | collective-permute-start | bytes 196616 | tf_op jit(solution)/shard_map/ppermute | solution.py:636
  18.6 1.3 %collective-permute-start.6 = (bf16[32,1024]{1,0:T(8,128)(2,1)S(1)}, bf16[32,1024]{1,0:T(8,128)(2,1)S(1)}, u32[]{:S(2)}, u32[]{:S(2)}) collective-permute-start(bf16[32,1024]{1,0:T(8,128)(2,1)S(1)} %collective-permute-done.5.refs_1_), channel_id=1, source_target_pairs={{0,1},{1,0},{2,3},{3,2},{4,5},{5,4},{6,7},{7,6},{8,9},{9,8},{10,11... | collective-permute-start | bytes 196616 | tf_op jit(solution)/shard_map/ppermute | solution.py:636
  18.7 1.3 %collective-permute-start.4 = (bf16[32,1024]{1,0:T(8,128)(2,1)S(1)}, bf16[32,1024]{1,0:T(8,128)(2,1)S(1)}, u32[]{:S(2)}, u32[]{:S(2)}) collective-permute-start(bf16[32,1024]{1,0:T(8,128)(2,1)S(1)} %collective-permute-done.3.refs_0_), channel_id=1, source_target_pairs={{0,1},{1,0},{2,3},{3,2},{4,5},{5,4},{6,7},{7,6},{8,9},{9,8},{10,11... | collective-permute-start | bytes 196616 | tf_op jit(solution)/shard_map/ppermute | solution.py:636

commit v12 on v11

--- a/solution.py
+++ b/solution.py
@@ -119,7 +119,7 @@
                     field_hbm.at[held, place], held_ref.at[0 : held.stop - held.start, place], arrived.at[part]
                 )
                 if begin:
-                    copy.start()
+                    copy.start(priority=1)
                     clear_rest(held_ref, held)
                 else:
                     copy.wait()

time: 22.1 us -> 22.1 us (level)
  transfers between devices with their start and end apart: 10 -> 10, of which waited for: 4 -> 5; matrix products, arithmetic and copies ran while one was open for 0% -> 0% of each run, Pallas kernels for 35% -> 35%
where the time goes in v12:
time: 22.1 us; the launch traced here: 21.8 us
  starting transfers between devices  10.6 us (48%)
  Pallas kernels  10.3 us (47%)
  waiting for transfers between devices  0.79 us (4%)
    ppermute x10, starting transfers between devices, swap(): lax.ppermute(array, axis, [(i, i ^ flip) for i in range(lax.axis_size(axi...  10.6 us
    pallas_call x1, Pallas kernels, ends_call(): pl.pallas_call(functools.partial(ends_kernel, levels, steps, total // col...  2.09 us
    pallas_call x1, Pallas kernels, keep_call(): pl.pallas_call(functools.partial(keep_kernel, cols), name='keep', in_spec...  1.94 us
    pallas_call x1, Pallas kernels, send_call(): pl.pallas_call(functools.partial(send_kernel, cols), name='send', in_spec...  1.77 us
    pallas_call x1, Pallas kernels, local_call(): pl.pallas_call(functools.partial(local_kernel, levels, total // cols), na...  1.02 us
    pallas_call x1, Pallas kernels, final_call(): pl.pallas_call(functools.partial(final_kernel, scale), name='final', in_s...  0.93 us
    pallas_call x1, Pallas kernels, rows_call(): pl.pallas_call(functools.partial(rows_kernel, levels, scale), name='rows'...  0.8 us
    pallas_call x1, Pallas kernels, join_call(): pl.pallas_call(functools.partial(join_kernel, levels), name='join', in_sp...  0.8 us
  transfers between devices with their start and end apart: 10, of which 5 were waited for; matrix products, arithmetic and copies ran while one was open for 0% of the time, Pallas kernels for 35%

profile of v12, /device:TPU:0, one launch (start us, length us, event | category | flops | bytes accessed | tf_op | source)
XLA Modules:
  0.0 21.8 jit_solution(3614135607664004917)
XLA Ops:
  0.0 0.5 %collective-permute-start.1 = (bf16[976,1024]{1,0:T(8,128)(2,1)}, bf16[976,1024]{1,0:T(8,128)(2,1)S(1)}, u32[]{:S(2)}, u32[]{:S(2)}) collective-permute-start(bf16[976,1024]{1,0:T(8,128)(2,1)} %bitcast.9), channel_id=1, source_target_pairs={{0,1},{1,0},{2,3},{3,2},{4,5},{5,4},{6,7},{7,6},{8,9},{9,8},{10,11... | collective-permute-start | bytes 5996552 | tf_op jit(solution)/shard_map/ppermute | solution.py:636
  0.5 0.0 copy-start
  0.5 0.0 copy-start.1
  0.5 2.1 %ends.1 = (bf16[2,32,1024]{2,1,0:T(8,128)(2,1)S(1)}, f32[4,16,32,256]{3,2,1,0:T(8,128)S(1)}, f32[3,2,1024]{2,1,0:T(2,128)S(1)}, bf16[64,256]{1,0:T(8,128)(2,1)S(...) custom-call(f32[16]{0:T(128)} %table_hbm.1, s32[2,1024]{1,0:T(2,128)} %entries_hbm.1, ...), custom_call_target="tpu_custom_call" | custom-call | flops 2415000064 | bytes 262144 | tf_op jit(solution)/shard_map/ends/pallas_call | solution.py:167
  2.6 2.6 %collective-permute-start = (bf16[2,32,1024]{2,1,0:T(8,128)(2,1)S(1)}, bf16[2,32,1024]{2,1,0:T(8,128)(2,1)S(1)}, u32[]{:S(2)}, u32[]{:S(2)}) collective-permute-start(bf16[2,32,1024]{2,1,0:T(8,128)(2,1)S(1)} %get-tuple-element.22.after_ref.refs_1_), channel_id=1, source_target_pairs={{0,4},{4,0},{8,12},{12,8},{16,20},{20,16},{24,28},{28,24},{1,5},{5... | collective-permute-start | bytes 393224 | tf_op jit(solution)/shard_map/ppermute | solution.py:636
  5.2 0.0 collective-permute-done.1.other_ref
  5.2 0.0 copy-done
  5.2 0.0 copy-done.1
  5.2 1.8 %send.1.after_ref = bf16[244,1024]{1,0:T(8,128)(2,1)S(1)} custom-call(bf16[64,256]{1,0:T(8,128)(2,1)S(1)} %get-tuple-element.23.perm_ref, bf16[256,256]{1,0:T(8,128)(2,1)S(1)} %get-tuple-element.24.local_ref, bf16[256,256]{1,0:T(8,128)(2,1)S(1)} %get-tuple-element.25.order_ref, bf16[976,1024]{1,0:T(8,128)(2,1)S(1)} %bitcast.6, ...), custom_call_target="tpu_custom_call" | custom-call | flops 2990000128 | bytes 262144 | tf_op jit(solution)/shard_map/send/pallas_call | solution.py:348
  6.9 2.1 %collective-permute-start.9 = (bf16[244,1024]{1,0:T(8,128)(2,1)S(1)}, bf16[244,1024]{1,0:T(8,128)(2,1)S(1)}, u32[]{:S(2)}, u32[]{:S(2)}) collective-permute-start(bf16[244,1024]{1,0:T(8,128)(2,1)S(1)} %send.1.after_ref), channel_id=1, source_target_pairs={{0,2},{1,3},{2,0},{3,1},{4,6},{5,7},{6,4},{7,5},{8,10},{9,11},{10,... | collective-permute-start | bytes 1499144 | tf_op jit(solution)/shard_map/ppermute | solution.py:636
  9.1 0.2 collective-permute-done.refs_2_
  9.3 0.1 merge.1
  9.4 2.9 %collective-permute-start.7 = (bf16[32,1024]{1,0:T(8,128)(2,1)S(1)}, bf16[32,1024]{1,0:T(8,128)(2,1)S(1)}, u32[]{:S(2)}, u32[]{:S(2)}) collective-permute-start(bf16[32,1024]{1,0:T(8,128)(2,1)S(1)} %get-tuple-element.32), channel_id=1, source_target_pairs={{0,16},{4,20},{8,24},{12,28},{16,0},{20,4},{24,8},{28,12},{1,17},{... | collective-permute-start | bytes 196616 | tf_op jit(solution)/shard_map/ppermute | solution.py:636
  12.3 1.4 %collective-permute-start.5 = (bf16[32,1024]{1,0:T(8,128)(2,1)S(1)}, bf16[32,1024]{1,0:T(8,128)(2,1)S(1)}, u32[]{:S(2)}, u32[]{:S(2)}) collective-permute-start(bf16[32,1024]{1,0:T(8,128)(2,1)S(1)} %get-tuple-element.32), channel_id=1, source_target_pairs={{0,24},{4,28},{8,16},{12,20},{16,8},{20,12},{24,0},{28,4},{1,25},{... | collective-permute-start | bytes 196616 | tf_op jit(solution)/shard_map/ppermute | solution.py:636
  13.6 0.2 %collective-permute-start.3 = (bf16[32,1024]{1,0:T(8,128)(2,1)S(1)}, bf16[32,1024]{1,0:T(8,128)(2,1)S(1)}, u32[]{:S(2)}, u32[]{:S(2)}) collective-permute-start(bf16[32,1024]{1,0:T(8,128)(2,1)S(1)} %get-tuple-element.26.after_ref), channel_id=1, source_target_pairs={{0,8},{4,12},{8,0},{12,4},{16,24},{20,28},{24,16},{28,20},{1,9},{5... | collective-permute-start | bytes 196616 | tf_op jit(solution)/shard_map/ppermute | solution.py:636
  13.9 0.0 collective-permute-start.2
  13.9 1.9 %keep.1.refs_4_ = f32[244,1024]{1,0:T(8,128)S(1)} custom-call(bf16[256,256]{1,0:T(8,128)(2,1)S(1)} %get-tuple-element.24.local_ref, bf16[256,256]{1,0:T(8,128)(2,1)S(1)} %get-tuple-element.25.order_ref, bf16[976,1024]{1,0:T(8,128)(2,1)S(1)} %bitcast.7, bf16[976,1024]{1,0:T(8,128)(2,1)S(1)} %bitcast.11, ...), custom_call_target="tpu_custom_call" | custom-call | flops 690000000 | bytes 262144 | tf_op jit(solution)/shard_map/keep/pallas_call | solution.py:364
  15.8 0.0 copy-start.2
  15.8 0.0 copy-start.3
  15.8 0.0 copy-start.4
  15.9 1.0 %local.1 = (f32[4,32,1024]{2,1,0:T(8,128)S(1)}, f32[4,32,1024]{2,1,0:T(8,128)S(1)}) custom-call(f32[3,2,1024]{2,1,0:T(2,128)S(1)} %get-tuple-element.20.lines_ref.refs_0_, f32[4,16,32,256]{3,2,1,0:T(8,128)S(1)} %get-tuple-element.21.states_ref, bf16[976,1024]{1,0:T(8,128)(2,1)S(1)} %bitcast.8, bf16[32,1024]{1,0:T(8,128)(2,1)S(1)} %get-tuple-element.26.after_ref), custom_call_target="tpu_custom_call" | custom-call | flops 575000000 | bytes 262144 | tf_op jit(solution)/shard_map/local/pallas_call | solution.py:242
  16.9 0.0 copy-done.2
  16.9 0.0 copy-done.3
  16.9 0.0 copy-done.4
  16.9 0.8 %tables.1 = (bf16[8,256,256]{2,1,0:T(8,128)(2,1)S(1)}, f32[4,8,256]{2,1,0:T(8,128)S(1)}, bf16[2,256,128]{2,1,0:T(8,128)(2,1)S(1)}) custom-call(f32[1,16]{1,0:T(1,128)S(1)} %bitcast.13, s32[2,128]{1,0:T(2,128)S(1)} %copy-done.3, bf16[60,60]{1,0:T(8,128)(2,1)S(1)} %bitcast.12, f32[4,32,1024]{2,1,0:T(8,128)S(1)} %get-tuple-element.27.after_ref.own_ref), custom_call_target="tpu_custom_call" | custom-call | flops 460000000 | bytes 262144 | tf_op jit(solution)/shard_map/tables/pallas_call | solution.py:423
  17.7 0.0 collective-permute-done.7.refs_2_
  17.7 0.6 %collective-permute-start.8 = (bf16[32,1024]{1,0:T(8,128)(2,1)S(1)}, bf16[32,1024]{1,0:T(8,128)(2,1)S(1)}, u32[]{:S(2)}, u32[]{:S(2)}) collective-permute-start(bf16[32,1024]{1,0:T(8,128)(2,1)S(1)} %collective-permute-done.7.refs_2_), channel_id=1, source_target_pairs={{0,1},{1,0},{2,3},{3,2},{4,5},{5,4},{6,7},{7,6},{8,9},{9,8},{10,11... | collective-permute-start | bytes 196616 | tf_op jit(solution)/shard_map/ppermute | solution.py:636
  18.3 0.2 %collective-permute-done.5.refs_1_ = bf16[32,1024]{1,0:T(8,128)(2,1)S(1)} collective-permute-done((bf16[32,1024]{1,0:T(8,128)(2,1)S(1)}, bf16[32,1024]{1,0:T(8,128)(2,1)S(1)}, u32[]{:S(2)}, u32[]{:S(2)}) %collective-permute-start.5) | collective-permute-done | bytes 65568 | tf_op jit(solution)/shard_map/ppermute | solution.py:636
  18.5 0.0 collective-permute-start.6
  18.5 0.1 collective-permute-done.3.refs_0_
  18.6 0.4 %collective-permute-start.4 = (bf16[32,1024]{1,0:T(8,128)(2,1)S(1)}, bf16[32,1024]{1,0:T(8,128)(2,1)S(1)}, u32[]{:S(2)}, u32[]{:S(2)}) collective-permute-start(bf16[32,1024]{1,0:T(8,128)(2,1)S(1)} %collective-permute-done.3.refs_0_), channel_id=1, source_target_pairs={{0,1},{1,0},{2,3},{3,2},{4,5},{5,4},{6,7},{7,6},{8,9},{9,8},{10,11... | collective-permute-start | bytes 196616 | tf_op jit(solution)/shard_map/ppermute | solution.py:636
  19.0 0.8 %rows.1.base_ref = f32[244,1024]{1,0:T(8,128)S(1)} custom-call(f32[4,32,1024]{2,1,0:T(8,128)S(1)} %get-tuple-element.34.own_ref, f32[2,19,2,1024]{3,2,1,0:T(2,128)S(1)} %get-tuple-element.28.coef_ref, bf16[8,256,256]{2,1,0:T(8,128)(2,1)S(1)} %get-tuple-element.29.mat_ref, f32[4,8,256]{2,1,0:T(8,128)S(1)} %get-tuple-element.30.row_coef_ref, ...), custom_call_target="tpu_custom_call" | custom-call | flops 1380000000 | bytes 262144 | tf_op jit(solution)/shard_map/rows/pallas_call | solution.py:508
  19.8 0.0 collective-permute-done.8.last_3_ref
  19.8 0.0 collective-permute-done.6.last_2_ref
  19.9 0.1 collective-permute-done.4.last_1_ref
  19.9 0.0 collective-permute-done.2.part_ref
  19.9 0.8 %join.1.total_ref = f32[244,1024]{1,0:T(8,128)S(1)} custom-call(f32[4,32,1024]{2,1,0:T(8,128)S(1)} %get-tuple-element.27.after_ref.own_ref, f32[2,19,2,1024]{3,2,1,0:T(2,128)S(1)} %get-tuple-element.28.coef_ref, bf16[8,256,256]{2,1,0:T(8,128)(2,1)S(1)} %get-tuple-element.29.mat_ref, f32[4,8,256]{2,1,0:T(8,128)S(1)} %get-tuple-element.30.row_coef_ref, ...), custom_call_target="tpu_custom_call" | custom-call | flops 920000000 | bytes 262144 | tf_op jit(solution)/shard_map/join/pallas_call | solution.py:534
  20.7 0.2 collective-permute-done.9.came_ref
  20.9 0.9 %final.1 = bf16[61,4,1024]{2,1,0:T(4,128)(2,1)} custom-call(f32[244,1024]{1,0:T(8,128)S(1)} %join.1.total_ref, bf16[244,1024]{1,0:T(8,128)(2,1)S(1)} %collective-permute-done.9.came_ref), custom_call_target="tpu_custom_call" | custom-call | flops 920000000 | bytes 262144 | tf_op jit(solution)/shard_map/final/pallas_call | solution.py:564
  (1 shorter events, 0.0 us)
Async XLA Ops:
  0.0 5.2 %collective-permute-start.1 = (bf16[976,1024]{1,0:T(8,128)(2,1)}, bf16[976,1024]{1,0:T(8,128)(2,1)S(1)}, u32[]{:S(2)}, u32[]{:S(2)}) collective-permute-start(bf16[976,1024]{1,0:T(8,128)(2,1)} %bitcast.9), channel_id=1, source_target_pairs={{0,1},{1,0},{2,3},{3,2},{4,5},{5,4},{6,7},{7,6},{8,9},{9,8},{10,11... | collective-permute-start | bytes 5996552 | tf_op jit(solution)/shard_map/ppermute | solution.py:636
  0.5 4.7 %copy-start = (bf16[61,16,1024]{2,1,0:T(8,128)(2,1)S(1)}, bf16[61,16,1024]{2,1,0:T(8,128)(2,1)}, u32[]{:S(2)}) copy-start(bf16[61,16,1024]{2,1,0:T(8,128)(2,1)} %param.7) | copy-start | bytes 5996548
  0.5 4.7 %copy-start.1 = (bf16[1,61,16,1024]{3,2,1,0:T(8,128)(2,1)S(1)}, bf16[1,61,16,1024]{3,2,1,0:T(8,128)(2,1)}, u32[]{:S(2)}) copy-start(bf16[1,61,16,1024]{3,2,1,0:T(8,128)(2,1)} %param.13) | copy-start | bytes 5996548
  2.6 6.7 %collective-permute-start = (bf16[2,32,1024]{2,1,0:T(8,128)(2,1)S(1)}, bf16[2,32,1024]{2,1,0:T(8,128)(2,1)S(1)}, u32[]{:S(2)}, u32[]{:S(2)}) collective-permute-start(bf16[2,32,1024]{2,1,0:T(8,128)(2,1)S(1)} %get-tuple-element.22.after_ref.refs_1_), channel_id=1, source_target_pairs={{0,4},{4,0},{8,12},{12,8},{16,20},{20,16},{24,28},{28,24},{1,5},{5... | collective-permute-start | bytes 393224 | tf_op jit(solution)/shard_map/ppermute | solution.py:636
  6.9 13.9 %collective-permute-start.9 = (bf16[244,1024]{1,0:T(8,128)(2,1)S(1)}, bf16[244,1024]{1,0:T(8,128)(2,1)S(1)}, u32[]{:S(2)}, u32[]{:S(2)}) collective-permute-start(bf16[244,1024]{1,0:T(8,128)(2,1)S(1)} %send.1.after_ref), channel_id=1, source_target_pairs={{0,2},{1,3},{2,0},{3,1},{4,6},{5,7},{6,4},{7,5},{8,10},{9,11},{10,... | collective-permute-start | bytes 1499144 | tf_op jit(solution)/shard_map/ppermute | solution.py:636
  9.4 8.3 %collective-permute-start.7 = (bf16[32,1024]{1,0:T(8,128)(2,1)S(1)}, bf16[32,1024]{1,0:T(8,128)(2,1)S(1)}, u32[]{:S(2)}, u32[]{:S(2)}) collective-permute-start(bf16[32,1024]{1,0:T(8,128)(2,1)S(1)} %get-tuple-element.32), channel_id=1, source_target_pairs={{0,16},{4,20},{8,24},{12,28},{16,0},{20,4},{24,8},{28,12},{1,17},{... | collective-permute-start | bytes 196616 | tf_op jit(solution)/shard_map/ppermute | solution.py:636
  12.3 6.2 %collective-permute-start.5 = (bf16[32,1024]{1,0:T(8,128)(2,1)S(1)}, bf16[32,1024]{1,0:T(8,128)(2,1)S(1)}, u32[]{:S(2)}, u32[]{:S(2)}) collective-permute-start(bf16[32,1024]{1,0:T(8,128)(2,1)S(1)} %get-tuple-element.32), channel_id=1, source_target_pairs={{0,24},{4,28},{8,16},{12,20},{16,8},{20,12},{24,0},{28,4},{1,25},{... | collective-permute-start | bytes 196616 | tf_op jit(solution)/shard_map/ppermute | solution.py:636
  13.6 5.0 %collective-permute-start.3 = (bf16[32,1024]{1,0:T(8,128)(2,1)S(1)}, bf16[32,1024]{1,0:T(8,128)(2,1)S(1)}, u32[]{:S(2)}, u32[]{:S(2)}) collective-permute-start(bf16[32,1024]{1,0:T(8,128)(2,1)S(1)} %get-tuple-element.26.after_ref), channel_id=1, source_target_pairs={{0,8},{4,12},{8,0},{12,4},{16,24},{20,28},{24,16},{28,20},{1,9},{5... | collective-permute-start | bytes 196616 | tf_op jit(solution)/shard_map/ppermute | solution.py:636
  13.9 6.1 %collective-permute-start.2 = (bf16[2,32,1024]{2,1,0:T(8,128)(2,1)S(1)}, bf16[2,32,1024]{2,1,0:T(8,128)(2,1)S(1)}, u32[]{:S(2)}, u32[]{:S(2)}) collective-permute-start(bf16[2,32,1024]{2,1,0:T(8,128)(2,1)S(1)} %get-tuple-element.31.part_ref), channel_id=1, source_target_pairs={{0,1},{1,0},{2,3},{3,2},{4,5},{5,4},{6,7},{7,6},{8,9},{9,8},{10,11... | collective-permute-start | bytes 393224 | tf_op jit(solution)/shard_map/ppermute | solution.py:636
  15.8 1.1 %copy-start.2 = (bf16[1,60,60]{2,1,0:T(8,128)(2,1)S(1)}, bf16[1,60,60]{2,1,0:T(8,128)(2,1)}, u32[]{:S(2)}) copy-start(bf16[1,60,60]{2,1,0:T(8,128)(2,1)} %param.8) | copy-start | bytes 21604
  15.8 1.1 %copy-start.3 = (s32[2,128]{1,0:T(2,128)S(1)}, s32[2,128]{1,0:T(2,128)}, u32[]{:S(2)}) copy-start(s32[2,128]{1,0:T(2,128)} %entries_ref.1) | copy-start | bytes 3076
  15.8 1.1 %copy-start.4 = (f32[16]{0:T(128)S(1)}, f32[16]{0:T(128)}, u32[]{:S(2)}) copy-start(f32[16]{0:T(128)} %table_hbm.1) | copy-start | bytes 196
  17.7 2.1 %collective-permute-start.8 = (bf16[32,1024]{1,0:T(8,128)(2,1)S(1)}, bf16[32,1024]{1,0:T(8,128)(2,1)S(1)}, u32[]{:S(2)}, u32[]{:S(2)}) collective-permute-start(bf16[32,1024]{1,0:T(8,128)(2,1)S(1)} %collective-permute-done.7.refs_2_), channel_id=1, source_target_pairs={{0,1},{1,0},{2,3},{3,2},{4,5},{5,4},{6,7},{7,6},{8,9},{9,8},{10,11... | collective-permute-start | bytes 196616 | tf_op jit(solution)/shard_map/ppermute | solution.py:636
  18.5 1.3 %collective-permute-start.6 = (bf16[32,1024]{1,0:T(8,128)(2,1)S(1)}, bf16[32,1024]{1,0:T(8,128)(2,1)S(1)}, u32[]{:S(2)}, u32[]{:S(2)}) collective-permute-start(bf16[32,1024]{1,0:T(8,128)(2,1)S(1)} %collective-permute-done.5.refs_1_), channel_id=1, source_target_pairs={{0,1},{1,0},{2,3},{3,2},{4,5},{5,4},{6,7},{7,6},{8,9},{9,8},{10,11... | collective-permute-start | bytes 196616 | tf_op jit(solution)/shard_map/ppermute | solution.py:636
  18.6 1.3 %collective-permute-start.4 = (bf16[32,1024]{1,0:T(8,128)(2,1)S(1)}, bf16[32,1024]{1,0:T(8,128)(2,1)S(1)}, u32[]{:S(2)}, u32[]{:S(2)}) collective-permute-start(bf16[32,1024]{1,0:T(8,128)(2,1)S(1)} %collective-permute-done.3.refs_0_), channel_id=1, source_target_pairs={{0,1},{1,0},{2,3},{3,2},{4,5},{5,4},{6,7},{7,6},{8,9},{9,8},{10,11... | collective-permute-start | bytes 196616 | tf_op jit(solution)/shard_map/ppermute | solution.py:636

commit v13 on v12

--- a/solution.py
+++ b/solution.py
@@ -12,7 +12,7 @@
 CORES = 2
 LANES = 256
 ORDER = (1, 3, 2)
-FETCHES = 1
+FETCHES = 2
 BLOCK = 256
 MIB = 1 << 20
 VMEM = 32 * MIB
@@ -108,19 +108,22 @@
     parts = arrived.shape[0]
 
     def fetch(part, begin):
-        width = rows // parts
-        place = pl.ds(part * width, width)
+        step = subs * cols // parts
         for core in range(CORES):
             held = share_rows(slab_count * cols, cols, subs, core)
+            size = min(step, held.stop - held.start - part * step)
 
             @pl.when(share == core)
             def _():
                 copy = pltpu.make_async_copy(
-                    field_hbm.at[held, place], held_ref.at[0 : held.stop - held.start, place], arrived.at[part]
+                    field_hbm.at[held.start + part * step : held.start + part * step + size],
+                    held_ref.at[part * step : part * step + size],
+                    arrived.at[part],
                 )
                 if begin:
-                    copy.start(priority=1)
-                    clear_rest(held_ref, held)
+                    copy.start(priority=1 - part % 2)
+                    if part == parts - 1:
+                        clear_rest(held_ref, held)
                 else:
                     copy.wait()
 
@@ -148,8 +151,9 @@
     behind = reflected(decay, turn, tile, steps)
     lines_ref[0], lines_ref[1], lines_ref[2] = pair, decay, behind
     for piece in range(pieces):
-        if piece % (pieces // parts) == 0:
-            fetch(piece // (pieces // parts), False)
+        if piece == 0:
+            for k in range(parts):
+                fetch(k, False)
         part = slice(piece * lanes, (piece + 1) * lanes)
         gain, is_level = sweep_share(levels, share, perm, pair[:, part], held_ref[:, part], work.at[piece])
         turned = (decay * behind)[:, part]

time: 22.1 us -> 22.1 us (level)
  no operation moved by 1% of the time
where the time goes in v13:
time: 22.1 us; the launch traced here: 21.8 us
  starting transfers between devices  10.6 us (48%)
  Pallas kernels  10.3 us (47%)
  waiting for transfers between devices  0.79 us (4%)
    ppermute x10, starting transfers between devices, swap(): lax.ppermute(array, axis, [(i, i ^ flip) for i in range(lax.axis_size(axi...  10.6 us
    pallas_call x1, Pallas kernels, ends_call(): pl.pallas_call(functools.partial(ends_kernel, levels, steps, total // col...  2.07 us
    pallas_call x1, Pallas kernels, keep_call(): pl.pallas_call(functools.partial(keep_kernel, cols), name='keep', in_spec...  1.93 us
    pallas_call x1, Pallas kernels, send_call(): pl.pallas_call(functools.partial(send_kernel, cols), name='send', in_spec...  1.77 us
    pallas_call x1, Pallas kernels, local_call(): pl.pallas_call(functools.partial(local_kernel, levels, total // cols), na...  1.01 us
    pallas_call x1, Pallas kernels, final_call(): pl.pallas_call(functools.partial(final_kernel, scale), name='final', in_s...  0.93 us
    pallas_call x1, Pallas kernels, rows_call(): pl.pallas_call(functools.partial(rows_kernel, levels, scale), name='rows'...  0.8 us
    pallas_call x1, Pallas kernels, join_call(): pl.pallas_call(functools.partial(join_kernel, levels), name='join', in_sp...  0.8 us
  transfers between devices with their start and end apart: 10, of which 5 were waited for; matrix products, arithmetic and copies ran while one was open for 0% of the time, Pallas kernels for 35%

profile of v13, /device:TPU:0, one launch (start us, length us, event | category | flops | bytes accessed | tf_op | source)
XLA Modules:
  0.0 21.8 jit_solution(10227827831159756196)
XLA Ops:
  0.0 0.5 %collective-permute-start.1 = (bf16[976,1024]{1,0:T(8,128)(2,1)}, bf16[976,1024]{1,0:T(8,128)(2,1)S(1)}, u32[]{:S(2)}, u32[]{:S(2)}) collective-permute-start(bf16[976,1024]{1,0:T(8,128)(2,1)} %bitcast.9), channel_id=1, source_target_pairs={{0,1},{1,0},{2,3},{3,2},{4,5},{5,4},{6,7},{7,6},{8,9},{9,8},{10,11... | collective-permute-start | bytes 5996552 | tf_op jit(solution)/shard_map/ppermute | solution.py:640
  0.5 0.0 copy-start
  0.5 0.0 copy-start.1
  0.5 2.1 %ends.1 = (bf16[2,32,1024]{2,1,0:T(8,128)(2,1)S(1)}, f32[4,16,32,256]{3,2,1,0:T(8,128)S(1)}, f32[3,2,1024]{2,1,0:T(2,128)S(1)}, bf16[64,256]{1,0:T(8,128)(2,1)S(...) custom-call(f32[16]{0:T(128)} %table_hbm.1, s32[2,1024]{1,0:T(2,128)} %entries_hbm.1, ...), custom_call_target="tpu_custom_call" | custom-call | flops 2415000064 | bytes 262144 | tf_op jit(solution)/shard_map/ends/pallas_call | solution.py:171
  2.5 2.6 %collective-permute-start = (bf16[2,32,1024]{2,1,0:T(8,128)(2,1)S(1)}, bf16[2,32,1024]{2,1,0:T(8,128)(2,1)S(1)}, u32[]{:S(2)}, u32[]{:S(2)}) collective-permute-start(bf16[2,32,1024]{2,1,0:T(8,128)(2,1)S(1)} %get-tuple-element.22.after_ref.refs_1_), channel_id=1, source_target_pairs={{0,4},{4,0},{8,12},{12,8},{16,20},{20,16},{24,28},{28,24},{1,5},{5... | collective-permute-start | bytes 393224 | tf_op jit(solution)/shard_map/ppermute | solution.py:640
  5.1 0.0 collective-permute-done.1.other_ref
  5.1 0.0 copy-done
  5.1 0.0 copy-done.1
  5.2 1.8 %send.1.after_ref = bf16[244,1024]{1,0:T(8,128)(2,1)S(1)} custom-call(bf16[64,256]{1,0:T(8,128)(2,1)S(1)} %get-tuple-element.23.perm_ref, bf16[256,256]{1,0:T(8,128)(2,1)S(1)} %get-tuple-element.24.local_ref, bf16[256,256]{1,0:T(8,128)(2,1)S(1)} %get-tuple-element.25.order_ref, bf16[976,1024]{1,0:T(8,128)(2,1)S(1)} %bitcast.6, ...), custom_call_target="tpu_custom_call" | custom-call | flops 2990000128 | bytes 262144 | tf_op jit(solution)/shard_map/send/pallas_call | solution.py:352
  6.9 2.1 %collective-permute-start.9 = (bf16[244,1024]{1,0:T(8,128)(2,1)S(1)}, bf16[244,1024]{1,0:T(8,128)(2,1)S(1)}, u32[]{:S(2)}, u32[]{:S(2)}) collective-permute-start(bf16[244,1024]{1,0:T(8,128)(2,1)S(1)} %send.1.after_ref), channel_id=1, source_target_pairs={{0,2},{1,3},{2,0},{3,1},{4,6},{5,7},{6,4},{7,5},{8,10},{9,11},{10,... | collective-permute-start | bytes 1499144 | tf_op jit(solution)/shard_map/ppermute | solution.py:640
  9.1 0.2 collective-permute-done.refs_2_
  9.3 0.1 merge.1
  9.4 2.9 %collective-permute-start.7 = (bf16[32,1024]{1,0:T(8,128)(2,1)S(1)}, bf16[32,1024]{1,0:T(8,128)(2,1)S(1)}, u32[]{:S(2)}, u32[]{:S(2)}) collective-permute-start(bf16[32,1024]{1,0:T(8,128)(2,1)S(1)} %get-tuple-element.32), channel_id=1, source_target_pairs={{0,16},{4,20},{8,24},{12,28},{16,0},{20,4},{24,8},{28,12},{1,17},{... | collective-permute-start | bytes 196616 | tf_op jit(solution)/shard_map/ppermute | solution.py:640
  12.3 1.3 %collective-permute-start.5 = (bf16[32,1024]{1,0:T(8,128)(2,1)S(1)}, bf16[32,1024]{1,0:T(8,128)(2,1)S(1)}, u32[]{:S(2)}, u32[]{:S(2)}) collective-permute-start(bf16[32,1024]{1,0:T(8,128)(2,1)S(1)} %get-tuple-element.32), channel_id=1, source_target_pairs={{0,24},{4,28},{8,16},{12,20},{16,8},{20,12},{24,0},{28,4},{1,25},{... | collective-permute-start | bytes 196616 | tf_op jit(solution)/shard_map/ppermute | solution.py:640
  13.6 0.2 %collective-permute-start.3 = (bf16[32,1024]{1,0:T(8,128)(2,1)S(1)}, bf16[32,1024]{1,0:T(8,128)(2,1)S(1)}, u32[]{:S(2)}, u32[]{:S(2)}) collective-permute-start(bf16[32,1024]{1,0:T(8,128)(2,1)S(1)} %get-tuple-element.26.after_ref), channel_id=1, source_target_pairs={{0,8},{4,12},{8,0},{12,4},{16,24},{20,28},{24,16},{28,20},{1,9},{5... | collective-permute-start | bytes 196616 | tf_op jit(solution)/shard_map/ppermute | solution.py:640
  13.9 0.0 collective-permute-start.2
  13.9 1.9 %keep.1.refs_4_ = f32[244,1024]{1,0:T(8,128)S(1)} custom-call(bf16[256,256]{1,0:T(8,128)(2,1)S(1)} %get-tuple-element.24.local_ref, bf16[256,256]{1,0:T(8,128)(2,1)S(1)} %get-tuple-element.25.order_ref, bf16[976,1024]{1,0:T(8,128)(2,1)S(1)} %bitcast.7, bf16[976,1024]{1,0:T(8,128)(2,1)S(1)} %bitcast.11, ...), custom_call_target="tpu_custom_call" | custom-call | flops 690000000 | bytes 262144 | tf_op jit(solution)/shard_map/keep/pallas_call | solution.py:368
  15.8 0.0 copy-start.2
  15.8 0.0 copy-start.3
  15.8 0.0 copy-start.4
  15.8 1.0 %local.1 = (f32[4,32,1024]{2,1,0:T(8,128)S(1)}, f32[4,32,1024]{2,1,0:T(8,128)S(1)}) custom-call(f32[3,2,1024]{2,1,0:T(2,128)S(1)} %get-tuple-element.20.lines_ref.refs_0_, f32[4,16,32,256]{3,2,1,0:T(8,128)S(1)} %get-tuple-element.21.states_ref, bf16[976,1024]{1,0:T(8,128)(2,1)S(1)} %bitcast.8, bf16[32,1024]{1,0:T(8,128)(2,1)S(1)} %get-tuple-element.26.after_ref), custom_call_target="tpu_custom_call" | custom-call | flops 575000000 | bytes 262144 | tf_op jit(solution)/shard_map/local/pallas_call | solution.py:246
  16.8 0.0 copy-done.2
  16.9 0.0 copy-done.3
  16.9 0.0 copy-done.4
  16.9 0.8 %tables.1 = (bf16[8,256,256]{2,1,0:T(8,128)(2,1)S(1)}, f32[4,8,256]{2,1,0:T(8,128)S(1)}, bf16[2,256,128]{2,1,0:T(8,128)(2,1)S(1)}) custom-call(f32[1,16]{1,0:T(1,128)S(1)} %bitcast.13, s32[2,128]{1,0:T(2,128)S(1)} %copy-done.3, bf16[60,60]{1,0:T(8,128)(2,1)S(1)} %bitcast.12, f32[4,32,1024]{2,1,0:T(8,128)S(1)} %get-tuple-element.27.after_ref.own_ref), custom_call_target="tpu_custom_call" | custom-call | flops 460000000 | bytes 262144 | tf_op jit(solution)/shard_map/tables/pallas_call | solution.py:427
  17.7 0.0 collective-permute-done.7.refs_2_
  17.7 0.6 %collective-permute-start.8 = (bf16[32,1024]{1,0:T(8,128)(2,1)S(1)}, bf16[32,1024]{1,0:T(8,128)(2,1)S(1)}, u32[]{:S(2)}, u32[]{:S(2)}) collective-permute-start(bf16[32,1024]{1,0:T(8,128)(2,1)S(1)} %collective-permute-done.7.refs_2_), channel_id=1, source_target_pairs={{0,1},{1,0},{2,3},{3,2},{4,5},{5,4},{6,7},{7,6},{8,9},{9,8},{10,11... | collective-permute-start | bytes 196616 | tf_op jit(solution)/shard_map/ppermute | solution.py:640
  18.3 0.2 %collective-permute-done.5.refs_1_ = bf16[32,1024]{1,0:T(8,128)(2,1)S(1)} collective-permute-done((bf16[32,1024]{1,0:T(8,128)(2,1)S(1)}, bf16[32,1024]{1,0:T(8,128)(2,1)S(1)}, u32[]{:S(2)}, u32[]{:S(2)}) %collective-permute-start.5) | collective-permute-done | bytes 65568 | tf_op jit(solution)/shard_map/ppermute | solution.py:640
  18.5 0.0 collective-permute-start.6
  18.5 0.1 collective-permute-done.3.refs_0_
  18.6 0.4 %collective-permute-start.4 = (bf16[32,1024]{1,0:T(8,128)(2,1)S(1)}, bf16[32,1024]{1,0:T(8,128)(2,1)S(1)}, u32[]{:S(2)}, u32[]{:S(2)}) collective-permute-start(bf16[32,1024]{1,0:T(8,128)(2,1)S(1)} %collective-permute-done.3.refs_0_), channel_id=1, source_target_pairs={{0,1},{1,0},{2,3},{3,2},{4,5},{5,4},{6,7},{7,6},{8,9},{9,8},{10,11... | collective-permute-start | bytes 196616 | tf_op jit(solution)/shard_map/ppermute | solution.py:640
  19.0 0.8 %rows.1.base_ref = f32[244,1024]{1,0:T(8,128)S(1)} custom-call(f32[4,32,1024]{2,1,0:T(8,128)S(1)} %get-tuple-element.34.own_ref, f32[2,19,2,1024]{3,2,1,0:T(2,128)S(1)} %get-tuple-element.28.coef_ref, bf16[8,256,256]{2,1,0:T(8,128)(2,1)S(1)} %get-tuple-element.29.mat_ref, f32[4,8,256]{2,1,0:T(8,128)S(1)} %get-tuple-element.30.row_coef_ref, ...), custom_call_target="tpu_custom_call" | custom-call | flops 1380000000 | bytes 262144 | tf_op jit(solution)/shard_map/rows/pallas_call | solution.py:512
  19.8 0.0 collective-permute-done.8.last_3_ref
  19.8 0.0 collective-permute-done.6.last_2_ref
  19.8 0.1 collective-permute-done.4.last_1_ref
  19.9 0.0 collective-permute-done.2.part_ref
  19.9 0.8 %join.1.total_ref = f32[244,1024]{1,0:T(8,128)S(1)} custom-call(f32[4,32,1024]{2,1,0:T(8,128)S(1)} %get-tuple-element.27.after_ref.own_ref, f32[2,19,2,1024]{3,2,1,0:T(2,128)S(1)} %get-tuple-element.28.coef_ref, bf16[8,256,256]{2,1,0:T(8,128)(2,1)S(1)} %get-tuple-element.29.mat_ref, f32[4,8,256]{2,1,0:T(8,128)S(1)} %get-tuple-element.30.row_coef_ref, ...), custom_call_target="tpu_custom_call" | custom-call | flops 920000000 | bytes 262144 | tf_op jit(solution)/shard_map/join/pallas_call | solution.py:538
  20.7 0.2 collective-permute-done.9.came_ref
  20.9 0.9 %final.1 = bf16[61,4,1024]{2,1,0:T(4,128)(2,1)} custom-call(f32[244,1024]{1,0:T(8,128)S(1)} %join.1.total_ref, bf16[244,1024]{1,0:T(8,128)(2,1)S(1)} %collective-permute-done.9.came_ref), custom_call_target="tpu_custom_call" | custom-call | flops 920000000 | bytes 262144 | tf_op jit(solution)/shard_map/final/pallas_call | solution.py:568
  (1 shorter events, 0.0 us)
Async XLA Ops:
  0.0 5.1 %collective-permute-start.1 = (bf16[976,1024]{1,0:T(8,128)(2,1)}, bf16[976,1024]{1,0:T(8,128)(2,1)S(1)}, u32[]{:S(2)}, u32[]{:S(2)}) collective-permute-start(bf16[976,1024]{1,0:T(8,128)(2,1)} %bitcast.9), channel_id=1, source_target_pairs={{0,1},{1,0},{2,3},{3,2},{4,5},{5,4},{6,7},{7,6},{8,9},{9,8},{10,11... | collective-permute-start | bytes 5996552 | tf_op jit(solution)/shard_map/ppermute | solution.py:640
  0.5 4.7 %copy-start = (bf16[61,16,1024]{2,1,0:T(8,128)(2,1)S(1)}, bf16[61,16,1024]{2,1,0:T(8,128)(2,1)}, u32[]{:S(2)}) copy-start(bf16[61,16,1024]{2,1,0:T(8,128)(2,1)} %param.7) | copy-start | bytes 5996548
  0.5 4.7 %copy-start.1 = (bf16[1,61,16,1024]{3,2,1,0:T(8,128)(2,1)S(1)}, bf16[1,61,16,1024]{3,2,1,0:T(8,128)(2,1)}, u32[]{:S(2)}) copy-start(bf16[1,61,16,1024]{3,2,1,0:T(8,128)(2,1)} %param.13) | copy-start | bytes 5996548
  2.5 6.7 %collective-permute-start = (bf16[2,32,1024]{2,1,0:T(8,128)(2,1)S(1)}, bf16[2,32,1024]{2,1,0:T(8,128)(2,1)S(1)}, u32[]{:S(2)}, u32[]{:S(2)}) collective-permute-start(bf16[2,32,1024]{2,1,0:T(8,128)(2,1)S(1)} %get-tuple-element.22.after_ref.refs_1_), channel_id=1, source_target_pairs={{0,4},{4,0},{8,12},{12,8},{16,20},{20,16},{24,28},{28,24},{1,5},{5... | collective-permute-start | bytes 393224 | tf_op jit(solution)/shard_map/ppermute | solution.py:640
  6.9 14.0 %collective-permute-start.9 = (bf16[244,1024]{1,0:T(8,128)(2,1)S(1)}, bf16[244,1024]{1,0:T(8,128)(2,1)S(1)}, u32[]{:S(2)}, u32[]{:S(2)}) collective-permute-start(bf16[244,1024]{1,0:T(8,128)(2,1)S(1)} %send.1.after_ref), channel_id=1, source_target_pairs={{0,2},{1,3},{2,0},{3,1},{4,6},{5,7},{6,4},{7,5},{8,10},{9,11},{10,... | collective-permute-start | bytes 1499144 | tf_op jit(solution)/shard_map/ppermute | solution.py:640
  9.4 8.3 %collective-permute-start.7 = (bf16[32,1024]{1,0:T(8,128)(2,1)S(1)}, bf16[32,1024]{1,0:T(8,128)(2,1)S(1)}, u32[]{:S(2)}, u32[]{:S(2)}) collective-permute-start(bf16[32,1024]{1,0:T(8,128)(2,1)S(1)} %get-tuple-element.32), channel_id=1, source_target_pairs={{0,16},{4,20},{8,24},{12,28},{16,0},{20,4},{24,8},{28,12},{1,17},{... | collective-permute-start | bytes 196616 | tf_op jit(solution)/shard_map/ppermute | solution.py:640
  12.3 6.2 %collective-permute-start.5 = (bf16[32,1024]{1,0:T(8,128)(2,1)S(1)}, bf16[32,1024]{1,0:T(8,128)(2,1)S(1)}, u32[]{:S(2)}, u32[]{:S(2)}) collective-permute-start(bf16[32,1024]{1,0:T(8,128)(2,1)S(1)} %get-tuple-element.32), channel_id=1, source_target_pairs={{0,24},{4,28},{8,16},{12,20},{16,8},{20,12},{24,0},{28,4},{1,25},{... | collective-permute-start | bytes 196616 | tf_op jit(solution)/shard_map/ppermute | solution.py:640
  13.6 5.0 %collective-permute-start.3 = (bf16[32,1024]{1,0:T(8,128)(2,1)S(1)}, bf16[32,1024]{1,0:T(8,128)(2,1)S(1)}, u32[]{:S(2)}, u32[]{:S(2)}) collective-permute-start(bf16[32,1024]{1,0:T(8,128)(2,1)S(1)} %get-tuple-element.26.after_ref), channel_id=1, source_target_pairs={{0,8},{4,12},{8,0},{12,4},{16,24},{20,28},{24,16},{28,20},{1,9},{5... | collective-permute-start | bytes 196616 | tf_op jit(solution)/shard_map/ppermute | solution.py:640
  13.9 6.1 %collective-permute-start.2 = (bf16[2,32,1024]{2,1,0:T(8,128)(2,1)S(1)}, bf16[2,32,1024]{2,1,0:T(8,128)(2,1)S(1)}, u32[]{:S(2)}, u32[]{:S(2)}) collective-permute-start(bf16[2,32,1024]{2,1,0:T(8,128)(2,1)S(1)} %get-tuple-element.31.part_ref), channel_id=1, source_target_pairs={{0,1},{1,0},{2,3},{3,2},{4,5},{5,4},{6,7},{7,6},{8,9},{9,8},{10,11... | collective-permute-start | bytes 393224 | tf_op jit(solution)/shard_map/ppermute | solution.py:640
  15.8 1.1 %copy-start.2 = (bf16[1,60,60]{2,1,0:T(8,128)(2,1)S(1)}, bf16[1,60,60]{2,1,0:T(8,128)(2,1)}, u32[]{:S(2)}) copy-start(bf16[1,60,60]{2,1,0:T(8,128)(2,1)} %param.8) | copy-start | bytes 21604
  15.8 1.0 %copy-start.3 = (s32[2,128]{1,0:T(2,128)S(1)}, s32[2,128]{1,0:T(2,128)}, u32[]{:S(2)}) copy-start(s32[2,128]{1,0:T(2,128)} %entries_ref.1) | copy-start | bytes 3076
  15.8 1.0 %copy-start.4 = (f32[16]{0:T(128)S(1)}, f32[16]{0:T(128)}, u32[]{:S(2)}) copy-start(f32[16]{0:T(128)} %table_hbm.1) | copy-start | bytes 196
  17.7 2.2 %collective-permute-start.8 = (bf16[32,1024]{1,0:T(8,128)(2,1)S(1)}, bf16[32,1024]{1,0:T(8,128)(2,1)S(1)}, u32[]{:S(2)}, u32[]{:S(2)}) collective-permute-start(bf16[32,1024]{1,0:T(8,128)(2,1)S(1)} %collective-permute-done.7.refs_2_), channel_id=1, source_target_pairs={{0,1},{1,0},{2,3},{3,2},{4,5},{5,4},{6,7},{7,6},{8,9},{9,8},{10,11... | collective-permute-start | bytes 196616 | tf_op jit(solution)/shard_map/ppermute | solution.py:640
  18.5 1.3 %collective-permute-start.6 = (bf16[32,1024]{1,0:T(8,128)(2,1)S(1)}, bf16[32,1024]{1,0:T(8,128)(2,1)S(1)}, u32[]{:S(2)}, u32[]{:S(2)}) collective-permute-start(bf16[32,1024]{1,0:T(8,128)(2,1)S(1)} %collective-permute-done.5.refs_1_), channel_id=1, source_target_pairs={{0,1},{1,0},{2,3},{3,2},{4,5},{5,4},{6,7},{7,6},{8,9},{9,8},{10,11... | collective-permute-start | bytes 196616 | tf_op jit(solution)/shard_map/ppermute | solution.py:640
  18.6 1.3 %collective-permute-start.4 = (bf16[32,1024]{1,0:T(8,128)(2,1)S(1)}, bf16[32,1024]{1,0:T(8,128)(2,1)S(1)}, u32[]{:S(2)}, u32[]{:S(2)}) collective-permute-start(bf16[32,1024]{1,0:T(8,128)(2,1)S(1)} %collective-permute-done.3.refs_0_), channel_id=1, source_target_pairs={{0,1},{1,0},{2,3},{3,2},{4,5},{5,4},{6,7},{7,6},{8,9},{9,8},{10,11... | collective-permute-start | bytes 196616 | tf_op jit(solution)/shard_map/ppermute | solution.py:640

commit v14 on v12

--- a/solution.py
+++ b/solution.py
@@ -11,7 +11,7 @@
 SUB = 16
 CORES = 2
 LANES = 256
-ORDER = (1, 3, 2)
+ORDER = (3, 1, 2)
 FETCHES = 1
 BLOCK = 256
 MIB = 1 << 20

time: 22.1 us -> 22.1 us (level)
  no operation moved by 1% of the time
where the time goes in v14:
time: 22.1 us; the launch traced here: 21.8 us
  starting transfers between devices  10.6 us (48%)
  Pallas kernels  10.3 us (47%)
  waiting for transfers between devices  0.79 us (4%)
    ppermute x10, starting transfers between devices, swap(): lax.ppermute(array, axis, [(i, i ^ flip) for i in range(lax.axis_size(axi...  10.6 us
    pallas_call x1, Pallas kernels, ends_call(): pl.pallas_call(functools.partial(ends_kernel, levels, steps, total // col...  2.09 us
    pallas_call x1, Pallas kernels, keep_call(): pl.pallas_call(functools.partial(keep_kernel, cols), name='keep', in_spec...  1.94 us
    pallas_call x1, Pallas kernels, send_call(): pl.pallas_call(functools.partial(send_kernel, cols), name='send', in_spec...  1.77 us
    pallas_call x1, Pallas kernels, local_call(): pl.pallas_call(functools.partial(local_kernel, levels, total // cols), na...  1.02 us
    pallas_call x1, Pallas kernels, final_call(): pl.pallas_call(functools.partial(final_kernel, scale), name='final', in_s...  0.93 us
    pallas_call x1, Pallas kernels, rows_call(): pl.pallas_call(functools.partial(rows_kernel, levels, scale), name='rows'...  0.8 us
    pallas_call x1, Pallas kernels, join_call(): pl.pallas_call(functools.partial(join_kernel, levels), name='join', in_sp...  0.8 us
  transfers between devices with their start and end apart: 10, of which 5 were waited for; matrix products, arithmetic and copies ran while one was open for 0% of the time, Pallas kernels for 35%

profile of v14, /device:TPU:0, one launch (start us, length us, event | category | flops | bytes accessed | tf_op | source)
XLA Modules:
  0.0 21.8 jit_solution(6732118942085209314)
XLA Ops:
  0.0 0.5 %collective-permute-start.1 = (bf16[976,1024]{1,0:T(8,128)(2,1)}, bf16[976,1024]{1,0:T(8,128)(2,1)S(1)}, u32[]{:S(2)}, u32[]{:S(2)}) collective-permute-start(bf16[976,1024]{1,0:T(8,128)(2,1)} %bitcast.9), channel_id=1, source_target_pairs={{0,1},{1,0},{2,3},{3,2},{4,5},{5,4},{6,7},{7,6},{8,9},{9,8},{10,11... | collective-permute-start | bytes 5996552 | tf_op jit(solution)/shard_map/ppermute | solution.py:636
  0.5 0.0 copy-start
  0.5 0.0 copy-start.1
  0.5 2.1 %ends.1 = (bf16[2,32,1024]{2,1,0:T(8,128)(2,1)S(1)}, f32[4,16,32,256]{3,2,1,0:T(8,128)S(1)}, f32[3,2,1024]{2,1,0:T(2,128)S(1)}, bf16[64,256]{1,0:T(8,128)(2,1)S(...) custom-call(f32[16]{0:T(128)} %table_hbm.1, s32[2,1024]{1,0:T(2,128)} %entries_hbm.1, ...), custom_call_target="tpu_custom_call" | custom-call | flops 2415000064 | bytes 262144 | tf_op jit(solution)/shard_map/ends/pallas_call | solution.py:167
  2.6 2.6 %collective-permute-start = (bf16[2,32,1024]{2,1,0:T(8,128)(2,1)S(1)}, bf16[2,32,1024]{2,1,0:T(8,128)(2,1)S(1)}, u32[]{:S(2)}, u32[]{:S(2)}) collective-permute-start(bf16[2,32,1024]{2,1,0:T(8,128)(2,1)S(1)} %get-tuple-element.22.after_ref.refs_1_), channel_id=1, source_target_pairs={{0,4},{4,0},{8,12},{12,8},{16,20},{20,16},{24,28},{28,24},{1,5},{5... | collective-permute-start | bytes 393224 | tf_op jit(solution)/shard_map/ppermute | solution.py:636
  5.2 0.0 collective-permute-done.1.other_ref
  5.2 0.0 copy-done
  5.2 0.0 copy-done.1
  5.2 1.8 %send.1.after_ref = bf16[244,1024]{1,0:T(8,128)(2,1)S(1)} custom-call(bf16[64,256]{1,0:T(8,128)(2,1)S(1)} %get-tuple-element.23.perm_ref, bf16[256,256]{1,0:T(8,128)(2,1)S(1)} %get-tuple-element.24.local_ref, bf16[256,256]{1,0:T(8,128)(2,1)S(1)} %get-tuple-element.25.order_ref, bf16[976,1024]{1,0:T(8,128)(2,1)S(1)} %bitcast.6, ...), custom_call_target="tpu_custom_call" | custom-call | flops 2990000128 | bytes 262144 | tf_op jit(solution)/shard_map/send/pallas_call | solution.py:348
  6.9 2.1 %collective-permute-start.9 = (bf16[244,1024]{1,0:T(8,128)(2,1)S(1)}, bf16[244,1024]{1,0:T(8,128)(2,1)S(1)}, u32[]{:S(2)}, u32[]{:S(2)}) collective-permute-start(bf16[244,1024]{1,0:T(8,128)(2,1)S(1)} %send.1.after_ref), channel_id=1, source_target_pairs={{0,2},{1,3},{2,0},{3,1},{4,6},{5,7},{6,4},{7,5},{8,10},{9,11},{10,... | collective-permute-start | bytes 1499144 | tf_op jit(solution)/shard_map/ppermute | solution.py:636
  9.1 0.2 collective-permute-done.refs_2_
  9.3 0.1 merge.1
  9.4 2.9 %collective-permute-start.7 = (bf16[32,1024]{1,0:T(8,128)(2,1)S(1)}, bf16[32,1024]{1,0:T(8,128)(2,1)S(1)}, u32[]{:S(2)}, u32[]{:S(2)}) collective-permute-start(bf16[32,1024]{1,0:T(8,128)(2,1)S(1)} %get-tuple-element.32), channel_id=1, source_target_pairs={{0,16},{4,20},{8,24},{12,28},{16,0},{20,4},{24,8},{28,12},{1,17},{... | collective-permute-start | bytes 196616 | tf_op jit(solution)/shard_map/ppermute | solution.py:636
  12.3 1.4 %collective-permute-start.3 = (bf16[32,1024]{1,0:T(8,128)(2,1)S(1)}, bf16[32,1024]{1,0:T(8,128)(2,1)S(1)}, u32[]{:S(2)}, u32[]{:S(2)}) collective-permute-start(bf16[32,1024]{1,0:T(8,128)(2,1)S(1)} %get-tuple-element.32), channel_id=1, source_target_pairs={{0,24},{4,28},{8,16},{12,20},{16,8},{20,12},{24,0},{28,4},{1,25},{... | collective-permute-start | bytes 196616 | tf_op jit(solution)/shard_map/ppermute | solution.py:636
  13.6 0.2 %collective-permute-start.5 = (bf16[32,1024]{1,0:T(8,128)(2,1)S(1)}, bf16[32,1024]{1,0:T(8,128)(2,1)S(1)}, u32[]{:S(2)}, u32[]{:S(2)}) collective-permute-start(bf16[32,1024]{1,0:T(8,128)(2,1)S(1)} %get-tuple-element.26.after_ref), channel_id=1, source_target_pairs={{0,8},{4,12},{8,0},{12,4},{16,24},{20,28},{24,16},{28,20},{1,9},{5... | collective-permute-start | bytes 196616 | tf_op jit(solution)/shard_map/ppermute | solution.py:636
  13.9 0.0 collective-permute-start.2
  13.9 1.9 %keep.1.refs_4_ = f32[244,1024]{1,0:T(8,128)S(1)} custom-call(bf16[256,256]{1,0:T(8,128)(2,1)S(1)} %get-tuple-element.24.local_ref, bf16[256,256]{1,0:T(8,128)(2,1)S(1)} %get-tuple-element.25.order_ref, bf16[976,1024]{1,0:T(8,128)(2,1)S(1)} %bitcast.7, bf16[976,1024]{1,0:T(8,128)(2,1)S(1)} %bitcast.11, ...), custom_call_target="tpu_custom_call" | custom-call | flops 690000000 | bytes 262144 | tf_op jit(solution)/shard_map/keep/pallas_call | solution.py:364
  15.8 0.0 copy-start.2
  15.8 0.0 copy-start.3
  15.8 0.0 copy-start.4
  15.9 1.0 %local.1 = (f32[4,32,1024]{2,1,0:T(8,128)S(1)}, f32[4,32,1024]{2,1,0:T(8,128)S(1)}) custom-call(f32[3,2,1024]{2,1,0:T(2,128)S(1)} %get-tuple-element.20.lines_ref.refs_0_, f32[4,16,32,256]{3,2,1,0:T(8,128)S(1)} %get-tuple-element.21.states_ref, bf16[976,1024]{1,0:T(8,128)(2,1)S(1)} %bitcast.8, bf16[32,1024]{1,0:T(8,128)(2,1)S(1)} %get-tuple-element.26.after_ref), custom_call_target="tpu_custom_call" | custom-call | flops 575000000 | bytes 262144 | tf_op jit(solution)/shard_map/local/pallas_call | solution.py:242
  16.9 0.0 copy-done.2
  16.9 0.0 copy-done.3
  16.9 0.0 copy-done.4
  16.9 0.8 %tables.1 = (bf16[8,256,256]{2,1,0:T(8,128)(2,1)S(1)}, f32[4,8,256]{2,1,0:T(8,128)S(1)}, bf16[2,256,128]{2,1,0:T(8,128)(2,1)S(1)}) custom-call(f32[1,16]{1,0:T(1,128)S(1)} %bitcast.13, s32[2,128]{1,0:T(2,128)S(1)} %copy-done.3, bf16[60,60]{1,0:T(8,128)(2,1)S(1)} %bitcast.12, f32[4,32,1024]{2,1,0:T(8,128)S(1)} %get-tuple-element.27.after_ref.own_ref), custom_call_target="tpu_custom_call" | custom-call | flops 460000000 | bytes 262144 | tf_op jit(solution)/shard_map/tables/pallas_call | solution.py:423
  17.7 0.0 collective-permute-done.7.refs_2_
  17.7 0.6 %collective-permute-start.8 = (bf16[32,1024]{1,0:T(8,128)(2,1)S(1)}, bf16[32,1024]{1,0:T(8,128)(2,1)S(1)}, u32[]{:S(2)}, u32[]{:S(2)}) collective-permute-start(bf16[32,1024]{1,0:T(8,128)(2,1)S(1)} %collective-permute-done.7.refs_2_), channel_id=1, source_target_pairs={{0,1},{1,0},{2,3},{3,2},{4,5},{5,4},{6,7},{7,6},{8,9},{9,8},{10,11... | collective-permute-start | bytes 196616 | tf_op jit(solution)/shard_map/ppermute | solution.py:636
  18.3 0.2 %collective-permute-done.3.refs_0_ = bf16[32,1024]{1,0:T(8,128)(2,1)S(1)} collective-permute-done((bf16[32,1024]{1,0:T(8,128)(2,1)S(1)}, bf16[32,1024]{1,0:T(8,128)(2,1)S(1)}, u32[]{:S(2)}, u32[]{:S(2)}) %collective-permute-start.3) | collective-permute-done | bytes 65568 | tf_op jit(solution)/shard_map/ppermute | solution.py:636
  18.5 0.0 collective-permute-start.4
  18.5 0.1 collective-permute-done.5.refs_1_
  18.6 0.4 %collective-permute-start.6 = (bf16[32,1024]{1,0:T(8,128)(2,1)S(1)}, bf16[32,1024]{1,0:T(8,128)(2,1)S(1)}, u32[]{:S(2)}, u32[]{:S(2)}) collective-permute-start(bf16[32,1024]{1,0:T(8,128)(2,1)S(1)} %collective-permute-done.5.refs_1_), channel_id=1, source_target_pairs={{0,1},{1,0},{2,3},{3,2},{4,5},{5,4},{6,7},{7,6},{8,9},{9,8},{10,11... | collective-permute-start | bytes 196616 | tf_op jit(solution)/shard_map/ppermute | solution.py:636
  19.0 0.8 %rows.1.base_ref = f32[244,1024]{1,0:T(8,128)S(1)} custom-call(f32[4,32,1024]{2,1,0:T(8,128)S(1)} %get-tuple-element.34.own_ref, f32[2,19,2,1024]{3,2,1,0:T(2,128)S(1)} %get-tuple-element.28.coef_ref, bf16[8,256,256]{2,1,0:T(8,128)(2,1)S(1)} %get-tuple-element.29.mat_ref, f32[4,8,256]{2,1,0:T(8,128)S(1)} %get-tuple-element.30.row_coef_ref, ...), custom_call_target="tpu_custom_call" | custom-call | flops 1380000000 | bytes 262144 | tf_op jit(solution)/shard_map/rows/pallas_call | solution.py:508
  19.8 0.0 collective-permute-done.8.last_3_ref
  19.8 0.0 collective-permute-done.4.last_1_ref
  19.9 0.1 collective-permute-done.6.last_2_ref
  19.9 0.0 collective-permute-done.2.part_ref
  19.9 0.8 %join.1.total_ref = f32[244,1024]{1,0:T(8,128)S(1)} custom-call(f32[4,32,1024]{2,1,0:T(8,128)S(1)} %get-tuple-element.27.after_ref.own_ref, f32[2,19,2,1024]{3,2,1,0:T(2,128)S(1)} %get-tuple-element.28.coef_ref, bf16[8,256,256]{2,1,0:T(8,128)(2,1)S(1)} %get-tuple-element.29.mat_ref, f32[4,8,256]{2,1,0:T(8,128)S(1)} %get-tuple-element.30.row_coef_ref, ...), custom_call_target="tpu_custom_call" | custom-call | flops 920000000 | bytes 262144 | tf_op jit(solution)/shard_map/join/pallas_call | solution.py:534
  20.7 0.2 collective-permute-done.9.came_ref
  20.9 0.9 %final.1 = bf16[61,4,1024]{2,1,0:T(4,128)(2,1)} custom-call(f32[244,1024]{1,0:T(8,128)S(1)} %join.1.total_ref, bf16[244,1024]{1,0:T(8,128)(2,1)S(1)} %collective-permute-done.9.came_ref), custom_call_target="tpu_custom_call" | custom-call | flops 920000000 | bytes 262144 | tf_op jit(solution)/shard_map/final/pallas_call | solution.py:564
  (1 shorter events, 0.0 us)
Async XLA Ops:
  0.0 5.2 %collective-permute-start.1 = (bf16[976,1024]{1,0:T(8,128)(2,1)}, bf16[976,1024]{1,0:T(8,128)(2,1)S(1)}, u32[]{:S(2)}, u32[]{:S(2)}) collective-permute-start(bf16[976,1024]{1,0:T(8,128)(2,1)} %bitcast.9), channel_id=1, source_target_pairs={{0,1},{1,0},{2,3},{3,2},{4,5},{5,4},{6,7},{7,6},{8,9},{9,8},{10,11... | collective-permute-start | bytes 5996552 | tf_op jit(solution)/shard_map/ppermute | solution.py:636
  0.5 4.7 %copy-start = (bf16[61,16,1024]{2,1,0:T(8,128)(2,1)S(1)}, bf16[61,16,1024]{2,1,0:T(8,128)(2,1)}, u32[]{:S(2)}) copy-start(bf16[61,16,1024]{2,1,0:T(8,128)(2,1)} %param.7) | copy-start | bytes 5996548
  0.5 4.7 %copy-start.1 = (bf16[1,61,16,1024]{3,2,1,0:T(8,128)(2,1)S(1)}, bf16[1,61,16,1024]{3,2,1,0:T(8,128)(2,1)}, u32[]{:S(2)}) copy-start(bf16[1,61,16,1024]{3,2,1,0:T(8,128)(2,1)} %param.13) | copy-start | bytes 5996548
  2.6 6.7 %collective-permute-start = (bf16[2,32,1024]{2,1,0:T(8,128)(2,1)S(1)}, bf16[2,32,1024]{2,1,0:T(8,128)(2,1)S(1)}, u32[]{:S(2)}, u32[]{:S(2)}) collective-permute-start(bf16[2,32,1024]{2,1,0:T(8,128)(2,1)S(1)} %get-tuple-element.22.after_ref.refs_1_), channel_id=1, source_target_pairs={{0,4},{4,0},{8,12},{12,8},{16,20},{20,16},{24,28},{28,24},{1,5},{5... | collective-permute-start | bytes 393224 | tf_op jit(solution)/shard_map/ppermute | solution.py:636
  6.9 13.9 %collective-permute-start.9 = (bf16[244,1024]{1,0:T(8,128)(2,1)S(1)}, bf16[244,1024]{1,0:T(8,128)(2,1)S(1)}, u32[]{:S(2)}, u32[]{:S(2)}) collective-permute-start(bf16[244,1024]{1,0:T(8,128)(2,1)S(1)} %send.1.after_ref), channel_id=1, source_target_pairs={{0,2},{1,3},{2,0},{3,1},{4,6},{5,7},{6,4},{7,5},{8,10},{9,11},{10,... | collective-permute-start | bytes 1499144 | tf_op jit(solution)/shard_map/ppermute | solution.py:636
  9.4 8.3 %collective-permute-start.7 = (bf16[32,1024]{1,0:T(8,128)(2,1)S(1)}, bf16[32,1024]{1,0:T(8,128)(2,1)S(1)}, u32[]{:S(2)}, u32[]{:S(2)}) collective-permute-start(bf16[32,1024]{1,0:T(8,128)(2,1)S(1)} %get-tuple-element.32), channel_id=1, source_target_pairs={{0,16},{4,20},{8,24},{12,28},{16,0},{20,4},{24,8},{28,12},{1,17},{... | collective-permute-start | bytes 196616 | tf_op jit(solution)/shard_map/ppermute | solution.py:636
  12.3 6.2 %collective-permute-start.3 = (bf16[32,1024]{1,0:T(8,128)(2,1)S(1)}, bf16[32,1024]{1,0:T(8,128)(2,1)S(1)}, u32[]{:S(2)}, u32[]{:S(2)}) collective-permute-start(bf16[32,1024]{1,0:T(8,128)(2,1)S(1)} %get-tuple-element.32), channel_id=1, source_target_pairs={{0,24},{4,28},{8,16},{12,20},{16,8},{20,12},{24,0},{28,4},{1,25},{... | collective-permute-start | bytes 196616 | tf_op jit(solution)/shard_map/ppermute | solution.py:636
  13.6 5.0 %collective-permute-start.5 = (bf16[32,1024]{1,0:T(8,128)(2,1)S(1)}, bf16[32,1024]{1,0:T(8,128)(2,1)S(1)}, u32[]{:S(2)}, u32[]{:S(2)}) collective-permute-start(bf16[32,1024]{1,0:T(8,128)(2,1)S(1)} %get-tuple-element.26.after_ref), channel_id=1, source_target_pairs={{0,8},{4,12},{8,0},{12,4},{16,24},{20,28},{24,16},{28,20},{1,9},{5... | collective-permute-start | bytes 196616 | tf_op jit(solution)/shard_map/ppermute | solution.py:636
  13.9 6.1 %collective-permute-start.2 = (bf16[2,32,1024]{2,1,0:T(8,128)(2,1)S(1)}, bf16[2,32,1024]{2,1,0:T(8,128)(2,1)S(1)}, u32[]{:S(2)}, u32[]{:S(2)}) collective-permute-start(bf16[2,32,1024]{2,1,0:T(8,128)(2,1)S(1)} %get-tuple-element.31.part_ref), channel_id=1, source_target_pairs={{0,1},{1,0},{2,3},{3,2},{4,5},{5,4},{6,7},{7,6},{8,9},{9,8},{10,11... | collective-permute-start | bytes 393224 | tf_op jit(solution)/shard_map/ppermute | solution.py:636
  15.8 1.1 %copy-start.2 = (bf16[1,60,60]{2,1,0:T(8,128)(2,1)S(1)}, bf16[1,60,60]{2,1,0:T(8,128)(2,1)}, u32[]{:S(2)}) copy-start(bf16[1,60,60]{2,1,0:T(8,128)(2,1)} %param.8) | copy-start | bytes 21604
  15.8 1.1 %copy-start.3 = (s32[2,128]{1,0:T(2,128)S(1)}, s32[2,128]{1,0:T(2,128)}, u32[]{:S(2)}) copy-start(s32[2,128]{1,0:T(2,128)} %entries_ref.1) | copy-start | bytes 3076
  15.8 1.1 %copy-start.4 = (f32[16]{0:T(128)S(1)}, f32[16]{0:T(128)}, u32[]{:S(2)}) copy-start(f32[16]{0:T(128)} %table_hbm.1) | copy-start | bytes 196
  17.7 2.1 %collective-permute-start.8 = (bf16[32,1024]{1,0:T(8,128)(2,1)S(1)}, bf16[32,1024]{1,0:T(8,128)(2,1)S(1)}, u32[]{:S(2)}, u32[]{:S(2)}) collective-permute-start(bf16[32,1024]{1,0:T(8,128)(2,1)S(1)} %collective-permute-done.7.refs_2_), channel_id=1, source_target_pairs={{0,1},{1,0},{2,3},{3,2},{4,5},{5,4},{6,7},{7,6},{8,9},{9,8},{10,11... | collective-permute-start | bytes 196616 | tf_op jit(solution)/shard_map/ppermute | solution.py:636
  18.5 1.3 %collective-permute-start.4 = (bf16[32,1024]{1,0:T(8,128)(2,1)S(1)}, bf16[32,1024]{1,0:T(8,128)(2,1)S(1)}, u32[]{:S(2)}, u32[]{:S(2)}) collective-permute-start(bf16[32,1024]{1,0:T(8,128)(2,1)S(1)} %collective-permute-done.3.refs_0_), channel_id=1, source_target_pairs={{0,1},{1,0},{2,3},{3,2},{4,5},{5,4},{6,7},{7,6},{8,9},{9,8},{10,11... | collective-permute-start | bytes 196616 | tf_op jit(solution)/shard_map/ppermute | solution.py:636
  18.6 1.3 %collective-permute-start.6 = (bf16[32,1024]{1,0:T(8,128)(2,1)S(1)}, bf16[32,1024]{1,0:T(8,128)(2,1)S(1)}, u32[]{:S(2)}, u32[]{:S(2)}) collective-permute-start(bf16[32,1024]{1,0:T(8,128)(2,1)S(1)} %collective-permute-done.5.refs_1_), channel_id=1, source_target_pairs={{0,1},{1,0},{2,3},{3,2},{4,5},{5,4},{6,7},{7,6},{8,9},{9,8},{10,11... | collective-permute-start | bytes 196616 | tf_op jit(solution)/shard_map/ppermute | solution.py:636
